TPU v7x, 32 devices: a whole 2x2x4 slice. The times are simulated.
32 devices in a mesh: dp: 8 (over z, x), mp: 4 (over y, core).
Axes of the slice: x: 2, y: 2, z: 4, core: 2. Of those that a mesh axis runs over, the one named last changes fastest.
Arguments:
- observations: bfloat16 [26624, 2048], P('dp', 'mp'), may hold values from -140 to 140
- layer_weights: bfloat16 [2, 2048, 2048], P(None, 'dp', 'mp'), may hold values from -0.1875 to 0.1875
- head_weights: bfloat16 [2048, 18], P('mp'), may hold values from -0.1875 to 0.1875
- rewards: float32 [416, 64], P('dp'), may hold values from -6 to 6
- actions: int32 [416, 64], P('dp'), may hold values from 0 to 17
- done_flags: int32 [416, 64], P('dp'), may hold values 0 or 1
- behaviour: float32 [416, 64], P('dp'), may hold values from 0.05 to 1
Outputs:
- targets: float32 [416, 64], P('dp')
All inputs are finite; a program needn't handle non-finite values. No bound on the sum of `done_flags` on one device may be relied on, other than what follows from the above.
Results may differ from a plain program's by a relative error of at most 0.0056.
Values may be sent and summed in bfloat16 or wider, within the bound.
No kernel may reach another device: no remote copies, remote signals or barrier semaphores. Data moves between devices by JAX's collectives and lax.ppermute only.
A program may use at most 128 MiB of HBM per device.

v0:
```python
import jax
import jax.numpy as jnp
from jax import lax
from jax.sharding import PartitionSpec as P


def retrace(qvals, rewards, actions, done_flags, behaviour):
    seqs = rewards.shape[0]
    length = rewards.shape[1]
    actcount = qvals.shape[1]
    qvals = qvals.reshape(seqs, length, actcount)
    probs = jax.nn.softmax(4.0 * qvals, axis=-1)
    value = jnp.sum(probs * qvals, axis=-1)
    onehot = (actions[:, :, None] == jnp.arange(actcount, dtype=jnp.int32)[None, None, :]).astype(
        jnp.float32
    )
    taken = jnp.sum(onehot * qvals, axis=-1)
    chosen = jnp.sum(onehot * probs, axis=-1)
    trace = 0.95 * jnp.minimum(1.0, chosen / behaviour)
    keep = 0.99 * (1.0 - done_flags.astype(jnp.float32))

    def stepper(later, inputs):
        reward_t, keep_t, value_n, trace_n, taken_n = inputs
        now = reward_t + keep_t * (value_n + trace_n * (later - taken_n))
        return (now, now)

    inputs = (rewards[:, :-1].T, keep[:, :-1].T, value[:, 1:].T, trace[:, 1:].T, taken[:, 1:].T)
    last = taken[:, length - 1]
    final, earlier = lax.scan(stepper, last, inputs, reverse=True)
    return jnp.concatenate([earlier.T, last[:, None]], axis=1)


def per_device(observations, layer_weights, head_weights, rewards, actions, done_flags, behaviour):
    layers = layer_weights.shape[0]
    hidden = observations
    for layer in range(layers):
        current = lax.all_gather(hidden, "mp", axis=1, tiled=True)
        block = lax.all_gather(layer_weights[layer], "dp", axis=0, tiled=True)
        summed = jnp.dot(current, block, preferred_element_type=jnp.float32)
        hidden = jax.nn.relu(summed).astype(jnp.bfloat16)
    partial_q = jnp.dot(hidden, head_weights, preferred_element_type=jnp.float32)
    qvals = lax.psum(partial_q, "mp")
    return retrace(qvals, rewards, actions, done_flags, behaviour)


def solution(mesh):
    in_specs = (
        P("dp", "mp"),
        P(None, "dp", "mp"),
        P("mp", None),
        P("dp", None),
        P("dp", None),
        P("dp", None),
        P("dp", None),
    )
    out_specs = P("dp", None)
    return jax.shard_map(
        per_device, mesh=mesh, in_specs=in_specs, out_specs=out_specs, check_vma=False
    )
```

profile of v0, /device:TPU:0, one launch (start us, length us, event | category | flops | bytes accessed | tf_op | source)
XLA Modules:
  0.0 350.2 jit_solution(4185694826085557256)
XLA Ops:
  6.5 0.0 copy-start
  6.5 0.0 all-gather.11.cloned.1.call-start
  6.5 1.9 fusion.25
  8.4 0.0 all-gather.11.cloned.1.call-update
  8.4 0.0 all-gather.7.cloned.1.call-start
  8.5 0.7 all-gather.7.cloned.1.call-update
  9.2 0.0 all-gather.13.cloned.1.call-start
  9.2 0.7 all-gather.13.cloned.1.call-update
  9.9 0.0 copy-start.2
  9.9 0.0 all-gather.9.cloned.1.call-start
  10.0 51.5 %all-gather.11.cloned.1.call-done = bf16[1,2048,512]{2,1,0:T(8,128)(2,1)} async-done(((bf16[1,256,512]{2,1,0:T(8,128)(2,1)}), bf16[1,2048,512]{2,1,0:T(8,128)(2,1)}) %all-gather.11.cloned.1.call-update) | async-done | bytes 2097168 | tf_op jit(solution)/shard_map/all_gather | solution.py:38
  61.5 88.1 %all-gather.7.cloned.1.call-done = bf16[3328,2048]{1,0:T(8,128)(2,1)} async-done(((bf16[3328,512]{1,0:T(8,128)(2,1)}), bf16[3328,2048]{1,0:T(8,128)(2,1)}) %all-gather.7.cloned.1.call-update) | async-done | bytes 13631504 | tf_op jit(solution)/shard_map/all_gather | solution.py:37
  149.7 13.9 %fusion.10 = bf16[3328,512]{1,0:T(8,128)(2,1)} fusion(bf16[3328,2048]{1,0:T(8,128)(2,1)} %all-gather.7.cloned.1.call-done, bf16[1,2048,512]{2,1,0:T(8,128)(2,1)} %all-gather.11.cloned.1.call-done), kind=kOutput, calls=%fused_computation.17 | convolution fusion | flops 6982729728 | bytes 19136512 | tf_op jit(solution)/shard_map/dot_general | solution.py:39
  163.5 0.0 all-gather.9.cloned.1.call-update
  163.6 0.0 all-reduce.2.cloned.1.call-start
  163.6 0.0 copy-done.2
  163.6 0.1 eq.17
  163.7 0.0 copy-start.1
  163.7 0.0 copy-start.3
  163.7 0.0 copy-start.4
  163.7 37.4 %all-gather.13.cloned.1.call-done = bf16[1,2048,512]{2,1,0:T(8,128)(2,1)} async-done(((bf16[1,256,512]{2,1,0:T(8,128)(2,1)}), bf16[1,2048,512]{2,1,0:T(8,128)(2,1)}) %all-gather.13.cloned.1.call-update) | async-done | bytes 2097168 | tf_op jit(solution)/shard_map/all_gather | solution.py:38
  201.1 88.0 %all-gather.9.cloned.1.call-done = bf16[3328,2048]{1,0:T(8,128)(2,1)} async-done(((bf16[3328,512]{1,0:T(8,128)(2,1)}), bf16[3328,2048]{1,0:T(8,128)(2,1)}) %all-gather.9.cloned.1.call-update) | async-done | bytes 13631504 | tf_op jit(solution)/shard_map/all_gather | solution.py:37
  289.1 0.0 copy-done
  289.1 12.4 %fusion.12 = f32[3328,18]{0,1:T(8,128)} fusion(bf16[512,18]{0,1:T(8,128)(2,1)S(1)} %copy-done, bf16[3328,2048]{1,0:T(8,128)(2,1)} %all-gather.9.cloned.1.call-done, bf16[1,2048,512]{2,1,0:T(8,128)(2,1)} %all-gather.13.cloned.1.call-done), kind=kOutput, calls=%fused_computation.19 | convolution fusion | flops 7044071424 | bytes 15986688 | tf_op jit(solution)/shard_map/dot_general | solution.py:41
  301.5 0.0 all-reduce.2.cloned.1.call-update
  301.5 0.0 copy-done.1
  301.5 0.1 copy.14
  301.6 0.0 copy-done.3
  301.6 0.1 copy.19
  301.7 32.0 %all-reduce.2.cloned.1.call-done = f32[3328,18]{0,1:T(8,128)} async-done(((f32[3328,18]{0,1:T(8,128)}), f32[3328,18]{0,1:T(8,128)}) %all-reduce.2.cloned.1.call-update) | async-done | bytes 239632 | tf_op jit(solution)/shard_map/psum | solution.py:42
  333.8 1.0 multiply_reduce_fusion.1
  334.8 1.1 fusion.17
  335.8 1.2 select_reduce_fusion
  337.0 0.1 reduce_sum.43
  337.1 0.2 slice_reduce_fusion
  337.3 0.1 slice_bitcast_fusion
  337.4 0.1 copy.17
  337.5 0.1 reduce_sum.46
  337.5 0.1 slice_bitcast_fusion.1
  337.6 0.1 copy.15
  337.7 0.1 reduce_sum.48
  337.8 0.0 copy-done.4
  337.8 0.1 fusion.20
  337.9 0.1 copy.16
  338.0 4.9 %while.16 = (s32[]{:T(128)}, f32[52]{0:T(128)S(1)}, f32[63,52]{1,0:T(8,128)S(1)}, f32[63,52]{1,0:T(8,128)S(1)}, f32[63,52]{1,0:T(8,128)S(1)}, /*index=5*/f32[63,...) while((s32[]{:T(128)}, f32[52]{0:T(128)S(1)}, ...), condition=%wide.region_7.8_spmd, body=%wide.region_6.7_spmd.sunk | while | flops 263 | bytes 2001 | solution.py:29
  342.9 0.1 copy.18
  343.0 0.7 pad_maximum_fusion
  (128 shorter events, 4.0 us)
Async XLA Ops:
  6.5 282.6 %copy-start = (bf16[512,18]{0,1:T(8,128)(2,1)S(1)}, bf16[512,18]{0,1:T(8,128)(2,1)}, u32[]{:S(2)}) copy-start(bf16[512,18]{0,1:T(8,128)(2,1)} %param.11) | copy-start | bytes 55300
  6.5 55.0 %all-gather.11.cloned.1.call-start = ((), (), s32[]{:S(2)}) async-start(), calls=%async_computation.3 | async-start | bytes 2359296 | tf_op jit(solution)/shard_map/all_gather | solution.py:38
  8.4 141.2 %all-gather.7.cloned.1.call-start = ((), (), s32[]{:S(2)}) async-start(), calls=%async_computation | async-start | bytes 17039360 | tf_op jit(solution)/shard_map/all_gather | solution.py:37
  9.2 191.9 %all-gather.13.cloned.1.call-start = ((), (), s32[]{:S(2)}) async-start(), calls=%async_computation.4 | async-start | bytes 2359296 | tf_op jit(solution)/shard_map/all_gather | solution.py:38
  9.9 153.7 %copy-start.2 = (s32[52,64]{1,0:T(8,128)S(1)}, s32[52,64]{1,0:T(8,128)}, u32[]{:S(2)}) copy-start(s32[52,64]{1,0:T(8,128)} %param.13) | copy-start | bytes 39940
  9.9 279.2 %all-gather.9.cloned.1.call-start = ((), (), s32[]{:S(2)}) async-start(), calls=%async_computation.1 | async-start | bytes 17039360 | tf_op jit(solution)/shard_map/all_gather | solution.py:37
  163.6 170.2 %all-reduce.2.cloned.1.call-start = ((), (), s32[]{:S(2)}) async-start(), calls=%async_computation.2 | async-start | bytes 638976 | tf_op jit(solution)/shard_map/psum | solution.py:42
  163.7 137.8 %copy-start.1 = (s32[52,64]{1,0:T(8,128)S(1)}, s32[52,64]{1,0:T(8,128)}, u32[]{:S(2)}) copy-start(s32[52,64]{1,0:T(8,128)} %param.14) | copy-start | bytes 39940
  163.7 137.9 %copy-start.3 = (f32[52,64]{1,0:T(8,128)S(1)}, f32[52,64]{1,0:T(8,128)}, u32[]{:S(2)}) copy-start(f32[52,64]{1,0:T(8,128)} %param.12) | copy-start | bytes 39940
  163.7 174.1 %copy-start.4 = (f32[52,64]{1,0:T(8,128)S(1)}, f32[52,64]{1,0:T(8,128)}, u32[]{:S(2)}) copy-start(f32[52,64]{1,0:T(8,128)} %param.15) | copy-start | bytes 39940
Sparse Core Ops, SparseCore 0:
  9.5 51.9 all-gather.10
  63.1 86.5 all-gather.6
  151.8 49.2 all-gather.12
  202.5 86.5 all-gather.8
  301.6 32.0 all-reduce.1
where the time goes:
time: 350 us
  waiting for transfers between devices  299 us (85%)
  matrix products  26.3 us (8%)
  between operations  13.2 us (4%)
  local copies, waits for them, and re-layouts  5.6 us (2%)
  other arithmetic  5.56 us (2%)
    all_gather x2, waiting for transfers between devices, per_device(): current = lax.all_gather(hidden, 'mp', axis=1, tiled=True)  176 us
    all_gather x2, waiting for transfers between devices, per_device(): block = lax.all_gather(layer_weights[layer], 'dp', axis=0, tiled=True)  88.9 us
    psum x1, waiting for transfers between devices, per_device(): qvals = lax.psum(partial_q, 'mp')  32 us
    dot_general x1, matrix products, per_device(): summed = jnp.dot(current, block, preferred_element_type=jnp.float32)  13.9 us
    dot_general x1, matrix products, per_device(): jnp.dot(hidden, head_weights, preferred_element_type=jnp.float32)  12.4 us
  transfers between devices with their start and end apart: 5, of which 5 were waited for; matrix products, arithmetic and copies ran while one was open for 4% of the time, Pallas kernels for 0%

commit v1 on v0

v1 whole, which is shorter than its diff:
```python
import functools

import jax
import jax.numpy as jnp
from jax import lax
from jax.experimental import pallas as pl
from jax.experimental.pallas import tpu as pltpu
from jax.sharding import PartitionSpec as P

LANES = 128


def tiles_of(rows, target):
    unit = LANES if rows % LANES == 0 else rows
    units = rows // unit
    count = max(1, -(-units * unit // target))
    sizes = [units // count + (1 if i < units % count else 0) for i in range(count)]
    starts = [sum(sizes[:i]) for i in range(count)]
    return [(s * unit, n * unit) for s, n in zip(starts, sizes) if n]


def layer_kernel(h_blocks, w_blocks, tiles, headed, added, *refs):
    refs = list(refs)
    pos = refs.pop(0)
    hs = [refs.pop(0) for _ in h_blocks]
    ws = [refs.pop(0) for _ in w_blocks]
    head = refs.pop(0) if headed else None
    before = refs.pop(0) if added else None
    out = refs.pop(0)
    hv, wv = refs.pop(0), refs.pop(0)
    ov = None if headed else refs.pop(0)
    hsem, wsem = refs.pop(0), refs.pop(0)
    osem = None if headed else refs.pop(0)

    at = 0
    w_copies = []
    for w, count in zip(ws, w_blocks):
        _, height, width = w.shape
        for j in range(count):
            row, col = pos[2 * at], pos[2 * at + 1]
            copy = pltpu.make_async_copy(
                w.at[j],
                wv.at[pl.ds(pl.multiple_of(row * height, height), height), pl.ds(pl.multiple_of(col * width, width), width)],
                wsem.at[at],
            )
            copy.start()
            w_copies.append(copy)
            at += 1
    h_copies = []
    base = 2 * at
    for t, (start, size) in enumerate(tiles):
        row_copies = []
        at = 0
        for h, count in zip(hs, h_blocks):
            width = h.shape[1] // count
            for j in range(count):
                col = pos[base + at]
                copy = pltpu.make_async_copy(
                    h.at[pl.ds(start, size), pl.ds(j * width, width)],
                    hv.at[pl.ds(start, size), pl.ds(pl.multiple_of(col * width, width), width)],
                    hsem.at[t, at],
                )
                copy.start()
                row_copies.append(copy)
                at += 1
        h_copies.append(row_copies)
    for copy in w_copies:
        copy.wait()
    out_copies = []
    for t, (start, size) in enumerate(tiles):
        for copy in h_copies[t]:
            copy.wait()
        summed = jnp.dot(hv[pl.ds(start, size), :], wv[...], preferred_element_type=jnp.float32)
        hidden = jnp.maximum(summed, 0.0).astype(jnp.bfloat16)
        if headed:
            part = lax.dot_general(head[...], hidden, (((1,), (1,)), ((), ())), preferred_element_type=jnp.float32)
            if added:
                part = part + before[:, pl.ds(start, size)]
            out[:, pl.ds(start, size)] = part
        else:
            ov[pl.ds(start, size), :] = hidden
            copy = pltpu.make_async_copy(ov.at[pl.ds(start, size)], out.at[pl.ds(start, size)], osem.at[t])
            copy.start()
            out_copies.append(copy)
    for copy in out_copies:
        copy.wait()


def layer(pos, hs, h_blocks, ws, depth, width, head=None, before=None):
    rows = hs[0].shape[0]
    w_blocks = tuple(w.shape[0] for w in ws)
    tiles = tiles_of(rows, 416)
    headed, added = head is not None, before is not None
    vmem = pl.BlockSpec(memory_space=pltpu.VMEM)
    anywhere = pl.BlockSpec(memory_space=pl.ANY)
    scratch = [pltpu.VMEM((rows, depth), jnp.bfloat16), pltpu.VMEM((depth, width), jnp.bfloat16)]
    if not headed:
        scratch.append(pltpu.VMEM((rows, width), jnp.bfloat16))
    scratch += [pltpu.SemaphoreType.DMA((len(tiles), sum(h_blocks))), pltpu.SemaphoreType.DMA((sum(w_blocks),))]
    if not headed:
        scratch.append(pltpu.SemaphoreType.DMA((len(tiles),)))
    if headed:
        out_shape = jax.ShapeDtypeStruct((head.shape[0], rows), jnp.float32)
    else:
        out_shape = jax.ShapeDtypeStruct((rows, width), jnp.bfloat16)
    extra = ([head] if headed else []) + ([before] if added else [])
    return pl.pallas_call(
        functools.partial(layer_kernel, h_blocks, w_blocks, tiles, headed, added),
        out_shape=out_shape,
        in_specs=[pl.BlockSpec(memory_space=pltpu.SMEM)] + [anywhere] * (len(hs) + len(ws)) + [vmem] * len(extra),
        out_specs=vmem if headed else anywhere,
        scratch_shapes=scratch,
        compiler_params=pltpu.CompilerParams(vmem_limit_bytes=48 * 1024 * 1024),
        cost_estimate=pl.CostEstimate(
            flops=2 * rows * depth * width, bytes_accessed=2 * (rows * depth + depth * width + rows * width), transcendentals=0
        ),
    )(pos, *hs, *ws, *extra)


def retrace_kernel(length, q0, q1, rewards, actions, done_flags, behaviour, out):
    q = q0[...] + q1[...]
    count, steps = q.shape
    scaled = 4.0 * q
    weights = jnp.exp(scaled - jnp.max(scaled, axis=0, keepdims=True))
    probs = weights / jnp.sum(weights, axis=0, keepdims=True)
    value = jnp.sum(probs * q, axis=0, keepdims=True)
    hit = lax.broadcasted_iota(jnp.int32, (count, steps), 0) == actions[...]
    taken = jnp.sum(jnp.where(hit, q, 0.0), axis=0, keepdims=True)
    chosen = jnp.sum(jnp.where(hit, probs, 0.0), axis=0, keepdims=True)
    trace = 0.95 * jnp.minimum(1.0, chosen / behaviour[...])
    keep = 0.99 * (1.0 - done_flags[...].astype(jnp.float32))

    def later(x, by):
        return pltpu.roll(x, steps - by, axis=1)

    last = lax.broadcasted_iota(jnp.int32, (1, steps), 1) % length == length - 1
    factor = jnp.where(last, 0.0, keep * later(trace, 1))
    offset = jnp.where(last, taken, rewards[...] + keep * later(value - trace * taken, 1))
    by = 1
    while by < length:
        offset = offset + factor * later(offset, by)
        factor = factor * later(factor, by)
        by *= 2
    out[...] = offset


def retrace(q0, q1, rewards, actions, done_flags, behaviour):
    seqs, length = rewards.shape
    flat = [x.reshape(1, seqs * length) for x in (rewards, actions, done_flags, behaviour)]
    out = pl.pallas_call(
        functools.partial(retrace_kernel, length),
        out_shape=jax.ShapeDtypeStruct((1, seqs * length), jnp.float32),
        in_specs=[pl.BlockSpec(memory_space=pltpu.VMEM)] * 6,
        out_specs=pl.BlockSpec(memory_space=pltpu.VMEM),
    )(q0, q1, *flat)
    return out.reshape(seqs, length)


def per_device(dp, mp, observations, layer_weights, head_weights, rewards, actions, done_flags, behaviour):
    across = mp // 2
    lines = dp // 2
    rank, group = lax.axis_index("mp"), lax.axis_index("dp")
    y, core = rank // 2, rank % 2
    z, x = group // 2, group % 2

    def to_core(a):
        return lax.ppermute(a, "mp", [(i, i ^ 1) for i in range(mp)])

    def to_y(a):
        return lax.ppermute(a, "mp", [(i, i ^ 2) for i in range(mp)])

    def to_x(a):
        return lax.ppermute(a, "dp", [(i, i ^ 1) for i in range(dp)])

    def to_z(a):
        return lax.ppermute(a, "dp", [(i, (i + 2) % dp) for i in range(dp)])

    def place(step, x_flip, y_flip):
        return [((z - step) % lines) * 2 + (x ^ x_flip), y ^ y_flip]

    width = layer_weights.shape[2]
    half = width // 2
    rows = observations.shape[0] // 2

    def y_z_x(own):
        ring = [jnp.concatenate([own, to_y(own)], axis=0)]
        for _ in range(lines - 1):
            ring.append(to_z(ring[-1]))
        pieces, places = [], []
        for step, piece in enumerate(ring):
            pieces += [piece, to_x(piece)]
            for x_flip in (0, 1):
                places += place(step, x_flip, 0) + place(step, x_flip, 1)
        return pieces, places

    def z_x_y(own):
        ring = [own]
        for _ in range(lines - 1):
            ring.append(to_z(ring[-1]))
        near = jnp.concatenate(ring, axis=0)
        far = to_x(near)
        pieces, places = [near, far, to_y(near), to_y(far)], []
        for y_flip in (0, 1):
            for x_flip in (0, 1):
                for step in range(lines):
                    places += place(step, x_flip, y_flip)
        return pieces, places

    first, first_places = y_z_x(layer_weights[:1])
    second_a, second_a_places = y_z_x(layer_weights[1:2, :, :half])
    second_b, second_b_places = z_x_y(layer_weights[1:2, :, half:])

    kept = lax.dynamic_slice_in_dim(observations, y * rows, rows)
    sent = lax.dynamic_slice_in_dim(observations, (1 - y) * rows, rows)
    came = to_y(sent)
    h0 = [kept, to_core(kept), came, to_core(came)]
    h0_places = [rank, rank ^ 1, rank ^ 2, rank ^ 3]

    depth = observations.shape[1] * mp
    h1 = layer(jnp.stack(first_places + h0_places), h0, (1, 1, 1, 1), first, depth, across * width)
    hs = [h1, to_core(h1)]
    h_blocks = (across, across)
    h1_places = [2 * i + core for i in range(across)] + [2 * i + 1 - core for i in range(across)]

    head = head_weights.T
    head_other = to_y(head)
    head_low = jnp.where(y == 0, head, head_other)
    head_high = jnp.where(y == 0, head_other, head)
    head_a = jnp.concatenate([head_low[:, :half], head_high[:, :half]], axis=1)
    head_b = jnp.concatenate([head_low[:, half:], head_high[:, half:]], axis=1)

    q_a = layer(jnp.stack(second_a_places + h1_places), hs, h_blocks, second_a, depth, across * half, head_a)
    q = layer(jnp.stack(second_b_places + h1_places), hs, h_blocks, second_b, depth, across * half, head_b, q_a)

    seqs = rewards.shape[0] // 2
    mine = [lax.dynamic_slice_in_dim(a, y * seqs, seqs) for a in (rewards, actions, done_flags, behaviour)]
    own = retrace(q, to_core(q), *mine)
    other = to_y(own)
    return jnp.concatenate([jnp.where(y == 0, own, other), jnp.where(y == 0, other, own)], axis=0)


def solution(mesh):
    in_specs = (
        P("dp", "mp"),
        P(None, "dp", "mp"),
        P("mp", None),
        P("dp", None),
        P("dp", None),
        P("dp", None),
        P("dp", None),
    )
    out_specs = P("dp", None)
    return jax.shard_map(
        functools.partial(per_device, mesh.shape["dp"], mesh.shape["mp"]),
        mesh=mesh,
        in_specs=in_specs,
        out_specs=out_specs,
        check_vma=False,
    )
```

time: 350 us -> 211 us (0.60)
  waiting for transfers between devices: 299 us -> 150 us
  Pallas kernels: 0 us -> 28.6 us
  matrix products: 26.3 us -> 0 us
  starting transfers between devices: 0.16 us -> 20.6 us
  between operations: 13.2 us -> 0.24 us
  local copies, waits for them, and re-layouts: 5.6 us -> 9.94 us
  other arithmetic: 5.56 us -> 1.5 us
    all_gather x4 -> x0, waiting for transfers between devices: 265 us -> none  [the longest x2 176 us: per_device(): current = lax.all_gather(hidden, 'mp', axis=1, tiled=True)]
    ppermute x0 -> x29, waiting for transfers between devices: none -> 150 us  [the longest x9 57 us: to_z(): return lax.ppermute(a, 'dp', [(i, (i + 2) % dp) for i in range(dp)])]
    psum x1 -> x0, waiting for transfers between devices: 32 us -> none  [per_device(): qvals = lax.psum(partial_q, 'mp')]
    pallas_call x0 -> x4, Pallas kernels: none -> 28.6 us  [the longest x3 26.3 us: layer(): pl.pallas_call(functools.partial(layer_kernel, h_blocks, w_blocks, tiles,...]
    dot_general x2 -> x0, matrix products: 26.3 us -> none  [the longest x1 13.9 us: per_device(): summed = jnp.dot(current, block, preferred_element_type=jnp.float32)]
    ppermute x0 -> x29, starting transfers between devices: none -> 20.6 us  [the longest x9 9.5 us: to_x(): return lax.ppermute(a, 'dp', [(i, i ^ 1) for i in range(dp)])]
    unnamed x11 -> x26, local copies, waits for them, and re-layouts: 0.12 us -> 4.53 us
  transfers between devices with their start and end apart: 5 -> 29, of which waited for: 5 -> 18; matrix products, arithmetic and copies ran while one was open for 4% -> 2% of each run, Pallas kernels for 0% -> 3%
where the time goes in v1:
time: 211 us
  waiting for transfers between devices  150 us (71%)
  Pallas kernels  28.6 us (14%)
  starting transfers between devices  20.6 us (10%)
  local copies, waits for them, and re-layouts  9.94 us (5%)
    ppermute x9, waiting for transfers between devices, to_z(): return lax.ppermute(a, 'dp', [(i, (i + 2) % dp) for i in range(dp)])  57 us
    ppermute x7, waiting for transfers between devices, to_y(): return lax.ppermute(a, 'mp', [(i, i ^ 2) for i in range(mp)])  53 us
    ppermute x9, waiting for transfers between devices, to_x(): return lax.ppermute(a, 'dp', [(i, i ^ 1) for i in range(dp)])  40 us
    pallas_call x3, Pallas kernels, layer(): pl.pallas_call(functools.partial(layer_kernel, h_blocks, w_blocks, tiles,...  26.3 us
    ppermute x9, starting transfers between devices, to_x(): return lax.ppermute(a, 'dp', [(i, i ^ 1) for i in range(dp)])  9.5 us
    ppermute x7, starting transfers between devices, to_y(): return lax.ppermute(a, 'mp', [(i, i ^ 2) for i in range(mp)])  8.16 us
    unnamed x26, local copies, waits for them, and re-layouts  4.53 us
  transfers between devices with their start and end apart: 29, of which 18 were waited for; matrix products, arithmetic and copies ran while one was open for 2% of the time, Pallas kernels for 3%

profile of v1, /device:TPU:0, one launch (start us, length us, event | category | flops | bytes accessed | tf_op | source)
XLA Modules:
  0.0 210.9 jit_solution(5675091559291532515)
XLA Ops:
  0.0 2.2 %constant_dynamic-slice_fusion.4 = (bf16[1664,512]{1,0:T(8,128)(2,1)S(1)}, bf16[1664,512]{1,0:T(8,128)(2,1)S(1)}) fusion(bf16[3328,512]{1,0:T(8,128)(2,1)} %param.7, s32[]{:T(128)S(6)} %select_n.168, s32[]{:T(128)S(6)} %select_n.167), kind=kLoop, calls=%fused_computation.14 | loop fusion | bytes 6815752 | tf_op jit(solution)/shard_map/dynamic_slice | solution.py:214
  2.2 3.0 %collective-permute-start.1 = (bf16[1664,512]{1,0:T(8,128)(2,1)S(1)}, bf16[1664,512]{1,0:T(8,128)(2,1)}, u32[]{:S(2)}, u32[]{:S(2)}) collective-permute-start(bf16[1664,512]{1,0:T(8,128)(2,1)S(1)} %get-tuple-element.5), channel_id=1, source_target_pairs={{0,2},{1,3},{2,0},{3,1},{4,6},{5,7},{6,4},{7,5},{8,10},{9,11},{10,... | collective-permute-start | bytes 5111816 | tf_op jit(solution)/shard_map/ppermute | solution.py:170
  5.3 0.1 collective-permute-start.3
  5.4 42.7 %collective-permute-done.3 = bf16[1,256,512]{2,1,0:T(8,128)(2,1)S(1)} collective-permute-done((bf16[1,256,512]{2,1,0:T(8,128)(2,1)S(1)}, bf16[1,256,512]{2,1,0:T(8,128)(2,1)S(1)}, u32[]{:S(2)}, u32[]{:S(2)}) %collective-permute-start.3) | collective-permute-done | bytes 262176 | tf_op jit(solution)/shard_map/ppermute | solution.py:170
  48.1 0.1 pad_maximum_fusion.refs_5_
  48.2 1.8 collective-permute-start.5
  50.0 0.5 collective-permute-start.2
  50.5 12.6 %collective-permute-done.5.refs_7_ = bf16[2,256,512]{2,1,0:T(8,128)(2,1)S(1)} collective-permute-done((bf16[2,256,512]{2,1,0:T(8,128)(2,1)S(1)}, bf16[2,256,512]{2,1,0:T(8,128)(2,1)S(1)}, u32[]{:S(2)}, u32[]{:S(2)}) %collective-permute-start.5) | collective-permute-done | bytes 524320 | tf_op jit(solution)/shard_map/ppermute | solution.py:176
  63.1 1.5 collective-permute-start.4
  64.6 12.5 %collective-permute-done.7.refs_9_ = bf16[2,256,512]{2,1,0:T(8,128)(2,1)S(1)} collective-permute-done((bf16[2,256,512]{2,1,0:T(8,128)(2,1)S(1)}, bf16[2,256,512]{2,1,0:T(8,128)(2,1)S(1)}, u32[]{:S(2)}, u32[]{:S(2)}) %collective-permute-start.7) | collective-permute-done | bytes 524320 | tf_op jit(solution)/shard_map/ppermute | solution.py:176
  77.1 1.2 collective-permute-start.6
  78.3 0.8 copy-done.3
  79.1 0.8 collective-permute-start.8
  79.9 10.3 %collective-permute-done.9.refs_11_ = bf16[2,256,512]{2,1,0:T(8,128)(2,1)} collective-permute-done((bf16[2,256,512]{2,1,0:T(8,128)(2,1)S(1)}, bf16[2,256,512]{2,1,0:T(8,128)(2,1)}, u32[]{:S(2)}, u32[]{:S(2)}) %collective-permute-start.9) | collective-permute-done | bytes 524320 | tf_op jit(solution)/shard_map/ppermute | solution.py:176
  90.3 1.0 collective-permute-start.10
  91.2 0.1 stack.61.refs_0_
  91.3 0.7 collective-permute-done.6.refs_8_
  92.1 11.2 %collective-permute-done.8.refs_10_ = bf16[2,256,512]{2,1,0:T(8,128)(2,1)} collective-permute-done((bf16[2,256,512]{2,1,0:T(8,128)(2,1)S(1)}, bf16[2,256,512]{2,1,0:T(8,128)(2,1)}, u32[]{:S(2)}, u32[]{:S(2)}) %collective-permute-start.8) | collective-permute-done | bytes 524320 | tf_op jit(solution)/shard_map/ppermute | solution.py:173
  103.3 7.6 %collective-permute-done.10.refs_12_ = bf16[2,256,512]{2,1,0:T(8,128)(2,1)} collective-permute-done((bf16[2,256,512]{2,1,0:T(8,128)(2,1)}, bf16[2,256,512]{2,1,0:T(8,128)(2,1)}, u32[]{:S(2)}, u32[]{:S(2)}) %collective-permute-start.10) | collective-permute-done | bytes 524320 | tf_op jit(solution)/shard_map/ppermute | solution.py:173
  110.9 1.0 copy-done.4
  112.0 11.6 %shard_map.73.refs_1_ = bf16[1664,1024]{1,0:T(8,128)(2,1)} custom-call(s32[36]{0:T(128)S(1)} %stack.61.refs_0_, bf16[1664,512]{1,0:T(8,128)(2,1)S(1)} %get-tuple-element.6.refs_1_, bf16[1664,512]{1,0:T(8,128)(2,1)} %collective-permute-done.refs_2_, bf16[1664,512]{1,0:T(8,128)(2,1)} %collective-permute-done.1.refs_3_, ...), custom_call_target="tpu_custom_call" | custom-call | flops 6979321856 | bytes 14417920 | tf_op jit(solution)/shard_map/pallas_call | solution.py:107
  123.6 0.0 copy-start.8
  123.7 0.1 collective-permute-start.11
  123.8 1.0 collective-permute-start.19
  124.8 4.9 %collective-permute-done.19 = bf16[1,256,256]{2,1,0:T(8,128)(2,1)S(1)} collective-permute-done((bf16[1,256,256]{2,1,0:T(8,128)(2,1)S(1)}, bf16[1,256,256]{2,1,0:T(8,128)(2,1)S(1)}, u32[]{:S(2)}, u32[]{:S(2)}) %collective-permute-start.19) | collective-permute-done | bytes 131104 | tf_op jit(solution)/shard_map/ppermute | solution.py:170
  129.8 0.1 collective-permute-start.21
  129.8 2.4 %collective-permute-done.12 = bf16[1,256,256]{2,1,0:T(8,128)(2,1)S(1)} collective-permute-done((bf16[1,256,256]{2,1,0:T(8,128)(2,1)S(1)}, bf16[1,256,256]{2,1,0:T(8,128)(2,1)S(1)}, u32[]{:S(2)}, u32[]{:S(2)}) %collective-permute-start.12) | collective-permute-done | bytes 131104 | tf_op jit(solution)/shard_map/ppermute | solution.py:176
  132.2 10.1 %collective-permute-done.13 = bf16[1,256,256]{2,1,0:T(8,128)(2,1)S(1)} collective-permute-done((bf16[1,256,256]{2,1,0:T(8,128)(2,1)S(1)}, bf16[1,256,256]{2,1,0:T(8,128)(2,1)S(1)}, u32[]{:S(2)}, u32[]{:S(2)}) %collective-permute-start.13) | collective-permute-done | bytes 131104 | tf_op jit(solution)/shard_map/ppermute | solution.py:176
  142.3 0.4 collective-permute-start.23
  142.7 7.8 %collective-permute-done.14 = bf16[1,256,256]{2,1,0:T(8,128)(2,1)S(1)} collective-permute-done((bf16[1,256,256]{2,1,0:T(8,128)(2,1)S(1)}, bf16[1,256,256]{2,1,0:T(8,128)(2,1)S(1)}, u32[]{:S(2)}, u32[]{:S(2)}) %collective-permute-start.14) | collective-permute-done | bytes 131104 | tf_op jit(solution)/shard_map/ppermute | solution.py:176
  150.6 0.1 pad_maximum_fusion.1.refs_3_
  150.6 1.0 collective-permute-start.15
  151.7 1.1 collective-permute-start.20
  152.7 1.2 collective-permute-done.23.refs_7_
  154.0 1.0 collective-permute-start.18
  155.0 0.1 stack.62.refs_0_
  155.1 0.1 stack.56.refs_0_
  155.2 2.6 %collective-permute-done.18 = bf16[18,512]{1,0:T(8,128)(2,1)S(1)} collective-permute-done((bf16[18,512]{1,0:T(8,128)(2,1)S(1)}, bf16[18,512]{1,0:T(8,128)(2,1)S(1)}, u32[]{:S(2)}, u32[]{:S(2)}) %collective-permute-start.18) | collective-permute-done | bytes 18464 | tf_op jit(solution)/shard_map/ppermute | solution.py:170
  157.8 1.0 collective-permute-start.22
  158.8 12.4 %collective-permute-done.20.refs_4_ = bf16[2,256,256]{2,1,0:T(8,128)(2,1)S(1)} collective-permute-done((bf16[2,256,256]{2,1,0:T(8,128)(2,1)S(1)}, bf16[2,256,256]{2,1,0:T(8,128)(2,1)S(1)}, u32[]{:S(2)}, u32[]{:S(2)}) %collective-permute-start.20) | collective-permute-done | bytes 262176 | tf_op jit(solution)/shard_map/ppermute | solution.py:173
  171.2 1.0 collective-permute-start.24
  172.1 1.1 collective-permute-start.26
  173.2 3.6 %collective-permute-done.22.refs_6_ = bf16[2,256,256]{2,1,0:T(8,128)(2,1)S(1)} collective-permute-done((bf16[2,256,256]{2,1,0:T(8,128)(2,1)S(1)}, bf16[2,256,256]{2,1,0:T(8,128)(2,1)S(1)}, u32[]{:S(2)}, u32[]{:S(2)}) %collective-permute-start.22) | collective-permute-done | bytes 262176 | tf_op jit(solution)/shard_map/ppermute | solution.py:173
  176.8 1.0 collective-permute-start.16
  177.8 1.0 collective-permute-start.17
  178.8 1.5 collective-permute-done.24.refs_8_
  180.4 2.8 %collective-permute-done.26.refs_10_ = bf16[2,256,256]{2,1,0:T(8,128)(2,1)S(1)} collective-permute-done((bf16[2,256,256]{2,1,0:T(8,128)(2,1)S(1)}, bf16[2,256,256]{2,1,0:T(8,128)(2,1)S(1)}, u32[]{:S(2)}, u32[]{:S(2)}) %collective-permute-start.26) | collective-permute-done | bytes 262176 | tf_op jit(solution)/shard_map/ppermute | solution.py:173
  183.2 2.0 copy-done.1
  185.2 7.4 %shard_map.74.refs_8_ = f32[18,1664]{1,0:T(8,128)S(1)} custom-call(s32[36]{0:T(128)S(1)} %stack.62.refs_0_, bf16[1664,1024]{1,0:T(8,128)(2,1)S(1)} %copy-done.1, bf16[1664,1024]{1,0:T(8,128)(2,1)} %collective-permute-done.11.refs_2_, bf16[2,256,256]{2,1,0:T(8,128)(2,1)S(1)} %pad_maximum_fusion.2.refs_3_, ...), custom_call_target="tpu_custom_call" | custom-call | flops 3489660928 | bytes 10616832 | tf_op jit(solution)/shard_map/pallas_call | solution.py:107
  192.5 0.0 copy-start.9
  192.6 0.0 copy-start.12
  192.6 7.3 %shard_map.75.q0 = f32[18,1664]{1,0:T(8,128)S(1)} custom-call(s32[36]{0:T(128)S(1)} %stack.56.refs_0_, bf16[1664,1024]{1,0:T(8,128)(2,1)S(1)} %copy-done.2, bf16[1664,1024]{1,0:T(8,128)(2,1)} %collective-permute-done.11.refs_2_, bf16[4,256,256]{2,1,0:T(8,128)(2,1)S(1)} %pad_maximum_fusion.1.refs_3_, ...), custom_call_target="tpu_custom_call" | custom-call | flops 3489660928 | bytes 10616832 | tf_op jit(solution)/shard_map/pallas_call | solution.py:107
  200.0 0.1 collective-permute-start.27
  200.1 0.7 reshape.15.rewards
  200.8 0.7 reshape.16.actions
  201.5 0.7 reshape.17.done_flags
  202.1 0.7 reshape.18.behaviour
  202.8 0.7 copy-done.7
  203.5 2.3 %shard_map.76 = f32[1,1664]{1,0:T(1,128)} custom-call(f32[18,1664]{1,0:T(8,128)} %copy-done, f32[18,1664]{1,0:T(8,128)} %copy-done.7, f32[1,1664]{1,0:T(1,128)} %reshape.15.rewards, s32[1,1664]{1,0:T(1,128)} %reshape.16.actions, s32[1,1664]{1,0:T(1,128)} %reshape.17.done_flags, f32[1,1664]{1,0:T(1,128)} %reshape.18.behaviour), custom_call_target="tpu_custom_call" | custom-call | tf_op jit(solution)/shard_map/pallas_call | solution.py:150
  205.8 0.7 reduce
  206.5 0.1 reshape.19
  206.5 1.0 collective-permute-start.28
  207.5 2.8 %collective-permute-done.28 = f32[26,64]{1,0:T(8,128)S(1)} collective-permute-done((f32[26,64]{1,0:T(8,128)S(1)}, f32[26,64]{1,0:T(8,128)S(1)}, u32[]{:S(2)}, u32[]{:S(2)}) %collective-permute-start.28) | collective-permute-done | bytes 6688 | tf_op jit(solution)/shard_map/ppermute | solution.py:170
  210.3 0.6 pad_maximum_fusion.3
  (47 shorter events, 0.2 us)
Async XLA Ops:
  0.0 5.3 %copy-start.5 = (bf16[2,256,512]{2,1,0:T(8,128)(2,1)S(1)}, bf16[2,256,512]{2,1,0:T(8,128)(2,1)}, u32[]{:S(2)}) copy-start(bf16[2,256,512]{2,1,0:T(8,128)(2,1)} %param.8) | copy-start | bytes 1572868
  2.2 47.8 %collective-permute-start.1 = (bf16[1664,512]{1,0:T(8,128)(2,1)S(1)}, bf16[1664,512]{1,0:T(8,128)(2,1)}, u32[]{:S(2)}, u32[]{:S(2)}) collective-permute-start(bf16[1664,512]{1,0:T(8,128)(2,1)S(1)} %get-tuple-element.5), channel_id=1, source_target_pairs={{0,2},{1,3},{2,0},{3,1},{4,6},{5,7},{6,4},{7,5},{8,10},{9,11},{10,... | collective-permute-start | bytes 5111816 | tf_op jit(solution)/shard_map/ppermute | solution.py:170
  5.3 42.8 %collective-permute-start.3 = (bf16[1,256,512]{2,1,0:T(8,128)(2,1)S(1)}, bf16[1,256,512]{2,1,0:T(8,128)(2,1)S(1)}, u32[]{:S(2)}, u32[]{:S(2)}) collective-permute-start(bf16[1,256,512]{2,1,0:T(8,128)(2,1)S(1)} %slice.21), channel_id=1, source_target_pairs={{0,2},{1,3},{2,0},{3,1},{4,6},{5,7},{6,4},{7,5},{8,10},{9,11},{10,... | collective-permute-start | bytes 786440 | tf_op jit(solution)/shard_map/ppermute | solution.py:170
  48.2 15.0 %collective-permute-start.5 = (bf16[2,256,512]{2,1,0:T(8,128)(2,1)S(1)}, bf16[2,256,512]{2,1,0:T(8,128)(2,1)S(1)}, u32[]{:S(2)}, u32[]{:S(2)}) collective-permute-start(bf16[2,256,512]{2,1,0:T(8,128)(2,1)S(1)} %pad_maximum_fusion.refs_5_), channel_id=1, source_target_pairs={{0,8},{4,12},{8,16},{12,20},{16,24},{20,28},{24,0},{28,4},{1,9},{5... | collective-permute-start | bytes 1572872 | tf_op jit(solution)/shard_map/ppermute | solution.py:176
  50.0 42.1 %collective-permute-start = (bf16[1664,512]{1,0:T(8,128)(2,1)S(1)}, bf16[1664,512]{1,0:T(8,128)(2,1)}, u32[]{:S(2)}, u32[]{:S(2)}) collective-permute-start(bf16[1664,512]{1,0:T(8,128)(2,1)S(1)} %get-tuple-element.6.refs_1_), channel_id=1, source_target_pairs={{0,1},{1,0},{2,3},{3,2},{4,5},{5,4},{6,7},{7,6},{8,9},{9,8},{10,11... | collective-permute-start | bytes 5111816 | tf_op jit(solution)/shard_map/ppermute | solution.py:167
  50.0 60.9 %collective-permute-start.2 = (bf16[1664,512]{1,0:T(8,128)(2,1)}, bf16[1664,512]{1,0:T(8,128)(2,1)}, u32[]{:S(2)}, u32[]{:S(2)}) collective-permute-start(bf16[1664,512]{1,0:T(8,128)(2,1)} %collective-permute-done.1.refs_3_), channel_id=1, source_target_pairs={{0,1},{1,0},{2,3},{3,2},{4,5},{5,4},{6,7},{7,6},{8,9},{9,8},{10,11... | collective-permute-start | bytes 5111816 | tf_op jit(solution)/shard_map/ppermute | solution.py:167
  63.1 14.0 %collective-permute-start.7 = (bf16[2,256,512]{2,1,0:T(8,128)(2,1)S(1)}, bf16[2,256,512]{2,1,0:T(8,128)(2,1)S(1)}, u32[]{:S(2)}, u32[]{:S(2)}) collective-permute-start(bf16[2,256,512]{2,1,0:T(8,128)(2,1)S(1)} %collective-permute-done.5.refs_7_), channel_id=1, source_target_pairs={{0,8},{4,12},{8,16},{12,20},{16,24},{20,28},{24,0},{28,4},{1,9},{5... | collective-permute-start | bytes 1572872 | tf_op jit(solution)/shard_map/ppermute | solution.py:176
  63.1 15.2 %collective-permute-start.4 = (bf16[2,256,512]{2,1,0:T(8,128)(2,1)S(1)}, bf16[2,256,512]{2,1,0:T(8,128)(2,1)S(1)}, u32[]{:S(2)}, u32[]{:S(2)}) collective-permute-start(bf16[2,256,512]{2,1,0:T(8,128)(2,1)S(1)} %pad_maximum_fusion.refs_5_), channel_id=1, source_target_pairs={{0,4},{4,0},{8,12},{12,8},{16,20},{20,16},{24,28},{28,24},{1,5},{5... | collective-permute-start | bytes 1572872 | tf_op jit(solution)/shard_map/ppermute | solution.py:173
  77.1 13.2 %collective-permute-start.9 = (bf16[2,256,512]{2,1,0:T(8,128)(2,1)S(1)}, bf16[2,256,512]{2,1,0:T(8,128)(2,1)}, u32[]{:S(2)}, u32[]{:S(2)}) collective-permute-start(bf16[2,256,512]{2,1,0:T(8,128)(2,1)S(1)} %collective-permute-done.7.refs_9_), channel_id=1, source_target_pairs={{0,8},{4,12},{8,16},{12,20},{16,24},{20,28},{24,0},{28,4},{1,9},{5... | collective-permute-start | bytes 1572872 | tf_op jit(solution)/shard_map/ppermute | solution.py:176
  77.1 15.0 %collective-permute-start.6 = (bf16[2,256,512]{2,1,0:T(8,128)(2,1)S(1)}, bf16[2,256,512]{2,1,0:T(8,128)(2,1)}, u32[]{:S(2)}, u32[]{:S(2)}) collective-permute-start(bf16[2,256,512]{2,1,0:T(8,128)(2,1)S(1)} %collective-permute-done.5.refs_7_), channel_id=1, source_target_pairs={{0,4},{4,0},{8,12},{12,8},{16,20},{20,16},{24,28},{28,24},{1,5},{5... | collective-permute-start | bytes 1572872 | tf_op jit(solution)/shard_map/ppermute | solution.py:173
  78.3 0.8 copy-start.3
  79.1 24.2 %collective-permute-start.8 = (bf16[2,256,512]{2,1,0:T(8,128)(2,1)S(1)}, bf16[2,256,512]{2,1,0:T(8,128)(2,1)}, u32[]{:S(2)}, u32[]{:S(2)}) collective-permute-start(bf16[2,256,512]{2,1,0:T(8,128)(2,1)S(1)} %collective-permute-done.7.refs_9_), channel_id=1, source_target_pairs={{0,4},{4,0},{8,12},{12,8},{16,20},{20,16},{24,28},{28,24},{1,5},{5... | collective-permute-start | bytes 1572872 | tf_op jit(solution)/shard_map/ppermute | solution.py:173
  90.3 20.7 %collective-permute-start.10 = (bf16[2,256,512]{2,1,0:T(8,128)(2,1)}, bf16[2,256,512]{2,1,0:T(8,128)(2,1)}, u32[]{:S(2)}, u32[]{:S(2)}) collective-permute-start(bf16[2,256,512]{2,1,0:T(8,128)(2,1)} %collective-permute-done.9.refs_11_), channel_id=1, source_target_pairs={{0,4},{4,0},{8,12},{12,8},{16,20},{20,16},{24,28},{28,24},{1,5},{5... | collective-permute-start | bytes 1572872 | tf_op jit(solution)/shard_map/ppermute | solution.py:173
  110.9 1.0 copy-start.4
  112.0 11.7 %copy-start.6 = (bf16[2,256,512]{2,1,0:T(8,128)(2,1)S(1)}, bf16[2,256,512]{2,1,0:T(8,128)(2,1)}, u32[]{:S(2)}) copy-start(bf16[2,256,512]{2,1,0:T(8,128)(2,1)} %param.8) | copy-start | bytes 1572868
  123.6 30.3 %copy-start.8 = (bf16[512,18]{0,1:T(8,128)(2,1)S(1)}, bf16[512,18]{0,1:T(8,128)(2,1)}, u32[]{:S(2)}) copy-start(bf16[512,18]{0,1:T(8,128)(2,1)} %param.9) | copy-start | bytes 55300
  123.7 59.5 %collective-permute-start.11 = (bf16[1664,1024]{1,0:T(8,128)(2,1)}, bf16[1664,1024]{1,0:T(8,128)(2,1)}, u32[]{:S(2)}, u32[]{:S(2)}) collective-permute-start(bf16[1664,1024]{1,0:T(8,128)(2,1)} %shard_map.73.refs_1_), channel_id=1, source_target_pairs={{0,1},{1,0},{2,3},{3,2},{4,5},{5,4},{6,7},{7,6},{8,9},{9,8},{10,11... | collective-permute-start | bytes 10223624 | tf_op jit(solution)/shard_map/ppermute | solution.py:167
  123.8 6.0 %collective-permute-start.19 = (bf16[1,256,256]{2,1,0:T(8,128)(2,1)S(1)}, bf16[1,256,256]{2,1,0:T(8,128)(2,1)S(1)}, u32[]{:S(2)}, u32[]{:S(2)}) collective-permute-start(bf16[1,256,256]{2,1,0:T(8,128)(2,1)S(1)} %get-tuple-element.7), channel_id=1, source_target_pairs={{0,2},{1,3},{2,0},{3,1},{4,6},{5,7},{6,4},{7,5},{8,10},{9,11},{10,... | collective-permute-start | bytes 393224 | tf_op jit(solution)/shard_map/ppermute | solution.py:170
  124.8 7.4 %collective-permute-start.12 = (bf16[1,256,256]{2,1,0:T(8,128)(2,1)S(1)}, bf16[1,256,256]{2,1,0:T(8,128)(2,1)S(1)}, u32[]{:S(2)}, u32[]{:S(2)}) collective-permute-start(bf16[1,256,256]{2,1,0:T(8,128)(2,1)S(1)} %get-tuple-element.8), channel_id=1, source_target_pairs={{0,8},{4,12},{8,16},{12,20},{16,24},{20,28},{24,0},{28,4},{1,9},{5... | collective-permute-start | bytes 393224 | tf_op jit(solution)/shard_map/ppermute | solution.py:176
  129.8 12.6 %collective-permute-start.21 = (bf16[2,256,256]{2,1,0:T(8,128)(2,1)S(1)}, bf16[2,256,256]{2,1,0:T(8,128)(2,1)S(1)}, u32[]{:S(2)}, u32[]{:S(2)}) collective-permute-start(bf16[2,256,256]{2,1,0:T(8,128)(2,1)S(1)} %pad_maximum_fusion.2.refs_3_), channel_id=1, source_target_pairs={{0,8},{4,12},{8,16},{12,20},{16,24},{20,28},{24,0},{28,4},{1,9},{5... | collective-permute-start | bytes 786440 | tf_op jit(solution)/shard_map/ppermute | solution.py:176
  132.2 10.1 %collective-permute-start.13 = (bf16[1,256,256]{2,1,0:T(8,128)(2,1)S(1)}, bf16[1,256,256]{2,1,0:T(8,128)(2,1)S(1)}, u32[]{:S(2)}, u32[]{:S(2)}) collective-permute-start(bf16[1,256,256]{2,1,0:T(8,128)(2,1)S(1)} %collective-permute-done.12), channel_id=1, source_target_pairs={{0,8},{4,12},{8,16},{12,20},{16,24},{20,28},{24,0},{28,4},{1,9},{5... | collective-permute-start | bytes 393224 | tf_op jit(solution)/shard_map/ppermute | solution.py:176
  142.3 8.2 %collective-permute-start.14 = (bf16[1,256,256]{2,1,0:T(8,128)(2,1)S(1)}, bf16[1,256,256]{2,1,0:T(8,128)(2,1)S(1)}, u32[]{:S(2)}, u32[]{:S(2)}) collective-permute-start(bf16[1,256,256]{2,1,0:T(8,128)(2,1)S(1)} %collective-permute-done.13), channel_id=1, source_target_pairs={{0,8},{4,12},{8,16},{12,20},{16,24},{20,28},{24,0},{28,4},{1,9},{5... | collective-permute-start | bytes 393224 | tf_op jit(solution)/shard_map/ppermute | solution.py:176
  142.3 11.6 %collective-permute-start.23 = (bf16[2,256,256]{2,1,0:T(8,128)(2,1)S(1)}, bf16[2,256,256]{2,1,0:T(8,128)(2,1)S(1)}, u32[]{:S(2)}, u32[]{:S(2)}) collective-permute-start(bf16[2,256,256]{2,1,0:T(8,128)(2,1)S(1)} %collective-permute-done.21.refs_5_), channel_id=1, source_target_pairs={{0,8},{4,12},{8,16},{12,20},{16,24},{20,28},{24,0},{28,4},{1,9},{5... | collective-permute-start | bytes 786440 | tf_op jit(solution)/shard_map/ppermute | solution.py:176
  150.6 27.1 %collective-permute-start.15 = (bf16[4,256,256]{2,1,0:T(8,128)(2,1)S(1)}, bf16[4,256,256]{2,1,0:T(8,128)(2,1)S(1)}, u32[]{:S(2)}, u32[]{:S(2)}) collective-permute-start(bf16[4,256,256]{2,1,0:T(8,128)(2,1)S(1)} %pad_maximum_fusion.1.refs_3_), channel_id=1, source_target_pairs={{0,4},{4,0},{8,12},{12,8},{16,20},{20,16},{24,28},{28,24},{1,5},{5... | collective-permute-start | bytes 1572872 | tf_op jit(solution)/shard_map/ppermute | solution.py:173
  151.7 19.5 %collective-permute-start.20 = (bf16[2,256,256]{2,1,0:T(8,128)(2,1)S(1)}, bf16[2,256,256]{2,1,0:T(8,128)(2,1)S(1)}, u32[]{:S(2)}, u32[]{:S(2)}) collective-permute-start(bf16[2,256,256]{2,1,0:T(8,128)(2,1)S(1)} %pad_maximum_fusion.2.refs_3_), channel_id=1, source_target_pairs={{0,4},{4,0},{8,12},{12,8},{16,20},{20,16},{24,28},{28,24},{1,5},{5... | collective-permute-start | bytes 786440 | tf_op jit(solution)/shard_map/ppermute | solution.py:173
  154.0 18.2 %collective-permute-start.25 = (bf16[2,256,256]{2,1,0:T(8,128)(2,1)S(1)}, bf16[2,256,256]{2,1,0:T(8,128)(2,1)S(1)}, u32[]{:S(2)}, u32[]{:S(2)}) collective-permute-start(bf16[2,256,256]{2,1,0:T(8,128)(2,1)S(1)} %collective-permute-done.23.refs_7_), channel_id=1, source_target_pairs={{0,8},{4,12},{8,16},{12,20},{16,24},{20,28},{24,0},{28,4},{1,9},{5... | collective-permute-start | bytes 786440 | tf_op jit(solution)/shard_map/ppermute | solution.py:176
  154.0 3.8 %collective-permute-start.18 = (bf16[18,512]{1,0:T(8,128)(2,1)S(1)}, bf16[18,512]{1,0:T(8,128)(2,1)S(1)}, u32[]{:S(2)}, u32[]{:S(2)}) collective-permute-start(bf16[18,512]{1,0:T(8,128)(2,1)S(1)} %bitcast.21), channel_id=1, source_target_pairs={{0,2},{1,3},{2,0},{3,1},{4,6},{5,7},{6,4},{7,5},{8,10},{9,11},{10,... | collective-permute-start | bytes 55304 | tf_op jit(solution)/shard_map/ppermute | solution.py:170
  157.8 19.0 %collective-permute-start.22 = (bf16[2,256,256]{2,1,0:T(8,128)(2,1)S(1)}, bf16[2,256,256]{2,1,0:T(8,128)(2,1)S(1)}, u32[]{:S(2)}, u32[]{:S(2)}) collective-permute-start(bf16[2,256,256]{2,1,0:T(8,128)(2,1)S(1)} %collective-permute-done.21.refs_5_), channel_id=1, source_target_pairs={{0,4},{4,0},{8,12},{12,8},{16,20},{20,16},{24,28},{28,24},{1,5},{5... | collective-permute-start | bytes 786440 | tf_op jit(solution)/shard_map/ppermute | solution.py:173
  171.2 9.2 %collective-permute-start.24 = (bf16[2,256,256]{2,1,0:T(8,128)(2,1)S(1)}, bf16[2,256,256]{2,1,0:T(8,128)(2,1)S(1)}, u32[]{:S(2)}, u32[]{:S(2)}) collective-permute-start(bf16[2,256,256]{2,1,0:T(8,128)(2,1)S(1)} %collective-permute-done.23.refs_7_), channel_id=1, source_target_pairs={{0,4},{4,0},{8,12},{12,8},{16,20},{20,16},{24,28},{28,24},{1,5},{5... | collective-permute-start | bytes 786440 | tf_op jit(solution)/shard_map/ppermute | solution.py:173
  172.1 11.1 %collective-permute-start.26 = (bf16[2,256,256]{2,1,0:T(8,128)(2,1)S(1)}, bf16[2,256,256]{2,1,0:T(8,128)(2,1)S(1)}, u32[]{:S(2)}, u32[]{:S(2)}) collective-permute-start(bf16[2,256,256]{2,1,0:T(8,128)(2,1)S(1)} %collective-permute-done.25.refs_9_), channel_id=1, source_target_pairs={{0,4},{4,0},{8,12},{12,8},{16,20},{20,16},{24,28},{28,24},{1,5},{5... | collective-permute-start | bytes 786440 | tf_op jit(solution)/shard_map/ppermute | solution.py:173
  176.8 15.8 %collective-permute-start.16 = (bf16[4,256,256]{2,1,0:T(8,128)(2,1)S(1)}, bf16[4,256,256]{2,1,0:T(8,128)(2,1)S(1)}, u32[]{:S(2)}, u32[]{:S(2)}) collective-permute-start(bf16[4,256,256]{2,1,0:T(8,128)(2,1)S(1)} %pad_maximum_fusion.1.refs_3_), channel_id=1, source_target_pairs={{0,2},{1,3},{2,0},{3,1},{4,6},{5,7},{6,4},{7,5},{8,10},{9,11},{10,... | collective-permute-start | bytes 1572872 | tf_op jit(solution)/shard_map/ppermute | solution.py:170
  177.8 14.8 %collective-permute-start.17 = (bf16[4,256,256]{2,1,0:T(8,128)(2,1)S(1)}, bf16[4,256,256]{2,1,0:T(8,128)(2,1)S(1)}, u32[]{:S(2)}, u32[]{:S(2)}) collective-permute-start(bf16[4,256,256]{2,1,0:T(8,128)(2,1)S(1)} %collective-permute-done.15.refs_4_), channel_id=1, source_target_pairs={{0,2},{1,3},{2,0},{3,1},{4,6},{5,7},{6,4},{7,5},{8,10},{9,11},{10,... | collective-permute-start | bytes 1572872 | tf_op jit(solution)/shard_map/ppermute | solution.py:170
  183.2 2.0 copy-start.1
  185.2 7.5 %copy-start.2 = (bf16[1664,1024]{1,0:T(8,128)(2,1)S(1)}, bf16[1664,1024]{1,0:T(8,128)(2,1)}, u32[]{:S(2)}) copy-start(bf16[1664,1024]{1,0:T(8,128)(2,1)} %shard_map.73.refs_1_) | copy-start | bytes 10223620
  192.5 7.5 %copy-start.9 = (f32[52,64]{1,0:T(8,128)S(1)}, f32[52,64]{1,0:T(8,128)}, u32[]{:S(2)}) copy-start(f32[52,64]{1,0:T(8,128)} %param.13) | copy-start | bytes 39940
  192.6 7.5 %copy-start.10 = (f32[52,64]{1,0:T(8,128)S(1)}, f32[52,64]{1,0:T(8,128)}, u32[]{:S(2)}) copy-start(f32[52,64]{1,0:T(8,128)} %param.10) | copy-start | bytes 39940
  192.6 8.2 %copy-start.11 = (s32[52,64]{1,0:T(8,128)S(1)}, s32[52,64]{1,0:T(8,128)}, u32[]{:S(2)}) copy-start(s32[52,64]{1,0:T(8,128)} %param.12) | copy-start | bytes 39940
  192.6 8.2 %copy-start.12 = (s32[52,64]{1,0:T(8,128)S(1)}, s32[52,64]{1,0:T(8,128)}, u32[]{:S(2)}) copy-start(s32[52,64]{1,0:T(8,128)} %param.11) | copy-start | bytes 39940
  200.0 2.8 %copy-start = (f32[18,1664]{1,0:T(8,128)}, f32[18,1664]{1,0:T(8,128)S(1)}, u32[]{:S(2)}) copy-start(f32[18,1664]{1,0:T(8,128)S(1)} %shard_map.75.q0) | copy-start | bytes 359428
  200.0 2.8 %collective-permute-start.27 = (f32[18,1664]{1,0:T(8,128)S(1)}, f32[18,1664]{1,0:T(8,128)S(1)}, u32[]{:S(2)}, u32[]{:S(2)}) collective-permute-start(f32[18,1664]{1,0:T(8,128)S(1)} %shard_map.75.q0), channel_id=1, source_target_pairs={{0,1},{1,0},{2,3},{3,2},{4,5},{5,4},{6,7},{7,6},{8,9},{9,8},{10,11... | collective-permute-start | bytes 359432 | tf_op jit(solution)/shard_map/ppermute | solution.py:167
  202.8 0.7 copy-start.7
  206.5 3.7 %collective-permute-start.28 = (f32[26,64]{1,0:T(8,128)S(1)}, f32[26,64]{1,0:T(8,128)S(1)}, u32[]{:S(2)}, u32[]{:S(2)}) collective-permute-start(f32[26,64]{1,0:T(8,128)S(1)} %reshape.19), channel_id=1, source_target_pairs={{0,2},{1,3},{2,0},{3,1},{4,6},{5,7},{6,4},{7,5},{8,10},{9,11},{10,... | collective-permute-start | bytes 19976 | tf_op jit(solution)/shard_map/ppermute | solution.py:170

commit v2 on v1

v2 whole, which is shorter than its diff:
```python
import functools

import jax
import jax.numpy as jnp
from jax import lax
from jax.experimental import pallas as pl
from jax.experimental.pallas import tpu as pltpu
from jax.sharding import PartitionSpec as P

LANES = 128


def tiles_of(rows, target):
    unit = LANES if rows % LANES == 0 else rows
    units = rows // unit
    count = max(1, -(-units * unit // target))
    sizes = [units // count + (1 if i < units % count else 0) for i in range(count)]
    starts = [sum(sizes[:i]) for i in range(count)]
    return [(s * unit, n * unit) for s, n in zip(starts, sizes) if n]


def cut_kernel(at, source, *refs):
    out, sem = refs[-2:]
    rows = source.shape[-2] if source.ndim == 2 else None
    if rows is None:
        copy = pltpu.make_async_copy(source.at[pl.ds(at[0], out.shape[0])], out, sem)
    else:
        copy = pltpu.make_async_copy(source.at[pl.ds(pl.multiple_of(at[0], 16), out.shape[0])], out, sem)
    copy.start()
    copy.wait()


def cut(source, at, size, after=()):
    shape = (size, *source.shape[1:])
    anywhere = pl.BlockSpec(memory_space=pl.ANY)
    return pl.pallas_call(
        cut_kernel,
        out_shape=jax.ShapeDtypeStruct(shape, source.dtype),
        in_specs=[pl.BlockSpec(memory_space=pltpu.SMEM)] + [anywhere] * (1 + len(after)),
        out_specs=pl.BlockSpec(memory_space=pltpu.VMEM),
        scratch_shapes=[pltpu.SemaphoreType.DMA],
        compiler_params=pltpu.CompilerParams(vmem_limit_bytes=16 * 1024 * 1024),
    )(jnp.asarray(at, jnp.int32).reshape(1), source, *after)


def layer_kernel(h_blocks, w_blocks, sizes, headed, waited, *refs):
    refs = list(refs)
    tiles = len(sizes)
    pos = refs.pop(0)
    hs = [[refs.pop(0) for _ in h_blocks] for _ in sizes]
    ws = [refs.pop(0) for _ in w_blocks]
    head = refs.pop(0) if headed else None
    del refs[:waited]
    outs = [refs.pop(0) for _ in range(1 if headed else tiles)]
    hv, wv = refs.pop(0), refs.pop(0)
    ov = None if headed else refs.pop(0)
    hsem, wsem = refs.pop(0), refs.pop(0)
    osem = None if headed else refs.pop(0)

    at = 0
    w_copies = []
    for w, count in zip(ws, w_blocks):
        _, height, width = w.shape
        for j in range(count):
            row, col = pos[2 * at], pos[2 * at + 1]
            copy = pltpu.make_async_copy(
                w.at[j],
                wv.at[pl.ds(pl.multiple_of(row * height, height), height), pl.ds(pl.multiple_of(col * width, width), width)],
                wsem.at[at],
            )
            copy.start()
            w_copies.append(copy)
            at += 1
    h_copies = []
    base = 2 * at
    start = 0
    for t, size in enumerate(sizes):
        row_copies = []
        at = 0
        for h, count in zip(hs[t], h_blocks):
            width = h.shape[1] // count
            for j in range(count):
                col = pos[base + at]
                copy = pltpu.make_async_copy(
                    h.at[:, pl.ds(j * width, width)],
                    hv.at[pl.ds(start, size), pl.ds(pl.multiple_of(col * width, width), width)],
                    hsem.at[t, at],
                )
                copy.start()
                row_copies.append(copy)
                at += 1
        h_copies.append(row_copies)
        start += size
    for copy in w_copies:
        copy.wait()
    out_copies = []
    start = 0
    for t, size in enumerate(sizes):
        for copy in h_copies[t]:
            copy.wait()
        summed = jnp.dot(hv[pl.ds(start, size), :], wv[...], preferred_element_type=jnp.float32)
        hidden = jnp.maximum(summed, 0.0).astype(jnp.bfloat16)
        if headed:
            outs[0][:, pl.ds(start, size)] = lax.dot_general(
                head[...], hidden, (((1,), (1,)), ((), ())), preferred_element_type=jnp.float32
            )
        else:
            ov[pl.ds(start, size), :] = hidden
            copy = pltpu.make_async_copy(ov.at[pl.ds(start, size)], outs[t], osem.at[t])
            copy.start()
            out_copies.append(copy)
        start += size
    for copy in out_copies:
        copy.wait()


def layer(pos, hs, h_blocks, ws, depth, width, head=None, after=()):
    sizes = [tile[0].shape[0] for tile in hs]
    rows = sum(sizes)
    w_blocks = tuple(w.shape[0] for w in ws)
    headed = head is not None
    vmem = pl.BlockSpec(memory_space=pltpu.VMEM)
    anywhere = pl.BlockSpec(memory_space=pl.ANY)
    scratch = [pltpu.VMEM((rows, depth), jnp.bfloat16), pltpu.VMEM((depth, width), jnp.bfloat16)]
    if not headed:
        scratch.append(pltpu.VMEM((rows, width), jnp.bfloat16))
    scratch += [pltpu.SemaphoreType.DMA((len(sizes), sum(h_blocks))), pltpu.SemaphoreType.DMA((sum(w_blocks),))]
    if headed:
        out_shape = jax.ShapeDtypeStruct((head.shape[0], rows), jnp.float32)
    else:
        scratch.append(pltpu.SemaphoreType.DMA((len(sizes),)))
        out_shape = [jax.ShapeDtypeStruct((size, width), jnp.bfloat16) for size in sizes]
    extra = [head] if headed else []
    pieces = [h for tile in hs for h in tile]
    return pl.pallas_call(
        functools.partial(layer_kernel, h_blocks, w_blocks, sizes, headed, len(after)),
        out_shape=out_shape,
        in_specs=[pl.BlockSpec(memory_space=pltpu.SMEM)]
        + [anywhere] * (len(pieces) + len(ws))
        + [vmem] * len(extra)
        + [anywhere] * len(after),
        out_specs=vmem if headed else [anywhere] * len(sizes),
        scratch_shapes=scratch,
        compiler_params=pltpu.CompilerParams(vmem_limit_bytes=32 * 1024 * 1024),
        cost_estimate=pl.CostEstimate(
            flops=2 * rows * depth * width, bytes_accessed=2 * (rows * depth + depth * width + rows * width), transcendentals=0
        ),
    )(pos, *pieces, *ws, *extra, *after)


def retrace_kernel(length, q0, q1, rewards, actions, done_flags, behaviour, out):
    q = q0[...] + q1[...]
    count, steps = q.shape
    scaled = 4.0 * q
    weights = jnp.exp(scaled - jnp.max(scaled, axis=0, keepdims=True))
    probs = weights / jnp.sum(weights, axis=0, keepdims=True)
    value = jnp.sum(probs * q, axis=0, keepdims=True)
    hit = lax.broadcasted_iota(jnp.int32, (count, steps), 0) == actions[...]
    taken = jnp.sum(jnp.where(hit, q, 0.0), axis=0, keepdims=True)
    chosen = jnp.sum(jnp.where(hit, probs, 0.0), axis=0, keepdims=True)
    trace = 0.95 * jnp.minimum(1.0, chosen / behaviour[...])
    keep = 0.99 * (1.0 - done_flags[...].astype(jnp.float32))

    def later(x, by):
        return pltpu.roll(x, steps - by, axis=1)

    last = lax.broadcasted_iota(jnp.int32, (1, steps), 1) % length == length - 1
    factor = jnp.where(last, 0.0, keep * later(trace, 1))
    offset = jnp.where(last, taken, rewards[...] + keep * later(value - trace * taken, 1))
    by = 1
    while by < length:
        offset = offset + factor * later(offset, by)
        factor = factor * later(factor, by)
        by *= 2
    out[...] = offset


def retrace(q0, q1, rewards, actions, done_flags, behaviour, length):
    return pl.pallas_call(
        functools.partial(retrace_kernel, length),
        out_shape=jax.ShapeDtypeStruct(rewards.shape, jnp.float32),
        in_specs=[pl.BlockSpec(memory_space=pltpu.VMEM)] * 6,
        out_specs=pl.BlockSpec(memory_space=pltpu.VMEM),
    )(q0, q1, rewards, actions, done_flags, behaviour)


def per_device(dp, mp, observations, layer_weights, head_weights, rewards, actions, done_flags, behaviour):
    across = mp // 2
    lines = dp // 2
    rank, group = lax.axis_index("mp"), lax.axis_index("dp")
    y, core = rank // 2, rank % 2
    cycle = list(range(0, dp, 2)) + list(range(dp - 1, 0, -2))
    at = jnp.where(group % 2 == 0, group // 2, dp - 1 - group // 2)

    def over(axis, pairs):
        return lambda a: lax.ppermute(a, axis, pairs)

    to_core = over("mp", [(i, i ^ 1) for i in range(mp)])
    to_y = over("mp", [(i, i ^ 2) for i in range(mp)])
    to_next = over("dp", [(cycle[i], cycle[(i + 1) % dp]) for i in range(dp)])
    to_last = over("dp", [(cycle[(i + 1) % dp], cycle[i]) for i in range(dp)])

    def member(steps):
        spot = (at - steps) % dp
        return jnp.where(spot < lines, 2 * spot, 2 * (dp - 1 - spot) + 1)

    def places(steps, flips):
        return [p for step in steps for flip in flips for p in (member(step), y ^ flip)]

    def one_way(send, own, other, hops):
        pairs = send(own)
        came = [pairs]
        if hops > 1:
            pairs = send(jnp.concatenate([pairs, other], axis=0))
            came.append(pairs)
        for _ in range(hops - 2):
            pairs = send(pairs)
            came.append(pairs)
        came.append(send(pairs[1:] if hops > 1 else other))
        return came

    def step_places(sign, hops):
        found = places([sign], (0,))
        for hop in range(2, hops + 1):
            found += places([sign * hop], (0,)) + places([sign * (hop - 1)], (1,))
        return found + places([sign * hops], (1,))

    width = layer_weights.shape[2]
    rows = observations.shape[0] // 2
    depth = observations.shape[1] * mp

    w1 = layer_weights[:1]
    w1_y = to_y(w1)
    w1_next = one_way(to_next, w1, w1_y, lines)
    w1_last = one_way(to_last, w1, w1_y, dp - 1 - lines)
    w2 = cut(layer_weights, 1, 1, [w1_y])
    w2_y = to_y(w2)
    w2_own = cut(layer_weights, 1, 1, [w1_next[0], w1_last[0]])
    w2_next = one_way(to_next, w2_own, w2_y, dp - 1 - lines)
    w2_last = one_way(to_last, w2_own, w2_y, lines)

    tiles = tiles_of(rows, 416)
    came = []
    for i, (start, size) in enumerate(tiles):
        waits = [w1_y] if i == 0 else [w1_next[min(i, lines)], w1_last[min(i, dp - 1 - lines)], w2_y if i == 1 else came[i - 2]]
        came.append(to_y(cut(observations, (1 - y) * rows + start, size, waits)))
    kept = [cut(observations, y * rows + start, size) for start, size in tiles]
    h0 = [[k, to_core(k), c, to_core(c)] for k, c in zip(kept, came)]
    h0_places = [rank, rank ^ 1, rank ^ 2, rank ^ 3]

    seqs = rewards.shape[0] // 2
    flat = [lax.dynamic_slice_in_dim(a, y * seqs, seqs).reshape(1, -1) for a in (rewards, actions, done_flags, behaviour)]
    head = head_weights.T
    head_y = to_y(head)
    heads = jnp.concatenate([jnp.where(y == 0, head, head_y), jnp.where(y == 0, head_y, head)], axis=1)

    first_places = jnp.stack(places([0], (0, 1)) + step_places(1, lines) + step_places(-1, dp - 1 - lines) + h0_places)
    h1 = []
    for part, after in (
        (h0[:2], [w2_next[0], w2_last[1], heads, *flat]),
        (h0[2:], [w2_next[1]]),
    ):
        h1 += layer(
            first_places, part, (1, 1, 1, 1), [w1, w1_y, *w1_next, *w1_last], depth, across * width, after=after
        )
    h1_places = [2 * i + core for i in range(across)] + [2 * i + 1 - core for i in range(across)]
    second_places = places([0], (0, 1)) + step_places(1, dp - 1 - lines) + step_places(-1, lines)
    q = layer(
        jnp.stack(second_places + h1_places),
        [[h, to_core(h)] for h in h1],
        (across, across),
        [w2, w2_y, *w2_next, *w2_last],
        depth,
        across * width,
        heads,
    )
    own = retrace(q, to_core(q), *flat, rewards.shape[1])
    other = to_y(own)
    whole = jnp.concatenate([jnp.where(y == 0, own, other), jnp.where(y == 0, other, own)], axis=1)
    return whole.reshape(rewards.shape)


def solution(mesh):
    in_specs = (
        P("dp", "mp"),
        P(None, "dp", "mp"),
        P("mp", None),
        P("dp", None),
        P("dp", None),
        P("dp", None),
        P("dp", None),
    )
    out_specs = P("dp", None)
    return jax.shard_map(
        functools.partial(per_device, mesh.shape["dp"], mesh.shape["mp"]),
        mesh=mesh,
        in_specs=in_specs,
        out_specs=out_specs,
        check_vma=False,
    )
```

time: 211 us -> 148 us (0.70)
  waiting for transfers between devices: 150 us -> 55.9 us
  starting transfers between devices: 20.6 us -> 32.4 us
  Pallas kernels: 28.6 us -> 37.6 us
  local copies, waits for them, and re-layouts: 9.94 us -> 18.2 us
    ppermute x29 -> x39, waiting for transfers between devices: 150 us -> 55.9 us  [over(): return lambda a: lax.ppermute(a, axis, pairs)]
    ppermute x29 -> x39, starting transfers between devices: 20.6 us -> 32.4 us  [over(): return lambda a: lax.ppermute(a, axis, pairs)]
    pallas_call x3 -> x13, Pallas kernels: 26.3 us -> 35.3 us  [the longest x3 27.2 us: layer(): pl.pallas_call(functools.partial(layer_kernel, h_blocks, w_blocks, sizes,...]
    unnamed x26 -> x62, local copies, waits for them, and re-layouts: 4.53 us -> 11.8 us
    slice x3 -> x5, local copies, waits for them, and re-layouts: 0.04 us -> 4.49 us  [the longest x4 3.37 us: one_way(): came.append(send(pairs[1:] if hops > 1 else other))]
  transfers between devices with their start and end apart: 29 -> 39, of which waited for: 18 -> 15; matrix products, arithmetic and copies ran while one was open for 2% -> 5% of each run, Pallas kernels for 3% -> 16%
where the time goes in v2:
time: 148 us
  waiting for transfers between devices  55.9 us (38%)
  Pallas kernels  37.6 us (25%)
  starting transfers between devices  32.4 us (22%)
  local copies, waits for them, and re-layouts  18.2 us (12%)
  other arithmetic  3.01 us (2%)
    ppermute x39, waiting for transfers between devices, over(): return lambda a: lax.ppermute(a, axis, pairs)  55.9 us
    ppermute x39, starting transfers between devices, over(): return lambda a: lax.ppermute(a, axis, pairs)  32.4 us
    pallas_call x3, Pallas kernels, layer(): pl.pallas_call(functools.partial(layer_kernel, h_blocks, w_blocks, sizes,...  27.2 us
    unnamed x62, local copies, waits for them, and re-layouts  11.8 us
    pallas_call x10, Pallas kernels, cut(): pl.pallas_call(cut_kernel, out_shape=jax.ShapeDtypeStruct(shape, source.d...  8.15 us
    slice x4, local copies, waits for them, and re-layouts, one_way(): came.append(send(pairs[1:] if hops > 1 else other))  3.37 us
  transfers between devices with their start and end apart: 39, of which 15 were waited for; matrix products, arithmetic and copies ran while one was open for 5% of the time, Pallas kernels for 16%

profile of v2, /device:TPU:0, one launch (start us, length us, event | category | flops | bytes accessed | tf_op | source)
XLA Modules:
  0.0 147.8 jit_solution(5607232725458740596)
XLA Ops:
  0.0 1.1 slice.15.refs_9_
  1.1 3.0 %collective-permute-start.1 = (bf16[1,256,512]{2,1,0:T(8,128)(2,1)S(1)}, bf16[1,256,512]{2,1,0:T(8,128)(2,1)S(1)}, u32[]{:S(2)}, u32[]{:S(2)}) collective-permute-start(bf16[1,256,512]{2,1,0:T(8,128)(2,1)S(1)} %slice.15.refs_9_), channel_id=1, source_target_pairs={{0,2},{1,3},{2,0},{3,1},{4,6},{5,7},{6,4},{7,5},{8,10},{9,11},{10,... | collective-permute-start | bytes 786440 | tf_op jit(solution)/shard_map/ppermute | solution.py:196
  4.2 1.5 %collective-permute-start.7 = (bf16[1,256,512]{2,1,0:T(8,128)(2,1)S(1)}, bf16[1,256,512]{2,1,0:T(8,128)(2,1)S(1)}, u32[]{:S(2)}, u32[]{:S(2)}) collective-permute-start(bf16[1,256,512]{2,1,0:T(8,128)(2,1)S(1)} %slice.15.refs_9_), channel_id=1, source_target_pairs={{8,0},{16,8},{24,16},{28,24},{20,28},{12,20},{4,12},{0,4},{9,1},{1... | collective-permute-start | bytes 786440 | tf_op jit(solution)/shard_map/ppermute | solution.py:196
  6.9 3.6 %collective-permute-done.1.refs_0_.refs_10_ = bf16[1,256,512]{2,1,0:T(8,128)(2,1)S(1)} collective-permute-done((bf16[1,256,512]{2,1,0:T(8,128)(2,1)S(1)}, bf16[1,256,512]{2,1,0:T(8,128)(2,1)S(1)}, u32[]{:S(2)}, u32[]{:S(2)}) %collective-permute-start.1) | collective-permute-done | bytes 262176 | tf_op jit(solution)/shard_map/ppermute | solution.py:196
  10.5 1.5 collective-permute-done.7.refs_1_.refs_16_
  11.9 1.2 collective-permute-done.5.refs_0_.refs_11_
  13.8 1.5 %collective-permute-start.8 = (bf16[2,256,512]{2,1,0:T(8,128)(2,1)S(1)}, bf16[2,256,512]{2,1,0:T(8,128)(2,1)}, u32[]{:S(2)}, u32[]{:S(2)}) collective-permute-start(bf16[2,256,512]{2,1,0:T(8,128)(2,1)S(1)} %get-tuple-element.15), channel_id=1, source_target_pairs={{8,0},{16,8},{24,16},{28,24},{20,28},{12,20},{4,12},{0,4},{9,1},{1... | collective-permute-start | bytes 1572872 | tf_op jit(solution)/shard_map/ppermute | solution.py:196
  15.3 10.3 %collective-permute-done.6.refs_0_.refs_12_ = bf16[2,256,512]{2,1,0:T(8,128)(2,1)} collective-permute-done((bf16[2,256,512]{2,1,0:T(8,128)(2,1)S(1)}, bf16[2,256,512]{2,1,0:T(8,128)(2,1)}, u32[]{:S(2)}, u32[]{:S(2)}) %collective-permute-start.6) | collective-permute-done | bytes 524320 | tf_op jit(solution)/shard_map/ppermute | solution.py:196
  26.2 1.4 collective-permute-start.15
  27.6 1.0 copy-done.1
  28.6 0.7 shard_map.76.refs_9_
  30.0 1.0 copy-done.2
  31.0 0.8 shard_map.78
  31.8 0.8 collective-permute-start.17
  32.6 1.4 collective-permute-start.20
  34.0 0.9 copy-done.4
  35.0 0.9 shard_map.74
  35.8 1.2 collective-permute-done.20
  37.1 1.3 collective-permute-start.2
  38.4 1.4 collective-permute-start.18
  39.7 0.9 shard_map.75.refs_5_
  40.7 2.0 %collective-permute-done.17.refs_20_.refs_11_ = bf16[1,256,512]{2,1,0:T(8,128)(2,1)} collective-permute-done((bf16[1,256,512]{2,1,0:T(8,128)(2,1)}, bf16[1,256,512]{2,1,0:T(8,128)(2,1)}, u32[]{:S(2)}, u32[]{:S(2)}) %collective-permute-start.17) | collective-permute-done | bytes 262176 | tf_op jit(solution)/shard_map/ppermute | solution.py:196
  42.8 0.8 collective-permute-start.13
  43.6 1.0 shard_map.77
  44.5 1.0 collective-permute-start.10
  45.5 0.9 shard_map.73.refs_1_
  46.4 1.7 %slice.21 = bf16[1,256,512]{2,1,0:T(8,128)(2,1)} slice(bf16[2,256,512]{2,1,0:T(8,128)(2,1)} %collective-permute-done.15.refs_18_.refs_1_), slice={[1:2], [0:256], [0:512]} | slice | bytes 524288 | tf_op jit(solution)/shard_map/slice | solution.py:219
  48.0 0.8 collective-permute-start.16
  48.9 2.2 %pad_maximum_fusion.2 = (bf16[2,256,512]{2,1,0:T(8,128)(2,1)}, bf16[2,256,512]{2,1,0:T(8,128)(2,1)}) fusion(bf16[1,256,512]{2,1,0:T(8,128)(2,1)} %collective-permute-done.9.refs_2_.refs_10_, bf16[1,256,512]{2,1,0:T(8,128)(2,1)} %collective-permute-done.17.refs_20_.refs_11_, bf16[1,256,512]{2,1,0:T(8,128)(2,1)} %collective-permute-done.18.refs_15_), kind=kLoop, calls=%fused_computation.2 | loop fusion | flops 524288 | bytes 1835008 | tf_op jit(solution)/shard_map/concatenate | solution.py:214
  51.1 1.6 %collective-permute-start.19 = (bf16[2,256,512]{2,1,0:T(8,128)(2,1)}, bf16[2,256,512]{2,1,0:T(8,128)(2,1)}, u32[]{:S(2)}, u32[]{:S(2)}) collective-permute-start(bf16[2,256,512]{2,1,0:T(8,128)(2,1)} %get-tuple-element.14), channel_id=1, source_target_pairs={{8,0},{16,8},{24,16},{28,24},{20,28},{12,20},{4,12},{0,4},{9,1},{1... | collective-permute-start | bytes 1572872 | tf_op jit(solution)/shard_map/ppermute | solution.py:196
  52.7 0.9 shard_map.80.refs_1_
  53.6 2.5 %collective-permute-done.10.refs_7_.refs_2_ = bf16[384,512]{1,0:T(8,128)(2,1)} collective-permute-done((bf16[384,512]{1,0:T(8,128)(2,1)}, bf16[384,512]{1,0:T(8,128)(2,1)}, u32[]{:S(2)}, u32[]{:S(2)}) %collective-permute-start.10) | collective-permute-done | bytes 393248 | tf_op jit(solution)/shard_map/ppermute | solution.py:196
  56.2 1.4 collective-permute-done.16.refs_19_.refs_1_
  57.5 1.4 collective-permute-start.29
  59.0 0.9 shard_map.81
  59.9 1.0 shard_map.83
  61.5 1.3 collective-permute-start.24
  62.8 5.0 %collective-permute-done.19.refs_21_.refs_16_ = bf16[2,256,512]{2,1,0:T(8,128)(2,1)} collective-permute-done((bf16[2,256,512]{2,1,0:T(8,128)(2,1)}, bf16[2,256,512]{2,1,0:T(8,128)(2,1)}, u32[]{:S(2)}, u32[]{:S(2)}) %collective-permute-start.19) | collective-permute-done | bytes 524320 | tf_op jit(solution)/shard_map/ppermute | solution.py:196
  67.7 1.1 collective-permute-start.27
  69.2 0.8 constant_dynamic-slice_fusion.1
  70.4 0.7 copy-done.13
  71.3 1.0 slice.20
  72.2 1.3 collective-permute-start.34
  73.5 0.8 collective-permute-start.14
  74.9 6.4 %collective-permute-done.27.refs_7_ = bf16[384,512]{1,0:T(8,128)(2,1)} collective-permute-done((bf16[384,512]{1,0:T(8,128)(2,1)}, bf16[384,512]{1,0:T(8,128)(2,1)}, u32[]{:S(2)}, u32[]{:S(2)}) %collective-permute-start.27) | collective-permute-done | bytes 393248 | tf_op jit(solution)/shard_map/ppermute | solution.py:196
  81.4 1.6 %collective-permute-start.32 = (bf16[2,256,512]{2,1,0:T(8,128)(2,1)}, bf16[2,256,512]{2,1,0:T(8,128)(2,1)S(1)}, u32[]{:S(2)}, u32[]{:S(2)}) collective-permute-start(bf16[2,256,512]{2,1,0:T(8,128)(2,1)} %collective-permute-done.29.refs_20_.refs_12_), channel_id=1, source_target_pairs={{0,8},{8,16},{16,24},{24,28},{28,20},{20,12},{12,4},{4,0},{1,9},{9... | collective-permute-start | bytes 1572872 | tf_op jit(solution)/shard_map/ppermute | solution.py:196
  83.0 0.9 copy-done.5
  83.9 0.9 copy-done.8
  84.9 0.9 copy-done.11
  85.8 0.9 copy-done.16
  86.8 8.7 %shard_map.79 = (bf16[512,1024]{1,0:T(8,128)(2,1)S(1)}, bf16[384,1024]{1,0:T(8,128)(2,1)}) custom-call(s32[36]{0:T(128)S(1)} %stack.62.refs_0_, bf16[512,512]{1,0:T(8,128)(2,1)} %shard_map.73.refs_1_, bf16[512,512]{1,0:T(8,128)(2,1)} %collective-permute-done.refs_2_, bf16[512,512]{1,0:T(8,128)(2,1)} %collective-permute-done.2.refs_3_.refs_2_, ...), custom_call_target="tpu_custom_call" | custom-call | flops 3758096384 | bytes 9699328 | tf_op jit(solution)/shard_map/pallas_call | solution.py:135
  96.7 7.5 %shard_map.84 = (bf16[384,1024]{1,0:T(8,128)(2,1)}, bf16[384,1024]{1,0:T(8,128)(2,1)}) custom-call(s32[36]{0:T(128)S(1)} %stack.62.refs_0_, bf16[384,512]{1,0:T(8,128)(2,1)} %shard_map.80.refs_1_, bf16[384,512]{1,0:T(8,128)(2,1)} %collective-permute-done.23.refs_2_, bf16[384,512]{1,0:T(8,128)(2,1)} %collective-permute-done.24.refs_3_, ...), custom_call_target="tpu_custom_call" | custom-call | flops 3221225472 | bytes 8912896 | tf_op jit(solution)/shard_map/pallas_call | solution.py:135
  104.8 4.9 %collective-permute-done.35.refs_18_ = bf16[2,256,512]{2,1,0:T(8,128)(2,1)S(1)} collective-permute-done((bf16[2,256,512]{2,1,0:T(8,128)(2,1)S(1)}, bf16[2,256,512]{2,1,0:T(8,128)(2,1)S(1)}, u32[]{:S(2)}, u32[]{:S(2)}) %collective-permute-start.35) | collective-permute-done | bytes 524320 | tf_op jit(solution)/shard_map/ppermute | solution.py:196
  109.7 1.4 collective-permute-start.33
  111.8 5.5 %collective-permute-done.33.refs_14_ = bf16[1,256,512]{2,1,0:T(8,128)(2,1)S(1)} collective-permute-done((bf16[1,256,512]{2,1,0:T(8,128)(2,1)S(1)}, bf16[1,256,512]{2,1,0:T(8,128)(2,1)S(1)}, u32[]{:S(2)}, u32[]{:S(2)}) %collective-permute-start.33) | collective-permute-done | bytes 262176 | tf_op jit(solution)/shard_map/ppermute | solution.py:196
  117.3 0.7 copy-done.25
  118.6 6.4 %collective-permute-done.36.refs_19_ = bf16[1,256,512]{2,1,0:T(8,128)(2,1)} collective-permute-done((bf16[1,256,512]{2,1,0:T(8,128)(2,1)}, bf16[1,256,512]{2,1,0:T(8,128)(2,1)}, u32[]{:S(2)}, u32[]{:S(2)}) %collective-permute-start.36) | collective-permute-done | bytes 262176 | tf_op jit(solution)/shard_map/ppermute | solution.py:196
  125.1 1.0 copy-done.24
  126.1 0.9 copy-done.26
  127.1 11.0 %shard_map.85.q0 = f32[18,1664]{1,0:T(8,128)S(1)} custom-call(s32[36]{0:T(128)S(1)} %stack.56.refs_0_, bf16[512,1024]{1,0:T(8,128)(2,1)S(1)} %get-tuple-element.9.refs_1_, bf16[512,1024]{1,0:T(8,128)(2,1)S(1)} %collective-permute-done.21.refs_2_, bf16[384,1024]{1,0:T(8,128)(2,1)} %get-tuple-element.10.refs_3_, ...), custom_call_target="tpu_custom_call" | custom-call | flops 6979321856 | bytes 14417920 | tf_op jit(solution)/shard_map/pallas_call | solution.py:135
  138.2 1.4 collective-permute-done.37.q1
  140.2 2.3 %shard_map.86 = f32[1,1664]{1,0:T(1,128)} custom-call(f32[18,1664]{1,0:T(8,128)} %copy-done.18, f32[18,1664]{1,0:T(8,128)} %copy-done.27, f32[1,1664]{1,0:T(1,128)} %copy-done.19, s32[1,1664]{1,0:T(1,128)} %copy-done.20, s32[1,1664]{1,0:T(1,128)} %copy-done.21, f32[1,1664]{1,0:T(1,128)} %copy-done.22), custom_call_target="tpu_custom_call" | custom-call | tf_op jit(solution)/shard_map/pallas_call | solution.py:179
  142.5 1.3 collective-permute-start.38
  143.8 2.5 %collective-permute-done.38 = f32[1,1664]{1,0:T(1,128)S(1)} collective-permute-done((f32[1,1664]{1,0:T(1,128)}, f32[1,1664]{1,0:T(1,128)S(1)}, u32[]{:S(2)}, u32[]{:S(2)}) %collective-permute-start.38) | collective-permute-done | bytes 6688 | tf_op jit(solution)/shard_map/ppermute | solution.py:196
  (110 shorter events, 10.1 us)
Async XLA Ops:
  0.0 34.0 %copy-start = (bf16[3328,512]{1,0:T(8,128)(2,1)S(1)}, bf16[3328,512]{1,0:T(8,128)(2,1)}, u32[]{:S(2)}) copy-start(bf16[3328,512]{1,0:T(8,128)(2,1)} %source.19) | copy-start | bytes 10223620
  1.1 9.3 %collective-permute-start.1 = (bf16[1,256,512]{2,1,0:T(8,128)(2,1)S(1)}, bf16[1,256,512]{2,1,0:T(8,128)(2,1)S(1)}, u32[]{:S(2)}, u32[]{:S(2)}) collective-permute-start(bf16[1,256,512]{2,1,0:T(8,128)(2,1)S(1)} %slice.15.refs_9_), channel_id=1, source_target_pairs={{0,2},{1,3},{2,0},{3,1},{4,6},{5,7},{6,4},{7,5},{8,10},{9,11},{10,... | collective-permute-start | bytes 786440 | tf_op jit(solution)/shard_map/ppermute | solution.py:196
  4.2 7.8 %collective-permute-start.7 = (bf16[1,256,512]{2,1,0:T(8,128)(2,1)S(1)}, bf16[1,256,512]{2,1,0:T(8,128)(2,1)S(1)}, u32[]{:S(2)}, u32[]{:S(2)}) collective-permute-start(bf16[1,256,512]{2,1,0:T(8,128)(2,1)S(1)} %slice.15.refs_9_), channel_id=1, source_target_pairs={{8,0},{16,8},{24,16},{28,24},{20,28},{12,20},{4,12},{0,4},{9,1},{1... | collective-permute-start | bytes 786440 | tf_op jit(solution)/shard_map/ppermute | solution.py:196
  5.6 7.5 %collective-permute-start.5 = (bf16[1,256,512]{2,1,0:T(8,128)(2,1)S(1)}, bf16[1,256,512]{2,1,0:T(8,128)(2,1)S(1)}, u32[]{:S(2)}, u32[]{:S(2)}) collective-permute-start(bf16[1,256,512]{2,1,0:T(8,128)(2,1)S(1)} %slice.15.refs_9_), channel_id=1, source_target_pairs={{0,8},{8,16},{16,24},{24,28},{28,20},{20,12},{12,4},{4,0},{1,9},{9... | collective-permute-start | bytes 786440 | tf_op jit(solution)/shard_map/ppermute | solution.py:196
  10.5 18.9 %copy-start.3 = (bf16[1,256,512]{2,1,0:T(8,128)(2,1)}, bf16[1,256,512]{2,1,0:T(8,128)(2,1)S(1)}, u32[]{:S(2)}) copy-start(bf16[1,256,512]{2,1,0:T(8,128)(2,1)S(1)} %collective-permute-done.1.refs_0_.refs_10_) | copy-start | bytes 786436
  11.9 19.9 %copy-start.7 = (bf16[1,256,512]{2,1,0:T(8,128)(2,1)}, bf16[1,256,512]{2,1,0:T(8,128)(2,1)S(1)}, u32[]{:S(2)}) copy-start(bf16[1,256,512]{2,1,0:T(8,128)(2,1)S(1)} %collective-permute-done.7.refs_1_.refs_16_) | copy-start | bytes 786436
  13.1 19.5 %copy-start.10 = (bf16[1,256,512]{2,1,0:T(8,128)(2,1)}, bf16[1,256,512]{2,1,0:T(8,128)(2,1)S(1)}, u32[]{:S(2)}) copy-start(bf16[1,256,512]{2,1,0:T(8,128)(2,1)S(1)} %collective-permute-done.5.refs_0_.refs_11_) | copy-start | bytes 786436
  13.2 12.3 %collective-permute-start.6 = (bf16[2,256,512]{2,1,0:T(8,128)(2,1)S(1)}, bf16[2,256,512]{2,1,0:T(8,128)(2,1)}, u32[]{:S(2)}, u32[]{:S(2)}) collective-permute-start(bf16[2,256,512]{2,1,0:T(8,128)(2,1)S(1)} %get-tuple-element.16), channel_id=1, source_target_pairs={{0,8},{8,16},{16,24},{24,28},{28,20},{20,12},{12,4},{4,0},{1,9},{9... | collective-permute-start | bytes 1572872 | tf_op jit(solution)/shard_map/ppermute | solution.py:196
  13.8 12.4 %collective-permute-start.8 = (bf16[2,256,512]{2,1,0:T(8,128)(2,1)S(1)}, bf16[2,256,512]{2,1,0:T(8,128)(2,1)}, u32[]{:S(2)}, u32[]{:S(2)}) collective-permute-start(bf16[2,256,512]{2,1,0:T(8,128)(2,1)S(1)} %get-tuple-element.15), channel_id=1, source_target_pairs={{8,0},{16,8},{24,16},{28,24},{20,28},{12,20},{4,12},{0,4},{9,1},{1... | collective-permute-start | bytes 1572872 | tf_op jit(solution)/shard_map/ppermute | solution.py:196
  25.6 17.2 %collective-permute-start.12 = (bf16[2,256,512]{2,1,0:T(8,128)(2,1)}, bf16[2,256,512]{2,1,0:T(8,128)(2,1)}, u32[]{:S(2)}, u32[]{:S(2)}) collective-permute-start(bf16[2,256,512]{2,1,0:T(8,128)(2,1)} %collective-permute-done.6.refs_0_.refs_12_), channel_id=1, source_target_pairs={{0,8},{8,16},{16,24},{24,28},{28,20},{20,12},{12,4},{4,0},{1,9},{9... | collective-permute-start | bytes 1572872 | tf_op jit(solution)/shard_map/ppermute | solution.py:196
  26.2 18.3 %collective-permute-start.15 = (bf16[2,256,512]{2,1,0:T(8,128)(2,1)}, bf16[2,256,512]{2,1,0:T(8,128)(2,1)}, u32[]{:S(2)}, u32[]{:S(2)}) collective-permute-start(bf16[2,256,512]{2,1,0:T(8,128)(2,1)} %collective-permute-done.8.refs_1_.refs_17_), channel_id=1, source_target_pairs={{8,0},{16,8},{24,16},{28,24},{20,28},{12,20},{4,12},{0,4},{9,1},{1... | collective-permute-start | bytes 1572872 | tf_op jit(solution)/shard_map/ppermute | solution.py:196
  27.6 1.0 copy-start.1
  29.4 9.0 %collective-permute-start.9 = (bf16[1,256,512]{2,1,0:T(8,128)(2,1)}, bf16[1,256,512]{2,1,0:T(8,128)(2,1)}, u32[]{:S(2)}, u32[]{:S(2)}) collective-permute-start(bf16[1,256,512]{2,1,0:T(8,128)(2,1)} %shard_map.76.refs_9_), channel_id=1, source_target_pairs={{0,2},{1,3},{2,0},{3,1},{4,6},{5,7},{6,4},{7,5},{8,10},{9,11},{10,... | collective-permute-start | bytes 786440 | tf_op jit(solution)/shard_map/ppermute | solution.py:196
  30.0 1.0 copy-start.2
  31.8 11.0 %collective-permute-start.17 = (bf16[1,256,512]{2,1,0:T(8,128)(2,1)}, bf16[1,256,512]{2,1,0:T(8,128)(2,1)}, u32[]{:S(2)}, u32[]{:S(2)}) collective-permute-start(bf16[1,256,512]{2,1,0:T(8,128)(2,1)} %shard_map.78), channel_id=1, source_target_pairs={{0,8},{8,16},{16,24},{24,28},{28,20},{20,12},{12,4},{4,0},{1,9},{9... | collective-permute-start | bytes 786440 | tf_op jit(solution)/shard_map/ppermute | solution.py:196
  32.6 4.5 %collective-permute-start.20 = (bf16[18,512]{1,0:T(8,128)(2,1)}, bf16[18,512]{1,0:T(8,128)(2,1)S(1)}, u32[]{:S(2)}, u32[]{:S(2)}) collective-permute-start(bf16[18,512]{1,0:T(8,128)(2,1)} %bitcast.30), channel_id=1, source_target_pairs={{0,2},{1,3},{2,0},{3,1},{4,6},{5,7},{6,4},{7,5},{8,10},{9,11},{10,... | collective-permute-start | bytes 55304 | tf_op jit(solution)/shard_map/ppermute | solution.py:196
  34.0 1.0 copy-start.4
  37.1 14.0 %collective-permute-start.2 = (bf16[512,512]{1,0:T(8,128)(2,1)}, bf16[512,512]{1,0:T(8,128)(2,1)}, u32[]{:S(2)}, u32[]{:S(2)}) collective-permute-start(bf16[512,512]{1,0:T(8,128)(2,1)} %shard_map.74), channel_id=1, source_target_pairs={{0,2},{1,3},{2,0},{3,1},{4,6},{5,7},{6,4},{7,5},{8,10},{9,11},{10,... | collective-permute-start | bytes 1572872 | tf_op jit(solution)/shard_map/ppermute | solution.py:196
  38.4 9.7 %collective-permute-start.18 = (bf16[1,256,512]{2,1,0:T(8,128)(2,1)}, bf16[1,256,512]{2,1,0:T(8,128)(2,1)}, u32[]{:S(2)}, u32[]{:S(2)}) collective-permute-start(bf16[1,256,512]{2,1,0:T(8,128)(2,1)} %shard_map.78), channel_id=1, source_target_pairs={{8,0},{16,8},{24,16},{28,24},{20,28},{12,20},{4,12},{0,4},{9,1},{1... | collective-permute-start | bytes 786440 | tf_op jit(solution)/shard_map/ppermute | solution.py:196
  42.7 8.3 %collective-permute-start.4 = (bf16[384,512]{1,0:T(8,128)(2,1)}, bf16[384,512]{1,0:T(8,128)(2,1)}, u32[]{:S(2)}, u32[]{:S(2)}) collective-permute-start(bf16[384,512]{1,0:T(8,128)(2,1)} %shard_map.75.refs_5_), channel_id=1, source_target_pairs={{0,1},{1,0},{2,3},{3,2},{4,5},{5,4},{6,7},{7,6},{8,9},{9,8},{10,11... | collective-permute-start | bytes 1179656 | tf_op jit(solution)/shard_map/ppermute | solution.py:196
  42.8 16.2 %collective-permute-start.13 = (bf16[2,256,512]{2,1,0:T(8,128)(2,1)}, bf16[2,256,512]{2,1,0:T(8,128)(2,1)}, u32[]{:S(2)}, u32[]{:S(2)}) collective-permute-start(bf16[2,256,512]{2,1,0:T(8,128)(2,1)} %collective-permute-done.12.refs_13_.refs_0_), channel_id=1, source_target_pairs={{0,8},{8,16},{16,24},{24,28},{28,20},{20,12},{12,4},{4,0},{1,9},{9... | collective-permute-start | bytes 1572872 | tf_op jit(solution)/shard_map/ppermute | solution.py:196
  44.5 11.6 %collective-permute-start.10 = (bf16[384,512]{1,0:T(8,128)(2,1)}, bf16[384,512]{1,0:T(8,128)(2,1)}, u32[]{:S(2)}, u32[]{:S(2)}) collective-permute-start(bf16[384,512]{1,0:T(8,128)(2,1)} %shard_map.77), channel_id=1, source_target_pairs={{0,2},{1,3},{2,0},{3,1},{4,6},{5,7},{6,4},{7,5},{8,10},{9,11},{10,... | collective-permute-start | bytes 1179656 | tf_op jit(solution)/shard_map/ppermute | solution.py:196
  48.0 9.5 %collective-permute-start.16 = (bf16[1,256,512]{2,1,0:T(8,128)(2,1)}, bf16[1,256,512]{2,1,0:T(8,128)(2,1)}, u32[]{:S(2)}, u32[]{:S(2)}) collective-permute-start(bf16[1,256,512]{2,1,0:T(8,128)(2,1)} %slice.21), channel_id=1, source_target_pairs={{8,0},{16,8},{24,16},{28,24},{20,28},{12,20},{4,12},{0,4},{9,1},{1... | collective-permute-start | bytes 786440 | tf_op jit(solution)/shard_map/ppermute | solution.py:196
  51.1 10.4 %collective-permute-start = (bf16[512,512]{1,0:T(8,128)(2,1)}, bf16[512,512]{1,0:T(8,128)(2,1)}, u32[]{:S(2)}, u32[]{:S(2)}) collective-permute-start(bf16[512,512]{1,0:T(8,128)(2,1)} %shard_map.73.refs_1_), channel_id=1, source_target_pairs={{0,1},{1,0},{2,3},{3,2},{4,5},{5,4},{6,7},{7,6},{8,9},{9,8},{10,11... | collective-permute-start | bytes 1572872 | tf_op jit(solution)/shard_map/ppermute | solution.py:196
  51.1 16.7 %collective-permute-start.19 = (bf16[2,256,512]{2,1,0:T(8,128)(2,1)}, bf16[2,256,512]{2,1,0:T(8,128)(2,1)}, u32[]{:S(2)}, u32[]{:S(2)}) collective-permute-start(bf16[2,256,512]{2,1,0:T(8,128)(2,1)} %get-tuple-element.14), channel_id=1, source_target_pairs={{8,0},{16,8},{24,16},{28,24},{20,28},{12,20},{4,12},{0,4},{9,1},{1... | collective-permute-start | bytes 1572872 | tf_op jit(solution)/shard_map/ppermute | solution.py:196
  56.2 4.8 %collective-permute-start.23 = (bf16[384,512]{1,0:T(8,128)(2,1)}, bf16[384,512]{1,0:T(8,128)(2,1)}, u32[]{:S(2)}, u32[]{:S(2)}) collective-permute-start(bf16[384,512]{1,0:T(8,128)(2,1)} %shard_map.80.refs_1_), channel_id=1, source_target_pairs={{0,1},{1,0},{2,3},{3,2},{4,5},{5,4},{6,7},{7,6},{8,9},{9,8},{10,11... | collective-permute-start | bytes 1179656 | tf_op jit(solution)/shard_map/ppermute | solution.py:196
  57.5 14.7 %collective-permute-start.29 = (bf16[2,256,512]{2,1,0:T(8,128)(2,1)}, bf16[2,256,512]{2,1,0:T(8,128)(2,1)}, u32[]{:S(2)}, u32[]{:S(2)}) collective-permute-start(bf16[2,256,512]{2,1,0:T(8,128)(2,1)} %get-tuple-element.13), channel_id=1, source_target_pairs={{0,8},{8,16},{16,24},{24,28},{28,20},{20,12},{12,4},{4,0},{1,9},{9... | collective-permute-start | bytes 1572872 | tf_op jit(solution)/shard_map/ppermute | solution.py:196
  59.0 14.6 %collective-permute-start.3 = (bf16[512,512]{1,0:T(8,128)(2,1)}, bf16[512,512]{1,0:T(8,128)(2,1)}, u32[]{:S(2)}, u32[]{:S(2)}) collective-permute-start(bf16[512,512]{1,0:T(8,128)(2,1)} %collective-permute-done.2.refs_3_.refs_2_), channel_id=1, source_target_pairs={{0,1},{1,0},{2,3},{3,2},{4,5},{5,4},{6,7},{7,6},{8,9},{9,8},{10,11... | collective-permute-start | bytes 1572872 | tf_op jit(solution)/shard_map/ppermute | solution.py:196
  59.9 9.0 %copy-start.29 = (f32[52,64]{1,0:T(8,128)S(1)}, f32[52,64]{1,0:T(8,128)}, u32[]{:S(2)}) copy-start(f32[52,64]{1,0:T(8,128)} %param.13) | copy-start | bytes 39940
  59.9 9.0 %copy-start.30 = (f32[52,64]{1,0:T(8,128)S(1)}, f32[52,64]{1,0:T(8,128)}, u32[]{:S(2)}) copy-start(f32[52,64]{1,0:T(8,128)} %param.10) | copy-start | bytes 39940
  60.9 13.4 %copy-start.28 = (bf16[512,18]{0,1:T(8,128)(2,1)S(1)}, bf16[512,18]{0,1:T(8,128)(2,1)}, u32[]{:S(2)}) copy-start(bf16[512,18]{0,1:T(8,128)(2,1)} %param.9) | copy-start | bytes 55300
  60.9 13.4 %collective-permute-start.11 = (bf16[384,512]{1,0:T(8,128)(2,1)}, bf16[384,512]{1,0:T(8,128)(2,1)}, u32[]{:S(2)}, u32[]{:S(2)}) collective-permute-start(bf16[384,512]{1,0:T(8,128)(2,1)} %collective-permute-done.10.refs_7_.refs_2_), channel_id=1, source_target_pairs={{0,1},{1,0},{2,3},{3,2},{4,5},{5,4},{6,7},{7,6},{8,9},{9,8},{10,11... | collective-permute-start | bytes 1179656 | tf_op jit(solution)/shard_map/ppermute | solution.py:196
  61.5 12.9 %collective-permute-start.24 = (bf16[384,512]{1,0:T(8,128)(2,1)}, bf16[384,512]{1,0:T(8,128)(2,1)}, u32[]{:S(2)}, u32[]{:S(2)}) collective-permute-start(bf16[384,512]{1,0:T(8,128)(2,1)} %shard_map.81), channel_id=1, source_target_pairs={{0,2},{1,3},{2,0},{3,1},{4,6},{5,7},{6,4},{7,5},{8,10},{9,11},{10,... | collective-permute-start | bytes 1179656 | tf_op jit(solution)/shard_map/ppermute | solution.py:196
  67.7 13.6 %collective-permute-start.27 = (bf16[384,512]{1,0:T(8,128)(2,1)}, bf16[384,512]{1,0:T(8,128)(2,1)}, u32[]{:S(2)}, u32[]{:S(2)}) collective-permute-start(bf16[384,512]{1,0:T(8,128)(2,1)} %shard_map.83), channel_id=1, source_target_pairs={{0,2},{1,3},{2,0},{3,1},{4,6},{5,7},{6,4},{7,5},{8,10},{9,11},{10,... | collective-permute-start | bytes 1179656 | tf_op jit(solution)/shard_map/ppermute | solution.py:196
  69.2 26.4 %copy-start.19 = (f32[1,1664]{1,0:T(1,128)}, f32[1,1664]{1,0:T(1,128)S(1)}, u32[]{:S(2)}) copy-start(f32[1,1664]{1,0:T(1,128)S(1)} %reshape.43.refs_23_.rewards) | copy-start | bytes 19972
  70.0 25.5 %copy-start.20 = (s32[1,1664]{1,0:T(1,128)}, s32[1,1664]{1,0:T(1,128)S(1)}, u32[]{:S(2)}) copy-start(s32[1,1664]{1,0:T(1,128)S(1)} %reshape.44.refs_24_.actions) | copy-start | bytes 19972
  70.1 25.5 %copy-start.21 = (s32[1,1664]{1,0:T(1,128)}, s32[1,1664]{1,0:T(1,128)S(1)}, u32[]{:S(2)}) copy-start(s32[1,1664]{1,0:T(1,128)S(1)} %reshape.45.refs_25_.done_flags) | copy-start | bytes 19972
  70.2 25.4 %copy-start.22 = (f32[1,1664]{1,0:T(1,128)}, f32[1,1664]{1,0:T(1,128)S(1)}, u32[]{:S(2)}) copy-start(f32[1,1664]{1,0:T(1,128)S(1)} %reshape.46.refs_26_.behaviour) | copy-start | bytes 19972
  72.2 23.3 %collective-permute-start.34 = (bf16[2,256,512]{2,1,0:T(8,128)(2,1)}, bf16[2,256,512]{2,1,0:T(8,128)(2,1)S(1)}, u32[]{:S(2)}, u32[]{:S(2)}) collective-permute-start(bf16[2,256,512]{2,1,0:T(8,128)(2,1)} %collective-permute-done.19.refs_21_.refs_16_), channel_id=1, source_target_pairs={{8,0},{16,8},{24,16},{28,24},{20,28},{12,20},{4,12},{0,4},{9,1},{1... | collective-permute-start | bytes 1572872 | tf_op jit(solution)/shard_map/ppermute | solution.py:196
  73.5 7.8 %collective-permute-start.14 = (bf16[1,256,512]{2,1,0:T(8,128)(2,1)S(1)}, bf16[1,256,512]{2,1,0:T(8,128)(2,1)S(1)}, u32[]{:S(2)}, u32[]{:S(2)}) collective-permute-start(bf16[1,256,512]{2,1,0:T(8,128)(2,1)S(1)} %slice.20), channel_id=1, source_target_pairs={{0,8},{8,16},{16,24},{24,28},{28,20},{20,12},{12,4},{4,0},{1,9},{9... | collective-permute-start | bytes 786440 | tf_op jit(solution)/shard_map/ppermute | solution.py:196
  74.3 21.8 %collective-permute-start.26 = (bf16[384,512]{1,0:T(8,128)(2,1)}, bf16[384,512]{1,0:T(8,128)(2,1)S(1)}, u32[]{:S(2)}, u32[]{:S(2)}) collective-permute-start(bf16[384,512]{1,0:T(8,128)(2,1)} %copy-done.13), channel_id=1, source_target_pairs={{0,1},{1,0},{2,3},{3,2},{4,5},{5,4},{6,7},{7,6},{8,9},{9,8},{10,11... | collective-permute-start | bytes 1179656 | tf_op jit(solution)/shard_map/ppermute | solution.py:196
  74.4 21.7 %collective-permute-start.25 = (bf16[384,512]{1,0:T(8,128)(2,1)}, bf16[384,512]{1,0:T(8,128)(2,1)S(1)}, u32[]{:S(2)}, u32[]{:S(2)}) collective-permute-start(bf16[384,512]{1,0:T(8,128)(2,1)} %collective-permute-done.24.refs_3_), channel_id=1, source_target_pairs={{0,1},{1,0},{2,3},{3,2},{4,5},{5,4},{6,7},{7,6},{8,9},{9,8},{10,11... | collective-permute-start | bytes 1179656 | tf_op jit(solution)/shard_map/ppermute | solution.py:196
  81.3 15.3 %collective-permute-start.28 = (bf16[384,512]{1,0:T(8,128)(2,1)}, bf16[384,512]{1,0:T(8,128)(2,1)S(1)}, u32[]{:S(2)}, u32[]{:S(2)}) collective-permute-start(bf16[384,512]{1,0:T(8,128)(2,1)} %collective-permute-done.27.refs_7_), channel_id=1, source_target_pairs={{0,1},{1,0},{2,3},{3,2},{4,5},{5,4},{6,7},{7,6},{8,9},{9,8},{10,11... | collective-permute-start | bytes 1179656 | tf_op jit(solution)/shard_map/ppermute | solution.py:196
  81.4 22.9 %collective-permute-start.32 = (bf16[2,256,512]{2,1,0:T(8,128)(2,1)}, bf16[2,256,512]{2,1,0:T(8,128)(2,1)S(1)}, u32[]{:S(2)}, u32[]{:S(2)}) collective-permute-start(bf16[2,256,512]{2,1,0:T(8,128)(2,1)} %collective-permute-done.29.refs_20_.refs_12_), channel_id=1, source_target_pairs={{0,8},{8,16},{16,24},{24,28},{28,20},{20,12},{12,4},{4,0},{1,9},{9... | collective-permute-start | bytes 1572872 | tf_op jit(solution)/shard_map/ppermute | solution.py:196
  83.0 0.9 copy-start.5
  83.9 0.9 copy-start.8
  84.9 0.9 copy-start.11
  86.8 9.8 %copy-start.6 = (bf16[1,256,512]{2,1,0:T(8,128)(2,1)S(1)}, bf16[1,256,512]{2,1,0:T(8,128)(2,1)}, u32[]{:S(2)}) copy-start(bf16[1,256,512]{2,1,0:T(8,128)(2,1)} %copy-done.3) | copy-start | bytes 786436
  86.8 9.8 %copy-start.9 = (bf16[1,256,512]{2,1,0:T(8,128)(2,1)S(1)}, bf16[1,256,512]{2,1,0:T(8,128)(2,1)}, u32[]{:S(2)}) copy-start(bf16[1,256,512]{2,1,0:T(8,128)(2,1)} %copy-done.7) | copy-start | bytes 786436
  86.8 9.8 %copy-start.12 = (bf16[1,256,512]{2,1,0:T(8,128)(2,1)S(1)}, bf16[1,256,512]{2,1,0:T(8,128)(2,1)}, u32[]{:S(2)}) copy-start(bf16[1,256,512]{2,1,0:T(8,128)(2,1)} %copy-done.10) | copy-start | bytes 786436
  86.8 9.8 %copy-start.14 = (bf16[384,512]{1,0:T(8,128)(2,1)S(1)}, bf16[384,512]{1,0:T(8,128)(2,1)}, u32[]{:S(2)}) copy-start(bf16[384,512]{1,0:T(8,128)(2,1)} %copy-done.13) | copy-start | bytes 1179652
  86.8 9.8 %copy-start.17 = (bf16[1,256,512]{2,1,0:T(8,128)(2,1)S(1)}, bf16[1,256,512]{2,1,0:T(8,128)(2,1)}, u32[]{:S(2)}) copy-start(bf16[1,256,512]{2,1,0:T(8,128)(2,1)} %copy-done.15) | copy-start | bytes 786436
  95.6 8.6 %copy-start.23 = (bf16[2,256,512]{2,1,0:T(8,128)(2,1)}, bf16[2,256,512]{2,1,0:T(8,128)(2,1)S(1)}, u32[]{:S(2)}) copy-start(bf16[2,256,512]{2,1,0:T(8,128)(2,1)S(1)} %collective-permute-done.34.refs_17_) | copy-start | bytes 1572868
  95.6 14.1 %collective-permute-start.35 = (bf16[2,256,512]{2,1,0:T(8,128)(2,1)S(1)}, bf16[2,256,512]{2,1,0:T(8,128)(2,1)S(1)}, u32[]{:S(2)}, u32[]{:S(2)}) collective-permute-start(bf16[2,256,512]{2,1,0:T(8,128)(2,1)S(1)} %collective-permute-done.34.refs_17_), channel_id=1, source_target_pairs={{8,0},{16,8},{24,16},{28,24},{20,28},{12,20},{4,12},{0,4},{9,1},{1... | collective-permute-start | bytes 1572872 | tf_op jit(solution)/shard_map/ppermute | solution.py:196
  96.1 29.0 %collective-permute-start.21 = (bf16[512,1024]{1,0:T(8,128)(2,1)S(1)}, bf16[512,1024]{1,0:T(8,128)(2,1)S(1)}, u32[]{:S(2)}, u32[]{:S(2)}) collective-permute-start(bf16[512,1024]{1,0:T(8,128)(2,1)S(1)} %get-tuple-element.9.refs_1_), channel_id=1, source_target_pairs={{0,1},{1,0},{2,3},{3,2},{4,5},{5,4},{6,7},{7,6},{8,9},{9,8},{10,11... | collective-permute-start | bytes 3145736 | tf_op jit(solution)/shard_map/ppermute | solution.py:196
  96.1 29.0 %collective-permute-start.22 = (bf16[384,1024]{1,0:T(8,128)(2,1)}, bf16[384,1024]{1,0:T(8,128)(2,1)}, u32[]{:S(2)}, u32[]{:S(2)}) collective-permute-start(bf16[384,1024]{1,0:T(8,128)(2,1)} %get-tuple-element.10.refs_3_), channel_id=1, source_target_pairs={{0,1},{1,0},{2,3},{3,2},{4,5},{5,4},{6,7},{7,6},{8,9},{9,8},{10,11... | collective-permute-start | bytes 2359304 | tf_op jit(solution)/shard_map/ppermute | solution.py:196
  104.2 20.9 %collective-permute-start.30 = (bf16[384,1024]{1,0:T(8,128)(2,1)}, bf16[384,1024]{1,0:T(8,128)(2,1)}, u32[]{:S(2)}, u32[]{:S(2)}) collective-permute-start(bf16[384,1024]{1,0:T(8,128)(2,1)} %get-tuple-element.11.refs_5_), channel_id=1, source_target_pairs={{0,1},{1,0},{2,3},{3,2},{4,5},{5,4},{6,7},{7,6},{8,9},{9,8},{10,11... | collective-permute-start | bytes 2359304 | tf_op jit(solution)/shard_map/ppermute | solution.py:196
  104.3 20.8 %collective-permute-start.31 = (bf16[384,1024]{1,0:T(8,128)(2,1)}, bf16[384,1024]{1,0:T(8,128)(2,1)}, u32[]{:S(2)}, u32[]{:S(2)}) collective-permute-start(bf16[384,1024]{1,0:T(8,128)(2,1)} %get-tuple-element.12.refs_7_), channel_id=1, source_target_pairs={{0,1},{1,0},{2,3},{3,2},{4,5},{5,4},{6,7},{7,6},{8,9},{9,8},{10,11... | collective-permute-start | bytes 2359304 | tf_op jit(solution)/shard_map/ppermute | solution.py:196
  109.7 7.6 %collective-permute-start.33 = (bf16[1,256,512]{2,1,0:T(8,128)(2,1)S(1)}, bf16[1,256,512]{2,1,0:T(8,128)(2,1)S(1)}, u32[]{:S(2)}, u32[]{:S(2)}) collective-permute-start(bf16[1,256,512]{2,1,0:T(8,128)(2,1)S(1)} %slice.22), channel_id=1, source_target_pairs={{0,8},{8,16},{16,24},{24,28},{28,20},{20,12},{12,4},{4,0},{1,9},{9... | collective-permute-start | bytes 786440 | tf_op jit(solution)/shard_map/ppermute | solution.py:196
  118.1 7.0 %collective-permute-start.36 = (bf16[1,256,512]{2,1,0:T(8,128)(2,1)}, bf16[1,256,512]{2,1,0:T(8,128)(2,1)}, u32[]{:S(2)}, u32[]{:S(2)}) collective-permute-start(bf16[1,256,512]{2,1,0:T(8,128)(2,1)} %slice.23), channel_id=1, source_target_pairs={{8,0},{16,8},{24,16},{28,24},{20,28},{12,20},{4,12},{0,4},{9,1},{1... | collective-permute-start | bytes 786440 | tf_op jit(solution)/shard_map/ppermute | solution.py:196
  125.1 1.0 copy-start.24
  138.1 1.5 copy-start.18
  138.1 1.5 collective-permute-start.37
  142.5 3.8 %collective-permute-start.38 = (f32[1,1664]{1,0:T(1,128)}, f32[1,1664]{1,0:T(1,128)S(1)}, u32[]{:S(2)}, u32[]{:S(2)}) collective-permute-start(f32[1,1664]{1,0:T(1,128)} %shard_map.86), channel_id=1, source_target_pairs={{0,2},{1,3},{2,0},{3,1},{4,6},{5,7},{6,4},{7,5},{8,10},{9,11},{10,... | collective-permute-start | bytes 19976 | tf_op jit(solution)/shard_map/ppermute | solution.py:196
  (6 other events, 4.8 us)

commit v3 on v0

v3 whole, which is shorter than its diff:
```python
import functools

import jax
import jax.numpy as jnp
from jax import lax
from jax.experimental import pallas as pl
from jax.experimental.pallas import tpu as pltpu
from jax.sharding import PartitionSpec as P

LANES = 128
TILE = 416


def tiles_of(rows, target):
    unit = LANES if rows % LANES == 0 else rows
    units = rows // unit
    count = max(1, -(-units * unit // target))
    sizes = [units // count + (1 if i < units % count else 0) for i in range(count)]
    starts = [sum(sizes[:i]) for i in range(count)]
    return [(s * unit, n * unit) for s, n in zip(starts, sizes) if n]


FREE = pl.CostEstimate(flops=0, bytes_accessed=0, transcendentals=0)


def cut_kernel(count, at, source, *refs):
    outs, sems = refs[-1 - count : -1], refs[-1]
    copies = []
    for i, out in enumerate(outs):
        first = at[i] if source.ndim > 2 else pl.multiple_of(at[i], 16)
        copies.append(pltpu.make_async_copy(source.at[pl.ds(first, out.shape[0])], out, sems.at[i]))
        copies[-1].start()
    for copy in copies:
        copy.wait()


def cut(source, at, sizes):
    return pl.pallas_call(
        functools.partial(cut_kernel, len(sizes)),
        out_shape=[jax.ShapeDtypeStruct((size, *source.shape[1:]), source.dtype) for size in sizes],
        in_specs=[pl.BlockSpec(memory_space=pltpu.SMEM), pl.BlockSpec(memory_space=pl.ANY)],
        out_specs=[pl.BlockSpec(memory_space=pltpu.VMEM)] * len(sizes),
        scratch_shapes=[pltpu.SemaphoreType.DMA((len(sizes),))],
        compiler_params=pltpu.CompilerParams(vmem_limit_bytes=40 * 1024 * 1024),
        cost_estimate=FREE,
    )(jnp.stack([jnp.asarray(a, jnp.int32) for a in at]), source)


def gate_kernel(messages, pieces, *refs):
    outs, sems = refs[-1 - len(messages) : -1], refs[-1]
    copies = []
    for out, message in zip(outs, messages):
        to = 0
        for operand, start, count in message:
            copies.append(
                pltpu.make_async_copy(refs[operand].at[pl.ds(start, count)], out.at[pl.ds(to, count)], sems.at[len(copies)])
            )
            copies[-1].start()
            to += count
    for copy in copies:
        copy.wait()


def gate(messages, after=()):
    arrays, plan, shapes = [], [], []
    for message in messages:
        plan.append([])
        for array, start, count in message:
            if not any(array is other for other in arrays):
                arrays.append(array)
            plan[-1].append(([array is other for other in arrays].index(True), start, count))
        first = message[0][0]
        shapes.append(jax.ShapeDtypeStruct((sum(n for _, _, n in message), *first.shape[1:]), first.dtype))
    pieces = sum(len(message) for message in messages)
    held = sum(shape.size * shape.dtype.itemsize for shape in shapes)
    return pl.pallas_call(
        functools.partial(gate_kernel, plan, pieces),
        out_shape=shapes,
        in_specs=[pl.BlockSpec(memory_space=pl.ANY)] * (len(arrays) + len(after)),
        out_specs=[pl.BlockSpec(memory_space=pltpu.VMEM)] * len(shapes),
        scratch_shapes=[pltpu.SemaphoreType.DMA((pieces,))],
        compiler_params=pltpu.CompilerParams(vmem_limit_bytes=held + 1024 * 1024),
        cost_estimate=FREE,
    )(*arrays, *after)


def layer_kernel(kinds, blocks, tiles, width, headed, added, waited, *refs):
    refs = list(refs)
    pos = refs.pop(0)
    hs = [[refs.pop(0) for _ in range(kind)] for kind in kinds]
    ws = [refs.pop(0) for _ in blocks]
    head = refs.pop(0) if headed else None
    before = refs.pop(0) if added else None
    del refs[:waited]
    hv, wv = refs[-6:-4] if not headed else refs[-4:-2]
    count = wv.shape[1] // width
    outs = [refs.pop(0) for _ in range(1 if headed else count)]
    refs = refs[2:]
    ov = None if headed else refs.pop(0)
    hsem, wsem = refs.pop(0), refs.pop(0)
    osem = None if headed else refs.pop(0)

    w_copies = []
    for i, (w, (j, col)) in enumerate(zip(ws, blocks)):
        height = w.shape[1]
        to = wv.at[pl.ds(pl.multiple_of(pos[i] * height, height), height), pl.ds(col * width, width)]
        w_copies.append(pltpu.make_async_copy(w.at[j], to, wsem.at[i]))
    h_copies = []
    for t, (start, size) in enumerate(tiles):
        h_copies.append([])
        for i, h in enumerate(hs):
            wide = h[0].shape[1]
            to = hv.at[pl.ds(start, size), pl.ds(pl.multiple_of(pos[len(blocks) + i] * wide, wide), wide)]
            source = h[t] if len(h) > 1 else h[0].at[pl.ds(start, size)]
            h_copies[-1].append(pltpu.make_async_copy(source, to, hsem.at[t, i]))
    for copy in h_copies[0] + w_copies:
        copy.start()
    for copy in w_copies:
        copy.wait()
    out_copies = []
    for t, (start, size) in enumerate(tiles):
        for copy in h_copies[t]:
            copy.wait()
        if t + 1 < len(tiles):
            for copy in h_copies[t + 1]:
                copy.start()
        summed = jnp.dot(hv[pl.ds(start, size), :], wv[...], preferred_element_type=jnp.float32)
        hidden = jnp.maximum(summed, 0.0).astype(jnp.bfloat16)
        if headed:
            q = lax.dot_general(head[...], hidden, (((1,), (1,)), ((), ())), preferred_element_type=jnp.float32)
            if added:
                q = q + before[:, pl.ds(start, size)]
            outs[0][:, pl.ds(start, size)] = q
        else:
            ov[pl.ds(start, size), :] = hidden
            for col, out in enumerate(outs):
                source = ov.at[pl.ds(start, size), pl.ds(col * width, width)]
                out_copies.append(pltpu.make_async_copy(source, out.at[pl.ds(start, size)], osem.at[t, col]))
                out_copies[-1].start()
    for copy in out_copies:
        copy.wait()


def layer(pos, hs, ws, head=None, before=None, after=()):
    rows = hs[0][0].shape[0]
    tiles = tiles_of(rows, TILE)
    blocks = [(j, col) for _, j, col in ws]
    ws = [w for w, _, _ in ws]
    count = 1 + max(col for _, col in blocks)
    width = ws[0].shape[2]
    depth = ws[0].shape[1] * len(ws) // count
    headed, added = head is not None, before is not None
    vmem = pl.BlockSpec(memory_space=pltpu.VMEM)
    anywhere = pl.BlockSpec(memory_space=pl.ANY)
    scratch = [pltpu.VMEM((rows, depth), jnp.bfloat16), pltpu.VMEM((depth, width * count), jnp.bfloat16)]
    if not headed:
        scratch.append(pltpu.VMEM((rows, width * count), jnp.bfloat16))
    scratch += [pltpu.SemaphoreType.DMA((len(tiles), len(hs))), pltpu.SemaphoreType.DMA((len(ws),))]
    if headed:
        out_shape = jax.ShapeDtypeStruct((head.shape[0], rows), jnp.float32)
    else:
        scratch.append(pltpu.SemaphoreType.DMA((len(tiles), count)))
        out_shape = [jax.ShapeDtypeStruct((rows, width), jnp.bfloat16)] * count
    extra = ([head] if headed else []) + ([before] if added else [])
    return pl.pallas_call(
        functools.partial(layer_kernel, [len(h) for h in hs], blocks, tiles, width, headed, added, len(after)),
        out_shape=out_shape,
        in_specs=[pl.BlockSpec(memory_space=pltpu.SMEM)]
        + [anywhere] * (sum(len(h) for h in hs) + len(ws))
        + [vmem] * len(extra)
        + [anywhere] * len(after),
        out_specs=vmem if headed else [anywhere] * count,
        scratch_shapes=scratch,
        compiler_params=pltpu.CompilerParams(vmem_limit_bytes=24 * 1024 * 1024),
        cost_estimate=pl.CostEstimate(flops=2 * rows * depth * width * count, bytes_accessed=0, transcendentals=0),
    )(pos, *[a for h in hs for a in h], *ws, *extra, *after)


def retrace_kernel(length, q0, q1, rewards, actions, done_flags, behaviour, out):
    q = q0[...] + q1[...]
    count, steps = q.shape
    scaled = 4.0 * q
    weights = jnp.exp(scaled - jnp.max(scaled, axis=0, keepdims=True))
    probs = weights / jnp.sum(weights, axis=0, keepdims=True)
    value = jnp.sum(probs * q, axis=0, keepdims=True)
    hit = lax.broadcasted_iota(jnp.int32, (count, steps), 0) == actions[...]
    taken = jnp.sum(jnp.where(hit, q, 0.0), axis=0, keepdims=True)
    chosen = jnp.sum(jnp.where(hit, probs, 0.0), axis=0, keepdims=True)
    trace = 0.95 * jnp.minimum(1.0, chosen / behaviour[...])
    keep = 0.99 * (1.0 - done_flags[...].astype(jnp.float32))

    def later(x, by):
        return pltpu.roll(x, steps - by, axis=1)

    last = lax.broadcasted_iota(jnp.int32, (1, steps), 1) % length == length - 1
    factor = jnp.where(last, 0.0, keep * later(trace, 1))
    offset = jnp.where(last, taken, rewards[...] + keep * later(value - trace * taken, 1))
    by = 1
    while by < length:
        offset = offset + factor * later(offset, by)
        factor = factor * later(factor, by)
        by *= 2
    out[...] = offset


def retrace(q0, q1, rewards, actions, done_flags, behaviour, length):
    return pl.pallas_call(
        functools.partial(retrace_kernel, length),
        out_shape=jax.ShapeDtypeStruct(rewards.shape, jnp.float32),
        in_specs=[pl.BlockSpec(memory_space=pltpu.VMEM)] * 6,
        out_specs=pl.BlockSpec(memory_space=pltpu.VMEM),
    )(q0, q1, rewards, actions, done_flags, behaviour)


def per_device(dp, mp, observations, layer_weights, head_weights, rewards, actions, done_flags, behaviour):
    lines = dp // 2
    rank, group = lax.axis_index("mp"), lax.axis_index("dp")
    y = rank // 2
    cycle = list(range(0, dp, 2)) + list(range(dp - 1, 0, -2))
    at = jnp.where(group % 2 == 0, group // 2, dp - 1 - group // 2)

    def over(axis, pairs):
        return lambda a: lax.ppermute(a, axis, pairs)

    to_core = over("mp", [(i, i ^ 1) for i in range(mp)])
    to_y = over("mp", [(i, i ^ 2) for i in range(mp)])
    to_next = over("dp", [(cycle[i], cycle[(i + 1) % dp]) for i in range(dp)])
    to_last = over("dp", [(cycle[(i + 1) % dp], cycle[i]) for i in range(dp)])

    def came_from(step):
        spot = (at - step) % dp
        return jnp.where(spot < lines, 2 * spot, 2 * (dp - 1 - spot) + 1)

    rows = observations.shape[0] // 2
    seqs = rewards.shape[0] // 2
    flat = [lax.dynamic_slice_in_dim(a, y * seqs, seqs).reshape(1, -1) for a in (rewards, actions, done_flags, behaviour)]
    head = head_weights.T
    head_y = to_y(head)

    short, long = dp - 1 - lines, lines
    order = [rank, rank ^ 1, rank ^ 2, rank ^ 3]

    def run(columns, hs, **rest):
        ws, steps = [], []
        for col, (local, chains) in enumerate(columns):
            ws += [(a, j, col) for a, j in ((local, 0), *chains[0], *chains[1])]
            steps += [0, *range(1, len(chains[0]) + 1), *range(-1, -len(chains[1]) - 1, -1)]
        return layer(jnp.stack([came_from(step) for step in steps] + order), hs, ws, **rest)

    kept, sent = cut(observations, [y * rows, (1 - y) * rows], [rows, rows])
    w1, w2 = cut(layer_weights, [0, 1], [1, 1])
    w1_y = to_y(w1)
    kept_c = to_core(kept)
    turns = (long, short)
    ways = ([to_next(w1)], [to_last(w1)])
    sizes = [size for _, size in tiles_of(rows, TILE)]
    parts, start, came, came_c = list(sizes), 0, [], []
    now = [*(way[0] for way in ways), w1_y, head_y]
    for i in range(1, dp):
        if i == 1:
            (w2_gated,) = gate([[(w2, 0, 1)]], now)
            w2_y = to_y(w2_gated)
        build = []
        for way, turn in zip(ways, turns):
            last = way[-1]
            if i == 1:
                build.append([(last, 0, 1), (w1_y, 0, 1)])
            elif i == turn:
                build.append([(last, 1, 1), (w2, 0, 1)])
            elif i == turn + 1:
                build.append([(last, 1, 1), (w2_y, 0, 1)])
            elif i == dp - 1:
                build.append([(last, 1, 1)])
            else:
                build.append(None)
        built = iter(gate([m for m in build if m], now)) if any(build) else None
        messages = [next(built) if m else way[-1] for m, way in zip(build, ways)]
        if parts:
            size = parts.pop(0)
            (part,) = gate([[(sent, start, size)]], [*now, *messages, *(came[-1:] or [w2_y, *flat])])
            start += size
        for send, way, message in zip((to_next, to_last), ways, messages):
            way.append(send(message))
        if start and len(came) < len(sizes):
            came.append(to_y(part))
            came_c.append(to_core(came[-1]))
        now = [way[-1] for way in ways]
        if i == long + 1:
            first = [[], []]
            for way, turn in zip(ways, turns):
                first[0].append([(way[h - 1], 0) for h in range(1, turn + 1)])
                first[1].append([(way[h], min(1, way[h].shape[0] - 1) if h < turn else 0) for h in range(1, turn + 1)])
            h1 = run([(w1, first[0]), (w1_y, first[1])], [[kept], [kept_c], came, came_c], after=flat)
            now = [*now, h1[0]]
            mine, theirs = gate([[(h1[0], 0, rows)], [(h1[1], 0, rows)]], now)
            h1 = [[mine], [to_core(mine)], [theirs], [to_core(theirs)]]
    second = [[], []]
    for way, turn in zip(ways, turns):
        second[0].append([(way[h], 1 if h == turn else 0) for h in range(turn, dp - 1)])
        second[1].append([(way[h + 1], 1 if h + 1 < dp - 1 else 0) for h in range(turn, dp - 1)])
    q = run([(w2, second[0])], h1, head=head, after=[ways[0][-2], ways[1][-2]])
    q = run([(w2_y, second[1])], h1, head=head_y, before=q)
    own = retrace(q, to_core(q), *flat, rewards.shape[1])
    other = to_y(own)
    whole = jnp.concatenate([jnp.where(y == 0, own, other), jnp.where(y == 0, other, own)], axis=1)
    return whole.reshape(rewards.shape)


def solution(mesh):
    in_specs = (
        P("dp", "mp"),
        P(None, "dp", "mp"),
        P("mp", None),
        P("dp", None),
        P("dp", None),
        P("dp", None),
        P("dp", None),
    )
    out_specs = P("dp", None)
    return jax.shard_map(
        functools.partial(per_device, mesh.shape["dp"], mesh.shape["mp"]),
        mesh=mesh,
        in_specs=in_specs,
        out_specs=out_specs,
        check_vma=False,
    )
```

time: 350 us -> 127 us (0.36)
  waiting for transfers between devices: 299 us -> 50.3 us
  Pallas kernels: 0 us -> 35 us
  starting transfers between devices: 0.16 us -> 33 us
  matrix products: 26.3 us -> 0 us
  between operations: 13.2 us -> 0.39 us
  other arithmetic: 5.56 us -> 0.82 us
    all_gather x4 -> x0, waiting for transfers between devices: 265 us -> none  [the longest x2 176 us: per_device(): current = lax.all_gather(hidden, 'mp', axis=1, tiled=True)]
    ppermute x0 -> x32, waiting for transfers between devices: none -> 50.3 us  [over(): return lambda a: lax.ppermute(a, axis, pairs)]
    pallas_call x0 -> x17, Pallas kernels: none -> 35 us  [the longest x3 26.3 us: layer(): pl.pallas_call(functools.partial(layer_kernel, [len(h) for h in hs], bloc...]
    ppermute x0 -> x32, starting transfers between devices: none -> 33 us  [over(): return lambda a: lax.ppermute(a, axis, pairs)]
    psum x1 -> x0, waiting for transfers between devices: 32 us -> none  [per_device(): qvals = lax.psum(partial_q, 'mp')]
    dot_general x2 -> x0, matrix products: 26.3 us -> none  [the longest x1 13.9 us: per_device(): summed = jnp.dot(current, block, preferred_element_type=jnp.float32)]
    unnamed x11 -> x42, local copies, waits for them, and re-layouts: 0.12 us -> 5.58 us
  transfers between devices with their start and end apart: 5 -> 32, of which waited for: 5 -> 15; matrix products, arithmetic and copies ran while one was open for 4% -> 0% of each run, Pallas kernels for 0% -> 17%
where the time goes in v3:
time: 127 us; the launch traced here: 126 us
  waiting for transfers between devices  50.3 us (40%)
  Pallas kernels  35 us (28%)
  starting transfers between devices  33 us (26%)
  local copies, waits for them, and re-layouts  6.77 us (5%)
    ppermute x32, waiting for transfers between devices, over(): return lambda a: lax.ppermute(a, axis, pairs)  50.3 us
    ppermute x32, starting transfers between devices, over(): return lambda a: lax.ppermute(a, axis, pairs)  33 us
    pallas_call x3, Pallas kernels, layer(): pl.pallas_call(functools.partial(layer_kernel, [len(h) for h in hs], bloc...  26.3 us
    unnamed x42, local copies, waits for them, and re-layouts  5.58 us
    pallas_call x11, Pallas kernels, gate(): pl.pallas_call(functools.partial(gate_kernel, plan, pieces), out_shape=sh...  3.37 us
    pallas_call x2, Pallas kernels, cut(): pl.pallas_call(functools.partial(cut_kernel, len(sizes)), out_shape=[jax....  2.96 us
  transfers between devices with their start and end apart: 32, of which 15 were waited for; matrix products, arithmetic and copies ran while one was open for 0% of the time, Pallas kernels for 17%

profile of v3, /device:TPU:0, one launch (start us, length us, event | category | flops | bytes accessed | tf_op | source)
XLA Modules:
  0.0 126.2 jit_solution(2647057496184949057)
XLA Ops:
  0.0 1.0 copy-done.7
  1.1 0.6 shard_map.74
  1.7 3.1 %collective-permute-start.1 = (bf16[1,256,512]{2,1,0:T(8,128)(2,1)S(1)}, bf16[1,256,512]{2,1,0:T(8,128)(2,1)S(1)}, u32[]{:S(2)}, u32[]{:S(2)}) collective-permute-start(bf16[1,256,512]{2,1,0:T(8,128)(2,1)S(1)} %get-tuple-element.21.refs_11_), channel_id=1, source_target_pairs={{0,8},{8,16},{16,24},{24,28},{28,20},{20,12},{12,4},{4,0},{1,9},{9... | collective-permute-start | bytes 786440 | tf_op jit(solution)/shard_map/ppermute | solution.py:223
  4.8 2.0 %collective-permute-start.3 = (bf16[1,256,512]{2,1,0:T(8,128)(2,1)S(1)}, bf16[1,256,512]{2,1,0:T(8,128)(2,1)S(1)}, u32[]{:S(2)}, u32[]{:S(2)}) collective-permute-start(bf16[1,256,512]{2,1,0:T(8,128)(2,1)S(1)} %get-tuple-element.21.refs_11_), channel_id=1, source_target_pairs={{0,2},{1,3},{2,0},{3,1},{4,6},{5,7},{6,4},{7,5},{8,10},{9,11},{10,... | collective-permute-start | bytes 786440 | tf_op jit(solution)/shard_map/ppermute | solution.py:223
  6.8 6.3 %collective-permute-done.4.refs_6_.refs_4_.refs_13_ = bf16[18,512]{1,0:T(8,128)(2,1)S(1)} collective-permute-done((bf16[18,512]{1,0:T(8,128)(2,1)}, bf16[18,512]{1,0:T(8,128)(2,1)S(1)}, u32[]{:S(2)}, u32[]{:S(2)}) %collective-permute-start.4) | collective-permute-done | bytes 18464 | tf_op jit(solution)/shard_map/ppermute | solution.py:223
  13.1 0.1 shard_map.75
  13.2 1.8 %collective-permute-start.7 = (bf16[2,256,512]{2,1,0:T(8,128)(2,1)S(1)}, bf16[2,256,512]{2,1,0:T(8,128)(2,1)S(1)}, u32[]{:S(2)}, u32[]{:S(2)}) collective-permute-start(bf16[2,256,512]{2,1,0:T(8,128)(2,1)S(1)} %get-tuple-element.22.refs_5_), channel_id=1, source_target_pairs={{0,8},{8,16},{16,24},{24,28},{28,20},{20,12},{12,4},{4,0},{1,9},{9... | collective-permute-start | bytes 1572872 | tf_op jit(solution)/shard_map/ppermute | solution.py:223
  15.0 0.3 collective-permute-start.8
  15.3 1.8 %collective-permute-start.5 = (bf16[1,256,512]{2,1,0:T(8,128)(2,1)S(1)}, bf16[1,256,512]{2,1,0:T(8,128)(2,1)S(1)}, u32[]{:S(2)}, u32[]{:S(2)}) collective-permute-start(bf16[1,256,512]{2,1,0:T(8,128)(2,1)S(1)} %shard_map.76), channel_id=1, source_target_pairs={{0,2},{1,3},{2,0},{3,1},{4,6},{5,7},{6,4},{7,5},{8,10},{9,11},{10,... | collective-permute-start | bytes 786440 | tf_op jit(solution)/shard_map/ppermute | solution.py:223
  17.1 0.1 reshape.15.refs_8_.refs_27_.rewards
  17.2 0.1 reshape.16.refs_9_.refs_28_.actions
  17.3 0.1 reshape.17.refs_10_.refs_29_.done_flags
  17.4 0.1 reshape.18.refs_11_.refs_30_.behaviour
  17.5 2.0 %copy-done = bf16[3328,512]{1,0:T(8,128)(2,1)S(1)} copy-done((bf16[3328,512]{1,0:T(8,128)(2,1)S(1)}, bf16[3328,512]{1,0:T(8,128)(2,1)}, u32[]{:S(2)}) %copy-start) | copy-done | bytes 3407896
  19.5 2.4 %shard_map.73 = (bf16[1664,512]{1,0:T(8,128)(2,1)}, bf16[1664,512]{1,0:T(8,128)(2,1)S(1)}) custom-call(s32[2]{0:T(128)S(1)} %pad_add_fusion.at, bf16[3328,512]{1,0:T(8,128)(2,1)S(1)} %copy-done), custom_call_target="tpu_custom_call" | custom-call | tf_op jit(solution)/shard_map/pallas_call | solution.py:38
  21.9 1.8 %collective-permute-start.6 = (bf16[512,512]{1,0:T(8,128)(2,1)S(1)}, bf16[512,512]{1,0:T(8,128)(2,1)}, u32[]{:S(2)}, u32[]{:S(2)}) collective-permute-start(bf16[512,512]{1,0:T(8,128)(2,1)S(1)} %shard_map.77), channel_id=1, source_target_pairs={{0,2},{1,3},{2,0},{3,1},{4,6},{5,7},{6,4},{7,5},{8,10},{9,11},{10,... | collective-permute-start | bytes 1572872 | tf_op jit(solution)/shard_map/ppermute | solution.py:223
  23.7 2.0 %collective-permute-done.7.refs_1_.refs_3_.refs_13_.refs_20_ = bf16[2,256,512]{2,1,0:T(8,128)(2,1)S(1)} collective-permute-done((bf16[2,256,512]{2,1,0:T(8,128)(2,1)S(1)}, bf16[2,256,512]{2,1,0:T(8,128)(2,1)S(1)}, u32[]{:S(2)}, u32[]{:S(2)}) %collective-permute-start.7) | collective-permute-done | bytes 524320 | tf_op jit(solution)/shard_map/ppermute | solution.py:223
  25.7 1.4 %collective-permute-start.10 = (bf16[2,256,512]{2,1,0:T(8,128)(2,1)S(1)}, bf16[2,256,512]{2,1,0:T(8,128)(2,1)S(1)}, u32[]{:S(2)}, u32[]{:S(2)}) collective-permute-start(bf16[2,256,512]{2,1,0:T(8,128)(2,1)S(1)} %collective-permute-done.7.refs_1_.refs_3_.refs_13_.refs_20_), channel_id=1, source_target_pairs={{0,8},{8,16},{16,24},{24,28},{28,20},{20,12},{12,4},{4,0},{1,9},{9... | collective-permute-start | bytes 1572872 | tf_op jit(solution)/shard_map/ppermute | solution.py:223
  27.2 0.6 collective-permute-start.11
  27.8 6.0 %collective-permute-done.6.refs_5_.refs_3_ = bf16[512,512]{1,0:T(8,128)(2,1)} collective-permute-done((bf16[512,512]{1,0:T(8,128)(2,1)S(1)}, bf16[512,512]{1,0:T(8,128)(2,1)}, u32[]{:S(2)}, u32[]{:S(2)}) %collective-permute-start.6) | collective-permute-done | bytes 524320 | tf_op jit(solution)/shard_map/ppermute | solution.py:223
  33.8 0.2 shard_map.78
  34.0 1.8 %collective-permute-start.9 = (bf16[384,512]{1,0:T(8,128)(2,1)S(1)}, bf16[384,512]{1,0:T(8,128)(2,1)}, u32[]{:S(2)}, u32[]{:S(2)}) collective-permute-start(bf16[384,512]{1,0:T(8,128)(2,1)S(1)} %shard_map.78), channel_id=1, source_target_pairs={{0,2},{1,3},{2,0},{3,1},{4,6},{5,7},{6,4},{7,5},{8,10},{9,11},{10,... | collective-permute-start | bytes 1179656 | tf_op jit(solution)/shard_map/ppermute | solution.py:223
  35.8 2.0 %collective-permute-done.10.refs_2_.refs_1_.refs_3_.refs_14_.refs_21_ = bf16[2,256,512]{2,1,0:T(8,128)(2,1)S(1)} collective-permute-done((bf16[2,256,512]{2,1,0:T(8,128)(2,1)S(1)}, bf16[2,256,512]{2,1,0:T(8,128)(2,1)S(1)}, u32[]{:S(2)}, u32[]{:S(2)}) %collective-permute-start.10) | collective-permute-done | bytes 524320 | tf_op jit(solution)/shard_map/ppermute | solution.py:223
  37.8 1.3 %collective-permute-start.13 = (bf16[2,256,512]{2,1,0:T(8,128)(2,1)S(1)}, bf16[2,256,512]{2,1,0:T(8,128)(2,1)S(1)}, u32[]{:S(2)}, u32[]{:S(2)}) collective-permute-start(bf16[2,256,512]{2,1,0:T(8,128)(2,1)S(1)} %collective-permute-done.10.refs_2_.refs_1_.refs_3_.refs_14_.refs_21_), channel_id=1, source_target_pairs={{0,8},{8,16},{16,24},{24,28},{28,20},{20,12},{12,4},{4,0},{1,9},{9... | collective-permute-start | bytes 1572872 | tf_op jit(solution)/shard_map/ppermute | solution.py:223
  39.2 0.7 collective-permute-start.14
  40.0 3.2 %collective-permute-done.9.refs_5_.refs_4_ = bf16[384,512]{1,0:T(8,128)(2,1)} collective-permute-done((bf16[384,512]{1,0:T(8,128)(2,1)S(1)}, bf16[384,512]{1,0:T(8,128)(2,1)}, u32[]{:S(2)}, u32[]{:S(2)}) %collective-permute-start.9) | collective-permute-done | bytes 393248 | tf_op jit(solution)/shard_map/ppermute | solution.py:223
  43.2 0.2 shard_map.80
  43.4 2.2 %collective-permute-start.12 = (bf16[384,512]{1,0:T(8,128)(2,1)S(1)}, bf16[384,512]{1,0:T(8,128)(2,1)}, u32[]{:S(2)}, u32[]{:S(2)}) collective-permute-start(bf16[384,512]{1,0:T(8,128)(2,1)S(1)} %shard_map.80), channel_id=1, source_target_pairs={{0,2},{1,3},{2,0},{3,1},{4,6},{5,7},{6,4},{7,5},{8,10},{9,11},{10,... | collective-permute-start | bytes 1179656 | tf_op jit(solution)/shard_map/ppermute | solution.py:223
  45.6 3.4 %collective-permute-done.13.refs_0_.refs_4_.refs_1_.refs_15_.refs_22_ = bf16[2,256,512]{2,1,0:T(8,128)(2,1)S(1)} collective-permute-done((bf16[2,256,512]{2,1,0:T(8,128)(2,1)S(1)}, bf16[2,256,512]{2,1,0:T(8,128)(2,1)S(1)}, u32[]{:S(2)}, u32[]{:S(2)}) %collective-permute-start.13) | collective-permute-done | bytes 524320 | tf_op jit(solution)/shard_map/ppermute | solution.py:223
  49.0 0.9 collective-permute-done.14.refs_2_.refs_5_.refs_26_.refs_9_
  49.9 0.1 shard_map.81
  50.0 1.6 %collective-permute-start.20 = (bf16[2,256,512]{2,1,0:T(8,128)(2,1)S(1)}, bf16[2,256,512]{2,1,0:T(8,128)(2,1)S(1)}, u32[]{:S(2)}, u32[]{:S(2)}) collective-permute-start(bf16[2,256,512]{2,1,0:T(8,128)(2,1)S(1)} %get-tuple-element.25.refs_3_), channel_id=1, source_target_pairs={{0,8},{8,16},{16,24},{24,28},{28,20},{20,12},{12,4},{4,0},{1,9},{9... | collective-permute-start | bytes 1572872 | tf_op jit(solution)/shard_map/ppermute | solution.py:223
  51.7 0.4 collective-permute-start.21
  52.1 0.9 collective-permute-done.12.refs_5_
  53.0 0.2 shard_map.82
  53.2 2.6 %collective-permute-start.15 = (bf16[384,512]{1,0:T(8,128)(2,1)S(1)}, bf16[384,512]{1,0:T(8,128)(2,1)}, u32[]{:S(2)}, u32[]{:S(2)}) collective-permute-start(bf16[384,512]{1,0:T(8,128)(2,1)S(1)} %shard_map.82), channel_id=1, source_target_pairs={{0,2},{1,3},{2,0},{3,1},{4,6},{5,7},{6,4},{7,5},{8,10},{9,11},{10,... | collective-permute-start | bytes 1179656 | tf_op jit(solution)/shard_map/ppermute | solution.py:223
  55.8 5.9 %collective-permute-done.15.refs_6_ = bf16[384,512]{1,0:T(8,128)(2,1)} collective-permute-done((bf16[384,512]{1,0:T(8,128)(2,1)S(1)}, bf16[384,512]{1,0:T(8,128)(2,1)}, u32[]{:S(2)}, u32[]{:S(2)}) %collective-permute-start.15) | collective-permute-done | bytes 393248 | tf_op jit(solution)/shard_map/ppermute | solution.py:223
  61.7 0.8 copy-done.3
  62.5 0.5 collective-permute-start.18
  63.0 0.1 stack.100.refs_0_
  63.1 1.0 copy-done.4
  64.2 1.6 %collective-permute-start.22 = (bf16[2,256,512]{2,1,0:T(8,128)(2,1)S(1)}, bf16[2,256,512]{2,1,0:T(8,128)(2,1)}, u32[]{:S(2)}, u32[]{:S(2)}) collective-permute-start(bf16[2,256,512]{2,1,0:T(8,128)(2,1)S(1)} %shard_map.84), channel_id=1, source_target_pairs={{0,8},{8,16},{16,24},{24,28},{28,20},{20,12},{12,4},{4,0},{1,9},{9... | collective-permute-start | bytes 1572872 | tf_op jit(solution)/shard_map/ppermute | solution.py:223
  65.8 0.6 collective-permute-start.23
  66.5 10.7 %shard_map.83 = (bf16[1664,512]{1,0:T(8,128)(2,1)S(1)}, bf16[1664,512]{1,0:T(8,128)(2,1)S(1)}) custom-call(s32[20]{0:T(128)S(1)} %stack.100.refs_0_, bf16[1664,512]{1,0:T(8,128)(2,1)} %get-tuple-element.19.refs_1_, bf16[1664,512]{1,0:T(8,128)(2,1)} %collective-permute-done.refs_2_, bf16[512,512]{1,0:T(8,128)(2,1)} %collective-permute-done.6.refs_5_.refs_3_, ...), custom_call_target="tpu_custom_call" | custom-call | flops 6979321856 | tf_op jit(solution)/shard_map/pallas_call | solution.py:165
  77.2 1.8 %collective-permute-done.22.refs_2_.refs_7_.refs_6_ = bf16[2,256,512]{2,1,0:T(8,128)(2,1)} collective-permute-done((bf16[2,256,512]{2,1,0:T(8,128)(2,1)S(1)}, bf16[2,256,512]{2,1,0:T(8,128)(2,1)}, u32[]{:S(2)}, u32[]{:S(2)}) %collective-permute-start.22) | collective-permute-done | bytes 524320 | tf_op jit(solution)/shard_map/ppermute | solution.py:223
  79.0 1.2 collective-permute-done.23.refs_3_.refs_11_.refs_10_
  80.2 2.3 %shard_map.85 = (bf16[1664,512]{1,0:T(8,128)(2,1)}, bf16[1664,512]{1,0:T(8,128)(2,1)}) custom-call(bf16[1664,512]{1,0:T(8,128)(2,1)S(1)} %get-tuple-element.27.refs_0_.refs_4_, bf16[1664,512]{1,0:T(8,128)(2,1)S(1)} %get-tuple-element.28.refs_1_, bf16[2,256,512]{2,1,0:T(8,128)(2,1)} %collective-permute-done.22.refs_2_.refs_7_.refs_6_, ...), custom_call_target="tpu_custom_call" | custom-call | tf_op jit(solution)/shard_map/pallas_call | solution.py:76
  82.6 0.5 collective-permute-start.25
  83.1 1.6 %collective-permute-start.26 = (bf16[2,256,512]{2,1,0:T(8,128)(2,1)}, bf16[2,256,512]{2,1,0:T(8,128)(2,1)S(1)}, u32[]{:S(2)}, u32[]{:S(2)}) collective-permute-start(bf16[2,256,512]{2,1,0:T(8,128)(2,1)} %collective-permute-done.22.refs_2_.refs_7_.refs_6_), channel_id=1, source_target_pairs={{0,8},{8,16},{16,24},{24,28},{28,20},{20,12},{12,4},{4,0},{1,9},{9... | collective-permute-start | bytes 1572872 | tf_op jit(solution)/shard_map/ppermute | solution.py:223
  84.7 0.4 collective-permute-start.27
  85.1 0.1 stack.48.refs_0_
  85.2 12.0 %collective-permute-done.26.refs_0_.refs_2_.refs_8_.refs_14_.refs_7_ = bf16[2,256,512]{2,1,0:T(8,128)(2,1)S(1)} collective-permute-done((bf16[2,256,512]{2,1,0:T(8,128)(2,1)}, bf16[2,256,512]{2,1,0:T(8,128)(2,1)S(1)}, u32[]{:S(2)}, u32[]{:S(2)}) %collective-permute-start.26) | collective-permute-done | bytes 524320 | tf_op jit(solution)/shard_map/ppermute | solution.py:223
  97.2 1.5 %collective-permute-done.27.refs_1_.refs_3_.refs_12_.refs_15_.refs_11_ = bf16[2,256,512]{2,1,0:T(8,128)(2,1)S(1)} collective-permute-done((bf16[2,256,512]{2,1,0:T(8,128)(2,1)}, bf16[2,256,512]{2,1,0:T(8,128)(2,1)S(1)}, u32[]{:S(2)}, u32[]{:S(2)}) %collective-permute-start.27) | collective-permute-done | bytes 524320 | tf_op jit(solution)/shard_map/ppermute | solution.py:223
  98.8 1.8 %collective-permute-start.28 = (bf16[1,256,512]{2,1,0:T(8,128)(2,1)S(1)}, bf16[1,256,512]{2,1,0:T(8,128)(2,1)S(1)}, u32[]{:S(2)}, u32[]{:S(2)}) collective-permute-start(bf16[1,256,512]{2,1,0:T(8,128)(2,1)S(1)} %get-tuple-element.31), channel_id=1, source_target_pairs={{0,8},{8,16},{16,24},{24,28},{28,20},{20,12},{12,4},{4,0},{1,9},{9... | collective-permute-start | bytes 786440 | tf_op jit(solution)/shard_map/ppermute | solution.py:223
  100.6 0.3 collective-permute-start.29
  100.9 7.8 %shard_map.87.refs_14_ = f32[18,1664]{1,0:T(8,128)S(1)} custom-call(s32[12]{0:T(128)S(1)} %stack.48.refs_0_, bf16[1664,512]{1,0:T(8,128)(2,1)} %get-tuple-element.29.refs_1_, bf16[1664,512]{1,0:T(8,128)(2,1)} %collective-permute-done.24.refs_2_, bf16[1664,512]{1,0:T(8,128)(2,1)} %get-tuple-element.30.refs_3_, ...), custom_call_target="tpu_custom_call" | custom-call | flops 3489660928 | tf_op jit(solution)/shard_map/pallas_call | solution.py:165
  108.7 7.8 %shard_map.88.q0 = f32[18,1664]{1,0:T(8,128)S(1)} custom-call(s32[12]{0:T(128)S(1)} %stack.48.refs_0_, bf16[1664,512]{1,0:T(8,128)(2,1)} %get-tuple-element.29.refs_1_, bf16[1664,512]{1,0:T(8,128)(2,1)} %collective-permute-done.24.refs_2_, bf16[1664,512]{1,0:T(8,128)(2,1)} %get-tuple-element.30.refs_3_, bf16[1664,512]{1,0:T(8,128)(2,1)} %collective-permute-done.25.refs_4_, ...), custom_call_target="tpu_custom_call" | custom-call | flops 3489660928 | tf_op jit(solution)/shard_map/pallas_call | solution.py:165
  116.6 1.4 %collective-permute-done.30.q1 = f32[18,1664]{1,0:T(8,128)S(1)} collective-permute-done((f32[18,1664]{1,0:T(8,128)S(1)}, f32[18,1664]{1,0:T(8,128)S(1)}, u32[]{:S(2)}, u32[]{:S(2)}) %collective-permute-start.30) | collective-permute-done | bytes 119840 | tf_op jit(solution)/shard_map/ppermute | solution.py:223
  118.0 0.7 copy-done.16
  118.7 2.3 %shard_map.89 = f32[1,1664]{1,0:T(1,128)} custom-call(f32[18,1664]{1,0:T(8,128)} %copy-done.8, f32[18,1664]{1,0:T(8,128)} %copy-done.16, f32[1,1664]{1,0:T(1,128)} %copy-done.9, s32[1,1664]{1,0:T(1,128)} %copy-done.10, s32[1,1664]{1,0:T(1,128)} %copy-done.11, f32[1,1664]{1,0:T(1,128)} %copy-done.12), custom_call_target="tpu_custom_call" | custom-call | tf_op jit(solution)/shard_map/pallas_call | solution.py:207
  120.9 2.0 %collective-permute-start.31 = (f32[1,1664]{1,0:T(1,128)}, f32[1,1664]{1,0:T(1,128)S(1)}, u32[]{:S(2)}, u32[]{:S(2)}) collective-permute-start(f32[1,1664]{1,0:T(1,128)} %shard_map.89), channel_id=1, source_target_pairs={{0,2},{1,3},{2,0},{3,1},{4,6},{5,7},{6,4},{7,5},{8,10},{9,11},{10,... | collective-permute-start | bytes 19976 | tf_op jit(solution)/shard_map/ppermute | solution.py:223
  123.0 1.8 %collective-permute-done.31 = f32[1,1664]{1,0:T(1,128)S(1)} collective-permute-done((f32[1,1664]{1,0:T(1,128)}, f32[1,1664]{1,0:T(1,128)S(1)}, u32[]{:S(2)}, u32[]{:S(2)}) %collective-permute-start.31) | collective-permute-done | bytes 6688 | tf_op jit(solution)/shard_map/ppermute | solution.py:223
  124.8 0.7 broadcast_select_fusion.1
  125.5 0.7 reshape.19
  (72 shorter events, 0.8 us)
Async XLA Ops:
  0.0 1.0 copy-start.7
  1.0 16.0 %copy-start.17 = (f32[52,64]{1,0:T(8,128)S(1)}, f32[52,64]{1,0:T(8,128)}, u32[]{:S(2)}) copy-start(f32[52,64]{1,0:T(8,128)} %param.13) | copy-start | bytes 39940
  1.0 16.0 %copy-start.18 = (f32[52,64]{1,0:T(8,128)S(1)}, f32[52,64]{1,0:T(8,128)}, u32[]{:S(2)}) copy-start(f32[52,64]{1,0:T(8,128)} %param.10) | copy-start | bytes 39940
  1.0 16.1 %copy-start.19 = (s32[52,64]{1,0:T(8,128)S(1)}, s32[52,64]{1,0:T(8,128)}, u32[]{:S(2)}) copy-start(s32[52,64]{1,0:T(8,128)} %param.12) | copy-start | bytes 39940
  1.1 16.1 %copy-start.20 = (s32[52,64]{1,0:T(8,128)S(1)}, s32[52,64]{1,0:T(8,128)}, u32[]{:S(2)}) copy-start(s32[52,64]{1,0:T(8,128)} %param.11) | copy-start | bytes 39940
  1.7 13.6 %copy-start.13 = (bf16[1,256,512]{2,1,0:T(8,128)(2,1)}, bf16[1,256,512]{2,1,0:T(8,128)(2,1)S(1)}, u32[]{:S(2)}) copy-start(bf16[1,256,512]{2,1,0:T(8,128)(2,1)S(1)} %get-tuple-element.21.refs_11_) | copy-start | bytes 786436
  1.7 11.4 %collective-permute-start.1 = (bf16[1,256,512]{2,1,0:T(8,128)(2,1)S(1)}, bf16[1,256,512]{2,1,0:T(8,128)(2,1)S(1)}, u32[]{:S(2)}, u32[]{:S(2)}) collective-permute-start(bf16[1,256,512]{2,1,0:T(8,128)(2,1)S(1)} %get-tuple-element.21.refs_11_), channel_id=1, source_target_pairs={{0,8},{8,16},{16,24},{24,28},{28,20},{20,12},{12,4},{4,0},{1,9},{9... | collective-permute-start | bytes 786440 | tf_op jit(solution)/shard_map/ppermute | solution.py:223
  4.8 8.3 %collective-permute-start.2 = (bf16[1,256,512]{2,1,0:T(8,128)(2,1)S(1)}, bf16[1,256,512]{2,1,0:T(8,128)(2,1)S(1)}, u32[]{:S(2)}, u32[]{:S(2)}) collective-permute-start(bf16[1,256,512]{2,1,0:T(8,128)(2,1)S(1)} %get-tuple-element.21.refs_11_), channel_id=1, source_target_pairs={{8,0},{16,8},{24,16},{28,24},{20,28},{12,20},{4,12},{0,4},{9,1},{1... | collective-permute-start | bytes 786440 | tf_op jit(solution)/shard_map/ppermute | solution.py:223
  4.8 8.3 %collective-permute-start.3 = (bf16[1,256,512]{2,1,0:T(8,128)(2,1)S(1)}, bf16[1,256,512]{2,1,0:T(8,128)(2,1)S(1)}, u32[]{:S(2)}, u32[]{:S(2)}) collective-permute-start(bf16[1,256,512]{2,1,0:T(8,128)(2,1)S(1)} %get-tuple-element.21.refs_11_), channel_id=1, source_target_pairs={{0,2},{1,3},{2,0},{3,1},{4,6},{5,7},{6,4},{7,5},{8,10},{9,11},{10,... | collective-permute-start | bytes 786440 | tf_op jit(solution)/shard_map/ppermute | solution.py:223
  6.7 6.3 %collective-permute-start.4 = (bf16[18,512]{1,0:T(8,128)(2,1)}, bf16[18,512]{1,0:T(8,128)(2,1)S(1)}, u32[]{:S(2)}, u32[]{:S(2)}) collective-permute-start(bf16[18,512]{1,0:T(8,128)(2,1)} %bitcast.16), channel_id=1, source_target_pairs={{0,2},{1,3},{2,0},{3,1},{4,6},{5,7},{6,4},{7,5},{8,10},{9,11},{10,... | collective-permute-start | bytes 55304 | tf_op jit(solution)/shard_map/ppermute | solution.py:223
  13.2 12.5 %collective-permute-start.7 = (bf16[2,256,512]{2,1,0:T(8,128)(2,1)S(1)}, bf16[2,256,512]{2,1,0:T(8,128)(2,1)S(1)}, u32[]{:S(2)}, u32[]{:S(2)}) collective-permute-start(bf16[2,256,512]{2,1,0:T(8,128)(2,1)S(1)} %get-tuple-element.22.refs_5_), channel_id=1, source_target_pairs={{0,8},{8,16},{16,24},{24,28},{28,20},{20,12},{12,4},{4,0},{1,9},{9... | collective-permute-start | bytes 1572872 | tf_op jit(solution)/shard_map/ppermute | solution.py:223
  15.0 12.2 %collective-permute-start.8 = (bf16[2,256,512]{2,1,0:T(8,128)(2,1)S(1)}, bf16[2,256,512]{2,1,0:T(8,128)(2,1)}, u32[]{:S(2)}, u32[]{:S(2)}) collective-permute-start(bf16[2,256,512]{2,1,0:T(8,128)(2,1)S(1)} %get-tuple-element.23.refs_6_), channel_id=1, source_target_pairs={{8,0},{16,8},{24,16},{28,24},{20,28},{12,20},{4,12},{0,4},{9,1},{1... | collective-permute-start | bytes 1572872 | tf_op jit(solution)/shard_map/ppermute | solution.py:223
  15.3 6.5 %collective-permute-start.5 = (bf16[1,256,512]{2,1,0:T(8,128)(2,1)S(1)}, bf16[1,256,512]{2,1,0:T(8,128)(2,1)S(1)}, u32[]{:S(2)}, u32[]{:S(2)}) collective-permute-start(bf16[1,256,512]{2,1,0:T(8,128)(2,1)S(1)} %shard_map.76), channel_id=1, source_target_pairs={{0,2},{1,3},{2,0},{3,1},{4,6},{5,7},{6,4},{7,5},{8,10},{9,11},{10,... | collective-permute-start | bytes 786440 | tf_op jit(solution)/shard_map/ppermute | solution.py:223
  17.2 49.2 %copy-start.9 = (f32[1,1664]{1,0:T(1,128)}, f32[1,1664]{1,0:T(1,128)S(1)}, u32[]{:S(2)}) copy-start(f32[1,1664]{1,0:T(1,128)S(1)} %reshape.15.refs_8_.refs_27_.rewards) | copy-start | bytes 19972
  17.3 49.1 %copy-start.10 = (s32[1,1664]{1,0:T(1,128)}, s32[1,1664]{1,0:T(1,128)S(1)}, u32[]{:S(2)}) copy-start(s32[1,1664]{1,0:T(1,128)S(1)} %reshape.16.refs_9_.refs_28_.actions) | copy-start | bytes 19972
  17.4 49.1 %copy-start.11 = (s32[1,1664]{1,0:T(1,128)}, s32[1,1664]{1,0:T(1,128)S(1)}, u32[]{:S(2)}) copy-start(s32[1,1664]{1,0:T(1,128)S(1)} %reshape.17.refs_10_.refs_29_.done_flags) | copy-start | bytes 19972
  17.5 49.0 %copy-start.12 = (f32[1,1664]{1,0:T(1,128)}, f32[1,1664]{1,0:T(1,128)S(1)}, u32[]{:S(2)}) copy-start(f32[1,1664]{1,0:T(1,128)S(1)} %reshape.18.refs_11_.refs_30_.behaviour) | copy-start | bytes 19972
  17.5 2.0 %copy-start = (bf16[3328,512]{1,0:T(8,128)(2,1)S(1)}, bf16[3328,512]{1,0:T(8,128)(2,1)}, u32[]{:S(2)}) copy-start(bf16[3328,512]{1,0:T(8,128)(2,1)} %source.2) | copy-start | bytes 10223620
  21.9 11.9 %collective-permute-start.6 = (bf16[512,512]{1,0:T(8,128)(2,1)S(1)}, bf16[512,512]{1,0:T(8,128)(2,1)}, u32[]{:S(2)}, u32[]{:S(2)}) collective-permute-start(bf16[512,512]{1,0:T(8,128)(2,1)S(1)} %shard_map.77), channel_id=1, source_target_pairs={{0,2},{1,3},{2,0},{3,1},{4,6},{5,7},{6,4},{7,5},{8,10},{9,11},{10,... | collective-permute-start | bytes 1572872 | tf_op jit(solution)/shard_map/ppermute | solution.py:223
  25.7 8.3 %copy-start.1 = (bf16[2,256,512]{2,1,0:T(8,128)(2,1)}, bf16[2,256,512]{2,1,0:T(8,128)(2,1)S(1)}, u32[]{:S(2)}) copy-start(bf16[2,256,512]{2,1,0:T(8,128)(2,1)S(1)} %collective-permute-done.7.refs_1_.refs_3_.refs_13_.refs_20_) | copy-start | bytes 1572868
  25.7 12.1 %collective-permute-start.10 = (bf16[2,256,512]{2,1,0:T(8,128)(2,1)S(1)}, bf16[2,256,512]{2,1,0:T(8,128)(2,1)S(1)}, u32[]{:S(2)}, u32[]{:S(2)}) collective-permute-start(bf16[2,256,512]{2,1,0:T(8,128)(2,1)S(1)} %collective-permute-done.7.refs_1_.refs_3_.refs_13_.refs_20_), channel_id=1, source_target_pairs={{0,8},{8,16},{16,24},{24,28},{28,20},{20,12},{12,4},{4,0},{1,9},{9... | collective-permute-start | bytes 1572872 | tf_op jit(solution)/shard_map/ppermute | solution.py:223
  27.2 12.0 %collective-permute-start.11 = (bf16[2,256,512]{2,1,0:T(8,128)(2,1)}, bf16[2,256,512]{2,1,0:T(8,128)(2,1)S(1)}, u32[]{:S(2)}, u32[]{:S(2)}) collective-permute-start(bf16[2,256,512]{2,1,0:T(8,128)(2,1)} %collective-permute-done.8.refs_2_.refs_4_.refs_17_.refs_24_), channel_id=1, source_target_pairs={{8,0},{16,8},{24,16},{28,24},{20,28},{12,20},{4,12},{0,4},{9,1},{1... | collective-permute-start | bytes 1572872 | tf_op jit(solution)/shard_map/ppermute | solution.py:223
  27.8 38.1 %collective-permute-start = (bf16[1664,512]{1,0:T(8,128)(2,1)}, bf16[1664,512]{1,0:T(8,128)(2,1)}, u32[]{:S(2)}, u32[]{:S(2)}) collective-permute-start(bf16[1664,512]{1,0:T(8,128)(2,1)} %get-tuple-element.19.refs_1_), channel_id=1, source_target_pairs={{0,1},{1,0},{2,3},{3,2},{4,5},{5,4},{6,7},{7,6},{8,9},{9,8},{10,11... | collective-permute-start | bytes 5111816 | tf_op jit(solution)/shard_map/ppermute | solution.py:223
  34.0 9.2 %collective-permute-start.9 = (bf16[384,512]{1,0:T(8,128)(2,1)S(1)}, bf16[384,512]{1,0:T(8,128)(2,1)}, u32[]{:S(2)}, u32[]{:S(2)}) collective-permute-start(bf16[384,512]{1,0:T(8,128)(2,1)S(1)} %shard_map.78), channel_id=1, source_target_pairs={{0,2},{1,3},{2,0},{3,1},{4,6},{5,7},{6,4},{7,5},{8,10},{9,11},{10,... | collective-permute-start | bytes 1179656 | tf_op jit(solution)/shard_map/ppermute | solution.py:223
  37.8 11.2 %collective-permute-start.13 = (bf16[2,256,512]{2,1,0:T(8,128)(2,1)S(1)}, bf16[2,256,512]{2,1,0:T(8,128)(2,1)S(1)}, u32[]{:S(2)}, u32[]{:S(2)}) collective-permute-start(bf16[2,256,512]{2,1,0:T(8,128)(2,1)S(1)} %collective-permute-done.10.refs_2_.refs_1_.refs_3_.refs_14_.refs_21_), channel_id=1, source_target_pairs={{0,8},{8,16},{16,24},{24,28},{28,20},{20,12},{12,4},{4,0},{1,9},{9... | collective-permute-start | bytes 1572872 | tf_op jit(solution)/shard_map/ppermute | solution.py:223
  39.2 10.7 %collective-permute-start.14 = (bf16[2,256,512]{2,1,0:T(8,128)(2,1)S(1)}, bf16[2,256,512]{2,1,0:T(8,128)(2,1)S(1)}, u32[]{:S(2)}, u32[]{:S(2)}) collective-permute-start(bf16[2,256,512]{2,1,0:T(8,128)(2,1)S(1)} %shard_map.79.refs_4_), channel_id=1, source_target_pairs={{8,0},{16,8},{24,16},{28,24},{20,28},{12,20},{4,12},{0,4},{9,1},{1... | collective-permute-start | bytes 1572872 | tf_op jit(solution)/shard_map/ppermute | solution.py:223
  43.4 9.6 %collective-permute-start.12 = (bf16[384,512]{1,0:T(8,128)(2,1)S(1)}, bf16[384,512]{1,0:T(8,128)(2,1)}, u32[]{:S(2)}, u32[]{:S(2)}) collective-permute-start(bf16[384,512]{1,0:T(8,128)(2,1)S(1)} %shard_map.80), channel_id=1, source_target_pairs={{0,2},{1,3},{2,0},{3,1},{4,6},{5,7},{6,4},{7,5},{8,10},{9,11},{10,... | collective-permute-start | bytes 1179656 | tf_op jit(solution)/shard_map/ppermute | solution.py:223
  50.0 11.6 %collective-permute-start.20 = (bf16[2,256,512]{2,1,0:T(8,128)(2,1)S(1)}, bf16[2,256,512]{2,1,0:T(8,128)(2,1)S(1)}, u32[]{:S(2)}, u32[]{:S(2)}) collective-permute-start(bf16[2,256,512]{2,1,0:T(8,128)(2,1)S(1)} %get-tuple-element.25.refs_3_), channel_id=1, source_target_pairs={{0,8},{8,16},{16,24},{24,28},{28,20},{20,12},{12,4},{4,0},{1,9},{9... | collective-permute-start | bytes 1572872 | tf_op jit(solution)/shard_map/ppermute | solution.py:223
  51.7 11.3 %collective-permute-start.21 = (bf16[2,256,512]{2,1,0:T(8,128)(2,1)S(1)}, bf16[2,256,512]{2,1,0:T(8,128)(2,1)}, u32[]{:S(2)}, u32[]{:S(2)}) collective-permute-start(bf16[2,256,512]{2,1,0:T(8,128)(2,1)S(1)} %get-tuple-element.26.refs_4_), channel_id=1, source_target_pairs={{8,0},{16,8},{24,16},{28,24},{20,28},{12,20},{4,12},{0,4},{9,1},{1... | collective-permute-start | bytes 1572872 | tf_op jit(solution)/shard_map/ppermute | solution.py:223
  53.2 8.4 %collective-permute-start.15 = (bf16[384,512]{1,0:T(8,128)(2,1)S(1)}, bf16[384,512]{1,0:T(8,128)(2,1)}, u32[]{:S(2)}, u32[]{:S(2)}) collective-permute-start(bf16[384,512]{1,0:T(8,128)(2,1)S(1)} %shard_map.82), channel_id=1, source_target_pairs={{0,2},{1,3},{2,0},{3,1},{4,6},{5,7},{6,4},{7,5},{8,10},{9,11},{10,... | collective-permute-start | bytes 1179656 | tf_op jit(solution)/shard_map/ppermute | solution.py:223
  55.8 8.4 %collective-permute-start.16 = (bf16[512,512]{1,0:T(8,128)(2,1)}, bf16[512,512]{1,0:T(8,128)(2,1)}, u32[]{:S(2)}, u32[]{:S(2)}) collective-permute-start(bf16[512,512]{1,0:T(8,128)(2,1)} %collective-permute-done.6.refs_5_.refs_3_), channel_id=1, source_target_pairs={{0,1},{1,0},{2,3},{3,2},{4,5},{5,4},{6,7},{7,6},{8,9},{9,8},{10,11... | collective-permute-start | bytes 1572872 | tf_op jit(solution)/shard_map/ppermute | solution.py:223
  61.6 4.8 %collective-permute-start.17 = (bf16[384,512]{1,0:T(8,128)(2,1)}, bf16[384,512]{1,0:T(8,128)(2,1)}, u32[]{:S(2)}, u32[]{:S(2)}) collective-permute-start(bf16[384,512]{1,0:T(8,128)(2,1)} %collective-permute-done.9.refs_5_.refs_4_), channel_id=1, source_target_pairs={{0,1},{1,0},{2,3},{3,2},{4,5},{5,4},{6,7},{7,6},{8,9},{9,8},{10,11... | collective-permute-start | bytes 1179656 | tf_op jit(solution)/shard_map/ppermute | solution.py:223
  61.6 0.8 copy-start.3
  62.5 3.9 %collective-permute-start.18 = (bf16[384,512]{1,0:T(8,128)(2,1)}, bf16[384,512]{1,0:T(8,128)(2,1)}, u32[]{:S(2)}, u32[]{:S(2)}) collective-permute-start(bf16[384,512]{1,0:T(8,128)(2,1)} %collective-permute-done.12.refs_5_), channel_id=1, source_target_pairs={{0,1},{1,0},{2,3},{3,2},{4,5},{5,4},{6,7},{7,6},{8,9},{9,8},{10,11... | collective-permute-start | bytes 1179656 | tf_op jit(solution)/shard_map/ppermute | solution.py:223
  63.0 3.4 %collective-permute-start.19 = (bf16[384,512]{1,0:T(8,128)(2,1)}, bf16[384,512]{1,0:T(8,128)(2,1)}, u32[]{:S(2)}, u32[]{:S(2)}) collective-permute-start(bf16[384,512]{1,0:T(8,128)(2,1)} %collective-permute-done.15.refs_6_), channel_id=1, source_target_pairs={{0,1},{1,0},{2,3},{3,2},{4,5},{5,4},{6,7},{7,6},{8,9},{9,8},{10,11... | collective-permute-start | bytes 1179656 | tf_op jit(solution)/shard_map/ppermute | solution.py:223
  63.1 1.0 copy-start.4
  64.1 2.3 %copy-start.2 = (bf16[2,256,512]{2,1,0:T(8,128)(2,1)S(1)}, bf16[2,256,512]{2,1,0:T(8,128)(2,1)}, u32[]{:S(2)}) copy-start(bf16[2,256,512]{2,1,0:T(8,128)(2,1)} %copy-done.1) | copy-start | bytes 1572868
  64.1 2.3 %copy-start.5 = (bf16[2,256,512]{2,1,0:T(8,128)(2,1)S(1)}, bf16[2,256,512]{2,1,0:T(8,128)(2,1)}, u32[]{:S(2)}) copy-start(bf16[2,256,512]{2,1,0:T(8,128)(2,1)} %copy-done.3) | copy-start | bytes 1572868
  64.1 2.4 %copy-start.14 = (bf16[1,256,512]{2,1,0:T(8,128)(2,1)S(1)}, bf16[1,256,512]{2,1,0:T(8,128)(2,1)}, u32[]{:S(2)}) copy-start(bf16[1,256,512]{2,1,0:T(8,128)(2,1)} %copy-done.13) | copy-start | bytes 786436
  64.2 14.8 %collective-permute-start.22 = (bf16[2,256,512]{2,1,0:T(8,128)(2,1)S(1)}, bf16[2,256,512]{2,1,0:T(8,128)(2,1)}, u32[]{:S(2)}, u32[]{:S(2)}) collective-permute-start(bf16[2,256,512]{2,1,0:T(8,128)(2,1)S(1)} %shard_map.84), channel_id=1, source_target_pairs={{0,8},{8,16},{16,24},{24,28},{28,20},{20,12},{12,4},{4,0},{1,9},{9... | collective-permute-start | bytes 1572872 | tf_op jit(solution)/shard_map/ppermute | solution.py:223
  65.8 14.4 %collective-permute-start.23 = (bf16[2,256,512]{2,1,0:T(8,128)(2,1)}, bf16[2,256,512]{2,1,0:T(8,128)(2,1)}, u32[]{:S(2)}, u32[]{:S(2)}) collective-permute-start(bf16[2,256,512]{2,1,0:T(8,128)(2,1)} %collective-permute-done.21.refs_3_.refs_10_.refs_9_), channel_id=1, source_target_pairs={{8,0},{16,8},{24,16},{28,24},{20,28},{12,20},{4,12},{0,4},{9,1},{1... | collective-permute-start | bytes 1572872 | tf_op jit(solution)/shard_map/ppermute | solution.py:223
  82.5 18.3 %copy-start.6 = (bf16[2,256,512]{2,1,0:T(8,128)(2,1)S(1)}, bf16[2,256,512]{2,1,0:T(8,128)(2,1)}, u32[]{:S(2)}) copy-start(bf16[2,256,512]{2,1,0:T(8,128)(2,1)} %copy-done.3) | copy-start | bytes 1572868
  82.5 18.3 %copy-start.15 = (bf16[512,18]{0,1:T(8,128)(2,1)S(1)}, bf16[512,18]{0,1:T(8,128)(2,1)}, u32[]{:S(2)}) copy-start(bf16[512,18]{0,1:T(8,128)(2,1)} %param.9) | copy-start | bytes 55300
  82.5 18.3 %collective-permute-start.24 = (bf16[1664,512]{1,0:T(8,128)(2,1)}, bf16[1664,512]{1,0:T(8,128)(2,1)}, u32[]{:S(2)}, u32[]{:S(2)}) collective-permute-start(bf16[1664,512]{1,0:T(8,128)(2,1)} %get-tuple-element.29.refs_1_), channel_id=1, source_target_pairs={{0,1},{1,0},{2,3},{3,2},{4,5},{5,4},{6,7},{7,6},{8,9},{9,8},{10,11... | collective-permute-start | bytes 5111816 | tf_op jit(solution)/shard_map/ppermute | solution.py:223
  82.6 18.2 %collective-permute-start.25 = (bf16[1664,512]{1,0:T(8,128)(2,1)}, bf16[1664,512]{1,0:T(8,128)(2,1)}, u32[]{:S(2)}, u32[]{:S(2)}) collective-permute-start(bf16[1664,512]{1,0:T(8,128)(2,1)} %get-tuple-element.30.refs_3_), channel_id=1, source_target_pairs={{0,1},{1,0},{2,3},{3,2},{4,5},{5,4},{6,7},{7,6},{8,9},{9,8},{10,11... | collective-permute-start | bytes 5111816 | tf_op jit(solution)/shard_map/ppermute | solution.py:223
  83.1 14.1 %collective-permute-start.26 = (bf16[2,256,512]{2,1,0:T(8,128)(2,1)}, bf16[2,256,512]{2,1,0:T(8,128)(2,1)S(1)}, u32[]{:S(2)}, u32[]{:S(2)}) collective-permute-start(bf16[2,256,512]{2,1,0:T(8,128)(2,1)} %collective-permute-done.22.refs_2_.refs_7_.refs_6_), channel_id=1, source_target_pairs={{0,8},{8,16},{16,24},{24,28},{28,20},{20,12},{12,4},{4,0},{1,9},{9... | collective-permute-start | bytes 1572872 | tf_op jit(solution)/shard_map/ppermute | solution.py:223
  84.7 14.0 %collective-permute-start.27 = (bf16[2,256,512]{2,1,0:T(8,128)(2,1)}, bf16[2,256,512]{2,1,0:T(8,128)(2,1)S(1)}, u32[]{:S(2)}, u32[]{:S(2)}) collective-permute-start(bf16[2,256,512]{2,1,0:T(8,128)(2,1)} %collective-permute-done.23.refs_3_.refs_11_.refs_10_), channel_id=1, source_target_pairs={{8,0},{16,8},{24,16},{28,24},{20,28},{12,20},{4,12},{0,4},{9,1},{1... | collective-permute-start | bytes 1572872 | tf_op jit(solution)/shard_map/ppermute | solution.py:223
  98.8 9.9 %collective-permute-start.28 = (bf16[1,256,512]{2,1,0:T(8,128)(2,1)S(1)}, bf16[1,256,512]{2,1,0:T(8,128)(2,1)S(1)}, u32[]{:S(2)}, u32[]{:S(2)}) collective-permute-start(bf16[1,256,512]{2,1,0:T(8,128)(2,1)S(1)} %get-tuple-element.31), channel_id=1, source_target_pairs={{0,8},{8,16},{16,24},{24,28},{28,20},{20,12},{12,4},{4,0},{1,9},{9... | collective-permute-start | bytes 786440 | tf_op jit(solution)/shard_map/ppermute | solution.py:223
  100.6 8.1 %collective-permute-start.29 = (bf16[1,256,512]{2,1,0:T(8,128)(2,1)S(1)}, bf16[1,256,512]{2,1,0:T(8,128)(2,1)S(1)}, u32[]{:S(2)}, u32[]{:S(2)}) collective-permute-start(bf16[1,256,512]{2,1,0:T(8,128)(2,1)S(1)} %get-tuple-element.32), channel_id=1, source_target_pairs={{8,0},{16,8},{24,16},{28,24},{20,28},{12,20},{4,12},{0,4},{9,1},{1... | collective-permute-start | bytes 786440 | tf_op jit(solution)/shard_map/ppermute | solution.py:223
  116.5 1.5 %copy-start.8 = (f32[18,1664]{1,0:T(8,128)}, f32[18,1664]{1,0:T(8,128)S(1)}, u32[]{:S(2)}) copy-start(f32[18,1664]{1,0:T(8,128)S(1)} %shard_map.88.q0) | copy-start | bytes 359428
  116.5 1.5 %collective-permute-start.30 = (f32[18,1664]{1,0:T(8,128)S(1)}, f32[18,1664]{1,0:T(8,128)S(1)}, u32[]{:S(2)}, u32[]{:S(2)}) collective-permute-start(f32[18,1664]{1,0:T(8,128)S(1)} %shard_map.88.q0), channel_id=1, source_target_pairs={{0,1},{1,0},{2,3},{3,2},{4,5},{5,4},{6,7},{7,6},{8,9},{9,8},{10,11... | collective-permute-start | bytes 359432 | tf_op jit(solution)/shard_map/ppermute | solution.py:223
  118.0 0.7 copy-start.16
  120.9 3.8 %collective-permute-start.31 = (f32[1,1664]{1,0:T(1,128)}, f32[1,1664]{1,0:T(1,128)S(1)}, u32[]{:S(2)}, u32[]{:S(2)}) collective-permute-start(f32[1,1664]{1,0:T(1,128)} %shard_map.89), channel_id=1, source_target_pairs={{0,2},{1,3},{2,0},{3,1},{4,6},{5,7},{6,4},{7,5},{8,10},{9,11},{10,... | collective-permute-start | bytes 19976 | tf_op jit(solution)/shard_map/ppermute | solution.py:223

commit v4 on v3

--- a/solution.py
+++ b/solution.py
@@ -80,6 +80,23 @@
         out_specs=[pl.BlockSpec(memory_space=pltpu.VMEM)] * len(shapes),
         scratch_shapes=[pltpu.SemaphoreType.DMA((pieces,))],
         compiler_params=pltpu.CompilerParams(vmem_limit_bytes=held + 1024 * 1024),
+        cost_estimate=FREE,
+    )(*arrays, *after)
+
+
+def hold_kernel(*refs):
+    pass
+
+
+def hold(arrays, after):
+    anywhere = pl.BlockSpec(memory_space=pl.ANY)
+    return pl.pallas_call(
+        hold_kernel,
+        out_shape=[jax.ShapeDtypeStruct(a.shape, a.dtype) for a in arrays],
+        in_specs=[anywhere] * (len(arrays) + len(after)),
+        out_specs=[anywhere] * len(arrays),
+        input_output_aliases={i: i for i in range(len(arrays))},
+        compiler_params=pltpu.CompilerParams(vmem_limit_bytes=1024 * 1024),
         cost_estimate=FREE,
     )(*arrays, *after)
 
@@ -171,7 +188,7 @@
         + [anywhere] * len(after),
         out_specs=vmem if headed else [anywhere] * count,
         scratch_shapes=scratch,
-        compiler_params=pltpu.CompilerParams(vmem_limit_bytes=24 * 1024 * 1024),
+        compiler_params=pltpu.CompilerParams(vmem_limit_bytes=56 * 1024 * 1024),
         cost_estimate=pl.CostEstimate(flops=2 * rows * depth * width * count, bytes_accessed=0, transcendentals=0),
     )(pos, *[a for h in hs for a in h], *ws, *extra, *after)
 
@@ -252,7 +269,7 @@
     w1_y = to_y(w1)
     kept_c = to_core(kept)
     turns = (long, short)
-    ways = ([to_next(w1)], [to_last(w1)])
+    ways = ([to_next(layer_weights)], [to_last(layer_weights)])
     sizes = [size for _, size in tiles_of(rows, TILE)]
     parts, start, came, came_c = list(sizes), 0, [], []
     now = [*(way[0] for way in ways), w1_y, head_y]
@@ -266,10 +283,10 @@
             if i == 1:
                 build.append([(last, 0, 1), (w1_y, 0, 1)])
             elif i == turn:
-                build.append([(last, 1, 1), (w2, 0, 1)])
+                build.append([(last, 1, 1), (way[0], 1, 1)])
             elif i == turn + 1:
                 build.append([(last, 1, 1), (w2_y, 0, 1)])
-            elif i == dp - 1:
+            elif i == dp - 2:
                 build.append([(last, 1, 1)])
             else:
                 build.append(None)
@@ -289,15 +306,15 @@
             first = [[], []]
             for way, turn in zip(ways, turns):
                 first[0].append([(way[h - 1], 0) for h in range(1, turn + 1)])
-                first[1].append([(way[h], min(1, way[h].shape[0] - 1) if h < turn else 0) for h in range(1, turn + 1)])
+                first[1].append([(way[h], 1 if h < turn else 0) for h in range(1, turn + 1)])
             h1 = run([(w1, first[0]), (w1_y, first[1])], [[kept], [kept_c], came, came_c], after=flat)
-            now = [*now, h1[0]]
-            mine, theirs = gate([[(h1[0], 0, rows)], [(h1[1], 0, rows)]], now)
+            mine, theirs = hold(h1, now)
+            now = [*now, mine]
             h1 = [[mine], [to_core(mine)], [theirs], [to_core(theirs)]]
     second = [[], []]
     for way, turn in zip(ways, turns):
-        second[0].append([(way[h], 1 if h == turn else 0) for h in range(turn, dp - 1)])
-        second[1].append([(way[h + 1], 1 if h + 1 < dp - 1 else 0) for h in range(turn, dp - 1)])
+        second[0].append([(way[0], 1), (way[turn], 1)] + [(way[h], 0) for h in range(turn + 1, dp - 2)])
+        second[1].append([(way[h], 1) for h in range(turn + 1, dp - 2)] + [(way[-2], 0), (way[-1], 0)])
     q = run([(w2, second[0])], h1, head=head, after=[ways[0][-2], ways[1][-2]])
     q = run([(w2_y, second[1])], h1, head=head_y, before=q)
     own = retrace(q, to_core(q), *flat, rewards.shape[1])

time: 127 us -> 124 us (0.976)
  waiting for transfers between devices: 50.3 us -> 44.4 us
  Pallas kernels: 35 us -> 37.8 us
  local copies, waits for them, and re-layouts: 6.77 us -> 9.04 us
  starting transfers between devices: 33 us -> 31.3 us
    ppermute x32, waiting for transfers between devices: 50.3 us -> 44.4 us  [over(): return lambda a: lax.ppermute(a, axis, pairs)]
    pallas_call x3, Pallas kernels: 26.3 us -> 30.8 us  [layer(): pl.pallas_call(functools.partial(layer_kernel, [len(h) for h in hs], bloc...]
    ppermute x32, starting transfers between devices: 33 us -> 31.3 us  [over(): return lambda a: lax.ppermute(a, axis, pairs)]
    pallas_call x11 -> x10, Pallas kernels: 3.37 us -> 1.76 us  [gate(): pl.pallas_call(functools.partial(gate_kernel, plan, pieces), out_shape=sh...]
    unnamed x42 -> x72, local copies, waits for them, and re-layouts: 5.58 us -> 6.65 us
  transfers between devices with their start and end apart: 32 -> 32, of which waited for: 15 -> 16; matrix products, arithmetic and copies ran while one was open for 0% -> 1% of each run, Pallas kernels for 17% -> 21%
where the time goes in v4:
time: 124 us
  waiting for transfers between devices  44.4 us (36%)
  Pallas kernels  37.8 us (30%)
  starting transfers between devices  31.3 us (25%)
  local copies, waits for them, and re-layouts  9.04 us (7%)
    ppermute x32, waiting for transfers between devices, over(): return lambda a: lax.ppermute(a, axis, pairs)  44.4 us
    ppermute x32, starting transfers between devices, over(): return lambda a: lax.ppermute(a, axis, pairs)  31.3 us
    pallas_call x3, Pallas kernels, layer(): pl.pallas_call(functools.partial(layer_kernel, [len(h) for h in hs], bloc...  30.8 us
    unnamed x72, local copies, waits for them, and re-layouts  6.65 us
    pallas_call x2, Pallas kernels, cut(): pl.pallas_call(functools.partial(cut_kernel, len(sizes)), out_shape=[jax....  2.92 us
  transfers between devices with their start and end apart: 32, of which 16 were waited for; matrix products, arithmetic and copies ran while one was open for 1% of the time, Pallas kernels for 21%

profile of v4, /device:TPU:0, one launch (start us, length us, event | category | flops | bytes accessed | tf_op | source)
XLA Modules:
  0.0 123.8 jit_solution(920668846027401187)
XLA Ops:
  0.0 3.0 %collective-permute-start.1 = (bf16[2,256,512]{2,1,0:T(8,128)(2,1)}, bf16[2,256,512]{2,1,0:T(8,128)(2,1)S(1)}, u32[]{:S(2)}, u32[]{:S(2)}) collective-permute-start(bf16[2,256,512]{2,1,0:T(8,128)(2,1)} %source.3), channel_id=1, source_target_pairs={{0,8},{8,16},{16,24},{24,28},{28,20},{20,12},{12,4},{4,0},{1,9},{9... | collective-permute-start | bytes 1572872 | tf_op jit(solution)/shard_map/ppermute | solution.py:240
  3.0 1.1 copy-done.14
  4.1 0.6 shard_map.74
  4.8 2.0 %collective-permute-start.3 = (bf16[1,256,512]{2,1,0:T(8,128)(2,1)S(1)}, bf16[1,256,512]{2,1,0:T(8,128)(2,1)S(1)}, u32[]{:S(2)}, u32[]{:S(2)}) collective-permute-start(bf16[1,256,512]{2,1,0:T(8,128)(2,1)S(1)} %get-tuple-element.21.refs_11_), channel_id=1, source_target_pairs={{0,2},{1,3},{2,0},{3,1},{4,6},{5,7},{6,4},{7,5},{8,10},{9,11},{10,... | collective-permute-start | bytes 786440 | tf_op jit(solution)/shard_map/ppermute | solution.py:240
  6.8 0.2 collective-permute-start.4
  6.9 6.2 %collective-permute-done.4.refs_6_.refs_4_.refs_13_ = bf16[18,512]{1,0:T(8,128)(2,1)S(1)} collective-permute-done((bf16[18,512]{1,0:T(8,128)(2,1)}, bf16[18,512]{1,0:T(8,128)(2,1)S(1)}, u32[]{:S(2)}, u32[]{:S(2)}) %collective-permute-start.4) | collective-permute-done | bytes 18464 | tf_op jit(solution)/shard_map/ppermute | solution.py:240
  13.1 1.9 %collective-permute-done.1.refs_0_.refs_3_.refs_1_.refs_12_.refs_6_ = bf16[2,256,512]{2,1,0:T(8,128)(2,1)S(1)} collective-permute-done((bf16[2,256,512]{2,1,0:T(8,128)(2,1)}, bf16[2,256,512]{2,1,0:T(8,128)(2,1)S(1)}, u32[]{:S(2)}, u32[]{:S(2)}) %collective-permute-start.1) | collective-permute-done | bytes 524320 | tf_op jit(solution)/shard_map/ppermute | solution.py:240
  15.1 1.5 %collective-permute-done.2.refs_2_.refs_4_.refs_1_.refs_16_.refs_9_ = bf16[2,256,512]{2,1,0:T(8,128)(2,1)S(1)} collective-permute-done((bf16[2,256,512]{2,1,0:T(8,128)(2,1)}, bf16[2,256,512]{2,1,0:T(8,128)(2,1)S(1)}, u32[]{:S(2)}, u32[]{:S(2)}) %collective-permute-start.2) | collective-permute-done | bytes 524320 | tf_op jit(solution)/shard_map/ppermute | solution.py:240
  16.7 1.6 %collective-permute-start.7 = (bf16[2,256,512]{2,1,0:T(8,128)(2,1)S(1)}, bf16[2,256,512]{2,1,0:T(8,128)(2,1)S(1)}, u32[]{:S(2)}, u32[]{:S(2)}) collective-permute-start(bf16[2,256,512]{2,1,0:T(8,128)(2,1)S(1)} %get-tuple-element.22.refs_5_), channel_id=1, source_target_pairs={{0,8},{8,16},{16,24},{24,28},{28,20},{20,12},{12,4},{4,0},{1,9},{9... | collective-permute-start | bytes 1572872 | tf_op jit(solution)/shard_map/ppermute | solution.py:240
  18.4 0.4 collective-permute-start.8
  18.8 0.7 shard_map.76
  19.6 1.6 %collective-permute-start.5 = (bf16[1,256,512]{2,1,0:T(8,128)(2,1)}, bf16[1,256,512]{2,1,0:T(8,128)(2,1)S(1)}, u32[]{:S(2)}, u32[]{:S(2)}) collective-permute-start(bf16[1,256,512]{2,1,0:T(8,128)(2,1)} %shard_map.76), channel_id=1, source_target_pairs={{0,2},{1,3},{2,0},{3,1},{4,6},{5,7},{6,4},{7,5},{8,10},{9,11},{10,... | collective-permute-start | bytes 786440 | tf_op jit(solution)/shard_map/ppermute | solution.py:240
  21.6 2.0 %copy-done.9 = bf16[3328,512]{1,0:T(8,128)(2,1)S(1)} copy-done((bf16[3328,512]{1,0:T(8,128)(2,1)S(1)}, bf16[3328,512]{1,0:T(8,128)(2,1)}, u32[]{:S(2)}) %copy-start.9) | copy-done | bytes 3407896
  23.6 2.3 %shard_map.73 = (bf16[1664,512]{1,0:T(8,128)(2,1)}, bf16[1664,512]{1,0:T(8,128)(2,1)S(1)}) custom-call(s32[2]{0:T(128)S(1)} %pad_add_fusion.at, bf16[3328,512]{1,0:T(8,128)(2,1)S(1)} %copy-done.9), custom_call_target="tpu_custom_call" | custom-call | tf_op jit(solution)/shard_map/pallas_call | solution.py:38
  25.9 0.3 collective-permute-done.5.refs_7_.refs_3_.refs_1_.refs_5_
  26.3 1.6 %collective-permute-start.6 = (bf16[512,512]{1,0:T(8,128)(2,1)S(1)}, bf16[512,512]{1,0:T(8,128)(2,1)S(1)}, u32[]{:S(2)}, u32[]{:S(2)}) collective-permute-start(bf16[512,512]{1,0:T(8,128)(2,1)S(1)} %shard_map.77), channel_id=1, source_target_pairs={{0,2},{1,3},{2,0},{3,1},{4,6},{5,7},{6,4},{7,5},{8,10},{9,11},{10,... | collective-permute-start | bytes 1572872 | tf_op jit(solution)/shard_map/ppermute | solution.py:240
  27.9 1.4 %collective-permute-done.7.refs_1_.refs_3_.refs_13_.refs_20_ = bf16[2,256,512]{2,1,0:T(8,128)(2,1)S(1)} collective-permute-done((bf16[2,256,512]{2,1,0:T(8,128)(2,1)S(1)}, bf16[2,256,512]{2,1,0:T(8,128)(2,1)S(1)}, u32[]{:S(2)}, u32[]{:S(2)}) %collective-permute-start.7) | collective-permute-done | bytes 524320 | tf_op jit(solution)/shard_map/ppermute | solution.py:240
  29.3 1.6 %collective-permute-start.10 = (bf16[2,256,512]{2,1,0:T(8,128)(2,1)S(1)}, bf16[2,256,512]{2,1,0:T(8,128)(2,1)S(1)}, u32[]{:S(2)}, u32[]{:S(2)}) collective-permute-start(bf16[2,256,512]{2,1,0:T(8,128)(2,1)S(1)} %collective-permute-done.7.refs_1_.refs_3_.refs_13_.refs_20_), channel_id=1, source_target_pairs={{0,8},{8,16},{16,24},{24,28},{28,20},{20,12},{12,4},{4,0},{1,9},{9... | collective-permute-start | bytes 1572872 | tf_op jit(solution)/shard_map/ppermute | solution.py:240
  30.9 0.5 collective-permute-start.11
  31.3 6.9 %collective-permute-done.6.refs_5_.refs_3_ = bf16[512,512]{1,0:T(8,128)(2,1)S(1)} collective-permute-done((bf16[512,512]{1,0:T(8,128)(2,1)S(1)}, bf16[512,512]{1,0:T(8,128)(2,1)S(1)}, u32[]{:S(2)}, u32[]{:S(2)}) %collective-permute-start.6) | collective-permute-done | bytes 524320 | tf_op jit(solution)/shard_map/ppermute | solution.py:240
  38.2 0.2 shard_map.78
  38.4 1.6 %collective-permute-start.9 = (bf16[384,512]{1,0:T(8,128)(2,1)S(1)}, bf16[384,512]{1,0:T(8,128)(2,1)S(1)}, u32[]{:S(2)}, u32[]{:S(2)}) collective-permute-start(bf16[384,512]{1,0:T(8,128)(2,1)S(1)} %shard_map.78), channel_id=1, source_target_pairs={{0,2},{1,3},{2,0},{3,1},{4,6},{5,7},{6,4},{7,5},{8,10},{9,11},{10,... | collective-permute-start | bytes 1179656 | tf_op jit(solution)/shard_map/ppermute | solution.py:240
  40.0 1.4 %collective-permute-done.10.refs_2_.refs_1_.refs_3_.refs_14_.refs_21_ = bf16[2,256,512]{2,1,0:T(8,128)(2,1)S(1)} collective-permute-done((bf16[2,256,512]{2,1,0:T(8,128)(2,1)S(1)}, bf16[2,256,512]{2,1,0:T(8,128)(2,1)S(1)}, u32[]{:S(2)}, u32[]{:S(2)}) %collective-permute-start.10) | collective-permute-done | bytes 524320 | tf_op jit(solution)/shard_map/ppermute | solution.py:240
  41.4 1.6 %collective-permute-start.13 = (bf16[2,256,512]{2,1,0:T(8,128)(2,1)S(1)}, bf16[2,256,512]{2,1,0:T(8,128)(2,1)S(1)}, u32[]{:S(2)}, u32[]{:S(2)}) collective-permute-start(bf16[2,256,512]{2,1,0:T(8,128)(2,1)S(1)} %collective-permute-done.10.refs_2_.refs_1_.refs_3_.refs_14_.refs_21_), channel_id=1, source_target_pairs={{0,8},{8,16},{16,24},{24,28},{28,20},{20,12},{12,4},{4,0},{1,9},{9... | collective-permute-start | bytes 1572872 | tf_op jit(solution)/shard_map/ppermute | solution.py:240
  43.0 0.5 collective-permute-start.14
  43.5 4.0 %collective-permute-done.9.refs_5_.refs_4_ = bf16[384,512]{1,0:T(8,128)(2,1)S(1)} collective-permute-done((bf16[384,512]{1,0:T(8,128)(2,1)S(1)}, bf16[384,512]{1,0:T(8,128)(2,1)S(1)}, u32[]{:S(2)}, u32[]{:S(2)}) %collective-permute-start.9) | collective-permute-done | bytes 393248 | tf_op jit(solution)/shard_map/ppermute | solution.py:240
  47.5 0.2 shard_map.80
  47.7 1.8 %collective-permute-start.12 = (bf16[384,512]{1,0:T(8,128)(2,1)S(1)}, bf16[384,512]{1,0:T(8,128)(2,1)S(1)}, u32[]{:S(2)}, u32[]{:S(2)}) collective-permute-start(bf16[384,512]{1,0:T(8,128)(2,1)S(1)} %shard_map.80), channel_id=1, source_target_pairs={{0,2},{1,3},{2,0},{3,1},{4,6},{5,7},{6,4},{7,5},{8,10},{9,11},{10,... | collective-permute-start | bytes 1179656 | tf_op jit(solution)/shard_map/ppermute | solution.py:240
  49.5 2.7 %collective-permute-done.13.refs_0_.refs_4_.refs_1_.refs_15_.refs_22_ = bf16[2,256,512]{2,1,0:T(8,128)(2,1)S(1)} collective-permute-done((bf16[2,256,512]{2,1,0:T(8,128)(2,1)S(1)}, bf16[2,256,512]{2,1,0:T(8,128)(2,1)S(1)}, u32[]{:S(2)}, u32[]{:S(2)}) %collective-permute-start.13) | collective-permute-done | bytes 524320 | tf_op jit(solution)/shard_map/ppermute | solution.py:240
  52.2 1.5 %collective-permute-done.14.refs_2_.refs_5_.refs_26_.refs_10_ = bf16[2,256,512]{2,1,0:T(8,128)(2,1)S(1)} collective-permute-done((bf16[2,256,512]{2,1,0:T(8,128)(2,1)S(1)}, bf16[2,256,512]{2,1,0:T(8,128)(2,1)S(1)}, u32[]{:S(2)}, u32[]{:S(2)}) %collective-permute-start.14) | collective-permute-done | bytes 524320 | tf_op jit(solution)/shard_map/ppermute | solution.py:240
  53.7 0.1 shard_map.81
  53.8 1.7 %collective-permute-start.20 = (bf16[2,256,512]{2,1,0:T(8,128)(2,1)S(1)}, bf16[2,256,512]{2,1,0:T(8,128)(2,1)S(1)}, u32[]{:S(2)}, u32[]{:S(2)}) collective-permute-start(bf16[2,256,512]{2,1,0:T(8,128)(2,1)S(1)} %get-tuple-element.25.refs_3_), channel_id=1, source_target_pairs={{0,8},{8,16},{16,24},{24,28},{28,20},{20,12},{12,4},{4,0},{1,9},{9... | collective-permute-start | bytes 1572872 | tf_op jit(solution)/shard_map/ppermute | solution.py:240
  55.5 0.4 collective-permute-start.21
  55.9 1.1 collective-permute-done.12.refs_5_
  57.0 0.2 shard_map.82
  57.2 2.0 %collective-permute-start.15 = (bf16[384,512]{1,0:T(8,128)(2,1)S(1)}, bf16[384,512]{1,0:T(8,128)(2,1)S(1)}, u32[]{:S(2)}, u32[]{:S(2)}) collective-permute-start(bf16[384,512]{1,0:T(8,128)(2,1)S(1)} %shard_map.82), channel_id=1, source_target_pairs={{0,2},{1,3},{2,0},{3,1},{4,6},{5,7},{6,4},{7,5},{8,10},{9,11},{10,... | collective-permute-start | bytes 1179656 | tf_op jit(solution)/shard_map/ppermute | solution.py:240
  59.2 5.8 %collective-permute-done.15.refs_6_ = bf16[384,512]{1,0:T(8,128)(2,1)S(1)} collective-permute-done((bf16[384,512]{1,0:T(8,128)(2,1)S(1)}, bf16[384,512]{1,0:T(8,128)(2,1)S(1)}, u32[]{:S(2)}, u32[]{:S(2)}) %collective-permute-start.15) | collective-permute-done | bytes 393248 | tf_op jit(solution)/shard_map/ppermute | solution.py:240
  65.1 0.5 collective-permute-start.18
  65.8 0.7 stack.100.refs_0_
  66.6 1.6 %collective-permute-start.22 = (bf16[2,256,512]{2,1,0:T(8,128)(2,1)S(1)}, bf16[2,256,512]{2,1,0:T(8,128)(2,1)S(1)}, u32[]{:S(2)}, u32[]{:S(2)}) collective-permute-start(bf16[2,256,512]{2,1,0:T(8,128)(2,1)S(1)} %shard_map.84), channel_id=1, source_target_pairs={{0,8},{8,16},{16,24},{24,28},{28,20},{20,12},{12,4},{4,0},{1,9},{9... | collective-permute-start | bytes 1572872 | tf_op jit(solution)/shard_map/ppermute | solution.py:240
  68.2 0.5 collective-permute-start.23
  68.7 12.4 %shard_map.83 = (bf16[1664,512]{1,0:T(8,128)(2,1)}, bf16[1664,512]{1,0:T(8,128)(2,1)}) custom-call(s32[20]{0:T(128)} %stack.100.refs_0_, bf16[1664,512]{1,0:T(8,128)(2,1)} %get-tuple-element.19.refs_1_, bf16[1664,512]{1,0:T(8,128)(2,1)} %collective-permute-done.refs_2_, bf16[512,512]{1,0:T(8,128)(2,1)} %copy-done.13, bf16[384,512]{1,0:T(8,128)(2,1)} %copy-done.16, ...), custom_call_target="tpu_custom_call" | custom-call | flops 6979321856 | tf_op jit(solution)/shard_map/pallas_call | solution.py:182
  81.2 0.9 collective-permute-done.23.refs_3_.refs_1_.refs_12_.refs_10_
  82.1 0.5 collective-permute-start.25
  82.6 0.3 copy-done.7
  82.9 2.0 %collective-permute-start.26 = (bf16[1,256,512]{2,1,0:T(8,128)(2,1)S(1)}, bf16[1,256,512]{2,1,0:T(8,128)(2,1)S(1)}, u32[]{:S(2)}, u32[]{:S(2)}) collective-permute-start(bf16[1,256,512]{2,1,0:T(8,128)(2,1)S(1)} %get-tuple-element.31), channel_id=1, source_target_pairs={{0,8},{8,16},{16,24},{24,28},{28,20},{20,12},{12,4},{4,0},{1,9},{9... | collective-permute-start | bytes 786440 | tf_op jit(solution)/shard_map/ppermute | solution.py:240
  84.9 0.1 collective-permute-start.28
  85.0 0.7 stack.48.refs_0_
  85.7 5.2 %collective-permute-done.26.refs_14_.refs_7_ = bf16[1,256,512]{2,1,0:T(8,128)(2,1)S(1)} collective-permute-done((bf16[1,256,512]{2,1,0:T(8,128)(2,1)S(1)}, bf16[1,256,512]{2,1,0:T(8,128)(2,1)S(1)}, u32[]{:S(2)}, u32[]{:S(2)}) %collective-permute-start.26) | collective-permute-done | bytes 262176 | tf_op jit(solution)/shard_map/ppermute | solution.py:240
  90.9 1.9 %collective-permute-start.27 = (bf16[1,256,512]{2,1,0:T(8,128)(2,1)S(1)}, bf16[1,256,512]{2,1,0:T(8,128)(2,1)S(1)}, u32[]{:S(2)}, u32[]{:S(2)}) collective-permute-start(bf16[1,256,512]{2,1,0:T(8,128)(2,1)S(1)} %collective-permute-done.26.refs_14_.refs_7_), channel_id=1, source_target_pairs={{0,8},{8,16},{16,24},{24,28},{28,20},{20,12},{12,4},{4,0},{1,9},{9... | collective-permute-start | bytes 786440 | tf_op jit(solution)/shard_map/ppermute | solution.py:240
  92.8 0.1 collective-permute-start.29
  93.0 0.6 copy-done.33
  93.5 0.6 copy-done.30
  94.2 9.1 %shard_map.87.refs_14_ = f32[18,1664]{1,0:T(8,128)} custom-call(s32[12]{0:T(128)} %stack.48.refs_0_, bf16[1664,512]{1,0:T(8,128)(2,1)} %get-tuple-element.29.refs_4_.refs_1_, bf16[1664,512]{1,0:T(8,128)(2,1)} %copy-done.30, bf16[1664,512]{1,0:T(8,128)(2,1)} %get-tuple-element.30.refs_3_, bf16[1664,512]{1,0:T(8,128)(2,1)} %collective-permute-done.25.refs_4_, ...), custom_call_target="tpu_custom_call" | custom-call | flops 3489660928 | tf_op jit(solution)/shard_map/pallas_call | solution.py:182
  103.3 0.7 copy-done.34
  104.0 0.7 copy-done.35
  104.7 9.2 %shard_map.88.q0 = f32[18,1664]{1,0:T(8,128)} custom-call(s32[12]{0:T(128)} %stack.48.refs_0_, bf16[1664,512]{1,0:T(8,128)(2,1)} %get-tuple-element.29.refs_4_.refs_1_, bf16[1664,512]{1,0:T(8,128)(2,1)} %copy-done.30, bf16[1664,512]{1,0:T(8,128)(2,1)} %get-tuple-element.30.refs_3_, bf16[1664,512]{1,0:T(8,128)(2,1)} %collective-permute-done.25.refs_4_, ...), custom_call_target="tpu_custom_call" | custom-call | flops 3489660928 | tf_op jit(solution)/shard_map/pallas_call | solution.py:182
  114.0 1.6 %collective-permute-done.30.q1 = f32[18,1664]{1,0:T(8,128)S(1)} collective-permute-done((f32[18,1664]{1,0:T(8,128)}, f32[18,1664]{1,0:T(8,128)S(1)}, u32[]{:S(2)}, u32[]{:S(2)}) %collective-permute-start.30) | collective-permute-done | bytes 119840 | tf_op jit(solution)/shard_map/ppermute | solution.py:240
  115.6 0.6 copy-done.25
  116.3 2.3 %shard_map.89 = f32[1,1664]{1,0:T(1,128)} custom-call(f32[18,1664]{1,0:T(8,128)} %shard_map.88.q0, f32[18,1664]{1,0:T(8,128)} %copy-done.25, f32[1,1664]{1,0:T(1,128)} %copy-done.20, s32[1,1664]{1,0:T(1,128)} %copy-done.21, s32[1,1664]{1,0:T(1,128)} %copy-done.22, f32[1,1664]{1,0:T(1,128)} %copy-done.23), custom_call_target="tpu_custom_call" | custom-call | tf_op jit(solution)/shard_map/pallas_call | solution.py:224
  118.5 1.9 %collective-permute-start.31 = (f32[1,1664]{1,0:T(1,128)}, f32[1,1664]{1,0:T(1,128)S(1)}, u32[]{:S(2)}, u32[]{:S(2)}) collective-permute-start(f32[1,1664]{1,0:T(1,128)} %shard_map.89), channel_id=1, source_target_pairs={{0,2},{1,3},{2,0},{3,1},{4,6},{5,7},{6,4},{7,5},{8,10},{9,11},{10,... | collective-permute-start | bytes 19976 | tf_op jit(solution)/shard_map/ppermute | solution.py:240
  120.5 1.9 %collective-permute-done.31 = f32[1,1664]{1,0:T(1,128)S(1)} collective-permute-done((f32[1,1664]{1,0:T(1,128)}, f32[1,1664]{1,0:T(1,128)S(1)}, u32[]{:S(2)}, u32[]{:S(2)}) %collective-permute-start.31) | collective-permute-done | bytes 6688 | tf_op jit(solution)/shard_map/ppermute | solution.py:240
  122.4 0.7 broadcast_select_fusion.1
  123.1 0.7 reshape.19
  (102 shorter events, 1.2 us)
Async XLA Ops:
  0.0 15.1 %collective-permute-start.1 = (bf16[2,256,512]{2,1,0:T(8,128)(2,1)}, bf16[2,256,512]{2,1,0:T(8,128)(2,1)S(1)}, u32[]{:S(2)}, u32[]{:S(2)}) collective-permute-start(bf16[2,256,512]{2,1,0:T(8,128)(2,1)} %source.3), channel_id=1, source_target_pairs={{0,8},{8,16},{16,24},{24,28},{28,20},{20,12},{12,4},{4,0},{1,9},{9... | collective-permute-start | bytes 1572872 | tf_op jit(solution)/shard_map/ppermute | solution.py:240
  3.0 13.6 %collective-permute-start.2 = (bf16[2,256,512]{2,1,0:T(8,128)(2,1)}, bf16[2,256,512]{2,1,0:T(8,128)(2,1)S(1)}, u32[]{:S(2)}, u32[]{:S(2)}) collective-permute-start(bf16[2,256,512]{2,1,0:T(8,128)(2,1)} %source.3), channel_id=1, source_target_pairs={{8,0},{16,8},{24,16},{28,24},{20,28},{12,20},{4,12},{0,4},{9,1},{1... | collective-permute-start | bytes 1572872 | tf_op jit(solution)/shard_map/ppermute | solution.py:240
  3.0 1.1 copy-start.14
  4.7 14.1 %copy-start.24 = (bf16[1,256,512]{2,1,0:T(8,128)(2,1)}, bf16[1,256,512]{2,1,0:T(8,128)(2,1)S(1)}, u32[]{:S(2)}) copy-start(bf16[1,256,512]{2,1,0:T(8,128)(2,1)S(1)} %get-tuple-element.21.refs_11_) | copy-start | bytes 786436
  4.8 14.8 %copy-start.18 = (bf16[1,256,512]{2,1,0:T(8,128)(2,1)}, bf16[1,256,512]{2,1,0:T(8,128)(2,1)S(1)}, u32[]{:S(2)}) copy-start(bf16[1,256,512]{2,1,0:T(8,128)(2,1)S(1)} %get-tuple-element.24.refs_0_.refs_5_) | copy-start | bytes 786436
  4.8 8.4 %collective-permute-start.3 = (bf16[1,256,512]{2,1,0:T(8,128)(2,1)S(1)}, bf16[1,256,512]{2,1,0:T(8,128)(2,1)S(1)}, u32[]{:S(2)}, u32[]{:S(2)}) collective-permute-start(bf16[1,256,512]{2,1,0:T(8,128)(2,1)S(1)} %get-tuple-element.21.refs_11_), channel_id=1, source_target_pairs={{0,2},{1,3},{2,0},{3,1},{4,6},{5,7},{6,4},{7,5},{8,10},{9,11},{10,... | collective-permute-start | bytes 786440 | tf_op jit(solution)/shard_map/ppermute | solution.py:240
  6.8 14.4 %copy-start.26 = (f32[52,64]{1,0:T(8,128)S(1)}, f32[52,64]{1,0:T(8,128)}, u32[]{:S(2)}) copy-start(f32[52,64]{1,0:T(8,128)} %param.13) | copy-start | bytes 39940
  6.8 14.4 %copy-start.27 = (f32[52,64]{1,0:T(8,128)S(1)}, f32[52,64]{1,0:T(8,128)}, u32[]{:S(2)}) copy-start(f32[52,64]{1,0:T(8,128)} %param.10) | copy-start | bytes 39940
  6.8 14.5 %copy-start.28 = (s32[52,64]{1,0:T(8,128)S(1)}, s32[52,64]{1,0:T(8,128)}, u32[]{:S(2)}) copy-start(s32[52,64]{1,0:T(8,128)} %param.12) | copy-start | bytes 39940
  6.8 14.5 %copy-start.29 = (s32[52,64]{1,0:T(8,128)S(1)}, s32[52,64]{1,0:T(8,128)}, u32[]{:S(2)}) copy-start(s32[52,64]{1,0:T(8,128)} %param.11) | copy-start | bytes 39940
  6.8 6.3 %collective-permute-start.4 = (bf16[18,512]{1,0:T(8,128)(2,1)}, bf16[18,512]{1,0:T(8,128)(2,1)S(1)}, u32[]{:S(2)}, u32[]{:S(2)}) collective-permute-start(bf16[18,512]{1,0:T(8,128)(2,1)} %bitcast.16), channel_id=1, source_target_pairs={{0,2},{1,3},{2,0},{3,1},{4,6},{5,7},{6,4},{7,5},{8,10},{9,11},{10,... | collective-permute-start | bytes 55304 | tf_op jit(solution)/shard_map/ppermute | solution.py:240
  13.1 13.1 %copy-start.19 = (bf16[18,512]{1,0:T(8,128)(2,1)}, bf16[18,512]{1,0:T(8,128)(2,1)S(1)}, u32[]{:S(2)}) copy-start(bf16[18,512]{1,0:T(8,128)(2,1)S(1)} %collective-permute-done.4.refs_6_.refs_4_.refs_13_) | copy-start | bytes 55300
  13.1 13.1 %copy-start.8 = (bf16[1,256,512]{2,1,0:T(8,128)(2,1)}, bf16[1,256,512]{2,1,0:T(8,128)(2,1)S(1)}, u32[]{:S(2)}) copy-start(bf16[1,256,512]{2,1,0:T(8,128)(2,1)S(1)} %collective-permute-done.3.refs_1_.refs_5_.refs_3_.refs_19_) | copy-start | bytes 786436
  15.1 38.6 %copy-start.1 = (bf16[2,256,512]{2,1,0:T(8,128)(2,1)}, bf16[2,256,512]{2,1,0:T(8,128)(2,1)S(1)}, u32[]{:S(2)}) copy-start(bf16[2,256,512]{2,1,0:T(8,128)(2,1)S(1)} %collective-permute-done.1.refs_0_.refs_3_.refs_1_.refs_12_.refs_6_) | copy-start | bytes 1572868
  16.6 26.3 %copy-start = (bf16[2,256,512]{2,1,0:T(8,128)(2,1)}, bf16[2,256,512]{2,1,0:T(8,128)(2,1)S(1)}, u32[]{:S(2)}) copy-start(bf16[2,256,512]{2,1,0:T(8,128)(2,1)S(1)} %collective-permute-done.2.refs_2_.refs_4_.refs_1_.refs_16_.refs_9_) | copy-start | bytes 1572868
  16.7 12.5 %collective-permute-start.7 = (bf16[2,256,512]{2,1,0:T(8,128)(2,1)S(1)}, bf16[2,256,512]{2,1,0:T(8,128)(2,1)S(1)}, u32[]{:S(2)}, u32[]{:S(2)}) collective-permute-start(bf16[2,256,512]{2,1,0:T(8,128)(2,1)S(1)} %get-tuple-element.22.refs_5_), channel_id=1, source_target_pairs={{0,8},{8,16},{16,24},{24,28},{28,20},{20,12},{12,4},{4,0},{1,9},{9... | collective-permute-start | bytes 1572872 | tf_op jit(solution)/shard_map/ppermute | solution.py:240
  18.4 12.5 %collective-permute-start.8 = (bf16[2,256,512]{2,1,0:T(8,128)(2,1)S(1)}, bf16[2,256,512]{2,1,0:T(8,128)(2,1)}, u32[]{:S(2)}, u32[]{:S(2)}) collective-permute-start(bf16[2,256,512]{2,1,0:T(8,128)(2,1)S(1)} %get-tuple-element.23.refs_6_), channel_id=1, source_target_pairs={{8,0},{16,8},{24,16},{28,24},{20,28},{12,20},{4,12},{0,4},{9,1},{1... | collective-permute-start | bytes 1572872 | tf_op jit(solution)/shard_map/ppermute | solution.py:240
  19.6 6.6 %collective-permute-start.5 = (bf16[1,256,512]{2,1,0:T(8,128)(2,1)}, bf16[1,256,512]{2,1,0:T(8,128)(2,1)S(1)}, u32[]{:S(2)}, u32[]{:S(2)}) collective-permute-start(bf16[1,256,512]{2,1,0:T(8,128)(2,1)} %shard_map.76), channel_id=1, source_target_pairs={{0,2},{1,3},{2,0},{3,1},{4,6},{5,7},{6,4},{7,5},{8,10},{9,11},{10,... | collective-permute-start | bytes 786440 | tf_op jit(solution)/shard_map/ppermute | solution.py:240
  21.3 5.0 %copy-start.20 = (f32[1,1664]{1,0:T(1,128)}, f32[1,1664]{1,0:T(1,128)S(1)}, u32[]{:S(2)}) copy-start(f32[1,1664]{1,0:T(1,128)S(1)} %reshape.15.refs_8_.refs_27_.rewards) | copy-start | bytes 19972
  21.4 4.9 %copy-start.21 = (s32[1,1664]{1,0:T(1,128)}, s32[1,1664]{1,0:T(1,128)S(1)}, u32[]{:S(2)}) copy-start(s32[1,1664]{1,0:T(1,128)S(1)} %reshape.16.refs_9_.refs_28_.actions) | copy-start | bytes 19972
  21.5 4.8 %copy-start.22 = (s32[1,1664]{1,0:T(1,128)}, s32[1,1664]{1,0:T(1,128)S(1)}, u32[]{:S(2)}) copy-start(s32[1,1664]{1,0:T(1,128)S(1)} %reshape.17.refs_10_.refs_29_.done_flags) | copy-start | bytes 19972
  21.5 4.7 %copy-start.23 = (f32[1,1664]{1,0:T(1,128)}, f32[1,1664]{1,0:T(1,128)S(1)}, u32[]{:S(2)}) copy-start(f32[1,1664]{1,0:T(1,128)S(1)} %reshape.18.refs_11_.refs_30_.behaviour) | copy-start | bytes 19972
  21.6 2.0 %copy-start.9 = (bf16[3328,512]{1,0:T(8,128)(2,1)S(1)}, bf16[3328,512]{1,0:T(8,128)(2,1)}, u32[]{:S(2)}) copy-start(bf16[3328,512]{1,0:T(8,128)(2,1)} %source.2) | copy-start | bytes 10223620
  26.2 40.3 %copy-start.10 = (bf16[1,256,512]{2,1,0:T(8,128)(2,1)}, bf16[1,256,512]{2,1,0:T(8,128)(2,1)S(1)}, u32[]{:S(2)}) copy-start(bf16[1,256,512]{2,1,0:T(8,128)(2,1)S(1)} %collective-permute-done.5.refs_7_.refs_3_.refs_1_.refs_5_) | copy-start | bytes 786436
  26.3 11.9 %collective-permute-start.6 = (bf16[512,512]{1,0:T(8,128)(2,1)S(1)}, bf16[512,512]{1,0:T(8,128)(2,1)S(1)}, u32[]{:S(2)}, u32[]{:S(2)}) collective-permute-start(bf16[512,512]{1,0:T(8,128)(2,1)S(1)} %shard_map.77), channel_id=1, source_target_pairs={{0,2},{1,3},{2,0},{3,1},{4,6},{5,7},{6,4},{7,5},{8,10},{9,11},{10,... | collective-permute-start | bytes 1572872 | tf_op jit(solution)/shard_map/ppermute | solution.py:240
  29.3 9.1 %copy-start.11 = (bf16[2,256,512]{2,1,0:T(8,128)(2,1)}, bf16[2,256,512]{2,1,0:T(8,128)(2,1)S(1)}, u32[]{:S(2)}) copy-start(bf16[2,256,512]{2,1,0:T(8,128)(2,1)S(1)} %collective-permute-done.7.refs_1_.refs_3_.refs_13_.refs_20_) | copy-start | bytes 1572868
  29.3 12.1 %collective-permute-start.10 = (bf16[2,256,512]{2,1,0:T(8,128)(2,1)S(1)}, bf16[2,256,512]{2,1,0:T(8,128)(2,1)S(1)}, u32[]{:S(2)}, u32[]{:S(2)}) collective-permute-start(bf16[2,256,512]{2,1,0:T(8,128)(2,1)S(1)} %collective-permute-done.7.refs_1_.refs_3_.refs_13_.refs_20_), channel_id=1, source_target_pairs={{0,8},{8,16},{16,24},{24,28},{28,20},{20,12},{12,4},{4,0},{1,9},{9... | collective-permute-start | bytes 1572872 | tf_op jit(solution)/shard_map/ppermute | solution.py:240
  30.9 12.1 %collective-permute-start.11 = (bf16[2,256,512]{2,1,0:T(8,128)(2,1)}, bf16[2,256,512]{2,1,0:T(8,128)(2,1)S(1)}, u32[]{:S(2)}, u32[]{:S(2)}) collective-permute-start(bf16[2,256,512]{2,1,0:T(8,128)(2,1)} %collective-permute-done.8.refs_2_.refs_4_.refs_17_.refs_24_), channel_id=1, source_target_pairs={{8,0},{16,8},{24,16},{28,24},{20,28},{12,20},{4,12},{0,4},{9,1},{1... | collective-permute-start | bytes 1572872 | tf_op jit(solution)/shard_map/ppermute | solution.py:240
  31.3 35.3 %collective-permute-start = (bf16[1664,512]{1,0:T(8,128)(2,1)}, bf16[1664,512]{1,0:T(8,128)(2,1)}, u32[]{:S(2)}, u32[]{:S(2)}) collective-permute-start(bf16[1664,512]{1,0:T(8,128)(2,1)} %get-tuple-element.19.refs_1_), channel_id=1, source_target_pairs={{0,1},{1,0},{2,3},{3,2},{4,5},{5,4},{6,7},{7,6},{8,9},{9,8},{10,11... | collective-permute-start | bytes 5111816 | tf_op jit(solution)/shard_map/ppermute | solution.py:240
  38.2 21.0 %copy-start.13 = (bf16[512,512]{1,0:T(8,128)(2,1)}, bf16[512,512]{1,0:T(8,128)(2,1)S(1)}, u32[]{:S(2)}) copy-start(bf16[512,512]{1,0:T(8,128)(2,1)S(1)} %collective-permute-done.6.refs_5_.refs_3_) | copy-start | bytes 1572868
  38.4 9.1 %collective-permute-start.9 = (bf16[384,512]{1,0:T(8,128)(2,1)S(1)}, bf16[384,512]{1,0:T(8,128)(2,1)S(1)}, u32[]{:S(2)}, u32[]{:S(2)}) collective-permute-start(bf16[384,512]{1,0:T(8,128)(2,1)S(1)} %shard_map.78), channel_id=1, source_target_pairs={{0,2},{1,3},{2,0},{3,1},{4,6},{5,7},{6,4},{7,5},{8,10},{9,11},{10,... | collective-permute-start | bytes 1179656 | tf_op jit(solution)/shard_map/ppermute | solution.py:240
  41.4 6.3 %copy-start.2 = (bf16[2,256,512]{2,1,0:T(8,128)(2,1)}, bf16[2,256,512]{2,1,0:T(8,128)(2,1)S(1)}, u32[]{:S(2)}) copy-start(bf16[2,256,512]{2,1,0:T(8,128)(2,1)S(1)} %collective-permute-done.10.refs_2_.refs_1_.refs_3_.refs_14_.refs_21_) | copy-start | bytes 1572868
  41.4 10.8 %collective-permute-start.13 = (bf16[2,256,512]{2,1,0:T(8,128)(2,1)S(1)}, bf16[2,256,512]{2,1,0:T(8,128)(2,1)S(1)}, u32[]{:S(2)}, u32[]{:S(2)}) collective-permute-start(bf16[2,256,512]{2,1,0:T(8,128)(2,1)S(1)} %collective-permute-done.10.refs_2_.refs_1_.refs_3_.refs_14_.refs_21_), channel_id=1, source_target_pairs={{0,8},{8,16},{16,24},{24,28},{28,20},{20,12},{12,4},{4,0},{1,9},{9... | collective-permute-start | bytes 1572872 | tf_op jit(solution)/shard_map/ppermute | solution.py:240
  43.0 4.7 %copy-start.3 = (bf16[2,256,512]{2,1,0:T(8,128)(2,1)}, bf16[2,256,512]{2,1,0:T(8,128)(2,1)S(1)}, u32[]{:S(2)}) copy-start(bf16[2,256,512]{2,1,0:T(8,128)(2,1)S(1)} %collective-permute-done.11.refs_0_.refs_3_.refs_2_.refs_18_.refs_25_) | copy-start | bytes 1572868
  43.0 10.7 %collective-permute-start.14 = (bf16[2,256,512]{2,1,0:T(8,128)(2,1)S(1)}, bf16[2,256,512]{2,1,0:T(8,128)(2,1)S(1)}, u32[]{:S(2)}, u32[]{:S(2)}) collective-permute-start(bf16[2,256,512]{2,1,0:T(8,128)(2,1)S(1)} %shard_map.79.refs_4_), channel_id=1, source_target_pairs={{8,0},{16,8},{24,16},{28,24},{20,28},{12,20},{4,12},{0,4},{9,1},{1... | collective-permute-start | bytes 1572872 | tf_op jit(solution)/shard_map/ppermute | solution.py:240
  47.5 17.6 %copy-start.16 = (bf16[384,512]{1,0:T(8,128)(2,1)}, bf16[384,512]{1,0:T(8,128)(2,1)S(1)}, u32[]{:S(2)}) copy-start(bf16[384,512]{1,0:T(8,128)(2,1)S(1)} %collective-permute-done.9.refs_5_.refs_4_) | copy-start | bytes 1179652
  47.7 9.3 %collective-permute-start.12 = (bf16[384,512]{1,0:T(8,128)(2,1)S(1)}, bf16[384,512]{1,0:T(8,128)(2,1)S(1)}, u32[]{:S(2)}, u32[]{:S(2)}) collective-permute-start(bf16[384,512]{1,0:T(8,128)(2,1)S(1)} %shard_map.80), channel_id=1, source_target_pairs={{0,2},{1,3},{2,0},{3,1},{4,6},{5,7},{6,4},{7,5},{8,10},{9,11},{10,... | collective-permute-start | bytes 1179656 | tf_op jit(solution)/shard_map/ppermute | solution.py:240
  52.2 5.0 %copy-start.5 = (bf16[2,256,512]{2,1,0:T(8,128)(2,1)}, bf16[2,256,512]{2,1,0:T(8,128)(2,1)S(1)}, u32[]{:S(2)}) copy-start(bf16[2,256,512]{2,1,0:T(8,128)(2,1)S(1)} %collective-permute-done.13.refs_0_.refs_4_.refs_1_.refs_15_.refs_22_) | copy-start | bytes 1572868
  53.7 3.5 %copy-start.4 = (bf16[2,256,512]{2,1,0:T(8,128)(2,1)}, bf16[2,256,512]{2,1,0:T(8,128)(2,1)S(1)}, u32[]{:S(2)}) copy-start(bf16[2,256,512]{2,1,0:T(8,128)(2,1)S(1)} %collective-permute-done.14.refs_2_.refs_5_.refs_26_.refs_10_) | copy-start | bytes 1572868
  53.8 11.2 %collective-permute-start.20 = (bf16[2,256,512]{2,1,0:T(8,128)(2,1)S(1)}, bf16[2,256,512]{2,1,0:T(8,128)(2,1)S(1)}, u32[]{:S(2)}, u32[]{:S(2)}) collective-permute-start(bf16[2,256,512]{2,1,0:T(8,128)(2,1)S(1)} %get-tuple-element.25.refs_3_), channel_id=1, source_target_pairs={{0,8},{8,16},{16,24},{24,28},{28,20},{20,12},{12,4},{4,0},{1,9},{9... | collective-permute-start | bytes 1572872 | tf_op jit(solution)/shard_map/ppermute | solution.py:240
  55.5 10.1 %collective-permute-start.21 = (bf16[2,256,512]{2,1,0:T(8,128)(2,1)S(1)}, bf16[2,256,512]{2,1,0:T(8,128)(2,1)S(1)}, u32[]{:S(2)}, u32[]{:S(2)}) collective-permute-start(bf16[2,256,512]{2,1,0:T(8,128)(2,1)S(1)} %get-tuple-element.26.refs_4_), channel_id=1, source_target_pairs={{8,0},{16,8},{24,16},{28,24},{20,28},{12,20},{4,12},{0,4},{9,1},{1... | collective-permute-start | bytes 1572872 | tf_op jit(solution)/shard_map/ppermute | solution.py:240
  57.0 8.1 %copy-start.17 = (bf16[384,512]{1,0:T(8,128)(2,1)}, bf16[384,512]{1,0:T(8,128)(2,1)S(1)}, u32[]{:S(2)}) copy-start(bf16[384,512]{1,0:T(8,128)(2,1)S(1)} %collective-permute-done.12.refs_5_) | copy-start | bytes 1179652
  57.2 7.8 %collective-permute-start.15 = (bf16[384,512]{1,0:T(8,128)(2,1)S(1)}, bf16[384,512]{1,0:T(8,128)(2,1)S(1)}, u32[]{:S(2)}, u32[]{:S(2)}) collective-permute-start(bf16[384,512]{1,0:T(8,128)(2,1)S(1)} %shard_map.82), channel_id=1, source_target_pairs={{0,2},{1,3},{2,0},{3,1},{4,6},{5,7},{6,4},{7,5},{8,10},{9,11},{10,... | collective-permute-start | bytes 1179656 | tf_op jit(solution)/shard_map/ppermute | solution.py:240
  59.2 9.0 %collective-permute-start.16 = (bf16[512,512]{1,0:T(8,128)(2,1)S(1)}, bf16[512,512]{1,0:T(8,128)(2,1)}, u32[]{:S(2)}, u32[]{:S(2)}) collective-permute-start(bf16[512,512]{1,0:T(8,128)(2,1)S(1)} %collective-permute-done.6.refs_5_.refs_3_), channel_id=1, source_target_pairs={{0,1},{1,0},{2,3},{3,2},{4,5},{5,4},{6,7},{7,6},{8,9},{9,8},{10,11... | collective-permute-start | bytes 1572872 | tf_op jit(solution)/shard_map/ppermute | solution.py:240
  65.0 3.6 %copy-start.31 = (bf16[384,512]{1,0:T(8,128)(2,1)}, bf16[384,512]{1,0:T(8,128)(2,1)S(1)}, u32[]{:S(2)}) copy-start(bf16[384,512]{1,0:T(8,128)(2,1)S(1)} %collective-permute-done.15.refs_6_) | copy-start | bytes 1179652
  65.0 3.6 %collective-permute-start.17 = (bf16[384,512]{1,0:T(8,128)(2,1)S(1)}, bf16[384,512]{1,0:T(8,128)(2,1)}, u32[]{:S(2)}, u32[]{:S(2)}) collective-permute-start(bf16[384,512]{1,0:T(8,128)(2,1)S(1)} %collective-permute-done.9.refs_5_.refs_4_), channel_id=1, source_target_pairs={{0,1},{1,0},{2,3},{3,2},{4,5},{5,4},{6,7},{7,6},{8,9},{9,8},{10,11... | collective-permute-start | bytes 1179656 | tf_op jit(solution)/shard_map/ppermute | solution.py:240
  65.1 3.6 %copy-start.12 = (bf16[2,256,512]{2,1,0:T(8,128)(2,1)}, bf16[2,256,512]{2,1,0:T(8,128)(2,1)S(1)}, u32[]{:S(2)}) copy-start(bf16[2,256,512]{2,1,0:T(8,128)(2,1)S(1)} %collective-permute-done.20.refs_23_.refs_0_.refs_2_.refs_7_) | copy-start | bytes 1572868
  65.1 3.6 %collective-permute-start.18 = (bf16[384,512]{1,0:T(8,128)(2,1)S(1)}, bf16[384,512]{1,0:T(8,128)(2,1)}, u32[]{:S(2)}, u32[]{:S(2)}) collective-permute-start(bf16[384,512]{1,0:T(8,128)(2,1)S(1)} %collective-permute-done.12.refs_5_), channel_id=1, source_target_pairs={{0,1},{1,0},{2,3},{3,2},{4,5},{5,4},{6,7},{7,6},{8,9},{9,8},{10,11... | collective-permute-start | bytes 1179656 | tf_op jit(solution)/shard_map/ppermute | solution.py:240
  65.6 15.5 %copy-start.15 = (bf16[2,256,512]{2,1,0:T(8,128)(2,1)}, bf16[2,256,512]{2,1,0:T(8,128)(2,1)S(1)}, u32[]{:S(2)}) copy-start(bf16[2,256,512]{2,1,0:T(8,128)(2,1)S(1)} %collective-permute-done.21.refs_3_.refs_11_.refs_9_) | copy-start | bytes 1572868
  65.6 3.0 %collective-permute-start.19 = (bf16[384,512]{1,0:T(8,128)(2,1)S(1)}, bf16[384,512]{1,0:T(8,128)(2,1)}, u32[]{:S(2)}, u32[]{:S(2)}) collective-permute-start(bf16[384,512]{1,0:T(8,128)(2,1)S(1)} %collective-permute-done.15.refs_6_), channel_id=1, source_target_pairs={{0,1},{1,0},{2,3},{3,2},{4,5},{5,4},{6,7},{7,6},{8,9},{9,8},{10,11... | collective-permute-start | bytes 1179656 | tf_op jit(solution)/shard_map/ppermute | solution.py:240
  66.6 14.6 %collective-permute-start.22 = (bf16[2,256,512]{2,1,0:T(8,128)(2,1)S(1)}, bf16[2,256,512]{2,1,0:T(8,128)(2,1)S(1)}, u32[]{:S(2)}, u32[]{:S(2)}) collective-permute-start(bf16[2,256,512]{2,1,0:T(8,128)(2,1)S(1)} %shard_map.84), channel_id=1, source_target_pairs={{0,8},{8,16},{16,24},{24,28},{28,20},{20,12},{12,4},{4,0},{1,9},{9... | collective-permute-start | bytes 1572872 | tf_op jit(solution)/shard_map/ppermute | solution.py:240
  68.2 13.9 %collective-permute-start.23 = (bf16[2,256,512]{2,1,0:T(8,128)(2,1)S(1)}, bf16[2,256,512]{2,1,0:T(8,128)(2,1)S(1)}, u32[]{:S(2)}, u32[]{:S(2)}) collective-permute-start(bf16[2,256,512]{2,1,0:T(8,128)(2,1)S(1)} %collective-permute-done.21.refs_3_.refs_11_.refs_9_), channel_id=1, source_target_pairs={{8,0},{16,8},{24,16},{28,24},{20,28},{12,20},{4,12},{0,4},{9,1},{1... | collective-permute-start | bytes 1572872 | tf_op jit(solution)/shard_map/ppermute | solution.py:240
  81.2 1.4 %copy-start.6 = (bf16[2,256,512]{2,1,0:T(8,128)(2,1)}, bf16[2,256,512]{2,1,0:T(8,128)(2,1)S(1)}, u32[]{:S(2)}) copy-start(bf16[2,256,512]{2,1,0:T(8,128)(2,1)S(1)} %collective-permute-done.22.refs_2_.refs_0_.refs_8_.refs_6_) | copy-start | bytes 1572868
  82.1 0.8 copy-start.7
  82.1 10.9 %collective-permute-start.24 = (bf16[1664,512]{1,0:T(8,128)(2,1)}, bf16[1664,512]{1,0:T(8,128)(2,1)S(1)}, u32[]{:S(2)}, u32[]{:S(2)}) collective-permute-start(bf16[1664,512]{1,0:T(8,128)(2,1)} %get-tuple-element.29.refs_4_.refs_1_), channel_id=1, source_target_pairs={{0,1},{1,0},{2,3},{3,2},{4,5},{5,4},{6,7},{7,6},{8,9},{9,8},{10,11... | collective-permute-start | bytes 5111816 | tf_op jit(solution)/shard_map/ppermute | solution.py:240
  82.1 10.9 %collective-permute-start.25 = (bf16[1664,512]{1,0:T(8,128)(2,1)}, bf16[1664,512]{1,0:T(8,128)(2,1)}, u32[]{:S(2)}, u32[]{:S(2)}) collective-permute-start(bf16[1664,512]{1,0:T(8,128)(2,1)} %get-tuple-element.30.refs_3_), channel_id=1, source_target_pairs={{0,1},{1,0},{2,3},{3,2},{4,5},{5,4},{6,7},{7,6},{8,9},{9,8},{10,11... | collective-permute-start | bytes 5111816 | tf_op jit(solution)/shard_map/ppermute | solution.py:240
  82.9 8.0 %collective-permute-start.26 = (bf16[1,256,512]{2,1,0:T(8,128)(2,1)S(1)}, bf16[1,256,512]{2,1,0:T(8,128)(2,1)S(1)}, u32[]{:S(2)}, u32[]{:S(2)}) collective-permute-start(bf16[1,256,512]{2,1,0:T(8,128)(2,1)S(1)} %get-tuple-element.31), channel_id=1, source_target_pairs={{0,8},{8,16},{16,24},{24,28},{28,20},{20,12},{12,4},{4,0},{1,9},{9... | collective-permute-start | bytes 786440 | tf_op jit(solution)/shard_map/ppermute | solution.py:240
  84.9 8.0 %collective-permute-start.28 = (bf16[1,256,512]{2,1,0:T(8,128)(2,1)S(1)}, bf16[1,256,512]{2,1,0:T(8,128)(2,1)S(1)}, u32[]{:S(2)}, u32[]{:S(2)}) collective-permute-start(bf16[1,256,512]{2,1,0:T(8,128)(2,1)S(1)} %get-tuple-element.32), channel_id=1, source_target_pairs={{8,0},{16,8},{24,16},{28,24},{20,28},{12,20},{4,12},{0,4},{9,1},{1... | collective-permute-start | bytes 786440 | tf_op jit(solution)/shard_map/ppermute | solution.py:240
  90.9 2.0 %copy-start.32 = (bf16[1,256,512]{2,1,0:T(8,128)(2,1)}, bf16[1,256,512]{2,1,0:T(8,128)(2,1)S(1)}, u32[]{:S(2)}) copy-start(bf16[1,256,512]{2,1,0:T(8,128)(2,1)S(1)} %collective-permute-done.26.refs_14_.refs_7_) | copy-start | bytes 786436
  90.9 12.3 %collective-permute-start.27 = (bf16[1,256,512]{2,1,0:T(8,128)(2,1)S(1)}, bf16[1,256,512]{2,1,0:T(8,128)(2,1)S(1)}, u32[]{:S(2)}, u32[]{:S(2)}) collective-permute-start(bf16[1,256,512]{2,1,0:T(8,128)(2,1)S(1)} %collective-permute-done.26.refs_14_.refs_7_), channel_id=1, source_target_pairs={{0,8},{8,16},{16,24},{24,28},{28,20},{20,12},{12,4},{4,0},{1,9},{9... | collective-permute-start | bytes 786440 | tf_op jit(solution)/shard_map/ppermute | solution.py:240
  92.8 10.4 %collective-permute-start.29 = (bf16[1,256,512]{2,1,0:T(8,128)(2,1)S(1)}, bf16[1,256,512]{2,1,0:T(8,128)(2,1)S(1)}, u32[]{:S(2)}, u32[]{:S(2)}) collective-permute-start(bf16[1,256,512]{2,1,0:T(8,128)(2,1)S(1)} %collective-permute-done.28.refs_15_.refs_11_), channel_id=1, source_target_pairs={{8,0},{16,8},{24,16},{28,24},{20,28},{12,20},{4,12},{0,4},{9,1},{1... | collective-permute-start | bytes 786440 | tf_op jit(solution)/shard_map/ppermute | solution.py:240
  93.0 1.2 copy-start.30
  113.9 1.7 %collective-permute-start.30 = (f32[18,1664]{1,0:T(8,128)}, f32[18,1664]{1,0:T(8,128)S(1)}, u32[]{:S(2)}, u32[]{:S(2)}) collective-permute-start(f32[18,1664]{1,0:T(8,128)} %shard_map.88.q0), channel_id=1, source_target_pairs={{0,1},{1,0},{2,3},{3,2},{4,5},{5,4},{6,7},{7,6},{8,9},{9,8},{10,11... | collective-permute-start | bytes 359432 | tf_op jit(solution)/shard_map/ppermute | solution.py:240
  118.5 3.8 %collective-permute-start.31 = (f32[1,1664]{1,0:T(1,128)}, f32[1,1664]{1,0:T(1,128)S(1)}, u32[]{:S(2)}, u32[]{:S(2)}) collective-permute-start(f32[1,1664]{1,0:T(1,128)} %shard_map.89), channel_id=1, source_target_pairs={{0,2},{1,3},{2,0},{3,1},{4,6},{5,7},{6,4},{7,5},{8,10},{9,11},{10,... | collective-permute-start | bytes 19976 | tf_op jit(solution)/shard_map/ppermute | solution.py:240
  (4 other events, 2.8 us)

commit v5 on v4

--- a/solution.py
+++ b/solution.py
@@ -101,13 +101,12 @@
     )(*arrays, *after)
 
 
-def layer_kernel(kinds, blocks, tiles, width, headed, added, waited, *refs):
+def layer_kernel(kinds, blocks, tiles, width, headed, waited, *refs):
     refs = list(refs)
     pos = refs.pop(0)
     hs = [[refs.pop(0) for _ in range(kind)] for kind in kinds]
     ws = [refs.pop(0) for _ in blocks]
-    head = refs.pop(0) if headed else None
-    before = refs.pop(0) if added else None
+    heads = [refs.pop(0) for _ in range(headed)]
     del refs[:waited]
     hv, wv = refs[-6:-4] if not headed else refs[-4:-2]
     count = wv.shape[1] // width
@@ -130,35 +129,43 @@
             to = hv.at[pl.ds(start, size), pl.ds(pl.multiple_of(pos[len(blocks) + i] * wide, wide), wide)]
             source = h[t] if len(h) > 1 else h[0].at[pl.ds(start, size)]
             h_copies[-1].append(pltpu.make_async_copy(source, to, hsem.at[t, i]))
-    for copy in h_copies[0] + w_copies:
+    w_columns = [[copy for copy, (_, at) in zip(w_copies, blocks) if at == col] for col in range(count)]
+    for copy in h_copies[0] + w_columns[0]:
         copy.start()
-    for copy in w_copies:
-        copy.wait()
     out_copies = []
     for t, (start, size) in enumerate(tiles):
+        rows = pl.ds(start, size)
         for copy in h_copies[t]:
             copy.wait()
-        if t + 1 < len(tiles):
-            for copy in h_copies[t + 1]:
-                copy.start()
-        summed = jnp.dot(hv[pl.ds(start, size), :], wv[...], preferred_element_type=jnp.float32)
-        hidden = jnp.maximum(summed, 0.0).astype(jnp.bfloat16)
+        total = None
+        for col in range(count):
+            if t == 0:
+                for copy in w_columns[col]:
+                    copy.wait()
+                for copy in w_columns[col + 1] if col + 1 < count else []:
+                    copy.start()
+            if col == 0 and t + 1 < len(tiles):
+                for copy in h_copies[t + 1]:
+                    copy.start()
+            units = pl.ds(col * width, width)
+            summed = jnp.dot(hv[rows, :], wv[:, units], preferred_element_type=jnp.float32)
+            hidden = jnp.maximum(summed, 0.0).astype(jnp.bfloat16)
+            if headed:
+                q = lax.dot_general(
+                    heads[col][...], hidden, (((1,), (1,)), ((), ())), preferred_element_type=jnp.float32
+                )
+                total = q if total is None else total + q
+            else:
+                ov[rows, units] = hidden
+                out_copies.append(pltpu.make_async_copy(ov.at[rows, units], outs[col].at[rows], osem.at[t, col]))
+                out_copies[-1].start()
         if headed:
-            q = lax.dot_general(head[...], hidden, (((1,), (1,)), ((), ())), preferred_element_type=jnp.float32)
-            if added:
-                q = q + before[:, pl.ds(start, size)]
-            outs[0][:, pl.ds(start, size)] = q
-        else:
-            ov[pl.ds(start, size), :] = hidden
-            for col, out in enumerate(outs):
-                source = ov.at[pl.ds(start, size), pl.ds(col * width, width)]
-                out_copies.append(pltpu.make_async_copy(source, out.at[pl.ds(start, size)], osem.at[t, col]))
-                out_copies[-1].start()
+            outs[0][:, rows] = total
     for copy in out_copies:
         copy.wait()
 
 
-def layer(pos, hs, ws, head=None, before=None, after=()):
+def layer(pos, hs, ws, heads=(), after=()):
     rows = hs[0][0].shape[0]
     tiles = tiles_of(rows, TILE)
     blocks = [(j, col) for _, j, col in ws]
@@ -166,7 +173,7 @@
     count = 1 + max(col for _, col in blocks)
     width = ws[0].shape[2]
     depth = ws[0].shape[1] * len(ws) // count
-    headed, added = head is not None, before is not None
+    headed = len(heads)
     vmem = pl.BlockSpec(memory_space=pltpu.VMEM)
     anywhere = pl.BlockSpec(memory_space=pl.ANY)
     scratch = [pltpu.VMEM((rows, depth), jnp.bfloat16), pltpu.VMEM((depth, width * count), jnp.bfloat16)]
@@ -174,23 +181,22 @@
         scratch.append(pltpu.VMEM((rows, width * count), jnp.bfloat16))
     scratch += [pltpu.SemaphoreType.DMA((len(tiles), len(hs))), pltpu.SemaphoreType.DMA((len(ws),))]
     if headed:
-        out_shape = jax.ShapeDtypeStruct((head.shape[0], rows), jnp.float32)
+        out_shape = jax.ShapeDtypeStruct((heads[0].shape[0], rows), jnp.float32)
     else:
         scratch.append(pltpu.SemaphoreType.DMA((len(tiles), count)))
         out_shape = [jax.ShapeDtypeStruct((rows, width), jnp.bfloat16)] * count
-    extra = ([head] if headed else []) + ([before] if added else [])
-    return pl.pallas_call(
-        functools.partial(layer_kernel, [len(h) for h in hs], blocks, tiles, width, headed, added, len(after)),
+    return pl.pallas_call(
+        functools.partial(layer_kernel, [len(h) for h in hs], blocks, tiles, width, headed, len(after)),
         out_shape=out_shape,
         in_specs=[pl.BlockSpec(memory_space=pltpu.SMEM)]
         + [anywhere] * (sum(len(h) for h in hs) + len(ws))
-        + [vmem] * len(extra)
+        + [vmem] * headed
         + [anywhere] * len(after),
         out_specs=vmem if headed else [anywhere] * count,
         scratch_shapes=scratch,
         compiler_params=pltpu.CompilerParams(vmem_limit_bytes=56 * 1024 * 1024),
         cost_estimate=pl.CostEstimate(flops=2 * rows * depth * width * count, bytes_accessed=0, transcendentals=0),
-    )(pos, *[a for h in hs for a in h], *ws, *extra, *after)
+    )(pos, *[a for h in hs for a in h], *ws, *heads, *after)
 
 
 def retrace_kernel(length, q0, q1, rewards, actions, done_flags, behaviour, out):
@@ -271,9 +277,10 @@
     turns = (long, short)
     ways = ([to_next(layer_weights)], [to_last(layer_weights)])
     sizes = [size for _, size in tiles_of(rows, TILE)]
+    over_y = []
     parts, start, came, came_c = list(sizes), 0, [], []
     now = [*(way[0] for way in ways), w1_y, head_y]
-    for i in range(1, dp):
+    for i in range(1, dp - 1):
         if i == 1:
             (w2_gated,) = gate([[(w2, 0, 1)]], now)
             w2_y = to_y(w2_gated)
@@ -287,11 +294,15 @@
             elif i == turn + 1:
                 build.append([(last, 1, 1), (w2_y, 0, 1)])
             elif i == dp - 2:
-                build.append([(last, 1, 1)])
+                build.append([(over_y[0], len(build), 1)])
             else:
                 build.append(None)
+        if i == dp - 3:
+            build.append([(way[-1], 1 if dp - 1 - turn == 3 else 0, 1) for way, turn in zip(ways, turns)])
         built = iter(gate([m for m in build if m], now)) if any(build) else None
         messages = [next(built) if m else way[-1] for m, way in zip(build, ways)]
+        if i == dp - 3:
+            over_y = [to_y(next(built))]
         if parts:
             size = parts.pop(0)
             (part,) = gate([[(sent, start, size)]], [*now, *messages, *(came[-1:] or [w2_y, *flat])])
@@ -308,15 +319,14 @@
                 first[0].append([(way[h - 1], 0) for h in range(1, turn + 1)])
                 first[1].append([(way[h], 1 if h < turn else 0) for h in range(1, turn + 1)])
             h1 = run([(w1, first[0]), (w1_y, first[1])], [[kept], [kept_c], came, came_c], after=flat)
-            mine, theirs = hold(h1, now)
+            mine, theirs = hold(h1, now + over_y)
             now = [*now, mine]
             h1 = [[mine], [to_core(mine)], [theirs], [to_core(theirs)]]
     second = [[], []]
-    for way, turn in zip(ways, turns):
+    for n, (way, turn) in enumerate(zip(ways, turns)):
         second[0].append([(way[0], 1), (way[turn], 1)] + [(way[h], 0) for h in range(turn + 1, dp - 2)])
-        second[1].append([(way[h], 1) for h in range(turn + 1, dp - 2)] + [(way[-2], 0), (way[-1], 0)])
-    q = run([(w2, second[0])], h1, head=head, after=[ways[0][-2], ways[1][-2]])
-    q = run([(w2_y, second[1])], h1, head=head_y, before=q)
+        second[1].append([(way[h], 1) for h in range(turn + 1, dp - 2)] + [(over_y[0], n), (way[-1], 0)])
+    q = run([(w2, second[0]), (w2_y, second[1])], h1, heads=[head, head_y])
     own = retrace(q, to_core(q), *flat, rewards.shape[1])
     other = to_y(own)
     whole = jnp.concatenate([jnp.where(y == 0, own, other), jnp.where(y == 0, other, own)], axis=1)

time: 124 us -> 119 us (0.960)
  Pallas kernels: 37.8 us -> 32.5 us
  waiting for transfers between devices: 44.4 us -> 47.6 us
  starting transfers between devices: 31.3 us -> 29.8 us
  local copies, waits for them, and re-layouts: 9.04 us -> 7.79 us
    pallas_call x3 -> x2, Pallas kernels: 30.8 us -> 25.5 us  [layer(): pl.pallas_call(functools.partial(layer_kernel, [len(h) for h in hs], bloc...]
    ppermute x32 -> x31, waiting for transfers between devices: 44.4 us -> 47.6 us  [over(): return lambda a: lax.ppermute(a, axis, pairs)]
    ppermute x32 -> x31, starting transfers between devices: 31.3 us -> 29.8 us  [over(): return lambda a: lax.ppermute(a, axis, pairs)]
    unnamed x72 -> x70, local copies, waits for them, and re-layouts: 6.65 us -> 5.45 us
  transfers between devices with their start and end apart: 32 -> 31, of which waited for: 16 -> 17; matrix products, arithmetic and copies ran while one was open for 1% -> 1% of each run, Pallas kernels for 21% -> 14%
where the time goes in v5:
time: 119 us
  waiting for transfers between devices  47.6 us (40%)
  Pallas kernels  32.5 us (27%)
  starting transfers between devices  29.8 us (25%)
  local copies, waits for them, and re-layouts  7.79 us (7%)
    ppermute x31, waiting for transfers between devices, over(): return lambda a: lax.ppermute(a, axis, pairs)  47.6 us
    ppermute x31, starting transfers between devices, over(): return lambda a: lax.ppermute(a, axis, pairs)  29.8 us
    pallas_call x2, Pallas kernels, layer(): pl.pallas_call(functools.partial(layer_kernel, [len(h) for h in hs], bloc...  25.5 us
    unnamed x70, local copies, waits for them, and re-layouts  5.45 us
    pallas_call x2, Pallas kernels, cut(): pl.pallas_call(functools.partial(cut_kernel, len(sizes)), out_shape=[jax....  2.94 us
  transfers between devices with their start and end apart: 31, of which 17 were waited for; matrix products, arithmetic and copies ran while one was open for 1% of the time, Pallas kernels for 14%

profile of v5, /device:TPU:0, one launch (start us, length us, event | category | flops | bytes accessed | tf_op | source)
XLA Modules:
  0.0 119.0 jit_solution(10297160697481870914)
XLA Ops:
  0.0 3.0 %collective-permute-start.1 = (bf16[2,256,512]{2,1,0:T(8,128)(2,1)}, bf16[2,256,512]{2,1,0:T(8,128)(2,1)S(1)}, u32[]{:S(2)}, u32[]{:S(2)}) collective-permute-start(bf16[2,256,512]{2,1,0:T(8,128)(2,1)} %source.3), channel_id=1, source_target_pairs={{0,8},{8,16},{16,24},{24,28},{28,20},{20,12},{12,4},{4,0},{1,9},{9... | collective-permute-start | bytes 1572872 | tf_op jit(solution)/shard_map/ppermute | solution.py:246
  3.0 1.1 copy-done.16
  4.1 0.6 shard_map.74
  4.8 2.0 %collective-permute-start.3 = (bf16[1,256,512]{2,1,0:T(8,128)(2,1)S(1)}, bf16[1,256,512]{2,1,0:T(8,128)(2,1)S(1)}, u32[]{:S(2)}, u32[]{:S(2)}) collective-permute-start(bf16[1,256,512]{2,1,0:T(8,128)(2,1)S(1)} %get-tuple-element.23.refs_11_), channel_id=1, source_target_pairs={{0,2},{1,3},{2,0},{3,1},{4,6},{5,7},{6,4},{7,5},{8,10},{9,11},{10,... | collective-permute-start | bytes 786440 | tf_op jit(solution)/shard_map/ppermute | solution.py:246
  6.8 0.2 collective-permute-start.4
  6.9 6.2 %collective-permute-done.4.refs_6_.refs_4_.refs_22_ = bf16[18,512]{1,0:T(8,128)(2,1)S(1)} collective-permute-done((bf16[18,512]{1,0:T(8,128)(2,1)}, bf16[18,512]{1,0:T(8,128)(2,1)S(1)}, u32[]{:S(2)}, u32[]{:S(2)}) %collective-permute-start.4) | collective-permute-done | bytes 18464 | tf_op jit(solution)/shard_map/ppermute | solution.py:246
  13.1 1.9 %collective-permute-done.1.refs_0_.refs_3_.refs_1_.refs_12_.refs_6_ = bf16[2,256,512]{2,1,0:T(8,128)(2,1)S(1)} collective-permute-done((bf16[2,256,512]{2,1,0:T(8,128)(2,1)}, bf16[2,256,512]{2,1,0:T(8,128)(2,1)S(1)}, u32[]{:S(2)}, u32[]{:S(2)}) %collective-permute-start.1) | collective-permute-done | bytes 524320 | tf_op jit(solution)/shard_map/ppermute | solution.py:246
  15.1 1.5 %collective-permute-done.2.refs_2_.refs_4_.refs_1_.refs_16_.refs_9_ = bf16[2,256,512]{2,1,0:T(8,128)(2,1)S(1)} collective-permute-done((bf16[2,256,512]{2,1,0:T(8,128)(2,1)}, bf16[2,256,512]{2,1,0:T(8,128)(2,1)S(1)}, u32[]{:S(2)}, u32[]{:S(2)}) %collective-permute-start.2) | collective-permute-done | bytes 524320 | tf_op jit(solution)/shard_map/ppermute | solution.py:246
  16.6 0.1 shard_map.75
  16.7 1.6 %collective-permute-start.7 = (bf16[2,256,512]{2,1,0:T(8,128)(2,1)S(1)}, bf16[2,256,512]{2,1,0:T(8,128)(2,1)S(1)}, u32[]{:S(2)}, u32[]{:S(2)}) collective-permute-start(bf16[2,256,512]{2,1,0:T(8,128)(2,1)S(1)} %get-tuple-element.24.refs_5_), channel_id=1, source_target_pairs={{0,8},{8,16},{16,24},{24,28},{28,20},{20,12},{12,4},{4,0},{1,9},{9... | collective-permute-start | bytes 1572872 | tf_op jit(solution)/shard_map/ppermute | solution.py:246
  18.4 0.4 collective-permute-start.8
  18.8 0.7 shard_map.76
  19.6 1.6 %collective-permute-start.5 = (bf16[1,256,512]{2,1,0:T(8,128)(2,1)}, bf16[1,256,512]{2,1,0:T(8,128)(2,1)S(1)}, u32[]{:S(2)}, u32[]{:S(2)}) collective-permute-start(bf16[1,256,512]{2,1,0:T(8,128)(2,1)} %shard_map.76), channel_id=1, source_target_pairs={{0,2},{1,3},{2,0},{3,1},{4,6},{5,7},{6,4},{7,5},{8,10},{9,11},{10,... | collective-permute-start | bytes 786440 | tf_op jit(solution)/shard_map/ppermute | solution.py:246
  21.6 2.0 %copy-done.7 = bf16[3328,512]{1,0:T(8,128)(2,1)S(1)} copy-done((bf16[3328,512]{1,0:T(8,128)(2,1)S(1)}, bf16[3328,512]{1,0:T(8,128)(2,1)}, u32[]{:S(2)}) %copy-start.7) | copy-done | bytes 3407896
  23.6 2.3 %shard_map.73 = (bf16[1664,512]{1,0:T(8,128)(2,1)}, bf16[1664,512]{1,0:T(8,128)(2,1)S(1)}) custom-call(s32[2]{0:T(128)S(1)} %pad_add_fusion.at, bf16[3328,512]{1,0:T(8,128)(2,1)S(1)} %copy-done.7), custom_call_target="tpu_custom_call" | custom-call | tf_op jit(solution)/shard_map/pallas_call | solution.py:38
  25.9 0.3 collective-permute-done.5.refs_7_.refs_3_.refs_1_.refs_13_
  26.3 1.6 %collective-permute-start.6 = (bf16[512,512]{1,0:T(8,128)(2,1)S(1)}, bf16[512,512]{1,0:T(8,128)(2,1)S(1)}, u32[]{:S(2)}, u32[]{:S(2)}) collective-permute-start(bf16[512,512]{1,0:T(8,128)(2,1)S(1)} %shard_map.77), channel_id=1, source_target_pairs={{0,2},{1,3},{2,0},{3,1},{4,6},{5,7},{6,4},{7,5},{8,10},{9,11},{10,... | collective-permute-start | bytes 1572872 | tf_op jit(solution)/shard_map/ppermute | solution.py:246
  27.9 1.4 %collective-permute-done.7.refs_1_.refs_3_.refs_13_.refs_20_ = bf16[2,256,512]{2,1,0:T(8,128)(2,1)S(1)} collective-permute-done((bf16[2,256,512]{2,1,0:T(8,128)(2,1)S(1)}, bf16[2,256,512]{2,1,0:T(8,128)(2,1)S(1)}, u32[]{:S(2)}, u32[]{:S(2)}) %collective-permute-start.7) | collective-permute-done | bytes 524320 | tf_op jit(solution)/shard_map/ppermute | solution.py:246
  29.3 1.6 %collective-permute-start.10 = (bf16[2,256,512]{2,1,0:T(8,128)(2,1)S(1)}, bf16[2,256,512]{2,1,0:T(8,128)(2,1)S(1)}, u32[]{:S(2)}, u32[]{:S(2)}) collective-permute-start(bf16[2,256,512]{2,1,0:T(8,128)(2,1)S(1)} %collective-permute-done.7.refs_1_.refs_3_.refs_13_.refs_20_), channel_id=1, source_target_pairs={{0,8},{8,16},{16,24},{24,28},{28,20},{20,12},{12,4},{4,0},{1,9},{9... | collective-permute-start | bytes 1572872 | tf_op jit(solution)/shard_map/ppermute | solution.py:246
  30.9 0.5 collective-permute-start.11
  31.3 6.9 %collective-permute-done.6.refs_5_.refs_3_ = bf16[512,512]{1,0:T(8,128)(2,1)S(1)} collective-permute-done((bf16[512,512]{1,0:T(8,128)(2,1)S(1)}, bf16[512,512]{1,0:T(8,128)(2,1)S(1)}, u32[]{:S(2)}, u32[]{:S(2)}) %collective-permute-start.6) | collective-permute-done | bytes 524320 | tf_op jit(solution)/shard_map/ppermute | solution.py:246
  38.2 0.2 shard_map.78
  38.4 1.6 %collective-permute-start.9 = (bf16[384,512]{1,0:T(8,128)(2,1)S(1)}, bf16[384,512]{1,0:T(8,128)(2,1)S(1)}, u32[]{:S(2)}, u32[]{:S(2)}) collective-permute-start(bf16[384,512]{1,0:T(8,128)(2,1)S(1)} %shard_map.78), channel_id=1, source_target_pairs={{0,2},{1,3},{2,0},{3,1},{4,6},{5,7},{6,4},{7,5},{8,10},{9,11},{10,... | collective-permute-start | bytes 1179656 | tf_op jit(solution)/shard_map/ppermute | solution.py:246
  40.0 1.3 %collective-permute-done.10.refs_2_.refs_1_.refs_3_.refs_14_.refs_21_ = bf16[2,256,512]{2,1,0:T(8,128)(2,1)S(1)} collective-permute-done((bf16[2,256,512]{2,1,0:T(8,128)(2,1)S(1)}, bf16[2,256,512]{2,1,0:T(8,128)(2,1)S(1)}, u32[]{:S(2)}, u32[]{:S(2)}) %collective-permute-start.10) | collective-permute-done | bytes 524320 | tf_op jit(solution)/shard_map/ppermute | solution.py:246
  41.4 1.6 %collective-permute-start.13 = (bf16[2,256,512]{2,1,0:T(8,128)(2,1)S(1)}, bf16[2,256,512]{2,1,0:T(8,128)(2,1)S(1)}, u32[]{:S(2)}, u32[]{:S(2)}) collective-permute-start(bf16[2,256,512]{2,1,0:T(8,128)(2,1)S(1)} %collective-permute-done.10.refs_2_.refs_1_.refs_3_.refs_14_.refs_21_), channel_id=1, source_target_pairs={{0,8},{8,16},{16,24},{24,28},{28,20},{20,12},{12,4},{4,0},{1,9},{9... | collective-permute-start | bytes 1572872 | tf_op jit(solution)/shard_map/ppermute | solution.py:246
  43.0 0.5 collective-permute-start.14
  43.5 3.9 %collective-permute-done.9.refs_5_.refs_4_ = bf16[384,512]{1,0:T(8,128)(2,1)S(1)} collective-permute-done((bf16[384,512]{1,0:T(8,128)(2,1)S(1)}, bf16[384,512]{1,0:T(8,128)(2,1)S(1)}, u32[]{:S(2)}, u32[]{:S(2)}) %collective-permute-start.9) | collective-permute-done | bytes 393248 | tf_op jit(solution)/shard_map/ppermute | solution.py:246
  47.5 0.2 shard_map.80
  47.7 1.8 %collective-permute-start.12 = (bf16[384,512]{1,0:T(8,128)(2,1)S(1)}, bf16[384,512]{1,0:T(8,128)(2,1)S(1)}, u32[]{:S(2)}, u32[]{:S(2)}) collective-permute-start(bf16[384,512]{1,0:T(8,128)(2,1)S(1)} %shard_map.80), channel_id=1, source_target_pairs={{0,2},{1,3},{2,0},{3,1},{4,6},{5,7},{6,4},{7,5},{8,10},{9,11},{10,... | collective-permute-start | bytes 1179656 | tf_op jit(solution)/shard_map/ppermute | solution.py:246
  49.5 2.7 %collective-permute-done.13.refs_0_.refs_4_.refs_1_.refs_15_.refs_22_ = bf16[2,256,512]{2,1,0:T(8,128)(2,1)S(1)} collective-permute-done((bf16[2,256,512]{2,1,0:T(8,128)(2,1)S(1)}, bf16[2,256,512]{2,1,0:T(8,128)(2,1)S(1)}, u32[]{:S(2)}, u32[]{:S(2)}) %collective-permute-start.13) | collective-permute-done | bytes 524320 | tf_op jit(solution)/shard_map/ppermute | solution.py:246
  52.2 1.5 %collective-permute-done.14.refs_2_.refs_5_.refs_26_.refs_10_ = bf16[2,256,512]{2,1,0:T(8,128)(2,1)S(1)} collective-permute-done((bf16[2,256,512]{2,1,0:T(8,128)(2,1)S(1)}, bf16[2,256,512]{2,1,0:T(8,128)(2,1)S(1)}, u32[]{:S(2)}, u32[]{:S(2)}) %collective-permute-start.14) | collective-permute-done | bytes 524320 | tf_op jit(solution)/shard_map/ppermute | solution.py:246
  53.7 0.1 shard_map.81
  53.8 1.7 %collective-permute-start.20 = (bf16[2,256,512]{2,1,0:T(8,128)(2,1)S(1)}, bf16[2,256,512]{2,1,0:T(8,128)(2,1)S(1)}, u32[]{:S(2)}, u32[]{:S(2)}) collective-permute-start(bf16[2,256,512]{2,1,0:T(8,128)(2,1)S(1)} %get-tuple-element.27.refs_3_), channel_id=1, source_target_pairs={{0,8},{8,16},{16,24},{24,28},{28,20},{20,12},{12,4},{4,0},{1,9},{9... | collective-permute-start | bytes 1572872 | tf_op jit(solution)/shard_map/ppermute | solution.py:246
  55.5 0.4 collective-permute-start.21
  55.9 1.1 collective-permute-done.12.refs_5_
  57.0 0.2 shard_map.82
  57.2 2.0 %collective-permute-start.15 = (bf16[384,512]{1,0:T(8,128)(2,1)S(1)}, bf16[384,512]{1,0:T(8,128)(2,1)}, u32[]{:S(2)}, u32[]{:S(2)}) collective-permute-start(bf16[384,512]{1,0:T(8,128)(2,1)S(1)} %shard_map.82), channel_id=1, source_target_pairs={{0,2},{1,3},{2,0},{3,1},{4,6},{5,7},{6,4},{7,5},{8,10},{9,11},{10,... | collective-permute-start | bytes 1179656 | tf_op jit(solution)/shard_map/ppermute | solution.py:246
  59.2 5.9 %collective-permute-done.15.refs_6_ = bf16[384,512]{1,0:T(8,128)(2,1)} collective-permute-done((bf16[384,512]{1,0:T(8,128)(2,1)S(1)}, bf16[384,512]{1,0:T(8,128)(2,1)}, u32[]{:S(2)}, u32[]{:S(2)}) %collective-permute-start.15) | collective-permute-done | bytes 393248 | tf_op jit(solution)/shard_map/ppermute | solution.py:246
  65.2 0.6 collective-permute-start.18
  65.9 0.6 stack.95.refs_0_
  66.5 0.1 shard_map.84
  66.7 1.6 %collective-permute-start.22 = (bf16[2,256,512]{2,1,0:T(8,128)(2,1)S(1)}, bf16[2,256,512]{2,1,0:T(8,128)(2,1)S(1)}, u32[]{:S(2)}, u32[]{:S(2)}) collective-permute-start(bf16[2,256,512]{2,1,0:T(8,128)(2,1)S(1)} %get-tuple-element.31), channel_id=1, source_target_pairs={{0,8},{8,16},{16,24},{24,28},{28,20},{20,12},{12,4},{4,0},{1,9},{9... | collective-permute-start | bytes 1572872 | tf_op jit(solution)/shard_map/ppermute | solution.py:246
  68.3 2.0 %collective-permute-start.24 = (bf16[2,256,512]{2,1,0:T(8,128)(2,1)S(1)}, bf16[2,256,512]{2,1,0:T(8,128)(2,1)S(1)}, u32[]{:S(2)}, u32[]{:S(2)}) collective-permute-start(bf16[2,256,512]{2,1,0:T(8,128)(2,1)S(1)} %get-tuple-element.32), channel_id=1, source_target_pairs={{0,2},{1,3},{2,0},{3,1},{4,6},{5,7},{6,4},{7,5},{8,10},{9,11},{10,... | collective-permute-start | bytes 1572872 | tf_op jit(solution)/shard_map/ppermute | solution.py:246
  70.3 0.5 collective-permute-start.23
  70.7 12.1 %shard_map.83 = (bf16[1664,512]{1,0:T(8,128)(2,1)}, bf16[1664,512]{1,0:T(8,128)(2,1)}) custom-call(s32[20]{0:T(128)} %stack.95.refs_0_, bf16[1664,512]{1,0:T(8,128)(2,1)} %get-tuple-element.21.refs_1_, bf16[1664,512]{1,0:T(8,128)(2,1)} %collective-permute-done.refs_2_, bf16[512,512]{1,0:T(8,128)(2,1)} %copy-done.15, bf16[384,512]{1,0:T(8,128)(2,1)} %copy-done.17, ...), custom_call_target="tpu_custom_call" | custom-call | flops 6979321856 | tf_op jit(solution)/shard_map/pallas_call | solution.py:188
  82.9 1.0 collective-permute-done.23.refs_3_.refs_2_.refs_12_.refs_18_
  83.9 0.5 collective-permute-start.26
  84.4 0.2 copy-done.12
  84.7 0.2 copy-done.11
  84.9 1.9 %collective-permute-start.27 = (bf16[1,256,512]{2,1,0:T(8,128)(2,1)S(1)}, bf16[1,256,512]{2,1,0:T(8,128)(2,1)S(1)}, u32[]{:S(2)}, u32[]{:S(2)}) collective-permute-start(bf16[1,256,512]{2,1,0:T(8,128)(2,1)S(1)} %get-tuple-element.35), channel_id=1, source_target_pairs={{0,8},{8,16},{16,24},{24,28},{28,20},{20,12},{12,4},{4,0},{1,9},{9... | collective-permute-start | bytes 786440 | tf_op jit(solution)/shard_map/ppermute | solution.py:246
  86.8 0.1 collective-permute-start.28
  87.0 0.7 stack.93.refs_0_
  87.7 5.2 %collective-permute-done.27.refs_16_ = bf16[1,256,512]{2,1,0:T(8,128)(2,1)S(1)} collective-permute-done((bf16[1,256,512]{2,1,0:T(8,128)(2,1)S(1)}, bf16[1,256,512]{2,1,0:T(8,128)(2,1)S(1)}, u32[]{:S(2)}, u32[]{:S(2)}) %collective-permute-start.27) | collective-permute-done | bytes 262176 | tf_op jit(solution)/shard_map/ppermute | solution.py:246
  92.9 1.6 %collective-permute-done.28.refs_20_ = bf16[1,256,512]{2,1,0:T(8,128)(2,1)S(1)} collective-permute-done((bf16[1,256,512]{2,1,0:T(8,128)(2,1)S(1)}, bf16[1,256,512]{2,1,0:T(8,128)(2,1)S(1)}, u32[]{:S(2)}, u32[]{:S(2)}) %collective-permute-start.28) | collective-permute-done | bytes 262176 | tf_op jit(solution)/shard_map/ppermute | solution.py:246
  94.5 0.7 copy-done.34
  95.2 0.5 copy-done.31
  95.7 13.4 %shard_map.87.q0 = f32[18,1664]{1,0:T(8,128)} custom-call(s32[20]{0:T(128)} %stack.93.refs_0_, bf16[1664,512]{1,0:T(8,128)(2,1)} %get-tuple-element.33.refs_3_.refs_1_, bf16[1664,512]{1,0:T(8,128)(2,1)} %copy-done.31, bf16[1664,512]{1,0:T(8,128)(2,1)} %get-tuple-element.34.refs_3_, bf16[1664,512]{1,0:T(8,128)(2,1)} %collective-permute-done.26.refs_4_, ...), custom_call_target="tpu_custom_call" | custom-call | flops 6979321856 | tf_op jit(solution)/shard_map/pallas_call | solution.py:188
  109.2 1.6 %collective-permute-done.29.q1 = f32[18,1664]{1,0:T(8,128)S(1)} collective-permute-done((f32[18,1664]{1,0:T(8,128)}, f32[18,1664]{1,0:T(8,128)S(1)}, u32[]{:S(2)}, u32[]{:S(2)}) %collective-permute-start.29) | collective-permute-done | bytes 119840 | tf_op jit(solution)/shard_map/ppermute | solution.py:246
  110.8 0.7 copy-done.26
  111.4 2.3 %shard_map.88 = f32[1,1664]{1,0:T(1,128)} custom-call(f32[18,1664]{1,0:T(8,128)} %shard_map.87.q0, f32[18,1664]{1,0:T(8,128)} %copy-done.26, f32[1,1664]{1,0:T(1,128)} %copy-done.21, s32[1,1664]{1,0:T(1,128)} %copy-done.22, s32[1,1664]{1,0:T(1,128)} %copy-done.23, f32[1,1664]{1,0:T(1,128)} %copy-done.24), custom_call_target="tpu_custom_call" | custom-call | tf_op jit(solution)/shard_map/pallas_call | solution.py:230
  113.7 0.3 collective-permute-start.30
  114.1 3.5 %collective-permute-done.30 = f32[1,1664]{1,0:T(1,128)S(1)} collective-permute-done((f32[1,1664]{1,0:T(1,128)}, f32[1,1664]{1,0:T(1,128)S(1)}, u32[]{:S(2)}, u32[]{:S(2)}) %collective-permute-start.30) | collective-permute-done | bytes 6688 | tf_op jit(solution)/shard_map/ppermute | solution.py:246
  117.6 0.7 broadcast_select_fusion.1
  118.3 0.7 reshape.19
  (97 shorter events, 1.0 us)
Async XLA Ops:
  0.0 15.1 %collective-permute-start.1 = (bf16[2,256,512]{2,1,0:T(8,128)(2,1)}, bf16[2,256,512]{2,1,0:T(8,128)(2,1)S(1)}, u32[]{:S(2)}, u32[]{:S(2)}) collective-permute-start(bf16[2,256,512]{2,1,0:T(8,128)(2,1)} %source.3), channel_id=1, source_target_pairs={{0,8},{8,16},{16,24},{24,28},{28,20},{20,12},{12,4},{4,0},{1,9},{9... | collective-permute-start | bytes 1572872 | tf_op jit(solution)/shard_map/ppermute | solution.py:246
  3.0 13.6 %collective-permute-start.2 = (bf16[2,256,512]{2,1,0:T(8,128)(2,1)}, bf16[2,256,512]{2,1,0:T(8,128)(2,1)S(1)}, u32[]{:S(2)}, u32[]{:S(2)}) collective-permute-start(bf16[2,256,512]{2,1,0:T(8,128)(2,1)} %source.3), channel_id=1, source_target_pairs={{8,0},{16,8},{24,16},{28,24},{20,28},{12,20},{4,12},{0,4},{9,1},{1... | collective-permute-start | bytes 1572872 | tf_op jit(solution)/shard_map/ppermute | solution.py:246
  3.0 1.1 copy-start.16
  4.7 14.1 %copy-start.25 = (bf16[1,256,512]{2,1,0:T(8,128)(2,1)}, bf16[1,256,512]{2,1,0:T(8,128)(2,1)S(1)}, u32[]{:S(2)}) copy-start(bf16[1,256,512]{2,1,0:T(8,128)(2,1)S(1)} %get-tuple-element.23.refs_11_) | copy-start | bytes 786436
  4.8 14.8 %copy-start.19 = (bf16[1,256,512]{2,1,0:T(8,128)(2,1)}, bf16[1,256,512]{2,1,0:T(8,128)(2,1)S(1)}, u32[]{:S(2)}) copy-start(bf16[1,256,512]{2,1,0:T(8,128)(2,1)S(1)} %get-tuple-element.26.refs_0_.refs_5_) | copy-start | bytes 786436
  4.8 8.4 %collective-permute-start.3 = (bf16[1,256,512]{2,1,0:T(8,128)(2,1)S(1)}, bf16[1,256,512]{2,1,0:T(8,128)(2,1)S(1)}, u32[]{:S(2)}, u32[]{:S(2)}) collective-permute-start(bf16[1,256,512]{2,1,0:T(8,128)(2,1)S(1)} %get-tuple-element.23.refs_11_), channel_id=1, source_target_pairs={{0,2},{1,3},{2,0},{3,1},{4,6},{5,7},{6,4},{7,5},{8,10},{9,11},{10,... | collective-permute-start | bytes 786440 | tf_op jit(solution)/shard_map/ppermute | solution.py:246
  6.8 14.4 %copy-start.27 = (f32[52,64]{1,0:T(8,128)S(1)}, f32[52,64]{1,0:T(8,128)}, u32[]{:S(2)}) copy-start(f32[52,64]{1,0:T(8,128)} %param.13) | copy-start | bytes 39940
  6.8 14.4 %copy-start.28 = (f32[52,64]{1,0:T(8,128)S(1)}, f32[52,64]{1,0:T(8,128)}, u32[]{:S(2)}) copy-start(f32[52,64]{1,0:T(8,128)} %param.10) | copy-start | bytes 39940
  6.8 14.5 %copy-start.29 = (s32[52,64]{1,0:T(8,128)S(1)}, s32[52,64]{1,0:T(8,128)}, u32[]{:S(2)}) copy-start(s32[52,64]{1,0:T(8,128)} %param.12) | copy-start | bytes 39940
  6.8 14.5 %copy-start.30 = (s32[52,64]{1,0:T(8,128)S(1)}, s32[52,64]{1,0:T(8,128)}, u32[]{:S(2)}) copy-start(s32[52,64]{1,0:T(8,128)} %param.11) | copy-start | bytes 39940
  6.8 6.3 %collective-permute-start.4 = (bf16[18,512]{1,0:T(8,128)(2,1)}, bf16[18,512]{1,0:T(8,128)(2,1)S(1)}, u32[]{:S(2)}, u32[]{:S(2)}) collective-permute-start(bf16[18,512]{1,0:T(8,128)(2,1)} %bitcast.16), channel_id=1, source_target_pairs={{0,2},{1,3},{2,0},{3,1},{4,6},{5,7},{6,4},{7,5},{8,10},{9,11},{10,... | collective-permute-start | bytes 55304 | tf_op jit(solution)/shard_map/ppermute | solution.py:246
  13.1 13.1 %copy-start.20 = (bf16[18,512]{1,0:T(8,128)(2,1)}, bf16[18,512]{1,0:T(8,128)(2,1)S(1)}, u32[]{:S(2)}) copy-start(bf16[18,512]{1,0:T(8,128)(2,1)S(1)} %collective-permute-done.4.refs_6_.refs_4_.refs_22_) | copy-start | bytes 55300
  13.1 13.1 %copy-start.6 = (bf16[1,256,512]{2,1,0:T(8,128)(2,1)}, bf16[1,256,512]{2,1,0:T(8,128)(2,1)S(1)}, u32[]{:S(2)}) copy-start(bf16[1,256,512]{2,1,0:T(8,128)(2,1)S(1)} %collective-permute-done.3.refs_1_.refs_5_.refs_3_.refs_19_) | copy-start | bytes 786436
  15.1 38.6 %copy-start.1 = (bf16[2,256,512]{2,1,0:T(8,128)(2,1)}, bf16[2,256,512]{2,1,0:T(8,128)(2,1)S(1)}, u32[]{:S(2)}) copy-start(bf16[2,256,512]{2,1,0:T(8,128)(2,1)S(1)} %collective-permute-done.1.refs_0_.refs_3_.refs_1_.refs_12_.refs_6_) | copy-start | bytes 1572868
  16.6 26.3 %copy-start = (bf16[2,256,512]{2,1,0:T(8,128)(2,1)}, bf16[2,256,512]{2,1,0:T(8,128)(2,1)S(1)}, u32[]{:S(2)}) copy-start(bf16[2,256,512]{2,1,0:T(8,128)(2,1)S(1)} %collective-permute-done.2.refs_2_.refs_4_.refs_1_.refs_16_.refs_9_) | copy-start | bytes 1572868
  16.7 12.5 %collective-permute-start.7 = (bf16[2,256,512]{2,1,0:T(8,128)(2,1)S(1)}, bf16[2,256,512]{2,1,0:T(8,128)(2,1)S(1)}, u32[]{:S(2)}, u32[]{:S(2)}) collective-permute-start(bf16[2,256,512]{2,1,0:T(8,128)(2,1)S(1)} %get-tuple-element.24.refs_5_), channel_id=1, source_target_pairs={{0,8},{8,16},{16,24},{24,28},{28,20},{20,12},{12,4},{4,0},{1,9},{9... | collective-permute-start | bytes 1572872 | tf_op jit(solution)/shard_map/ppermute | solution.py:246
  18.4 12.5 %collective-permute-start.8 = (bf16[2,256,512]{2,1,0:T(8,128)(2,1)S(1)}, bf16[2,256,512]{2,1,0:T(8,128)(2,1)}, u32[]{:S(2)}, u32[]{:S(2)}) collective-permute-start(bf16[2,256,512]{2,1,0:T(8,128)(2,1)S(1)} %get-tuple-element.25.refs_6_), channel_id=1, source_target_pairs={{8,0},{16,8},{24,16},{28,24},{20,28},{12,20},{4,12},{0,4},{9,1},{1... | collective-permute-start | bytes 1572872 | tf_op jit(solution)/shard_map/ppermute | solution.py:246
  19.6 6.6 %collective-permute-start.5 = (bf16[1,256,512]{2,1,0:T(8,128)(2,1)}, bf16[1,256,512]{2,1,0:T(8,128)(2,1)S(1)}, u32[]{:S(2)}, u32[]{:S(2)}) collective-permute-start(bf16[1,256,512]{2,1,0:T(8,128)(2,1)} %shard_map.76), channel_id=1, source_target_pairs={{0,2},{1,3},{2,0},{3,1},{4,6},{5,7},{6,4},{7,5},{8,10},{9,11},{10,... | collective-permute-start | bytes 786440 | tf_op jit(solution)/shard_map/ppermute | solution.py:246
  21.3 5.0 %copy-start.21 = (f32[1,1664]{1,0:T(1,128)}, f32[1,1664]{1,0:T(1,128)S(1)}, u32[]{:S(2)}) copy-start(f32[1,1664]{1,0:T(1,128)S(1)} %reshape.15.refs_8_.refs_27_.rewards) | copy-start | bytes 19972
  21.4 4.9 %copy-start.22 = (s32[1,1664]{1,0:T(1,128)}, s32[1,1664]{1,0:T(1,128)S(1)}, u32[]{:S(2)}) copy-start(s32[1,1664]{1,0:T(1,128)S(1)} %reshape.16.refs_9_.refs_28_.actions) | copy-start | bytes 19972
  21.5 4.8 %copy-start.23 = (s32[1,1664]{1,0:T(1,128)}, s32[1,1664]{1,0:T(1,128)S(1)}, u32[]{:S(2)}) copy-start(s32[1,1664]{1,0:T(1,128)S(1)} %reshape.17.refs_10_.refs_29_.done_flags) | copy-start | bytes 19972
  21.6 4.7 %copy-start.24 = (f32[1,1664]{1,0:T(1,128)}, f32[1,1664]{1,0:T(1,128)S(1)}, u32[]{:S(2)}) copy-start(f32[1,1664]{1,0:T(1,128)S(1)} %reshape.18.refs_11_.refs_30_.behaviour) | copy-start | bytes 19972
  21.6 2.0 %copy-start.7 = (bf16[3328,512]{1,0:T(8,128)(2,1)S(1)}, bf16[3328,512]{1,0:T(8,128)(2,1)}, u32[]{:S(2)}) copy-start(bf16[3328,512]{1,0:T(8,128)(2,1)} %source.2) | copy-start | bytes 10223620
  26.2 40.3 %copy-start.8 = (bf16[1,256,512]{2,1,0:T(8,128)(2,1)}, bf16[1,256,512]{2,1,0:T(8,128)(2,1)S(1)}, u32[]{:S(2)}) copy-start(bf16[1,256,512]{2,1,0:T(8,128)(2,1)S(1)} %collective-permute-done.5.refs_7_.refs_3_.refs_1_.refs_13_) | copy-start | bytes 786436
  26.3 11.9 %collective-permute-start.6 = (bf16[512,512]{1,0:T(8,128)(2,1)S(1)}, bf16[512,512]{1,0:T(8,128)(2,1)S(1)}, u32[]{:S(2)}, u32[]{:S(2)}) collective-permute-start(bf16[512,512]{1,0:T(8,128)(2,1)S(1)} %shard_map.77), channel_id=1, source_target_pairs={{0,2},{1,3},{2,0},{3,1},{4,6},{5,7},{6,4},{7,5},{8,10},{9,11},{10,... | collective-permute-start | bytes 1572872 | tf_op jit(solution)/shard_map/ppermute | solution.py:246
  29.3 9.1 %copy-start.9 = (bf16[2,256,512]{2,1,0:T(8,128)(2,1)}, bf16[2,256,512]{2,1,0:T(8,128)(2,1)S(1)}, u32[]{:S(2)}) copy-start(bf16[2,256,512]{2,1,0:T(8,128)(2,1)S(1)} %collective-permute-done.7.refs_1_.refs_3_.refs_13_.refs_20_) | copy-start | bytes 1572868
  29.3 12.1 %collective-permute-start.10 = (bf16[2,256,512]{2,1,0:T(8,128)(2,1)S(1)}, bf16[2,256,512]{2,1,0:T(8,128)(2,1)S(1)}, u32[]{:S(2)}, u32[]{:S(2)}) collective-permute-start(bf16[2,256,512]{2,1,0:T(8,128)(2,1)S(1)} %collective-permute-done.7.refs_1_.refs_3_.refs_13_.refs_20_), channel_id=1, source_target_pairs={{0,8},{8,16},{16,24},{24,28},{28,20},{20,12},{12,4},{4,0},{1,9},{9... | collective-permute-start | bytes 1572872 | tf_op jit(solution)/shard_map/ppermute | solution.py:246
  30.9 12.1 %collective-permute-start.11 = (bf16[2,256,512]{2,1,0:T(8,128)(2,1)}, bf16[2,256,512]{2,1,0:T(8,128)(2,1)S(1)}, u32[]{:S(2)}, u32[]{:S(2)}) collective-permute-start(bf16[2,256,512]{2,1,0:T(8,128)(2,1)} %collective-permute-done.8.refs_2_.refs_4_.refs_17_.refs_24_), channel_id=1, source_target_pairs={{8,0},{16,8},{24,16},{28,24},{20,28},{12,20},{4,12},{0,4},{9,1},{1... | collective-permute-start | bytes 1572872 | tf_op jit(solution)/shard_map/ppermute | solution.py:246
  31.3 35.4 %collective-permute-start = (bf16[1664,512]{1,0:T(8,128)(2,1)}, bf16[1664,512]{1,0:T(8,128)(2,1)}, u32[]{:S(2)}, u32[]{:S(2)}) collective-permute-start(bf16[1664,512]{1,0:T(8,128)(2,1)} %get-tuple-element.21.refs_1_), channel_id=1, source_target_pairs={{0,1},{1,0},{2,3},{3,2},{4,5},{5,4},{6,7},{7,6},{8,9},{9,8},{10,11... | collective-permute-start | bytes 5111816 | tf_op jit(solution)/shard_map/ppermute | solution.py:246
  38.2 21.0 %copy-start.15 = (bf16[512,512]{1,0:T(8,128)(2,1)}, bf16[512,512]{1,0:T(8,128)(2,1)S(1)}, u32[]{:S(2)}) copy-start(bf16[512,512]{1,0:T(8,128)(2,1)S(1)} %collective-permute-done.6.refs_5_.refs_3_) | copy-start | bytes 1572868
  38.4 9.0 %collective-permute-start.9 = (bf16[384,512]{1,0:T(8,128)(2,1)S(1)}, bf16[384,512]{1,0:T(8,128)(2,1)S(1)}, u32[]{:S(2)}, u32[]{:S(2)}) collective-permute-start(bf16[384,512]{1,0:T(8,128)(2,1)S(1)} %shard_map.78), channel_id=1, source_target_pairs={{0,2},{1,3},{2,0},{3,1},{4,6},{5,7},{6,4},{7,5},{8,10},{9,11},{10,... | collective-permute-start | bytes 1179656 | tf_op jit(solution)/shard_map/ppermute | solution.py:246
  41.4 6.3 %copy-start.2 = (bf16[2,256,512]{2,1,0:T(8,128)(2,1)}, bf16[2,256,512]{2,1,0:T(8,128)(2,1)S(1)}, u32[]{:S(2)}) copy-start(bf16[2,256,512]{2,1,0:T(8,128)(2,1)S(1)} %collective-permute-done.10.refs_2_.refs_1_.refs_3_.refs_14_.refs_21_) | copy-start | bytes 1572868
  41.4 10.8 %collective-permute-start.13 = (bf16[2,256,512]{2,1,0:T(8,128)(2,1)S(1)}, bf16[2,256,512]{2,1,0:T(8,128)(2,1)S(1)}, u32[]{:S(2)}, u32[]{:S(2)}) collective-permute-start(bf16[2,256,512]{2,1,0:T(8,128)(2,1)S(1)} %collective-permute-done.10.refs_2_.refs_1_.refs_3_.refs_14_.refs_21_), channel_id=1, source_target_pairs={{0,8},{8,16},{16,24},{24,28},{28,20},{20,12},{12,4},{4,0},{1,9},{9... | collective-permute-start | bytes 1572872 | tf_op jit(solution)/shard_map/ppermute | solution.py:246
  43.0 4.7 %copy-start.3 = (bf16[2,256,512]{2,1,0:T(8,128)(2,1)}, bf16[2,256,512]{2,1,0:T(8,128)(2,1)S(1)}, u32[]{:S(2)}) copy-start(bf16[2,256,512]{2,1,0:T(8,128)(2,1)S(1)} %collective-permute-done.11.refs_0_.refs_3_.refs_2_.refs_18_.refs_25_) | copy-start | bytes 1572868
  43.0 10.7 %collective-permute-start.14 = (bf16[2,256,512]{2,1,0:T(8,128)(2,1)S(1)}, bf16[2,256,512]{2,1,0:T(8,128)(2,1)S(1)}, u32[]{:S(2)}, u32[]{:S(2)}) collective-permute-start(bf16[2,256,512]{2,1,0:T(8,128)(2,1)S(1)} %shard_map.79.refs_4_), channel_id=1, source_target_pairs={{8,0},{16,8},{24,16},{28,24},{20,28},{12,20},{4,12},{0,4},{9,1},{1... | collective-permute-start | bytes 1572872 | tf_op jit(solution)/shard_map/ppermute | solution.py:246
  47.5 17.7 %copy-start.17 = (bf16[384,512]{1,0:T(8,128)(2,1)}, bf16[384,512]{1,0:T(8,128)(2,1)S(1)}, u32[]{:S(2)}) copy-start(bf16[384,512]{1,0:T(8,128)(2,1)S(1)} %collective-permute-done.9.refs_5_.refs_4_) | copy-start | bytes 1179652
  47.7 9.3 %collective-permute-start.12 = (bf16[384,512]{1,0:T(8,128)(2,1)S(1)}, bf16[384,512]{1,0:T(8,128)(2,1)S(1)}, u32[]{:S(2)}, u32[]{:S(2)}) collective-permute-start(bf16[384,512]{1,0:T(8,128)(2,1)S(1)} %shard_map.80), channel_id=1, source_target_pairs={{0,2},{1,3},{2,0},{3,1},{4,6},{5,7},{6,4},{7,5},{8,10},{9,11},{10,... | collective-permute-start | bytes 1179656 | tf_op jit(solution)/shard_map/ppermute | solution.py:246
  52.2 5.0 %copy-start.5 = (bf16[2,256,512]{2,1,0:T(8,128)(2,1)}, bf16[2,256,512]{2,1,0:T(8,128)(2,1)S(1)}, u32[]{:S(2)}) copy-start(bf16[2,256,512]{2,1,0:T(8,128)(2,1)S(1)} %collective-permute-done.13.refs_0_.refs_4_.refs_1_.refs_15_.refs_22_) | copy-start | bytes 1572868
  53.7 3.5 %copy-start.4 = (bf16[2,256,512]{2,1,0:T(8,128)(2,1)}, bf16[2,256,512]{2,1,0:T(8,128)(2,1)S(1)}, u32[]{:S(2)}) copy-start(bf16[2,256,512]{2,1,0:T(8,128)(2,1)S(1)} %collective-permute-done.14.refs_2_.refs_5_.refs_26_.refs_10_) | copy-start | bytes 1572868
  53.8 11.3 %collective-permute-start.20 = (bf16[2,256,512]{2,1,0:T(8,128)(2,1)S(1)}, bf16[2,256,512]{2,1,0:T(8,128)(2,1)S(1)}, u32[]{:S(2)}, u32[]{:S(2)}) collective-permute-start(bf16[2,256,512]{2,1,0:T(8,128)(2,1)S(1)} %get-tuple-element.27.refs_3_), channel_id=1, source_target_pairs={{0,8},{8,16},{16,24},{24,28},{28,20},{20,12},{12,4},{4,0},{1,9},{9... | collective-permute-start | bytes 1572872 | tf_op jit(solution)/shard_map/ppermute | solution.py:246
  55.5 10.2 %collective-permute-start.21 = (bf16[2,256,512]{2,1,0:T(8,128)(2,1)S(1)}, bf16[2,256,512]{2,1,0:T(8,128)(2,1)S(1)}, u32[]{:S(2)}, u32[]{:S(2)}) collective-permute-start(bf16[2,256,512]{2,1,0:T(8,128)(2,1)S(1)} %get-tuple-element.28.refs_4_), channel_id=1, source_target_pairs={{8,0},{16,8},{24,16},{28,24},{20,28},{12,20},{4,12},{0,4},{9,1},{1... | collective-permute-start | bytes 1572872 | tf_op jit(solution)/shard_map/ppermute | solution.py:246
  57.0 8.2 %copy-start.18 = (bf16[384,512]{1,0:T(8,128)(2,1)}, bf16[384,512]{1,0:T(8,128)(2,1)S(1)}, u32[]{:S(2)}) copy-start(bf16[384,512]{1,0:T(8,128)(2,1)S(1)} %collective-permute-done.12.refs_5_) | copy-start | bytes 1179652
  57.2 7.9 %collective-permute-start.15 = (bf16[384,512]{1,0:T(8,128)(2,1)S(1)}, bf16[384,512]{1,0:T(8,128)(2,1)}, u32[]{:S(2)}, u32[]{:S(2)}) collective-permute-start(bf16[384,512]{1,0:T(8,128)(2,1)S(1)} %shard_map.82), channel_id=1, source_target_pairs={{0,2},{1,3},{2,0},{3,1},{4,6},{5,7},{6,4},{7,5},{8,10},{9,11},{10,... | collective-permute-start | bytes 1179656 | tf_op jit(solution)/shard_map/ppermute | solution.py:246
  59.2 9.1 %collective-permute-start.16 = (bf16[512,512]{1,0:T(8,128)(2,1)S(1)}, bf16[512,512]{1,0:T(8,128)(2,1)S(1)}, u32[]{:S(2)}, u32[]{:S(2)}) collective-permute-start(bf16[512,512]{1,0:T(8,128)(2,1)S(1)} %collective-permute-done.6.refs_5_.refs_3_), channel_id=1, source_target_pairs={{0,1},{1,0},{2,3},{3,2},{4,5},{5,4},{6,7},{7,6},{8,9},{9,8},{10,11... | collective-permute-start | bytes 1572872 | tf_op jit(solution)/shard_map/ppermute | solution.py:246
  65.1 5.1 %collective-permute-start.17 = (bf16[384,512]{1,0:T(8,128)(2,1)S(1)}, bf16[384,512]{1,0:T(8,128)(2,1)}, u32[]{:S(2)}, u32[]{:S(2)}) collective-permute-start(bf16[384,512]{1,0:T(8,128)(2,1)S(1)} %collective-permute-done.9.refs_5_.refs_4_), channel_id=1, source_target_pairs={{0,1},{1,0},{2,3},{3,2},{4,5},{5,4},{6,7},{7,6},{8,9},{9,8},{10,11... | collective-permute-start | bytes 1179656 | tf_op jit(solution)/shard_map/ppermute | solution.py:246
  65.2 5.6 %copy-start.13 = (bf16[2,256,512]{2,1,0:T(8,128)(2,1)}, bf16[2,256,512]{2,1,0:T(8,128)(2,1)S(1)}, u32[]{:S(2)}) copy-start(bf16[2,256,512]{2,1,0:T(8,128)(2,1)S(1)} %collective-permute-done.20.refs_23_.refs_0_.refs_3_.refs_7_) | copy-start | bytes 1572868
  65.2 5.6 %collective-permute-start.18 = (bf16[384,512]{1,0:T(8,128)(2,1)S(1)}, bf16[384,512]{1,0:T(8,128)(2,1)}, u32[]{:S(2)}, u32[]{:S(2)}) collective-permute-start(bf16[384,512]{1,0:T(8,128)(2,1)S(1)} %collective-permute-done.12.refs_5_), channel_id=1, source_target_pairs={{0,1},{1,0},{2,3},{3,2},{4,5},{5,4},{6,7},{7,6},{8,9},{9,8},{10,11... | collective-permute-start | bytes 1179656 | tf_op jit(solution)/shard_map/ppermute | solution.py:246
  65.7 17.1 %copy-start.14 = (bf16[2,256,512]{2,1,0:T(8,128)(2,1)}, bf16[2,256,512]{2,1,0:T(8,128)(2,1)S(1)}, u32[]{:S(2)}) copy-start(bf16[2,256,512]{2,1,0:T(8,128)(2,1)S(1)} %collective-permute-done.21.refs_2_.refs_4_.refs_11_.refs_17_) | copy-start | bytes 1572868
  65.7 5.0 %collective-permute-start.19 = (bf16[384,512]{1,0:T(8,128)(2,1)}, bf16[384,512]{1,0:T(8,128)(2,1)}, u32[]{:S(2)}, u32[]{:S(2)}) collective-permute-start(bf16[384,512]{1,0:T(8,128)(2,1)} %collective-permute-done.15.refs_6_), channel_id=1, source_target_pairs={{0,1},{1,0},{2,3},{3,2},{4,5},{5,4},{6,7},{7,6},{8,9},{9,8},{10,11... | collective-permute-start | bytes 1179656 | tf_op jit(solution)/shard_map/ppermute | solution.py:246
  66.7 16.2 %collective-permute-start.22 = (bf16[2,256,512]{2,1,0:T(8,128)(2,1)S(1)}, bf16[2,256,512]{2,1,0:T(8,128)(2,1)S(1)}, u32[]{:S(2)}, u32[]{:S(2)}) collective-permute-start(bf16[2,256,512]{2,1,0:T(8,128)(2,1)S(1)} %get-tuple-element.31), channel_id=1, source_target_pairs={{0,8},{8,16},{16,24},{24,28},{28,20},{20,12},{12,4},{4,0},{1,9},{9... | collective-permute-start | bytes 1572872 | tf_op jit(solution)/shard_map/ppermute | solution.py:246
  68.3 2.4 %copy-start.32 = (bf16[512,512]{1,0:T(8,128)(2,1)}, bf16[512,512]{1,0:T(8,128)(2,1)S(1)}, u32[]{:S(2)}) copy-start(bf16[512,512]{1,0:T(8,128)(2,1)S(1)} %collective-permute-done.16.refs_7_) | copy-start | bytes 1572868
  68.3 15.5 %collective-permute-start.24 = (bf16[2,256,512]{2,1,0:T(8,128)(2,1)S(1)}, bf16[2,256,512]{2,1,0:T(8,128)(2,1)S(1)}, u32[]{:S(2)}, u32[]{:S(2)}) collective-permute-start(bf16[2,256,512]{2,1,0:T(8,128)(2,1)S(1)} %get-tuple-element.32), channel_id=1, source_target_pairs={{0,2},{1,3},{2,0},{3,1},{4,6},{5,7},{6,4},{7,5},{8,10},{9,11},{10,... | collective-permute-start | bytes 1572872 | tf_op jit(solution)/shard_map/ppermute | solution.py:246
  70.3 13.6 %collective-permute-start.23 = (bf16[2,256,512]{2,1,0:T(8,128)(2,1)S(1)}, bf16[2,256,512]{2,1,0:T(8,128)(2,1)S(1)}, u32[]{:S(2)}, u32[]{:S(2)}) collective-permute-start(bf16[2,256,512]{2,1,0:T(8,128)(2,1)S(1)} %collective-permute-done.21.refs_2_.refs_4_.refs_11_.refs_17_), channel_id=1, source_target_pairs={{8,0},{16,8},{24,16},{28,24},{20,28},{12,20},{4,12},{0,4},{9,1},{1... | collective-permute-start | bytes 1572872 | tf_op jit(solution)/shard_map/ppermute | solution.py:246
  82.9 1.6 %copy-start.10 = (bf16[2,256,512]{2,1,0:T(8,128)(2,1)}, bf16[2,256,512]{2,1,0:T(8,128)(2,1)S(1)}, u32[]{:S(2)}) copy-start(bf16[2,256,512]{2,1,0:T(8,128)(2,1)S(1)} %collective-permute-done.22.refs_2_.refs_1_.refs_8_.refs_14_) | copy-start | bytes 1572868
  83.9 0.8 copy-start.12
  83.9 1.0 copy-start.11
  83.9 10.6 %collective-permute-start.25 = (bf16[1664,512]{1,0:T(8,128)(2,1)}, bf16[1664,512]{1,0:T(8,128)(2,1)S(1)}, u32[]{:S(2)}, u32[]{:S(2)}) collective-permute-start(bf16[1664,512]{1,0:T(8,128)(2,1)} %get-tuple-element.33.refs_3_.refs_1_), channel_id=1, source_target_pairs={{0,1},{1,0},{2,3},{3,2},{4,5},{5,4},{6,7},{7,6},{8,9},{9,8},{10,11... | collective-permute-start | bytes 5111816 | tf_op jit(solution)/shard_map/ppermute | solution.py:246
  83.9 10.5 %collective-permute-start.26 = (bf16[1664,512]{1,0:T(8,128)(2,1)}, bf16[1664,512]{1,0:T(8,128)(2,1)}, u32[]{:S(2)}, u32[]{:S(2)}) collective-permute-start(bf16[1664,512]{1,0:T(8,128)(2,1)} %get-tuple-element.34.refs_3_), channel_id=1, source_target_pairs={{0,1},{1,0},{2,3},{3,2},{4,5},{5,4},{6,7},{7,6},{8,9},{9,8},{10,11... | collective-permute-start | bytes 5111816 | tf_op jit(solution)/shard_map/ppermute | solution.py:246
  84.9 8.0 %collective-permute-start.27 = (bf16[1,256,512]{2,1,0:T(8,128)(2,1)S(1)}, bf16[1,256,512]{2,1,0:T(8,128)(2,1)S(1)}, u32[]{:S(2)}, u32[]{:S(2)}) collective-permute-start(bf16[1,256,512]{2,1,0:T(8,128)(2,1)S(1)} %get-tuple-element.35), channel_id=1, source_target_pairs={{0,8},{8,16},{16,24},{24,28},{28,20},{20,12},{12,4},{4,0},{1,9},{9... | collective-permute-start | bytes 786440 | tf_op jit(solution)/shard_map/ppermute | solution.py:246
  86.8 7.6 %collective-permute-start.28 = (bf16[1,256,512]{2,1,0:T(8,128)(2,1)S(1)}, bf16[1,256,512]{2,1,0:T(8,128)(2,1)S(1)}, u32[]{:S(2)}, u32[]{:S(2)}) collective-permute-start(bf16[1,256,512]{2,1,0:T(8,128)(2,1)S(1)} %get-tuple-element.36), channel_id=1, source_target_pairs={{8,0},{16,8},{24,16},{28,24},{20,28},{12,20},{4,12},{0,4},{9,1},{1... | collective-permute-start | bytes 786440 | tf_op jit(solution)/shard_map/ppermute | solution.py:246
  92.9 1.6 %copy-start.33 = (bf16[1,256,512]{2,1,0:T(8,128)(2,1)}, bf16[1,256,512]{2,1,0:T(8,128)(2,1)S(1)}, u32[]{:S(2)}) copy-start(bf16[1,256,512]{2,1,0:T(8,128)(2,1)S(1)} %collective-permute-done.27.refs_16_) | copy-start | bytes 786436
  94.5 1.3 %copy-start.31 = (bf16[1664,512]{1,0:T(8,128)(2,1)}, bf16[1664,512]{1,0:T(8,128)(2,1)S(1)}, u32[]{:S(2)}) copy-start(bf16[1664,512]{1,0:T(8,128)(2,1)S(1)} %collective-permute-done.25.refs_2_) | copy-start | bytes 5111812
  109.1 1.7 %collective-permute-start.29 = (f32[18,1664]{1,0:T(8,128)}, f32[18,1664]{1,0:T(8,128)S(1)}, u32[]{:S(2)}, u32[]{:S(2)}) collective-permute-start(f32[18,1664]{1,0:T(8,128)} %shard_map.87.q0), channel_id=1, source_target_pairs={{0,1},{1,0},{2,3},{3,2},{4,5},{5,4},{6,7},{7,6},{8,9},{9,8},{10,11... | collective-permute-start | bytes 359432 | tf_op jit(solution)/shard_map/ppermute | solution.py:246
  113.7 3.8 %collective-permute-start.30 = (f32[1,1664]{1,0:T(1,128)}, f32[1,1664]{1,0:T(1,128)S(1)}, u32[]{:S(2)}, u32[]{:S(2)}) collective-permute-start(f32[1,1664]{1,0:T(1,128)} %shard_map.88), channel_id=1, source_target_pairs={{0,2},{1,3},{2,0},{3,1},{4,6},{5,7},{6,4},{7,5},{8,10},{9,11},{10,... | collective-permute-start | bytes 19976 | tf_op jit(solution)/shard_map/ppermute | solution.py:246
  (2 other events, 1.4 us)

commit v6 on v5

--- a/solution.py
+++ b/solution.py
@@ -194,7 +194,7 @@
         + [anywhere] * len(after),
         out_specs=vmem if headed else [anywhere] * count,
         scratch_shapes=scratch,
-        compiler_params=pltpu.CompilerParams(vmem_limit_bytes=56 * 1024 * 1024),
+        compiler_params=pltpu.CompilerParams(vmem_limit_bytes=52 * 1024 * 1024),
         cost_estimate=pl.CostEstimate(flops=2 * rows * depth * width * count, bytes_accessed=0, transcendentals=0),
     )(pos, *[a for h in hs for a in h], *ws, *heads, *after)
 

time: 119 us -> 116 us (0.975)
  local copies, waits for them, and re-layouts: 7.79 us -> 6.35 us
  Pallas kernels: 32.5 us -> 31.2 us
    pallas_call x2, Pallas kernels: 25.5 us -> 24 us  [layer(): pl.pallas_call(functools.partial(layer_kernel, [len(h) for h in hs], bloc...]
    unnamed x70 -> x58, local copies, waits for them, and re-layouts: 5.45 us -> 5.14 us
where the time goes in v6:
time: 116 us
  waiting for transfers between devices  47.9 us (41%)
  Pallas kernels  31.2 us (27%)
  starting transfers between devices  28.9 us (25%)
  local copies, waits for them, and re-layouts  6.35 us (5%)
    ppermute x31, waiting for transfers between devices, over(): return lambda a: lax.ppermute(a, axis, pairs)  47.9 us
    ppermute x31, starting transfers between devices, over(): return lambda a: lax.ppermute(a, axis, pairs)  28.9 us
    pallas_call x2, Pallas kernels, layer(): pl.pallas_call(functools.partial(layer_kernel, [len(h) for h in hs], bloc...  24 us
    unnamed x58, local copies, waits for them, and re-layouts  5.14 us
    pallas_call x2, Pallas kernels, cut(): pl.pallas_call(functools.partial(cut_kernel, len(sizes)), out_shape=[jax....  2.95 us
  transfers between devices with their start and end apart: 31, of which 17 were waited for; matrix products, arithmetic and copies ran while one was open for 1% of the time, Pallas kernels for 14%

profile of v6, /device:TPU:0, one launch (start us, length us, event | category | flops | bytes accessed | tf_op | source)
XLA Modules:
  0.0 115.6 jit_solution(16928204547522839326)
XLA Ops:
  0.0 3.0 %collective-permute-start.1 = (bf16[2,256,512]{2,1,0:T(8,128)(2,1)}, bf16[2,256,512]{2,1,0:T(8,128)(2,1)S(1)}, u32[]{:S(2)}, u32[]{:S(2)}) collective-permute-start(bf16[2,256,512]{2,1,0:T(8,128)(2,1)} %source.3), channel_id=1, source_target_pairs={{0,8},{8,16},{16,24},{24,28},{28,20},{20,12},{12,4},{4,0},{1,9},{9... | collective-permute-start | bytes 1572872 | tf_op jit(solution)/shard_map/ppermute | solution.py:246
  3.0 1.1 copy-done.15
  4.1 0.6 shard_map.74
  4.8 2.0 %collective-permute-start.3 = (bf16[1,256,512]{2,1,0:T(8,128)(2,1)S(1)}, bf16[1,256,512]{2,1,0:T(8,128)(2,1)S(1)}, u32[]{:S(2)}, u32[]{:S(2)}) collective-permute-start(bf16[1,256,512]{2,1,0:T(8,128)(2,1)S(1)} %get-tuple-element.23.refs_11_), channel_id=1, source_target_pairs={{0,2},{1,3},{2,0},{3,1},{4,6},{5,7},{6,4},{7,5},{8,10},{9,11},{10,... | collective-permute-start | bytes 786440 | tf_op jit(solution)/shard_map/ppermute | solution.py:246
  6.8 0.2 collective-permute-start.4
  6.9 6.2 %collective-permute-done.4.refs_6_.refs_4_.refs_22_ = bf16[18,512]{1,0:T(8,128)(2,1)S(1)} collective-permute-done((bf16[18,512]{1,0:T(8,128)(2,1)}, bf16[18,512]{1,0:T(8,128)(2,1)S(1)}, u32[]{:S(2)}, u32[]{:S(2)}) %collective-permute-start.4) | collective-permute-done | bytes 18464 | tf_op jit(solution)/shard_map/ppermute | solution.py:246
  13.1 1.9 %collective-permute-done.1.refs_0_.refs_3_.refs_1_.refs_12_.refs_6_ = bf16[2,256,512]{2,1,0:T(8,128)(2,1)S(1)} collective-permute-done((bf16[2,256,512]{2,1,0:T(8,128)(2,1)}, bf16[2,256,512]{2,1,0:T(8,128)(2,1)S(1)}, u32[]{:S(2)}, u32[]{:S(2)}) %collective-permute-start.1) | collective-permute-done | bytes 524320 | tf_op jit(solution)/shard_map/ppermute | solution.py:246
  15.1 1.5 %collective-permute-done.2.refs_2_.refs_4_.refs_1_.refs_16_.refs_9_ = bf16[2,256,512]{2,1,0:T(8,128)(2,1)S(1)} collective-permute-done((bf16[2,256,512]{2,1,0:T(8,128)(2,1)}, bf16[2,256,512]{2,1,0:T(8,128)(2,1)S(1)}, u32[]{:S(2)}, u32[]{:S(2)}) %collective-permute-start.2) | collective-permute-done | bytes 524320 | tf_op jit(solution)/shard_map/ppermute | solution.py:246
  16.6 1.0 shard_map.75
  17.7 1.6 %collective-permute-start.7 = (bf16[2,256,512]{2,1,0:T(8,128)(2,1)}, bf16[2,256,512]{2,1,0:T(8,128)(2,1)S(1)}, u32[]{:S(2)}, u32[]{:S(2)}) collective-permute-start(bf16[2,256,512]{2,1,0:T(8,128)(2,1)} %get-tuple-element.24.refs_5_), channel_id=1, source_target_pairs={{0,8},{8,16},{16,24},{24,28},{28,20},{20,12},{12,4},{4,0},{1,9},{9... | collective-permute-start | bytes 1572872 | tf_op jit(solution)/shard_map/ppermute | solution.py:246
  19.3 0.4 collective-permute-start.8
  19.8 1.6 %collective-permute-start.5 = (bf16[1,256,512]{2,1,0:T(8,128)(2,1)S(1)}, bf16[1,256,512]{2,1,0:T(8,128)(2,1)S(1)}, u32[]{:S(2)}, u32[]{:S(2)}) collective-permute-start(bf16[1,256,512]{2,1,0:T(8,128)(2,1)S(1)} %shard_map.76), channel_id=1, source_target_pairs={{0,2},{1,3},{2,0},{3,1},{4,6},{5,7},{6,4},{7,5},{8,10},{9,11},{10,... | collective-permute-start | bytes 786440 | tf_op jit(solution)/shard_map/ppermute | solution.py:246
  21.4 0.1 reshape.15.refs_8_.refs_27_.rewards
  21.5 0.1 reshape.16.refs_9_.refs_28_.actions
  21.6 0.1 reshape.17.refs_10_.refs_29_.done_flags
  21.8 2.0 %copy-done.7 = bf16[3328,512]{1,0:T(8,128)(2,1)S(1)} copy-done((bf16[3328,512]{1,0:T(8,128)(2,1)S(1)}, bf16[3328,512]{1,0:T(8,128)(2,1)}, u32[]{:S(2)}) %copy-start.7) | copy-done | bytes 3407896
  23.8 2.3 %shard_map.73 = (bf16[1664,512]{1,0:T(8,128)(2,1)}, bf16[1664,512]{1,0:T(8,128)(2,1)S(1)}) custom-call(s32[2]{0:T(128)S(1)} %pad_add_fusion.at, bf16[3328,512]{1,0:T(8,128)(2,1)S(1)} %copy-done.7), custom_call_target="tpu_custom_call" | custom-call | tf_op jit(solution)/shard_map/pallas_call | solution.py:38
  26.3 1.6 %collective-permute-start.6 = (bf16[512,512]{1,0:T(8,128)(2,1)S(1)}, bf16[512,512]{1,0:T(8,128)(2,1)S(1)}, u32[]{:S(2)}, u32[]{:S(2)}) collective-permute-start(bf16[512,512]{1,0:T(8,128)(2,1)S(1)} %shard_map.77), channel_id=1, source_target_pairs={{0,2},{1,3},{2,0},{3,1},{4,6},{5,7},{6,4},{7,5},{8,10},{9,11},{10,... | collective-permute-start | bytes 1572872 | tf_op jit(solution)/shard_map/ppermute | solution.py:246
  27.9 2.5 %collective-permute-done.7.refs_1_.refs_3_.refs_13_.refs_20_ = bf16[2,256,512]{2,1,0:T(8,128)(2,1)S(1)} collective-permute-done((bf16[2,256,512]{2,1,0:T(8,128)(2,1)}, bf16[2,256,512]{2,1,0:T(8,128)(2,1)S(1)}, u32[]{:S(2)}, u32[]{:S(2)}) %collective-permute-start.7) | collective-permute-done | bytes 524320 | tf_op jit(solution)/shard_map/ppermute | solution.py:246
  30.4 1.6 %collective-permute-start.10 = (bf16[2,256,512]{2,1,0:T(8,128)(2,1)S(1)}, bf16[2,256,512]{2,1,0:T(8,128)(2,1)S(1)}, u32[]{:S(2)}, u32[]{:S(2)}) collective-permute-start(bf16[2,256,512]{2,1,0:T(8,128)(2,1)S(1)} %collective-permute-done.7.refs_1_.refs_3_.refs_13_.refs_20_), channel_id=1, source_target_pairs={{0,8},{8,16},{16,24},{24,28},{28,20},{20,12},{12,4},{4,0},{1,9},{9... | collective-permute-start | bytes 1572872 | tf_op jit(solution)/shard_map/ppermute | solution.py:246
  32.0 0.5 collective-permute-start.11
  32.4 5.7 %collective-permute-done.6.refs_5_.refs_3_ = bf16[512,512]{1,0:T(8,128)(2,1)S(1)} collective-permute-done((bf16[512,512]{1,0:T(8,128)(2,1)S(1)}, bf16[512,512]{1,0:T(8,128)(2,1)S(1)}, u32[]{:S(2)}, u32[]{:S(2)}) %collective-permute-start.6) | collective-permute-done | bytes 524320 | tf_op jit(solution)/shard_map/ppermute | solution.py:246
  38.2 0.2 shard_map.78
  38.4 1.6 %collective-permute-start.9 = (bf16[384,512]{1,0:T(8,128)(2,1)S(1)}, bf16[384,512]{1,0:T(8,128)(2,1)S(1)}, u32[]{:S(2)}, u32[]{:S(2)}) collective-permute-start(bf16[384,512]{1,0:T(8,128)(2,1)S(1)} %shard_map.78), channel_id=1, source_target_pairs={{0,2},{1,3},{2,0},{3,1},{4,6},{5,7},{6,4},{7,5},{8,10},{9,11},{10,... | collective-permute-start | bytes 1179656 | tf_op jit(solution)/shard_map/ppermute | solution.py:246
  40.0 2.5 %collective-permute-done.10.refs_2_.refs_1_.refs_3_.refs_14_.refs_21_ = bf16[2,256,512]{2,1,0:T(8,128)(2,1)S(1)} collective-permute-done((bf16[2,256,512]{2,1,0:T(8,128)(2,1)S(1)}, bf16[2,256,512]{2,1,0:T(8,128)(2,1)S(1)}, u32[]{:S(2)}, u32[]{:S(2)}) %collective-permute-start.10) | collective-permute-done | bytes 524320 | tf_op jit(solution)/shard_map/ppermute | solution.py:246
  42.5 1.6 %collective-permute-start.13 = (bf16[2,256,512]{2,1,0:T(8,128)(2,1)S(1)}, bf16[2,256,512]{2,1,0:T(8,128)(2,1)S(1)}, u32[]{:S(2)}, u32[]{:S(2)}) collective-permute-start(bf16[2,256,512]{2,1,0:T(8,128)(2,1)S(1)} %collective-permute-done.10.refs_2_.refs_1_.refs_3_.refs_14_.refs_21_), channel_id=1, source_target_pairs={{0,8},{8,16},{16,24},{24,28},{28,20},{20,12},{12,4},{4,0},{1,9},{9... | collective-permute-start | bytes 1572872 | tf_op jit(solution)/shard_map/ppermute | solution.py:246
  44.2 0.5 collective-permute-start.14
  44.7 2.8 %collective-permute-done.9.refs_5_.refs_4_ = bf16[384,512]{1,0:T(8,128)(2,1)S(1)} collective-permute-done((bf16[384,512]{1,0:T(8,128)(2,1)S(1)}, bf16[384,512]{1,0:T(8,128)(2,1)S(1)}, u32[]{:S(2)}, u32[]{:S(2)}) %collective-permute-start.9) | collective-permute-done | bytes 393248 | tf_op jit(solution)/shard_map/ppermute | solution.py:246
  47.4 0.2 shard_map.80
  47.7 1.8 %collective-permute-start.12 = (bf16[384,512]{1,0:T(8,128)(2,1)S(1)}, bf16[384,512]{1,0:T(8,128)(2,1)S(1)}, u32[]{:S(2)}, u32[]{:S(2)}) collective-permute-start(bf16[384,512]{1,0:T(8,128)(2,1)S(1)} %shard_map.80), channel_id=1, source_target_pairs={{0,2},{1,3},{2,0},{3,1},{4,6},{5,7},{6,4},{7,5},{8,10},{9,11},{10,... | collective-permute-start | bytes 1179656 | tf_op jit(solution)/shard_map/ppermute | solution.py:246
  49.4 3.9 %collective-permute-done.13.refs_0_.refs_4_.refs_1_.refs_15_.refs_22_ = bf16[2,256,512]{2,1,0:T(8,128)(2,1)S(1)} collective-permute-done((bf16[2,256,512]{2,1,0:T(8,128)(2,1)S(1)}, bf16[2,256,512]{2,1,0:T(8,128)(2,1)S(1)}, u32[]{:S(2)}, u32[]{:S(2)}) %collective-permute-start.13) | collective-permute-done | bytes 524320 | tf_op jit(solution)/shard_map/ppermute | solution.py:246
  53.3 1.5 %collective-permute-done.14.refs_2_.refs_5_.refs_26_.refs_10_ = bf16[2,256,512]{2,1,0:T(8,128)(2,1)S(1)} collective-permute-done((bf16[2,256,512]{2,1,0:T(8,128)(2,1)S(1)}, bf16[2,256,512]{2,1,0:T(8,128)(2,1)S(1)}, u32[]{:S(2)}, u32[]{:S(2)}) %collective-permute-start.14) | collective-permute-done | bytes 524320 | tf_op jit(solution)/shard_map/ppermute | solution.py:246
  54.8 0.1 shard_map.81
  55.0 1.7 %collective-permute-start.20 = (bf16[2,256,512]{2,1,0:T(8,128)(2,1)S(1)}, bf16[2,256,512]{2,1,0:T(8,128)(2,1)S(1)}, u32[]{:S(2)}, u32[]{:S(2)}) collective-permute-start(bf16[2,256,512]{2,1,0:T(8,128)(2,1)S(1)} %get-tuple-element.27.refs_3_), channel_id=1, source_target_pairs={{0,8},{8,16},{16,24},{24,28},{28,20},{20,12},{12,4},{4,0},{1,9},{9... | collective-permute-start | bytes 1572872 | tf_op jit(solution)/shard_map/ppermute | solution.py:246
  56.7 0.4 collective-permute-start.21
  57.0 0.2 shard_map.82
  57.3 1.6 %collective-permute-start.15 = (bf16[384,512]{1,0:T(8,128)(2,1)S(1)}, bf16[384,512]{1,0:T(8,128)(2,1)}, u32[]{:S(2)}, u32[]{:S(2)}) collective-permute-start(bf16[384,512]{1,0:T(8,128)(2,1)S(1)} %shard_map.82), channel_id=1, source_target_pairs={{0,2},{1,3},{2,0},{3,1},{4,6},{5,7},{6,4},{7,5},{8,10},{9,11},{10,... | collective-permute-start | bytes 1179656 | tf_op jit(solution)/shard_map/ppermute | solution.py:246
  58.8 6.4 %collective-permute-done.15.refs_6_ = bf16[384,512]{1,0:T(8,128)(2,1)} collective-permute-done((bf16[384,512]{1,0:T(8,128)(2,1)S(1)}, bf16[384,512]{1,0:T(8,128)(2,1)}, u32[]{:S(2)}, u32[]{:S(2)}) %collective-permute-start.15) | collective-permute-done | bytes 393248 | tf_op jit(solution)/shard_map/ppermute | solution.py:246
  65.2 0.5 collective-permute-start.18
  65.7 0.3 collective-permute-done.21.refs_2_.refs_4_.refs_11_.refs_17_
  66.1 0.1 stack.95.refs_0_
  66.2 0.1 shard_map.84
  66.3 2.0 %collective-permute-start.22 = (bf16[2,256,512]{2,1,0:T(8,128)(2,1)S(1)}, bf16[2,256,512]{2,1,0:T(8,128)(2,1)S(1)}, u32[]{:S(2)}, u32[]{:S(2)}) collective-permute-start(bf16[2,256,512]{2,1,0:T(8,128)(2,1)S(1)} %get-tuple-element.31), channel_id=1, source_target_pairs={{0,8},{8,16},{16,24},{24,28},{28,20},{20,12},{12,4},{4,0},{1,9},{9... | collective-permute-start | bytes 1572872 | tf_op jit(solution)/shard_map/ppermute | solution.py:246
  68.3 1.5 %collective-permute-start.24 = (bf16[2,256,512]{2,1,0:T(8,128)(2,1)S(1)}, bf16[2,256,512]{2,1,0:T(8,128)(2,1)S(1)}, u32[]{:S(2)}, u32[]{:S(2)}) collective-permute-start(bf16[2,256,512]{2,1,0:T(8,128)(2,1)S(1)} %get-tuple-element.32), channel_id=1, source_target_pairs={{0,2},{1,3},{2,0},{3,1},{4,6},{5,7},{6,4},{7,5},{8,10},{9,11},{10,... | collective-permute-start | bytes 1572872 | tf_op jit(solution)/shard_map/ppermute | solution.py:246
  69.8 0.1 collective-permute-start.23
  70.0 0.9 copy-done.22
  70.9 11.9 %shard_map.83 = (bf16[1664,512]{1,0:T(8,128)(2,1)}, bf16[1664,512]{1,0:T(8,128)(2,1)}) custom-call(s32[20]{0:T(128)S(1)} %stack.95.refs_0_, bf16[1664,512]{1,0:T(8,128)(2,1)} %get-tuple-element.21.refs_1_, bf16[1664,512]{1,0:T(8,128)(2,1)} %collective-permute-done.refs_2_, bf16[512,512]{1,0:T(8,128)(2,1)} %copy-done.14, ...), custom_call_target="tpu_custom_call" | custom-call | flops 6979321856 | tf_op jit(solution)/shard_map/pallas_call | solution.py:188
  82.9 0.7 collective-permute-done.23.refs_3_.refs_2_.refs_12_.refs_18_
  83.7 0.5 collective-permute-start.26
  84.2 0.2 copy-done.11
  84.4 0.2 copy-done.10
  84.6 1.6 %collective-permute-start.27 = (bf16[1,256,512]{2,1,0:T(8,128)(2,1)S(1)}, bf16[1,256,512]{2,1,0:T(8,128)(2,1)S(1)}, u32[]{:S(2)}, u32[]{:S(2)}) collective-permute-start(bf16[1,256,512]{2,1,0:T(8,128)(2,1)S(1)} %get-tuple-element.35), channel_id=1, source_target_pairs={{0,8},{8,16},{16,24},{24,28},{28,20},{20,12},{12,4},{4,0},{1,9},{9... | collective-permute-start | bytes 786440 | tf_op jit(solution)/shard_map/ppermute | solution.py:246
  86.2 0.5 collective-permute-start.28
  86.7 0.1 stack.93.refs_0_
  86.8 5.8 %collective-permute-done.27.refs_16_ = bf16[1,256,512]{2,1,0:T(8,128)(2,1)S(1)} collective-permute-done((bf16[1,256,512]{2,1,0:T(8,128)(2,1)S(1)}, bf16[1,256,512]{2,1,0:T(8,128)(2,1)S(1)}, u32[]{:S(2)}, u32[]{:S(2)}) %collective-permute-start.27) | collective-permute-done | bytes 262176 | tf_op jit(solution)/shard_map/ppermute | solution.py:246
  92.6 1.3 %collective-permute-done.28.refs_20_ = bf16[1,256,512]{2,1,0:T(8,128)(2,1)S(1)} collective-permute-done((bf16[1,256,512]{2,1,0:T(8,128)(2,1)S(1)}, bf16[1,256,512]{2,1,0:T(8,128)(2,1)S(1)}, u32[]{:S(2)}, u32[]{:S(2)}) %collective-permute-start.28) | collective-permute-done | bytes 262176 | tf_op jit(solution)/shard_map/ppermute | solution.py:246
  93.9 12.0 %shard_map.87.q0 = f32[18,1664]{1,0:T(8,128)S(1)} custom-call(s32[20]{0:T(128)S(1)} %stack.93.refs_0_, bf16[1664,512]{1,0:T(8,128)(2,1)} %get-tuple-element.33.refs_3_.refs_1_, bf16[1664,512]{1,0:T(8,128)(2,1)} %collective-permute-done.25.refs_2_, bf16[1664,512]{1,0:T(8,128)(2,1)} %get-tuple-element.34.refs_3_, ...), custom_call_target="tpu_custom_call" | custom-call | flops 6979321856 | tf_op jit(solution)/shard_map/pallas_call | solution.py:188
  106.0 1.4 %collective-permute-done.29.q1 = f32[18,1664]{1,0:T(8,128)S(1)} collective-permute-done((f32[18,1664]{1,0:T(8,128)S(1)}, f32[18,1664]{1,0:T(8,128)S(1)}, u32[]{:S(2)}, u32[]{:S(2)}) %collective-permute-start.29) | collective-permute-done | bytes 119840 | tf_op jit(solution)/shard_map/ppermute | solution.py:246
  107.4 0.7 copy-done.24
  108.1 2.3 %shard_map.88 = f32[1,1664]{1,0:T(1,128)} custom-call(f32[18,1664]{1,0:T(8,128)} %copy-done.16, f32[18,1664]{1,0:T(8,128)} %copy-done.24, f32[1,1664]{1,0:T(1,128)} %copy-done.17, s32[1,1664]{1,0:T(1,128)} %copy-done.18, s32[1,1664]{1,0:T(1,128)} %copy-done.19, f32[1,1664]{1,0:T(1,128)} %copy-done.20), custom_call_target="tpu_custom_call" | custom-call | tf_op jit(solution)/shard_map/pallas_call | solution.py:230
  110.4 0.5 collective-permute-start.30
  110.9 3.3 %collective-permute-done.30 = f32[1,1664]{1,0:T(1,128)S(1)} collective-permute-done((f32[1,1664]{1,0:T(1,128)}, f32[1,1664]{1,0:T(1,128)S(1)}, u32[]{:S(2)}, u32[]{:S(2)}) %collective-permute-start.30) | collective-permute-done | bytes 6688 | tf_op jit(solution)/shard_map/ppermute | solution.py:246
  114.2 0.7 broadcast_select_fusion.1
  115.0 0.7 reshape.19
  (85 shorter events, 0.8 us)
Async XLA Ops:
  0.0 15.1 %collective-permute-start.1 = (bf16[2,256,512]{2,1,0:T(8,128)(2,1)}, bf16[2,256,512]{2,1,0:T(8,128)(2,1)S(1)}, u32[]{:S(2)}, u32[]{:S(2)}) collective-permute-start(bf16[2,256,512]{2,1,0:T(8,128)(2,1)} %source.3), channel_id=1, source_target_pairs={{0,8},{8,16},{16,24},{24,28},{28,20},{20,12},{12,4},{4,0},{1,9},{9... | collective-permute-start | bytes 1572872 | tf_op jit(solution)/shard_map/ppermute | solution.py:246
  3.0 13.6 %collective-permute-start.2 = (bf16[2,256,512]{2,1,0:T(8,128)(2,1)}, bf16[2,256,512]{2,1,0:T(8,128)(2,1)S(1)}, u32[]{:S(2)}, u32[]{:S(2)}) collective-permute-start(bf16[2,256,512]{2,1,0:T(8,128)(2,1)} %source.3), channel_id=1, source_target_pairs={{8,0},{16,8},{24,16},{28,24},{20,28},{12,20},{4,12},{0,4},{9,1},{1... | collective-permute-start | bytes 1572872 | tf_op jit(solution)/shard_map/ppermute | solution.py:246
  3.0 1.1 copy-start.15
  4.7 14.6 %copy-start.21 = (bf16[1,256,512]{2,1,0:T(8,128)(2,1)}, bf16[1,256,512]{2,1,0:T(8,128)(2,1)S(1)}, u32[]{:S(2)}) copy-start(bf16[1,256,512]{2,1,0:T(8,128)(2,1)S(1)} %get-tuple-element.23.refs_11_) | copy-start | bytes 786436
  4.8 8.4 %collective-permute-start.3 = (bf16[1,256,512]{2,1,0:T(8,128)(2,1)S(1)}, bf16[1,256,512]{2,1,0:T(8,128)(2,1)S(1)}, u32[]{:S(2)}, u32[]{:S(2)}) collective-permute-start(bf16[1,256,512]{2,1,0:T(8,128)(2,1)S(1)} %get-tuple-element.23.refs_11_), channel_id=1, source_target_pairs={{0,2},{1,3},{2,0},{3,1},{4,6},{5,7},{6,4},{7,5},{8,10},{9,11},{10,... | collective-permute-start | bytes 786440 | tf_op jit(solution)/shard_map/ppermute | solution.py:246
  6.8 14.6 %copy-start.25 = (f32[52,64]{1,0:T(8,128)S(1)}, f32[52,64]{1,0:T(8,128)}, u32[]{:S(2)}) copy-start(f32[52,64]{1,0:T(8,128)} %param.13) | copy-start | bytes 39940
  6.8 14.6 %copy-start.26 = (f32[52,64]{1,0:T(8,128)S(1)}, f32[52,64]{1,0:T(8,128)}, u32[]{:S(2)}) copy-start(f32[52,64]{1,0:T(8,128)} %param.10) | copy-start | bytes 39940
  6.8 14.7 %copy-start.27 = (s32[52,64]{1,0:T(8,128)S(1)}, s32[52,64]{1,0:T(8,128)}, u32[]{:S(2)}) copy-start(s32[52,64]{1,0:T(8,128)} %param.12) | copy-start | bytes 39940
  6.8 14.7 %copy-start.28 = (s32[52,64]{1,0:T(8,128)S(1)}, s32[52,64]{1,0:T(8,128)}, u32[]{:S(2)}) copy-start(s32[52,64]{1,0:T(8,128)} %param.11) | copy-start | bytes 39940
  6.8 6.3 %collective-permute-start.4 = (bf16[18,512]{1,0:T(8,128)(2,1)}, bf16[18,512]{1,0:T(8,128)(2,1)S(1)}, u32[]{:S(2)}, u32[]{:S(2)}) collective-permute-start(bf16[18,512]{1,0:T(8,128)(2,1)} %bitcast.16), channel_id=1, source_target_pairs={{0,2},{1,3},{2,0},{3,1},{4,6},{5,7},{6,4},{7,5},{8,10},{9,11},{10,... | collective-permute-start | bytes 55304 | tf_op jit(solution)/shard_map/ppermute | solution.py:246
  15.1 39.8 %copy-start.1 = (bf16[2,256,512]{2,1,0:T(8,128)(2,1)}, bf16[2,256,512]{2,1,0:T(8,128)(2,1)S(1)}, u32[]{:S(2)}) copy-start(bf16[2,256,512]{2,1,0:T(8,128)(2,1)S(1)} %collective-permute-done.1.refs_0_.refs_3_.refs_1_.refs_12_.refs_6_) | copy-start | bytes 1572868
  16.6 27.5 %copy-start = (bf16[2,256,512]{2,1,0:T(8,128)(2,1)}, bf16[2,256,512]{2,1,0:T(8,128)(2,1)S(1)}, u32[]{:S(2)}) copy-start(bf16[2,256,512]{2,1,0:T(8,128)(2,1)S(1)} %collective-permute-done.2.refs_2_.refs_4_.refs_1_.refs_16_.refs_9_) | copy-start | bytes 1572868
  17.7 12.7 %collective-permute-start.7 = (bf16[2,256,512]{2,1,0:T(8,128)(2,1)}, bf16[2,256,512]{2,1,0:T(8,128)(2,1)S(1)}, u32[]{:S(2)}, u32[]{:S(2)}) collective-permute-start(bf16[2,256,512]{2,1,0:T(8,128)(2,1)} %get-tuple-element.24.refs_5_), channel_id=1, source_target_pairs={{0,8},{8,16},{16,24},{24,28},{28,20},{20,12},{12,4},{4,0},{1,9},{9... | collective-permute-start | bytes 1572872 | tf_op jit(solution)/shard_map/ppermute | solution.py:246
  19.3 12.7 %collective-permute-start.8 = (bf16[2,256,512]{2,1,0:T(8,128)(2,1)S(1)}, bf16[2,256,512]{2,1,0:T(8,128)(2,1)}, u32[]{:S(2)}, u32[]{:S(2)}) collective-permute-start(bf16[2,256,512]{2,1,0:T(8,128)(2,1)S(1)} %get-tuple-element.25.refs_6_), channel_id=1, source_target_pairs={{8,0},{16,8},{24,16},{28,24},{20,28},{12,20},{4,12},{0,4},{9,1},{1... | collective-permute-start | bytes 1572872 | tf_op jit(solution)/shard_map/ppermute | solution.py:246
  19.8 6.4 %collective-permute-start.5 = (bf16[1,256,512]{2,1,0:T(8,128)(2,1)S(1)}, bf16[1,256,512]{2,1,0:T(8,128)(2,1)S(1)}, u32[]{:S(2)}, u32[]{:S(2)}) collective-permute-start(bf16[1,256,512]{2,1,0:T(8,128)(2,1)S(1)} %shard_map.76), channel_id=1, source_target_pairs={{0,2},{1,3},{2,0},{3,1},{4,6},{5,7},{6,4},{7,5},{8,10},{9,11},{10,... | collective-permute-start | bytes 786440 | tf_op jit(solution)/shard_map/ppermute | solution.py:246
  21.5 48.4 %copy-start.17 = (f32[1,1664]{1,0:T(1,128)}, f32[1,1664]{1,0:T(1,128)S(1)}, u32[]{:S(2)}) copy-start(f32[1,1664]{1,0:T(1,128)S(1)} %reshape.15.refs_8_.refs_27_.rewards) | copy-start | bytes 19972
  21.6 48.3 %copy-start.18 = (s32[1,1664]{1,0:T(1,128)}, s32[1,1664]{1,0:T(1,128)S(1)}, u32[]{:S(2)}) copy-start(s32[1,1664]{1,0:T(1,128)S(1)} %reshape.16.refs_9_.refs_28_.actions) | copy-start | bytes 19972
  21.7 48.2 %copy-start.19 = (s32[1,1664]{1,0:T(1,128)}, s32[1,1664]{1,0:T(1,128)S(1)}, u32[]{:S(2)}) copy-start(s32[1,1664]{1,0:T(1,128)S(1)} %reshape.17.refs_10_.refs_29_.done_flags) | copy-start | bytes 19972
  21.8 48.2 %copy-start.20 = (f32[1,1664]{1,0:T(1,128)}, f32[1,1664]{1,0:T(1,128)S(1)}, u32[]{:S(2)}) copy-start(f32[1,1664]{1,0:T(1,128)S(1)} %reshape.18.refs_11_.refs_30_.behaviour) | copy-start | bytes 19972
  21.8 2.0 %copy-start.7 = (bf16[3328,512]{1,0:T(8,128)(2,1)S(1)}, bf16[3328,512]{1,0:T(8,128)(2,1)}, u32[]{:S(2)}) copy-start(bf16[3328,512]{1,0:T(8,128)(2,1)} %source.2) | copy-start | bytes 10223620
  26.3 11.9 %collective-permute-start.6 = (bf16[512,512]{1,0:T(8,128)(2,1)S(1)}, bf16[512,512]{1,0:T(8,128)(2,1)S(1)}, u32[]{:S(2)}, u32[]{:S(2)}) collective-permute-start(bf16[512,512]{1,0:T(8,128)(2,1)S(1)} %shard_map.77), channel_id=1, source_target_pairs={{0,2},{1,3},{2,0},{3,1},{4,6},{5,7},{6,4},{7,5},{8,10},{9,11},{10,... | collective-permute-start | bytes 1572872 | tf_op jit(solution)/shard_map/ppermute | solution.py:246
  30.4 8.0 %copy-start.8 = (bf16[2,256,512]{2,1,0:T(8,128)(2,1)}, bf16[2,256,512]{2,1,0:T(8,128)(2,1)S(1)}, u32[]{:S(2)}) copy-start(bf16[2,256,512]{2,1,0:T(8,128)(2,1)S(1)} %collective-permute-done.7.refs_1_.refs_3_.refs_13_.refs_20_) | copy-start | bytes 1572868
  30.4 12.1 %collective-permute-start.10 = (bf16[2,256,512]{2,1,0:T(8,128)(2,1)S(1)}, bf16[2,256,512]{2,1,0:T(8,128)(2,1)S(1)}, u32[]{:S(2)}, u32[]{:S(2)}) collective-permute-start(bf16[2,256,512]{2,1,0:T(8,128)(2,1)S(1)} %collective-permute-done.7.refs_1_.refs_3_.refs_13_.refs_20_), channel_id=1, source_target_pairs={{0,8},{8,16},{16,24},{24,28},{28,20},{20,12},{12,4},{4,0},{1,9},{9... | collective-permute-start | bytes 1572872 | tf_op jit(solution)/shard_map/ppermute | solution.py:246
  32.0 12.1 %collective-permute-start.11 = (bf16[2,256,512]{2,1,0:T(8,128)(2,1)}, bf16[2,256,512]{2,1,0:T(8,128)(2,1)S(1)}, u32[]{:S(2)}, u32[]{:S(2)}) collective-permute-start(bf16[2,256,512]{2,1,0:T(8,128)(2,1)} %collective-permute-done.8.refs_2_.refs_4_.refs_17_.refs_24_), channel_id=1, source_target_pairs={{8,0},{16,8},{24,16},{28,24},{20,28},{12,20},{4,12},{0,4},{9,1},{1... | collective-permute-start | bytes 1572872 | tf_op jit(solution)/shard_map/ppermute | solution.py:246
  32.4 33.8 %collective-permute-start = (bf16[1664,512]{1,0:T(8,128)(2,1)}, bf16[1664,512]{1,0:T(8,128)(2,1)}, u32[]{:S(2)}, u32[]{:S(2)}) collective-permute-start(bf16[1664,512]{1,0:T(8,128)(2,1)} %get-tuple-element.21.refs_1_), channel_id=1, source_target_pairs={{0,1},{1,0},{2,3},{3,2},{4,5},{5,4},{6,7},{7,6},{8,9},{9,8},{10,11... | collective-permute-start | bytes 5111816 | tf_op jit(solution)/shard_map/ppermute | solution.py:246
  38.2 20.7 %copy-start.14 = (bf16[512,512]{1,0:T(8,128)(2,1)}, bf16[512,512]{1,0:T(8,128)(2,1)S(1)}, u32[]{:S(2)}) copy-start(bf16[512,512]{1,0:T(8,128)(2,1)S(1)} %collective-permute-done.6.refs_5_.refs_3_) | copy-start | bytes 1572868
  38.4 9.1 %collective-permute-start.9 = (bf16[384,512]{1,0:T(8,128)(2,1)S(1)}, bf16[384,512]{1,0:T(8,128)(2,1)S(1)}, u32[]{:S(2)}, u32[]{:S(2)}) collective-permute-start(bf16[384,512]{1,0:T(8,128)(2,1)S(1)} %shard_map.78), channel_id=1, source_target_pairs={{0,2},{1,3},{2,0},{3,1},{4,6},{5,7},{6,4},{7,5},{8,10},{9,11},{10,... | collective-permute-start | bytes 1179656 | tf_op jit(solution)/shard_map/ppermute | solution.py:246
  42.5 5.1 %copy-start.3 = (bf16[2,256,512]{2,1,0:T(8,128)(2,1)}, bf16[2,256,512]{2,1,0:T(8,128)(2,1)S(1)}, u32[]{:S(2)}) copy-start(bf16[2,256,512]{2,1,0:T(8,128)(2,1)S(1)} %collective-permute-done.10.refs_2_.refs_1_.refs_3_.refs_14_.refs_21_) | copy-start | bytes 1572868
  42.5 10.8 %collective-permute-start.13 = (bf16[2,256,512]{2,1,0:T(8,128)(2,1)S(1)}, bf16[2,256,512]{2,1,0:T(8,128)(2,1)S(1)}, u32[]{:S(2)}, u32[]{:S(2)}) collective-permute-start(bf16[2,256,512]{2,1,0:T(8,128)(2,1)S(1)} %collective-permute-done.10.refs_2_.refs_1_.refs_3_.refs_14_.refs_21_), channel_id=1, source_target_pairs={{0,8},{8,16},{16,24},{24,28},{28,20},{20,12},{12,4},{4,0},{1,9},{9... | collective-permute-start | bytes 1572872 | tf_op jit(solution)/shard_map/ppermute | solution.py:246
  44.1 3.5 %copy-start.4 = (bf16[2,256,512]{2,1,0:T(8,128)(2,1)}, bf16[2,256,512]{2,1,0:T(8,128)(2,1)S(1)}, u32[]{:S(2)}) copy-start(bf16[2,256,512]{2,1,0:T(8,128)(2,1)S(1)} %collective-permute-done.11.refs_0_.refs_3_.refs_2_.refs_18_.refs_25_) | copy-start | bytes 1572868
  44.2 10.7 %collective-permute-start.14 = (bf16[2,256,512]{2,1,0:T(8,128)(2,1)S(1)}, bf16[2,256,512]{2,1,0:T(8,128)(2,1)S(1)}, u32[]{:S(2)}, u32[]{:S(2)}) collective-permute-start(bf16[2,256,512]{2,1,0:T(8,128)(2,1)S(1)} %shard_map.79.refs_4_), channel_id=1, source_target_pairs={{8,0},{16,8},{24,16},{28,24},{20,28},{12,20},{4,12},{0,4},{9,1},{1... | collective-permute-start | bytes 1572872 | tf_op jit(solution)/shard_map/ppermute | solution.py:246
  47.7 9.4 %collective-permute-start.12 = (bf16[384,512]{1,0:T(8,128)(2,1)S(1)}, bf16[384,512]{1,0:T(8,128)(2,1)S(1)}, u32[]{:S(2)}, u32[]{:S(2)}) collective-permute-start(bf16[384,512]{1,0:T(8,128)(2,1)S(1)} %shard_map.80), channel_id=1, source_target_pairs={{0,2},{1,3},{2,0},{3,1},{4,6},{5,7},{6,4},{7,5},{8,10},{9,11},{10,... | collective-permute-start | bytes 1179656 | tf_op jit(solution)/shard_map/ppermute | solution.py:246
  53.3 3.9 %copy-start.6 = (bf16[2,256,512]{2,1,0:T(8,128)(2,1)}, bf16[2,256,512]{2,1,0:T(8,128)(2,1)S(1)}, u32[]{:S(2)}) copy-start(bf16[2,256,512]{2,1,0:T(8,128)(2,1)S(1)} %collective-permute-done.13.refs_0_.refs_4_.refs_1_.refs_15_.refs_22_) | copy-start | bytes 1572868
  54.8 2.4 %copy-start.5 = (bf16[2,256,512]{2,1,0:T(8,128)(2,1)}, bf16[2,256,512]{2,1,0:T(8,128)(2,1)S(1)}, u32[]{:S(2)}) copy-start(bf16[2,256,512]{2,1,0:T(8,128)(2,1)S(1)} %collective-permute-done.14.refs_2_.refs_5_.refs_26_.refs_10_) | copy-start | bytes 1572868
  55.0 10.3 %collective-permute-start.20 = (bf16[2,256,512]{2,1,0:T(8,128)(2,1)S(1)}, bf16[2,256,512]{2,1,0:T(8,128)(2,1)S(1)}, u32[]{:S(2)}, u32[]{:S(2)}) collective-permute-start(bf16[2,256,512]{2,1,0:T(8,128)(2,1)S(1)} %get-tuple-element.27.refs_3_), channel_id=1, source_target_pairs={{0,8},{8,16},{16,24},{24,28},{28,20},{20,12},{12,4},{4,0},{1,9},{9... | collective-permute-start | bytes 1572872 | tf_op jit(solution)/shard_map/ppermute | solution.py:246
  56.7 9.4 %collective-permute-start.21 = (bf16[2,256,512]{2,1,0:T(8,128)(2,1)S(1)}, bf16[2,256,512]{2,1,0:T(8,128)(2,1)S(1)}, u32[]{:S(2)}, u32[]{:S(2)}) collective-permute-start(bf16[2,256,512]{2,1,0:T(8,128)(2,1)S(1)} %get-tuple-element.28.refs_4_), channel_id=1, source_target_pairs={{8,0},{16,8},{24,16},{28,24},{20,28},{12,20},{4,12},{0,4},{9,1},{1... | collective-permute-start | bytes 1572872 | tf_op jit(solution)/shard_map/ppermute | solution.py:246
  57.3 7.9 %collective-permute-start.15 = (bf16[384,512]{1,0:T(8,128)(2,1)S(1)}, bf16[384,512]{1,0:T(8,128)(2,1)}, u32[]{:S(2)}, u32[]{:S(2)}) collective-permute-start(bf16[384,512]{1,0:T(8,128)(2,1)S(1)} %shard_map.82), channel_id=1, source_target_pairs={{0,2},{1,3},{2,0},{3,1},{4,6},{5,7},{6,4},{7,5},{8,10},{9,11},{10,... | collective-permute-start | bytes 1179656 | tf_op jit(solution)/shard_map/ppermute | solution.py:246
  58.8 9.4 %collective-permute-start.16 = (bf16[512,512]{1,0:T(8,128)(2,1)S(1)}, bf16[512,512]{1,0:T(8,128)(2,1)}, u32[]{:S(2)}, u32[]{:S(2)}) collective-permute-start(bf16[512,512]{1,0:T(8,128)(2,1)S(1)} %collective-permute-done.6.refs_5_.refs_3_), channel_id=1, source_target_pairs={{0,1},{1,0},{2,3},{3,2},{4,5},{5,4},{6,7},{7,6},{8,9},{9,8},{10,11... | collective-permute-start | bytes 1572872 | tf_op jit(solution)/shard_map/ppermute | solution.py:246
  65.2 4.6 %collective-permute-start.17 = (bf16[384,512]{1,0:T(8,128)(2,1)S(1)}, bf16[384,512]{1,0:T(8,128)(2,1)}, u32[]{:S(2)}, u32[]{:S(2)}) collective-permute-start(bf16[384,512]{1,0:T(8,128)(2,1)S(1)} %collective-permute-done.9.refs_5_.refs_4_), channel_id=1, source_target_pairs={{0,1},{1,0},{2,3},{3,2},{4,5},{5,4},{6,7},{7,6},{8,9},{9,8},{10,11... | collective-permute-start | bytes 1179656 | tf_op jit(solution)/shard_map/ppermute | solution.py:246
  65.2 4.7 %copy-start.12 = (bf16[2,256,512]{2,1,0:T(8,128)(2,1)}, bf16[2,256,512]{2,1,0:T(8,128)(2,1)S(1)}, u32[]{:S(2)}) copy-start(bf16[2,256,512]{2,1,0:T(8,128)(2,1)S(1)} %collective-permute-done.20.refs_23_.refs_0_.refs_3_.refs_7_) | copy-start | bytes 1572868
  65.2 4.7 %collective-permute-start.18 = (bf16[384,512]{1,0:T(8,128)(2,1)S(1)}, bf16[384,512]{1,0:T(8,128)(2,1)}, u32[]{:S(2)}, u32[]{:S(2)}) collective-permute-start(bf16[384,512]{1,0:T(8,128)(2,1)S(1)} %collective-permute-done.12.refs_5_), channel_id=1, source_target_pairs={{0,1},{1,0},{2,3},{3,2},{4,5},{5,4},{6,7},{7,6},{8,9},{9,8},{10,11... | collective-permute-start | bytes 1179656 | tf_op jit(solution)/shard_map/ppermute | solution.py:246
  66.0 16.8 %copy-start.13 = (bf16[2,256,512]{2,1,0:T(8,128)(2,1)}, bf16[2,256,512]{2,1,0:T(8,128)(2,1)S(1)}, u32[]{:S(2)}) copy-start(bf16[2,256,512]{2,1,0:T(8,128)(2,1)S(1)} %collective-permute-done.21.refs_2_.refs_4_.refs_11_.refs_17_) | copy-start | bytes 1572868
  66.0 3.9 %collective-permute-start.19 = (bf16[384,512]{1,0:T(8,128)(2,1)}, bf16[384,512]{1,0:T(8,128)(2,1)}, u32[]{:S(2)}, u32[]{:S(2)}) collective-permute-start(bf16[384,512]{1,0:T(8,128)(2,1)} %collective-permute-done.15.refs_6_), channel_id=1, source_target_pairs={{0,1},{1,0},{2,3},{3,2},{4,5},{5,4},{6,7},{7,6},{8,9},{9,8},{10,11... | collective-permute-start | bytes 1179656 | tf_op jit(solution)/shard_map/ppermute | solution.py:246
  66.3 16.6 %collective-permute-start.22 = (bf16[2,256,512]{2,1,0:T(8,128)(2,1)S(1)}, bf16[2,256,512]{2,1,0:T(8,128)(2,1)S(1)}, u32[]{:S(2)}, u32[]{:S(2)}) collective-permute-start(bf16[2,256,512]{2,1,0:T(8,128)(2,1)S(1)} %get-tuple-element.31), channel_id=1, source_target_pairs={{0,8},{8,16},{16,24},{24,28},{28,20},{20,12},{12,4},{4,0},{1,9},{9... | collective-permute-start | bytes 1572872 | tf_op jit(solution)/shard_map/ppermute | solution.py:246
  68.3 15.3 %collective-permute-start.24 = (bf16[2,256,512]{2,1,0:T(8,128)(2,1)S(1)}, bf16[2,256,512]{2,1,0:T(8,128)(2,1)S(1)}, u32[]{:S(2)}, u32[]{:S(2)}) collective-permute-start(bf16[2,256,512]{2,1,0:T(8,128)(2,1)S(1)} %get-tuple-element.32), channel_id=1, source_target_pairs={{0,2},{1,3},{2,0},{3,1},{4,6},{5,7},{6,4},{7,5},{8,10},{9,11},{10,... | collective-permute-start | bytes 1572872 | tf_op jit(solution)/shard_map/ppermute | solution.py:246
  69.8 13.8 %collective-permute-start.23 = (bf16[2,256,512]{2,1,0:T(8,128)(2,1)S(1)}, bf16[2,256,512]{2,1,0:T(8,128)(2,1)S(1)}, u32[]{:S(2)}, u32[]{:S(2)}) collective-permute-start(bf16[2,256,512]{2,1,0:T(8,128)(2,1)S(1)} %collective-permute-done.21.refs_2_.refs_4_.refs_11_.refs_17_), channel_id=1, source_target_pairs={{8,0},{16,8},{24,16},{28,24},{20,28},{12,20},{4,12},{0,4},{9,1},{1... | collective-permute-start | bytes 1572872 | tf_op jit(solution)/shard_map/ppermute | solution.py:246
  69.9 1.0 copy-start.22
  82.9 1.4 %copy-start.9 = (bf16[2,256,512]{2,1,0:T(8,128)(2,1)}, bf16[2,256,512]{2,1,0:T(8,128)(2,1)S(1)}, u32[]{:S(2)}) copy-start(bf16[2,256,512]{2,1,0:T(8,128)(2,1)S(1)} %collective-permute-done.22.refs_2_.refs_1_.refs_8_.refs_14_) | copy-start | bytes 1572868
  83.6 0.8 copy-start.11
  83.6 1.0 copy-start.10
  83.6 10.3 %copy-start.2 = (bf16[2,256,512]{2,1,0:T(8,128)(2,1)S(1)}, bf16[2,256,512]{2,1,0:T(8,128)(2,1)}, u32[]{:S(2)}) copy-start(bf16[2,256,512]{2,1,0:T(8,128)(2,1)} %copy-done.1) | copy-start | bytes 1572868
  83.6 10.3 %copy-start.23 = (bf16[512,18]{0,1:T(8,128)(2,1)S(1)}, bf16[512,18]{0,1:T(8,128)(2,1)}, u32[]{:S(2)}) copy-start(bf16[512,18]{0,1:T(8,128)(2,1)} %param.9) | copy-start | bytes 55300
  83.6 10.3 %collective-permute-start.25 = (bf16[1664,512]{1,0:T(8,128)(2,1)}, bf16[1664,512]{1,0:T(8,128)(2,1)}, u32[]{:S(2)}, u32[]{:S(2)}) collective-permute-start(bf16[1664,512]{1,0:T(8,128)(2,1)} %get-tuple-element.33.refs_3_.refs_1_), channel_id=1, source_target_pairs={{0,1},{1,0},{2,3},{3,2},{4,5},{5,4},{6,7},{7,6},{8,9},{9,8},{10,11... | collective-permute-start | bytes 5111816 | tf_op jit(solution)/shard_map/ppermute | solution.py:246
  83.7 10.2 %collective-permute-start.26 = (bf16[1664,512]{1,0:T(8,128)(2,1)}, bf16[1664,512]{1,0:T(8,128)(2,1)}, u32[]{:S(2)}, u32[]{:S(2)}) collective-permute-start(bf16[1664,512]{1,0:T(8,128)(2,1)} %get-tuple-element.34.refs_3_), channel_id=1, source_target_pairs={{0,1},{1,0},{2,3},{3,2},{4,5},{5,4},{6,7},{7,6},{8,9},{9,8},{10,11... | collective-permute-start | bytes 5111816 | tf_op jit(solution)/shard_map/ppermute | solution.py:246
  84.6 8.0 %collective-permute-start.27 = (bf16[1,256,512]{2,1,0:T(8,128)(2,1)S(1)}, bf16[1,256,512]{2,1,0:T(8,128)(2,1)S(1)}, u32[]{:S(2)}, u32[]{:S(2)}) collective-permute-start(bf16[1,256,512]{2,1,0:T(8,128)(2,1)S(1)} %get-tuple-element.35), channel_id=1, source_target_pairs={{0,8},{8,16},{16,24},{24,28},{28,20},{20,12},{12,4},{4,0},{1,9},{9... | collective-permute-start | bytes 786440 | tf_op jit(solution)/shard_map/ppermute | solution.py:246
  86.2 7.6 %collective-permute-start.28 = (bf16[1,256,512]{2,1,0:T(8,128)(2,1)S(1)}, bf16[1,256,512]{2,1,0:T(8,128)(2,1)S(1)}, u32[]{:S(2)}, u32[]{:S(2)}) collective-permute-start(bf16[1,256,512]{2,1,0:T(8,128)(2,1)S(1)} %get-tuple-element.36), channel_id=1, source_target_pairs={{8,0},{16,8},{24,16},{28,24},{20,28},{12,20},{4,12},{0,4},{9,1},{1... | collective-permute-start | bytes 786440 | tf_op jit(solution)/shard_map/ppermute | solution.py:246
  105.9 1.5 %copy-start.16 = (f32[18,1664]{1,0:T(8,128)}, f32[18,1664]{1,0:T(8,128)S(1)}, u32[]{:S(2)}) copy-start(f32[18,1664]{1,0:T(8,128)S(1)} %shard_map.87.q0) | copy-start | bytes 359428
  105.9 1.5 %collective-permute-start.29 = (f32[18,1664]{1,0:T(8,128)S(1)}, f32[18,1664]{1,0:T(8,128)S(1)}, u32[]{:S(2)}, u32[]{:S(2)}) collective-permute-start(f32[18,1664]{1,0:T(8,128)S(1)} %shard_map.87.q0), channel_id=1, source_target_pairs={{0,1},{1,0},{2,3},{3,2},{4,5},{5,4},{6,7},{7,6},{8,9},{9,8},{10,11... | collective-permute-start | bytes 359432 | tf_op jit(solution)/shard_map/ppermute | solution.py:246
  107.4 0.7 copy-start.24
  110.4 3.8 %collective-permute-start.30 = (f32[1,1664]{1,0:T(1,128)}, f32[1,1664]{1,0:T(1,128)S(1)}, u32[]{:S(2)}, u32[]{:S(2)}) collective-permute-start(f32[1,1664]{1,0:T(1,128)} %shard_map.88), channel_id=1, source_target_pairs={{0,2},{1,3},{2,0},{3,1},{4,6},{5,7},{6,4},{7,5},{8,10},{9,11},{10,... | collective-permute-start | bytes 19976 | tf_op jit(solution)/shard_map/ppermute | solution.py:246

commit v7 on v6

--- a/solution.py
+++ b/solution.py
@@ -204,11 +204,11 @@
     count, steps = q.shape
     scaled = 4.0 * q
     weights = jnp.exp(scaled - jnp.max(scaled, axis=0, keepdims=True))
-    probs = weights / jnp.sum(weights, axis=0, keepdims=True)
-    value = jnp.sum(probs * q, axis=0, keepdims=True)
+    share = 1.0 / jnp.sum(weights, axis=0, keepdims=True)
+    value = jnp.sum(weights * q, axis=0, keepdims=True) * share
     hit = lax.broadcasted_iota(jnp.int32, (count, steps), 0) == actions[...]
     taken = jnp.sum(jnp.where(hit, q, 0.0), axis=0, keepdims=True)
-    chosen = jnp.sum(jnp.where(hit, probs, 0.0), axis=0, keepdims=True)
+    chosen = jnp.sum(jnp.where(hit, weights, 0.0), axis=0, keepdims=True) * share
     trace = 0.95 * jnp.minimum(1.0, chosen / behaviour[...])
     keep = 0.99 * (1.0 - done_flags[...].astype(jnp.float32))
 

time: 116 us -> 116 us (level)
  no operation moved by 1% of the time
where the time goes in v7:
time: 116 us
  waiting for transfers between devices  47.9 us (41%)
  Pallas kernels  31.2 us (27%)
  starting transfers between devices  28.9 us (25%)
  local copies, waits for them, and re-layouts  6.35 us (5%)
    ppermute x31, waiting for transfers between devices, over(): return lambda a: lax.ppermute(a, axis, pairs)  47.9 us
    ppermute x31, starting transfers between devices, over(): return lambda a: lax.ppermute(a, axis, pairs)  28.9 us
    pallas_call x2, Pallas kernels, layer(): pl.pallas_call(functools.partial(layer_kernel, [len(h) for h in hs], bloc...  24 us
    unnamed x58, local copies, waits for them, and re-layouts  5.14 us
    pallas_call x2, Pallas kernels, cut(): pl.pallas_call(functools.partial(cut_kernel, len(sizes)), out_shape=[jax....  2.95 us
  transfers between devices with their start and end apart: 31, of which 17 were waited for; matrix products, arithmetic and copies ran while one was open for 1% of the time, Pallas kernels for 14%

profile of v7, /device:TPU:0, one launch (start us, length us, event | category | flops | bytes accessed | tf_op | source)
XLA Modules:
  0.0 115.6 jit_solution(2636668944383845596)
XLA Ops:
  0.0 3.0 %collective-permute-start.1 = (bf16[2,256,512]{2,1,0:T(8,128)(2,1)}, bf16[2,256,512]{2,1,0:T(8,128)(2,1)S(1)}, u32[]{:S(2)}, u32[]{:S(2)}) collective-permute-start(bf16[2,256,512]{2,1,0:T(8,128)(2,1)} %source.3), channel_id=1, source_target_pairs={{0,8},{8,16},{16,24},{24,28},{28,20},{20,12},{12,4},{4,0},{1,9},{9... | collective-permute-start | bytes 1572872 | tf_op jit(solution)/shard_map/ppermute | solution.py:246
  3.0 1.1 copy-done.15
  4.1 0.6 shard_map.74
  4.8 2.0 %collective-permute-start.3 = (bf16[1,256,512]{2,1,0:T(8,128)(2,1)S(1)}, bf16[1,256,512]{2,1,0:T(8,128)(2,1)S(1)}, u32[]{:S(2)}, u32[]{:S(2)}) collective-permute-start(bf16[1,256,512]{2,1,0:T(8,128)(2,1)S(1)} %get-tuple-element.23.refs_11_), channel_id=1, source_target_pairs={{0,2},{1,3},{2,0},{3,1},{4,6},{5,7},{6,4},{7,5},{8,10},{9,11},{10,... | collective-permute-start | bytes 786440 | tf_op jit(solution)/shard_map/ppermute | solution.py:246
  6.8 0.2 collective-permute-start.4
  6.9 6.2 %collective-permute-done.4.refs_6_.refs_4_.refs_22_ = bf16[18,512]{1,0:T(8,128)(2,1)S(1)} collective-permute-done((bf16[18,512]{1,0:T(8,128)(2,1)}, bf16[18,512]{1,0:T(8,128)(2,1)S(1)}, u32[]{:S(2)}, u32[]{:S(2)}) %collective-permute-start.4) | collective-permute-done | bytes 18464 | tf_op jit(solution)/shard_map/ppermute | solution.py:246
  13.1 1.9 %collective-permute-done.1.refs_0_.refs_3_.refs_1_.refs_12_.refs_6_ = bf16[2,256,512]{2,1,0:T(8,128)(2,1)S(1)} collective-permute-done((bf16[2,256,512]{2,1,0:T(8,128)(2,1)}, bf16[2,256,512]{2,1,0:T(8,128)(2,1)S(1)}, u32[]{:S(2)}, u32[]{:S(2)}) %collective-permute-start.1) | collective-permute-done | bytes 524320 | tf_op jit(solution)/shard_map/ppermute | solution.py:246
  15.1 1.5 %collective-permute-done.2.refs_2_.refs_4_.refs_1_.refs_16_.refs_9_ = bf16[2,256,512]{2,1,0:T(8,128)(2,1)S(1)} collective-permute-done((bf16[2,256,512]{2,1,0:T(8,128)(2,1)}, bf16[2,256,512]{2,1,0:T(8,128)(2,1)S(1)}, u32[]{:S(2)}, u32[]{:S(2)}) %collective-permute-start.2) | collective-permute-done | bytes 524320 | tf_op jit(solution)/shard_map/ppermute | solution.py:246
  16.6 1.0 shard_map.75
  17.7 1.6 %collective-permute-start.7 = (bf16[2,256,512]{2,1,0:T(8,128)(2,1)}, bf16[2,256,512]{2,1,0:T(8,128)(2,1)S(1)}, u32[]{:S(2)}, u32[]{:S(2)}) collective-permute-start(bf16[2,256,512]{2,1,0:T(8,128)(2,1)} %get-tuple-element.24.refs_5_), channel_id=1, source_target_pairs={{0,8},{8,16},{16,24},{24,28},{28,20},{20,12},{12,4},{4,0},{1,9},{9... | collective-permute-start | bytes 1572872 | tf_op jit(solution)/shard_map/ppermute | solution.py:246
  19.3 0.4 collective-permute-start.8
  19.8 1.6 %collective-permute-start.5 = (bf16[1,256,512]{2,1,0:T(8,128)(2,1)S(1)}, bf16[1,256,512]{2,1,0:T(8,128)(2,1)S(1)}, u32[]{:S(2)}, u32[]{:S(2)}) collective-permute-start(bf16[1,256,512]{2,1,0:T(8,128)(2,1)S(1)} %shard_map.76), channel_id=1, source_target_pairs={{0,2},{1,3},{2,0},{3,1},{4,6},{5,7},{6,4},{7,5},{8,10},{9,11},{10,... | collective-permute-start | bytes 786440 | tf_op jit(solution)/shard_map/ppermute | solution.py:246
  21.4 0.1 reshape.15.refs_8_.refs_27_.rewards
  21.5 0.1 reshape.16.refs_9_.refs_28_.actions
  21.6 0.1 reshape.17.refs_10_.refs_29_.done_flags
  21.8 2.0 %copy-done.7 = bf16[3328,512]{1,0:T(8,128)(2,1)S(1)} copy-done((bf16[3328,512]{1,0:T(8,128)(2,1)S(1)}, bf16[3328,512]{1,0:T(8,128)(2,1)}, u32[]{:S(2)}) %copy-start.7) | copy-done | bytes 3407896
  23.8 2.3 %shard_map.73 = (bf16[1664,512]{1,0:T(8,128)(2,1)}, bf16[1664,512]{1,0:T(8,128)(2,1)S(1)}) custom-call(s32[2]{0:T(128)S(1)} %pad_add_fusion.at, bf16[3328,512]{1,0:T(8,128)(2,1)S(1)} %copy-done.7), custom_call_target="tpu_custom_call" | custom-call | tf_op jit(solution)/shard_map/pallas_call | solution.py:38
  26.3 1.6 %collective-permute-start.6 = (bf16[512,512]{1,0:T(8,128)(2,1)S(1)}, bf16[512,512]{1,0:T(8,128)(2,1)S(1)}, u32[]{:S(2)}, u32[]{:S(2)}) collective-permute-start(bf16[512,512]{1,0:T(8,128)(2,1)S(1)} %shard_map.77), channel_id=1, source_target_pairs={{0,2},{1,3},{2,0},{3,1},{4,6},{5,7},{6,4},{7,5},{8,10},{9,11},{10,... | collective-permute-start | bytes 1572872 | tf_op jit(solution)/shard_map/ppermute | solution.py:246
  27.9 2.5 %collective-permute-done.7.refs_1_.refs_3_.refs_13_.refs_20_ = bf16[2,256,512]{2,1,0:T(8,128)(2,1)S(1)} collective-permute-done((bf16[2,256,512]{2,1,0:T(8,128)(2,1)}, bf16[2,256,512]{2,1,0:T(8,128)(2,1)S(1)}, u32[]{:S(2)}, u32[]{:S(2)}) %collective-permute-start.7) | collective-permute-done | bytes 524320 | tf_op jit(solution)/shard_map/ppermute | solution.py:246
  30.4 1.6 %collective-permute-start.10 = (bf16[2,256,512]{2,1,0:T(8,128)(2,1)S(1)}, bf16[2,256,512]{2,1,0:T(8,128)(2,1)S(1)}, u32[]{:S(2)}, u32[]{:S(2)}) collective-permute-start(bf16[2,256,512]{2,1,0:T(8,128)(2,1)S(1)} %collective-permute-done.7.refs_1_.refs_3_.refs_13_.refs_20_), channel_id=1, source_target_pairs={{0,8},{8,16},{16,24},{24,28},{28,20},{20,12},{12,4},{4,0},{1,9},{9... | collective-permute-start | bytes 1572872 | tf_op jit(solution)/shard_map/ppermute | solution.py:246
  32.0 0.5 collective-permute-start.11
  32.4 5.7 %collective-permute-done.6.refs_5_.refs_3_ = bf16[512,512]{1,0:T(8,128)(2,1)S(1)} collective-permute-done((bf16[512,512]{1,0:T(8,128)(2,1)S(1)}, bf16[512,512]{1,0:T(8,128)(2,1)S(1)}, u32[]{:S(2)}, u32[]{:S(2)}) %collective-permute-start.6) | collective-permute-done | bytes 524320 | tf_op jit(solution)/shard_map/ppermute | solution.py:246
  38.2 0.2 shard_map.78
  38.4 1.6 %collective-permute-start.9 = (bf16[384,512]{1,0:T(8,128)(2,1)S(1)}, bf16[384,512]{1,0:T(8,128)(2,1)S(1)}, u32[]{:S(2)}, u32[]{:S(2)}) collective-permute-start(bf16[384,512]{1,0:T(8,128)(2,1)S(1)} %shard_map.78), channel_id=1, source_target_pairs={{0,2},{1,3},{2,0},{3,1},{4,6},{5,7},{6,4},{7,5},{8,10},{9,11},{10,... | collective-permute-start | bytes 1179656 | tf_op jit(solution)/shard_map/ppermute | solution.py:246
  40.0 2.5 %collective-permute-done.10.refs_2_.refs_1_.refs_3_.refs_14_.refs_21_ = bf16[2,256,512]{2,1,0:T(8,128)(2,1)S(1)} collective-permute-done((bf16[2,256,512]{2,1,0:T(8,128)(2,1)S(1)}, bf16[2,256,512]{2,1,0:T(8,128)(2,1)S(1)}, u32[]{:S(2)}, u32[]{:S(2)}) %collective-permute-start.10) | collective-permute-done | bytes 524320 | tf_op jit(solution)/shard_map/ppermute | solution.py:246
  42.5 1.6 %collective-permute-start.13 = (bf16[2,256,512]{2,1,0:T(8,128)(2,1)S(1)}, bf16[2,256,512]{2,1,0:T(8,128)(2,1)S(1)}, u32[]{:S(2)}, u32[]{:S(2)}) collective-permute-start(bf16[2,256,512]{2,1,0:T(8,128)(2,1)S(1)} %collective-permute-done.10.refs_2_.refs_1_.refs_3_.refs_14_.refs_21_), channel_id=1, source_target_pairs={{0,8},{8,16},{16,24},{24,28},{28,20},{20,12},{12,4},{4,0},{1,9},{9... | collective-permute-start | bytes 1572872 | tf_op jit(solution)/shard_map/ppermute | solution.py:246
  44.2 0.5 collective-permute-start.14
  44.7 2.8 %collective-permute-done.9.refs_5_.refs_4_ = bf16[384,512]{1,0:T(8,128)(2,1)S(1)} collective-permute-done((bf16[384,512]{1,0:T(8,128)(2,1)S(1)}, bf16[384,512]{1,0:T(8,128)(2,1)S(1)}, u32[]{:S(2)}, u32[]{:S(2)}) %collective-permute-start.9) | collective-permute-done | bytes 393248 | tf_op jit(solution)/shard_map/ppermute | solution.py:246
  47.4 0.2 shard_map.80
  47.7 1.8 %collective-permute-start.12 = (bf16[384,512]{1,0:T(8,128)(2,1)S(1)}, bf16[384,512]{1,0:T(8,128)(2,1)S(1)}, u32[]{:S(2)}, u32[]{:S(2)}) collective-permute-start(bf16[384,512]{1,0:T(8,128)(2,1)S(1)} %shard_map.80), channel_id=1, source_target_pairs={{0,2},{1,3},{2,0},{3,1},{4,6},{5,7},{6,4},{7,5},{8,10},{9,11},{10,... | collective-permute-start | bytes 1179656 | tf_op jit(solution)/shard_map/ppermute | solution.py:246
  49.4 3.9 %collective-permute-done.13.refs_0_.refs_4_.refs_1_.refs_15_.refs_22_ = bf16[2,256,512]{2,1,0:T(8,128)(2,1)S(1)} collective-permute-done((bf16[2,256,512]{2,1,0:T(8,128)(2,1)S(1)}, bf16[2,256,512]{2,1,0:T(8,128)(2,1)S(1)}, u32[]{:S(2)}, u32[]{:S(2)}) %collective-permute-start.13) | collective-permute-done | bytes 524320 | tf_op jit(solution)/shard_map/ppermute | solution.py:246
  53.3 1.5 %collective-permute-done.14.refs_2_.refs_5_.refs_26_.refs_10_ = bf16[2,256,512]{2,1,0:T(8,128)(2,1)S(1)} collective-permute-done((bf16[2,256,512]{2,1,0:T(8,128)(2,1)S(1)}, bf16[2,256,512]{2,1,0:T(8,128)(2,1)S(1)}, u32[]{:S(2)}, u32[]{:S(2)}) %collective-permute-start.14) | collective-permute-done | bytes 524320 | tf_op jit(solution)/shard_map/ppermute | solution.py:246
  54.8 0.1 shard_map.81
  55.0 1.7 %collective-permute-start.20 = (bf16[2,256,512]{2,1,0:T(8,128)(2,1)S(1)}, bf16[2,256,512]{2,1,0:T(8,128)(2,1)S(1)}, u32[]{:S(2)}, u32[]{:S(2)}) collective-permute-start(bf16[2,256,512]{2,1,0:T(8,128)(2,1)S(1)} %get-tuple-element.27.refs_3_), channel_id=1, source_target_pairs={{0,8},{8,16},{16,24},{24,28},{28,20},{20,12},{12,4},{4,0},{1,9},{9... | collective-permute-start | bytes 1572872 | tf_op jit(solution)/shard_map/ppermute | solution.py:246
  56.7 0.4 collective-permute-start.21
  57.0 0.2 shard_map.82
  57.3 1.6 %collective-permute-start.15 = (bf16[384,512]{1,0:T(8,128)(2,1)S(1)}, bf16[384,512]{1,0:T(8,128)(2,1)}, u32[]{:S(2)}, u32[]{:S(2)}) collective-permute-start(bf16[384,512]{1,0:T(8,128)(2,1)S(1)} %shard_map.82), channel_id=1, source_target_pairs={{0,2},{1,3},{2,0},{3,1},{4,6},{5,7},{6,4},{7,5},{8,10},{9,11},{10,... | collective-permute-start | bytes 1179656 | tf_op jit(solution)/shard_map/ppermute | solution.py:246
  58.8 6.4 %collective-permute-done.15.refs_6_ = bf16[384,512]{1,0:T(8,128)(2,1)} collective-permute-done((bf16[384,512]{1,0:T(8,128)(2,1)S(1)}, bf16[384,512]{1,0:T(8,128)(2,1)}, u32[]{:S(2)}, u32[]{:S(2)}) %collective-permute-start.15) | collective-permute-done | bytes 393248 | tf_op jit(solution)/shard_map/ppermute | solution.py:246
  65.2 0.5 collective-permute-start.18
  65.7 0.3 collective-permute-done.21.refs_2_.refs_4_.refs_11_.refs_17_
  66.1 0.1 stack.95.refs_0_
  66.2 0.1 shard_map.84
  66.3 2.0 %collective-permute-start.22 = (bf16[2,256,512]{2,1,0:T(8,128)(2,1)S(1)}, bf16[2,256,512]{2,1,0:T(8,128)(2,1)S(1)}, u32[]{:S(2)}, u32[]{:S(2)}) collective-permute-start(bf16[2,256,512]{2,1,0:T(8,128)(2,1)S(1)} %get-tuple-element.31), channel_id=1, source_target_pairs={{0,8},{8,16},{16,24},{24,28},{28,20},{20,12},{12,4},{4,0},{1,9},{9... | collective-permute-start | bytes 1572872 | tf_op jit(solution)/shard_map/ppermute | solution.py:246
  68.3 1.5 %collective-permute-start.24 = (bf16[2,256,512]{2,1,0:T(8,128)(2,1)S(1)}, bf16[2,256,512]{2,1,0:T(8,128)(2,1)S(1)}, u32[]{:S(2)}, u32[]{:S(2)}) collective-permute-start(bf16[2,256,512]{2,1,0:T(8,128)(2,1)S(1)} %get-tuple-element.32), channel_id=1, source_target_pairs={{0,2},{1,3},{2,0},{3,1},{4,6},{5,7},{6,4},{7,5},{8,10},{9,11},{10,... | collective-permute-start | bytes 1572872 | tf_op jit(solution)/shard_map/ppermute | solution.py:246
  69.8 0.1 collective-permute-start.23
  70.0 0.9 copy-done.22
  70.9 11.9 %shard_map.83 = (bf16[1664,512]{1,0:T(8,128)(2,1)}, bf16[1664,512]{1,0:T(8,128)(2,1)}) custom-call(s32[20]{0:T(128)S(1)} %stack.95.refs_0_, bf16[1664,512]{1,0:T(8,128)(2,1)} %get-tuple-element.21.refs_1_, bf16[1664,512]{1,0:T(8,128)(2,1)} %collective-permute-done.refs_2_, bf16[512,512]{1,0:T(8,128)(2,1)} %copy-done.14, ...), custom_call_target="tpu_custom_call" | custom-call | flops 6979321856 | tf_op jit(solution)/shard_map/pallas_call | solution.py:188
  82.9 0.7 collective-permute-done.23.refs_3_.refs_2_.refs_12_.refs_18_
  83.7 0.5 collective-permute-start.26
  84.2 0.2 copy-done.11
  84.4 0.2 copy-done.10
  84.6 1.6 %collective-permute-start.27 = (bf16[1,256,512]{2,1,0:T(8,128)(2,1)S(1)}, bf16[1,256,512]{2,1,0:T(8,128)(2,1)S(1)}, u32[]{:S(2)}, u32[]{:S(2)}) collective-permute-start(bf16[1,256,512]{2,1,0:T(8,128)(2,1)S(1)} %get-tuple-element.35), channel_id=1, source_target_pairs={{0,8},{8,16},{16,24},{24,28},{28,20},{20,12},{12,4},{4,0},{1,9},{9... | collective-permute-start | bytes 786440 | tf_op jit(solution)/shard_map/ppermute | solution.py:246
  86.2 0.5 collective-permute-start.28
  86.7 0.1 stack.93.refs_0_
  86.8 5.8 %collective-permute-done.27.refs_16_ = bf16[1,256,512]{2,1,0:T(8,128)(2,1)S(1)} collective-permute-done((bf16[1,256,512]{2,1,0:T(8,128)(2,1)S(1)}, bf16[1,256,512]{2,1,0:T(8,128)(2,1)S(1)}, u32[]{:S(2)}, u32[]{:S(2)}) %collective-permute-start.27) | collective-permute-done | bytes 262176 | tf_op jit(solution)/shard_map/ppermute | solution.py:246
  92.6 1.3 %collective-permute-done.28.refs_20_ = bf16[1,256,512]{2,1,0:T(8,128)(2,1)S(1)} collective-permute-done((bf16[1,256,512]{2,1,0:T(8,128)(2,1)S(1)}, bf16[1,256,512]{2,1,0:T(8,128)(2,1)S(1)}, u32[]{:S(2)}, u32[]{:S(2)}) %collective-permute-start.28) | collective-permute-done | bytes 262176 | tf_op jit(solution)/shard_map/ppermute | solution.py:246
  93.9 12.0 %shard_map.87.q0 = f32[18,1664]{1,0:T(8,128)S(1)} custom-call(s32[20]{0:T(128)S(1)} %stack.93.refs_0_, bf16[1664,512]{1,0:T(8,128)(2,1)} %get-tuple-element.33.refs_3_.refs_1_, bf16[1664,512]{1,0:T(8,128)(2,1)} %collective-permute-done.25.refs_2_, bf16[1664,512]{1,0:T(8,128)(2,1)} %get-tuple-element.34.refs_3_, ...), custom_call_target="tpu_custom_call" | custom-call | flops 6979321856 | tf_op jit(solution)/shard_map/pallas_call | solution.py:188
  106.0 1.4 %collective-permute-done.29.q1 = f32[18,1664]{1,0:T(8,128)S(1)} collective-permute-done((f32[18,1664]{1,0:T(8,128)S(1)}, f32[18,1664]{1,0:T(8,128)S(1)}, u32[]{:S(2)}, u32[]{:S(2)}) %collective-permute-start.29) | collective-permute-done | bytes 119840 | tf_op jit(solution)/shard_map/ppermute | solution.py:246
  107.4 0.7 copy-done.24
  108.1 2.3 %shard_map.88 = f32[1,1664]{1,0:T(1,128)} custom-call(f32[18,1664]{1,0:T(8,128)} %copy-done.16, f32[18,1664]{1,0:T(8,128)} %copy-done.24, f32[1,1664]{1,0:T(1,128)} %copy-done.17, s32[1,1664]{1,0:T(1,128)} %copy-done.18, s32[1,1664]{1,0:T(1,128)} %copy-done.19, f32[1,1664]{1,0:T(1,128)} %copy-done.20), custom_call_target="tpu_custom_call" | custom-call | tf_op jit(solution)/shard_map/pallas_call | solution.py:230
  110.3 0.5 collective-permute-start.30
  110.9 3.3 %collective-permute-done.30 = f32[1,1664]{1,0:T(1,128)S(1)} collective-permute-done((f32[1,1664]{1,0:T(1,128)}, f32[1,1664]{1,0:T(1,128)S(1)}, u32[]{:S(2)}, u32[]{:S(2)}) %collective-permute-start.30) | collective-permute-done | bytes 6688 | tf_op jit(solution)/shard_map/ppermute | solution.py:246
  114.2 0.7 broadcast_select_fusion.1
  115.0 0.7 reshape.19
  (85 shorter events, 0.8 us)
Async XLA Ops:
  0.0 15.1 %collective-permute-start.1 = (bf16[2,256,512]{2,1,0:T(8,128)(2,1)}, bf16[2,256,512]{2,1,0:T(8,128)(2,1)S(1)}, u32[]{:S(2)}, u32[]{:S(2)}) collective-permute-start(bf16[2,256,512]{2,1,0:T(8,128)(2,1)} %source.3), channel_id=1, source_target_pairs={{0,8},{8,16},{16,24},{24,28},{28,20},{20,12},{12,4},{4,0},{1,9},{9... | collective-permute-start | bytes 1572872 | tf_op jit(solution)/shard_map/ppermute | solution.py:246
  3.0 13.6 %collective-permute-start.2 = (bf16[2,256,512]{2,1,0:T(8,128)(2,1)}, bf16[2,256,512]{2,1,0:T(8,128)(2,1)S(1)}, u32[]{:S(2)}, u32[]{:S(2)}) collective-permute-start(bf16[2,256,512]{2,1,0:T(8,128)(2,1)} %source.3), channel_id=1, source_target_pairs={{8,0},{16,8},{24,16},{28,24},{20,28},{12,20},{4,12},{0,4},{9,1},{1... | collective-permute-start | bytes 1572872 | tf_op jit(solution)/shard_map/ppermute | solution.py:246
  3.0 1.1 copy-start.15
  4.7 14.6 %copy-start.21 = (bf16[1,256,512]{2,1,0:T(8,128)(2,1)}, bf16[1,256,512]{2,1,0:T(8,128)(2,1)S(1)}, u32[]{:S(2)}) copy-start(bf16[1,256,512]{2,1,0:T(8,128)(2,1)S(1)} %get-tuple-element.23.refs_11_) | copy-start | bytes 786436
  4.8 8.4 %collective-permute-start.3 = (bf16[1,256,512]{2,1,0:T(8,128)(2,1)S(1)}, bf16[1,256,512]{2,1,0:T(8,128)(2,1)S(1)}, u32[]{:S(2)}, u32[]{:S(2)}) collective-permute-start(bf16[1,256,512]{2,1,0:T(8,128)(2,1)S(1)} %get-tuple-element.23.refs_11_), channel_id=1, source_target_pairs={{0,2},{1,3},{2,0},{3,1},{4,6},{5,7},{6,4},{7,5},{8,10},{9,11},{10,... | collective-permute-start | bytes 786440 | tf_op jit(solution)/shard_map/ppermute | solution.py:246
  6.8 14.6 %copy-start.25 = (f32[52,64]{1,0:T(8,128)S(1)}, f32[52,64]{1,0:T(8,128)}, u32[]{:S(2)}) copy-start(f32[52,64]{1,0:T(8,128)} %param.13) | copy-start | bytes 39940
  6.8 14.6 %copy-start.26 = (f32[52,64]{1,0:T(8,128)S(1)}, f32[52,64]{1,0:T(8,128)}, u32[]{:S(2)}) copy-start(f32[52,64]{1,0:T(8,128)} %param.10) | copy-start | bytes 39940
  6.8 14.7 %copy-start.27 = (s32[52,64]{1,0:T(8,128)S(1)}, s32[52,64]{1,0:T(8,128)}, u32[]{:S(2)}) copy-start(s32[52,64]{1,0:T(8,128)} %param.12) | copy-start | bytes 39940
  6.8 14.7 %copy-start.28 = (s32[52,64]{1,0:T(8,128)S(1)}, s32[52,64]{1,0:T(8,128)}, u32[]{:S(2)}) copy-start(s32[52,64]{1,0:T(8,128)} %param.11) | copy-start | bytes 39940
  6.8 6.3 %collective-permute-start.4 = (bf16[18,512]{1,0:T(8,128)(2,1)}, bf16[18,512]{1,0:T(8,128)(2,1)S(1)}, u32[]{:S(2)}, u32[]{:S(2)}) collective-permute-start(bf16[18,512]{1,0:T(8,128)(2,1)} %bitcast.16), channel_id=1, source_target_pairs={{0,2},{1,3},{2,0},{3,1},{4,6},{5,7},{6,4},{7,5},{8,10},{9,11},{10,... | collective-permute-start | bytes 55304 | tf_op jit(solution)/shard_map/ppermute | solution.py:246
  15.1 39.8 %copy-start.1 = (bf16[2,256,512]{2,1,0:T(8,128)(2,1)}, bf16[2,256,512]{2,1,0:T(8,128)(2,1)S(1)}, u32[]{:S(2)}) copy-start(bf16[2,256,512]{2,1,0:T(8,128)(2,1)S(1)} %collective-permute-done.1.refs_0_.refs_3_.refs_1_.refs_12_.refs_6_) | copy-start | bytes 1572868
  16.6 27.5 %copy-start = (bf16[2,256,512]{2,1,0:T(8,128)(2,1)}, bf16[2,256,512]{2,1,0:T(8,128)(2,1)S(1)}, u32[]{:S(2)}) copy-start(bf16[2,256,512]{2,1,0:T(8,128)(2,1)S(1)} %collective-permute-done.2.refs_2_.refs_4_.refs_1_.refs_16_.refs_9_) | copy-start | bytes 1572868
  17.7 12.7 %collective-permute-start.7 = (bf16[2,256,512]{2,1,0:T(8,128)(2,1)}, bf16[2,256,512]{2,1,0:T(8,128)(2,1)S(1)}, u32[]{:S(2)}, u32[]{:S(2)}) collective-permute-start(bf16[2,256,512]{2,1,0:T(8,128)(2,1)} %get-tuple-element.24.refs_5_), channel_id=1, source_target_pairs={{0,8},{8,16},{16,24},{24,28},{28,20},{20,12},{12,4},{4,0},{1,9},{9... | collective-permute-start | bytes 1572872 | tf_op jit(solution)/shard_map/ppermute | solution.py:246
  19.3 12.7 %collective-permute-start.8 = (bf16[2,256,512]{2,1,0:T(8,128)(2,1)S(1)}, bf16[2,256,512]{2,1,0:T(8,128)(2,1)}, u32[]{:S(2)}, u32[]{:S(2)}) collective-permute-start(bf16[2,256,512]{2,1,0:T(8,128)(2,1)S(1)} %get-tuple-element.25.refs_6_), channel_id=1, source_target_pairs={{8,0},{16,8},{24,16},{28,24},{20,28},{12,20},{4,12},{0,4},{9,1},{1... | collective-permute-start | bytes 1572872 | tf_op jit(solution)/shard_map/ppermute | solution.py:246
  19.8 6.4 %collective-permute-start.5 = (bf16[1,256,512]{2,1,0:T(8,128)(2,1)S(1)}, bf16[1,256,512]{2,1,0:T(8,128)(2,1)S(1)}, u32[]{:S(2)}, u32[]{:S(2)}) collective-permute-start(bf16[1,256,512]{2,1,0:T(8,128)(2,1)S(1)} %shard_map.76), channel_id=1, source_target_pairs={{0,2},{1,3},{2,0},{3,1},{4,6},{5,7},{6,4},{7,5},{8,10},{9,11},{10,... | collective-permute-start | bytes 786440 | tf_op jit(solution)/shard_map/ppermute | solution.py:246
  21.5 48.4 %copy-start.17 = (f32[1,1664]{1,0:T(1,128)}, f32[1,1664]{1,0:T(1,128)S(1)}, u32[]{:S(2)}) copy-start(f32[1,1664]{1,0:T(1,128)S(1)} %reshape.15.refs_8_.refs_27_.rewards) | copy-start | bytes 19972
  21.6 48.3 %copy-start.18 = (s32[1,1664]{1,0:T(1,128)}, s32[1,1664]{1,0:T(1,128)S(1)}, u32[]{:S(2)}) copy-start(s32[1,1664]{1,0:T(1,128)S(1)} %reshape.16.refs_9_.refs_28_.actions) | copy-start | bytes 19972
  21.7 48.2 %copy-start.19 = (s32[1,1664]{1,0:T(1,128)}, s32[1,1664]{1,0:T(1,128)S(1)}, u32[]{:S(2)}) copy-start(s32[1,1664]{1,0:T(1,128)S(1)} %reshape.17.refs_10_.refs_29_.done_flags) | copy-start | bytes 19972
  21.8 48.2 %copy-start.20 = (f32[1,1664]{1,0:T(1,128)}, f32[1,1664]{1,0:T(1,128)S(1)}, u32[]{:S(2)}) copy-start(f32[1,1664]{1,0:T(1,128)S(1)} %reshape.18.refs_11_.refs_30_.behaviour) | copy-start | bytes 19972
  21.8 2.0 %copy-start.7 = (bf16[3328,512]{1,0:T(8,128)(2,1)S(1)}, bf16[3328,512]{1,0:T(8,128)(2,1)}, u32[]{:S(2)}) copy-start(bf16[3328,512]{1,0:T(8,128)(2,1)} %source.2) | copy-start | bytes 10223620
  26.3 11.9 %collective-permute-start.6 = (bf16[512,512]{1,0:T(8,128)(2,1)S(1)}, bf16[512,512]{1,0:T(8,128)(2,1)S(1)}, u32[]{:S(2)}, u32[]{:S(2)}) collective-permute-start(bf16[512,512]{1,0:T(8,128)(2,1)S(1)} %shard_map.77), channel_id=1, source_target_pairs={{0,2},{1,3},{2,0},{3,1},{4,6},{5,7},{6,4},{7,5},{8,10},{9,11},{10,... | collective-permute-start | bytes 1572872 | tf_op jit(solution)/shard_map/ppermute | solution.py:246
  30.4 8.0 %copy-start.8 = (bf16[2,256,512]{2,1,0:T(8,128)(2,1)}, bf16[2,256,512]{2,1,0:T(8,128)(2,1)S(1)}, u32[]{:S(2)}) copy-start(bf16[2,256,512]{2,1,0:T(8,128)(2,1)S(1)} %collective-permute-done.7.refs_1_.refs_3_.refs_13_.refs_20_) | copy-start | bytes 1572868
  30.4 12.1 %collective-permute-start.10 = (bf16[2,256,512]{2,1,0:T(8,128)(2,1)S(1)}, bf16[2,256,512]{2,1,0:T(8,128)(2,1)S(1)}, u32[]{:S(2)}, u32[]{:S(2)}) collective-permute-start(bf16[2,256,512]{2,1,0:T(8,128)(2,1)S(1)} %collective-permute-done.7.refs_1_.refs_3_.refs_13_.refs_20_), channel_id=1, source_target_pairs={{0,8},{8,16},{16,24},{24,28},{28,20},{20,12},{12,4},{4,0},{1,9},{9... | collective-permute-start | bytes 1572872 | tf_op jit(solution)/shard_map/ppermute | solution.py:246
  32.0 12.1 %collective-permute-start.11 = (bf16[2,256,512]{2,1,0:T(8,128)(2,1)}, bf16[2,256,512]{2,1,0:T(8,128)(2,1)S(1)}, u32[]{:S(2)}, u32[]{:S(2)}) collective-permute-start(bf16[2,256,512]{2,1,0:T(8,128)(2,1)} %collective-permute-done.8.refs_2_.refs_4_.refs_17_.refs_24_), channel_id=1, source_target_pairs={{8,0},{16,8},{24,16},{28,24},{20,28},{12,20},{4,12},{0,4},{9,1},{1... | collective-permute-start | bytes 1572872 | tf_op jit(solution)/shard_map/ppermute | solution.py:246
  32.4 33.8 %collective-permute-start = (bf16[1664,512]{1,0:T(8,128)(2,1)}, bf16[1664,512]{1,0:T(8,128)(2,1)}, u32[]{:S(2)}, u32[]{:S(2)}) collective-permute-start(bf16[1664,512]{1,0:T(8,128)(2,1)} %get-tuple-element.21.refs_1_), channel_id=1, source_target_pairs={{0,1},{1,0},{2,3},{3,2},{4,5},{5,4},{6,7},{7,6},{8,9},{9,8},{10,11... | collective-permute-start | bytes 5111816 | tf_op jit(solution)/shard_map/ppermute | solution.py:246
  38.2 20.7 %copy-start.14 = (bf16[512,512]{1,0:T(8,128)(2,1)}, bf16[512,512]{1,0:T(8,128)(2,1)S(1)}, u32[]{:S(2)}) copy-start(bf16[512,512]{1,0:T(8,128)(2,1)S(1)} %collective-permute-done.6.refs_5_.refs_3_) | copy-start | bytes 1572868
  38.4 9.1 %collective-permute-start.9 = (bf16[384,512]{1,0:T(8,128)(2,1)S(1)}, bf16[384,512]{1,0:T(8,128)(2,1)S(1)}, u32[]{:S(2)}, u32[]{:S(2)}) collective-permute-start(bf16[384,512]{1,0:T(8,128)(2,1)S(1)} %shard_map.78), channel_id=1, source_target_pairs={{0,2},{1,3},{2,0},{3,1},{4,6},{5,7},{6,4},{7,5},{8,10},{9,11},{10,... | collective-permute-start | bytes 1179656 | tf_op jit(solution)/shard_map/ppermute | solution.py:246
  42.5 5.1 %copy-start.3 = (bf16[2,256,512]{2,1,0:T(8,128)(2,1)}, bf16[2,256,512]{2,1,0:T(8,128)(2,1)S(1)}, u32[]{:S(2)}) copy-start(bf16[2,256,512]{2,1,0:T(8,128)(2,1)S(1)} %collective-permute-done.10.refs_2_.refs_1_.refs_3_.refs_14_.refs_21_) | copy-start | bytes 1572868
  42.5 10.8 %collective-permute-start.13 = (bf16[2,256,512]{2,1,0:T(8,128)(2,1)S(1)}, bf16[2,256,512]{2,1,0:T(8,128)(2,1)S(1)}, u32[]{:S(2)}, u32[]{:S(2)}) collective-permute-start(bf16[2,256,512]{2,1,0:T(8,128)(2,1)S(1)} %collective-permute-done.10.refs_2_.refs_1_.refs_3_.refs_14_.refs_21_), channel_id=1, source_target_pairs={{0,8},{8,16},{16,24},{24,28},{28,20},{20,12},{12,4},{4,0},{1,9},{9... | collective-permute-start | bytes 1572872 | tf_op jit(solution)/shard_map/ppermute | solution.py:246
  44.1 3.5 %copy-start.4 = (bf16[2,256,512]{2,1,0:T(8,128)(2,1)}, bf16[2,256,512]{2,1,0:T(8,128)(2,1)S(1)}, u32[]{:S(2)}) copy-start(bf16[2,256,512]{2,1,0:T(8,128)(2,1)S(1)} %collective-permute-done.11.refs_0_.refs_3_.refs_2_.refs_18_.refs_25_) | copy-start | bytes 1572868
  44.2 10.7 %collective-permute-start.14 = (bf16[2,256,512]{2,1,0:T(8,128)(2,1)S(1)}, bf16[2,256,512]{2,1,0:T(8,128)(2,1)S(1)}, u32[]{:S(2)}, u32[]{:S(2)}) collective-permute-start(bf16[2,256,512]{2,1,0:T(8,128)(2,1)S(1)} %shard_map.79.refs_4_), channel_id=1, source_target_pairs={{8,0},{16,8},{24,16},{28,24},{20,28},{12,20},{4,12},{0,4},{9,1},{1... | collective-permute-start | bytes 1572872 | tf_op jit(solution)/shard_map/ppermute | solution.py:246
  47.7 9.4 %collective-permute-start.12 = (bf16[384,512]{1,0:T(8,128)(2,1)S(1)}, bf16[384,512]{1,0:T(8,128)(2,1)S(1)}, u32[]{:S(2)}, u32[]{:S(2)}) collective-permute-start(bf16[384,512]{1,0:T(8,128)(2,1)S(1)} %shard_map.80), channel_id=1, source_target_pairs={{0,2},{1,3},{2,0},{3,1},{4,6},{5,7},{6,4},{7,5},{8,10},{9,11},{10,... | collective-permute-start | bytes 1179656 | tf_op jit(solution)/shard_map/ppermute | solution.py:246
  53.3 3.9 %copy-start.6 = (bf16[2,256,512]{2,1,0:T(8,128)(2,1)}, bf16[2,256,512]{2,1,0:T(8,128)(2,1)S(1)}, u32[]{:S(2)}) copy-start(bf16[2,256,512]{2,1,0:T(8,128)(2,1)S(1)} %collective-permute-done.13.refs_0_.refs_4_.refs_1_.refs_15_.refs_22_) | copy-start | bytes 1572868
  54.8 2.4 %copy-start.5 = (bf16[2,256,512]{2,1,0:T(8,128)(2,1)}, bf16[2,256,512]{2,1,0:T(8,128)(2,1)S(1)}, u32[]{:S(2)}) copy-start(bf16[2,256,512]{2,1,0:T(8,128)(2,1)S(1)} %collective-permute-done.14.refs_2_.refs_5_.refs_26_.refs_10_) | copy-start | bytes 1572868
  55.0 10.3 %collective-permute-start.20 = (bf16[2,256,512]{2,1,0:T(8,128)(2,1)S(1)}, bf16[2,256,512]{2,1,0:T(8,128)(2,1)S(1)}, u32[]{:S(2)}, u32[]{:S(2)}) collective-permute-start(bf16[2,256,512]{2,1,0:T(8,128)(2,1)S(1)} %get-tuple-element.27.refs_3_), channel_id=1, source_target_pairs={{0,8},{8,16},{16,24},{24,28},{28,20},{20,12},{12,4},{4,0},{1,9},{9... | collective-permute-start | bytes 1572872 | tf_op jit(solution)/shard_map/ppermute | solution.py:246
  56.7 9.4 %collective-permute-start.21 = (bf16[2,256,512]{2,1,0:T(8,128)(2,1)S(1)}, bf16[2,256,512]{2,1,0:T(8,128)(2,1)S(1)}, u32[]{:S(2)}, u32[]{:S(2)}) collective-permute-start(bf16[2,256,512]{2,1,0:T(8,128)(2,1)S(1)} %get-tuple-element.28.refs_4_), channel_id=1, source_target_pairs={{8,0},{16,8},{24,16},{28,24},{20,28},{12,20},{4,12},{0,4},{9,1},{1... | collective-permute-start | bytes 1572872 | tf_op jit(solution)/shard_map/ppermute | solution.py:246
  57.3 7.9 %collective-permute-start.15 = (bf16[384,512]{1,0:T(8,128)(2,1)S(1)}, bf16[384,512]{1,0:T(8,128)(2,1)}, u32[]{:S(2)}, u32[]{:S(2)}) collective-permute-start(bf16[384,512]{1,0:T(8,128)(2,1)S(1)} %shard_map.82), channel_id=1, source_target_pairs={{0,2},{1,3},{2,0},{3,1},{4,6},{5,7},{6,4},{7,5},{8,10},{9,11},{10,... | collective-permute-start | bytes 1179656 | tf_op jit(solution)/shard_map/ppermute | solution.py:246
  58.8 9.4 %collective-permute-start.16 = (bf16[512,512]{1,0:T(8,128)(2,1)S(1)}, bf16[512,512]{1,0:T(8,128)(2,1)}, u32[]{:S(2)}, u32[]{:S(2)}) collective-permute-start(bf16[512,512]{1,0:T(8,128)(2,1)S(1)} %collective-permute-done.6.refs_5_.refs_3_), channel_id=1, source_target_pairs={{0,1},{1,0},{2,3},{3,2},{4,5},{5,4},{6,7},{7,6},{8,9},{9,8},{10,11... | collective-permute-start | bytes 1572872 | tf_op jit(solution)/shard_map/ppermute | solution.py:246
  65.2 4.6 %collective-permute-start.17 = (bf16[384,512]{1,0:T(8,128)(2,1)S(1)}, bf16[384,512]{1,0:T(8,128)(2,1)}, u32[]{:S(2)}, u32[]{:S(2)}) collective-permute-start(bf16[384,512]{1,0:T(8,128)(2,1)S(1)} %collective-permute-done.9.refs_5_.refs_4_), channel_id=1, source_target_pairs={{0,1},{1,0},{2,3},{3,2},{4,5},{5,4},{6,7},{7,6},{8,9},{9,8},{10,11... | collective-permute-start | bytes 1179656 | tf_op jit(solution)/shard_map/ppermute | solution.py:246
  65.2 4.7 %copy-start.12 = (bf16[2,256,512]{2,1,0:T(8,128)(2,1)}, bf16[2,256,512]{2,1,0:T(8,128)(2,1)S(1)}, u32[]{:S(2)}) copy-start(bf16[2,256,512]{2,1,0:T(8,128)(2,1)S(1)} %collective-permute-done.20.refs_23_.refs_0_.refs_3_.refs_7_) | copy-start | bytes 1572868
  65.2 4.7 %collective-permute-start.18 = (bf16[384,512]{1,0:T(8,128)(2,1)S(1)}, bf16[384,512]{1,0:T(8,128)(2,1)}, u32[]{:S(2)}, u32[]{:S(2)}) collective-permute-start(bf16[384,512]{1,0:T(8,128)(2,1)S(1)} %collective-permute-done.12.refs_5_), channel_id=1, source_target_pairs={{0,1},{1,0},{2,3},{3,2},{4,5},{5,4},{6,7},{7,6},{8,9},{9,8},{10,11... | collective-permute-start | bytes 1179656 | tf_op jit(solution)/shard_map/ppermute | solution.py:246
  66.0 16.8 %copy-start.13 = (bf16[2,256,512]{2,1,0:T(8,128)(2,1)}, bf16[2,256,512]{2,1,0:T(8,128)(2,1)S(1)}, u32[]{:S(2)}) copy-start(bf16[2,256,512]{2,1,0:T(8,128)(2,1)S(1)} %collective-permute-done.21.refs_2_.refs_4_.refs_11_.refs_17_) | copy-start | bytes 1572868
  66.0 3.9 %collective-permute-start.19 = (bf16[384,512]{1,0:T(8,128)(2,1)}, bf16[384,512]{1,0:T(8,128)(2,1)}, u32[]{:S(2)}, u32[]{:S(2)}) collective-permute-start(bf16[384,512]{1,0:T(8,128)(2,1)} %collective-permute-done.15.refs_6_), channel_id=1, source_target_pairs={{0,1},{1,0},{2,3},{3,2},{4,5},{5,4},{6,7},{7,6},{8,9},{9,8},{10,11... | collective-permute-start | bytes 1179656 | tf_op jit(solution)/shard_map/ppermute | solution.py:246
  66.3 16.6 %collective-permute-start.22 = (bf16[2,256,512]{2,1,0:T(8,128)(2,1)S(1)}, bf16[2,256,512]{2,1,0:T(8,128)(2,1)S(1)}, u32[]{:S(2)}, u32[]{:S(2)}) collective-permute-start(bf16[2,256,512]{2,1,0:T(8,128)(2,1)S(1)} %get-tuple-element.31), channel_id=1, source_target_pairs={{0,8},{8,16},{16,24},{24,28},{28,20},{20,12},{12,4},{4,0},{1,9},{9... | collective-permute-start | bytes 1572872 | tf_op jit(solution)/shard_map/ppermute | solution.py:246
  68.3 15.3 %collective-permute-start.24 = (bf16[2,256,512]{2,1,0:T(8,128)(2,1)S(1)}, bf16[2,256,512]{2,1,0:T(8,128)(2,1)S(1)}, u32[]{:S(2)}, u32[]{:S(2)}) collective-permute-start(bf16[2,256,512]{2,1,0:T(8,128)(2,1)S(1)} %get-tuple-element.32), channel_id=1, source_target_pairs={{0,2},{1,3},{2,0},{3,1},{4,6},{5,7},{6,4},{7,5},{8,10},{9,11},{10,... | collective-permute-start | bytes 1572872 | tf_op jit(solution)/shard_map/ppermute | solution.py:246
  69.8 13.8 %collective-permute-start.23 = (bf16[2,256,512]{2,1,0:T(8,128)(2,1)S(1)}, bf16[2,256,512]{2,1,0:T(8,128)(2,1)S(1)}, u32[]{:S(2)}, u32[]{:S(2)}) collective-permute-start(bf16[2,256,512]{2,1,0:T(8,128)(2,1)S(1)} %collective-permute-done.21.refs_2_.refs_4_.refs_11_.refs_17_), channel_id=1, source_target_pairs={{8,0},{16,8},{24,16},{28,24},{20,28},{12,20},{4,12},{0,4},{9,1},{1... | collective-permute-start | bytes 1572872 | tf_op jit(solution)/shard_map/ppermute | solution.py:246
  69.9 1.0 copy-start.22
  82.9 1.4 %copy-start.9 = (bf16[2,256,512]{2,1,0:T(8,128)(2,1)}, bf16[2,256,512]{2,1,0:T(8,128)(2,1)S(1)}, u32[]{:S(2)}) copy-start(bf16[2,256,512]{2,1,0:T(8,128)(2,1)S(1)} %collective-permute-done.22.refs_2_.refs_1_.refs_8_.refs_14_) | copy-start | bytes 1572868
  83.6 0.8 copy-start.11
  83.6 1.0 copy-start.10
  83.6 10.3 %copy-start.2 = (bf16[2,256,512]{2,1,0:T(8,128)(2,1)S(1)}, bf16[2,256,512]{2,1,0:T(8,128)(2,1)}, u32[]{:S(2)}) copy-start(bf16[2,256,512]{2,1,0:T(8,128)(2,1)} %copy-done.1) | copy-start | bytes 1572868
  83.6 10.3 %copy-start.23 = (bf16[512,18]{0,1:T(8,128)(2,1)S(1)}, bf16[512,18]{0,1:T(8,128)(2,1)}, u32[]{:S(2)}) copy-start(bf16[512,18]{0,1:T(8,128)(2,1)} %param.9) | copy-start | bytes 55300
  83.6 10.3 %collective-permute-start.25 = (bf16[1664,512]{1,0:T(8,128)(2,1)}, bf16[1664,512]{1,0:T(8,128)(2,1)}, u32[]{:S(2)}, u32[]{:S(2)}) collective-permute-start(bf16[1664,512]{1,0:T(8,128)(2,1)} %get-tuple-element.33.refs_3_.refs_1_), channel_id=1, source_target_pairs={{0,1},{1,0},{2,3},{3,2},{4,5},{5,4},{6,7},{7,6},{8,9},{9,8},{10,11... | collective-permute-start | bytes 5111816 | tf_op jit(solution)/shard_map/ppermute | solution.py:246
  83.7 10.2 %collective-permute-start.26 = (bf16[1664,512]{1,0:T(8,128)(2,1)}, bf16[1664,512]{1,0:T(8,128)(2,1)}, u32[]{:S(2)}, u32[]{:S(2)}) collective-permute-start(bf16[1664,512]{1,0:T(8,128)(2,1)} %get-tuple-element.34.refs_3_), channel_id=1, source_target_pairs={{0,1},{1,0},{2,3},{3,2},{4,5},{5,4},{6,7},{7,6},{8,9},{9,8},{10,11... | collective-permute-start | bytes 5111816 | tf_op jit(solution)/shard_map/ppermute | solution.py:246
  84.6 8.0 %collective-permute-start.27 = (bf16[1,256,512]{2,1,0:T(8,128)(2,1)S(1)}, bf16[1,256,512]{2,1,0:T(8,128)(2,1)S(1)}, u32[]{:S(2)}, u32[]{:S(2)}) collective-permute-start(bf16[1,256,512]{2,1,0:T(8,128)(2,1)S(1)} %get-tuple-element.35), channel_id=1, source_target_pairs={{0,8},{8,16},{16,24},{24,28},{28,20},{20,12},{12,4},{4,0},{1,9},{9... | collective-permute-start | bytes 786440 | tf_op jit(solution)/shard_map/ppermute | solution.py:246
  86.2 7.6 %collective-permute-start.28 = (bf16[1,256,512]{2,1,0:T(8,128)(2,1)S(1)}, bf16[1,256,512]{2,1,0:T(8,128)(2,1)S(1)}, u32[]{:S(2)}, u32[]{:S(2)}) collective-permute-start(bf16[1,256,512]{2,1,0:T(8,128)(2,1)S(1)} %get-tuple-element.36), channel_id=1, source_target_pairs={{8,0},{16,8},{24,16},{28,24},{20,28},{12,20},{4,12},{0,4},{9,1},{1... | collective-permute-start | bytes 786440 | tf_op jit(solution)/shard_map/ppermute | solution.py:246
  105.9 1.5 %copy-start.16 = (f32[18,1664]{1,0:T(8,128)}, f32[18,1664]{1,0:T(8,128)S(1)}, u32[]{:S(2)}) copy-start(f32[18,1664]{1,0:T(8,128)S(1)} %shard_map.87.q0) | copy-start | bytes 359428
  105.9 1.5 %collective-permute-start.29 = (f32[18,1664]{1,0:T(8,128)S(1)}, f32[18,1664]{1,0:T(8,128)S(1)}, u32[]{:S(2)}, u32[]{:S(2)}) collective-permute-start(f32[18,1664]{1,0:T(8,128)S(1)} %shard_map.87.q0), channel_id=1, source_target_pairs={{0,1},{1,0},{2,3},{3,2},{4,5},{5,4},{6,7},{7,6},{8,9},{9,8},{10,11... | collective-permute-start | bytes 359432 | tf_op jit(solution)/shard_map/ppermute | solution.py:246
  107.4 0.7 copy-start.24
  110.3 3.8 %collective-permute-start.30 = (f32[1,1664]{1,0:T(1,128)}, f32[1,1664]{1,0:T(1,128)S(1)}, u32[]{:S(2)}, u32[]{:S(2)}) collective-permute-start(f32[1,1664]{1,0:T(1,128)} %shard_map.88), channel_id=1, source_target_pairs={{0,2},{1,3},{2,0},{3,1},{4,6},{5,7},{6,4},{7,5},{8,10},{9,11},{10,... | collective-permute-start | bytes 19976 | tf_op jit(solution)/shard_map/ppermute | solution.py:246
